TPU v7x, 32 devices: a whole 2x2x4 slice. The times are simulated.
32 devices in a mesh: head: 8 (over y, x, core), seq: 4 (over z).
Axes of the slice: x: 2, y: 2, z: 4, core: 2. Of those that a mesh axis runs over, the one named last changes fastest.
Arguments:
- inputs: bfloat16 [4, 4, 1024, 1024], P(None, 'seq', 'head'), may hold values from -6 to 6
- skips: bfloat16 [4, 4, 1024, 1024], P(None, 'seq', 'head'), may hold values from -6 to 6
- flow_time: float32 [4, 4, 1024], P(None, 'seq', 'head'), may hold values from 0 to 1, as said below
- segment_ids: int32 [4, 4, 1024], P(None, 'seq', 'head'), may hold values from 0 to 7, as said below
- frame_mask: int32 [4, 4, 1024], P(None, 'seq', 'head'), may hold values from 0 to 1, as said below
- cotangent: bfloat16 [4, 4, 1024, 1024], P(None, 'seq', 'head'), may hold values from -6 to 6
- w_skip: bfloat16 [2048, 1024], replicated, may hold values from -0.125 to 0.125
- w_time: bfloat16 [256, 4096], replicated, may hold values from -0.375 to 0.375
- w_qkv: bfloat16 [1024, 3072], replicated, may hold values from -0.1875 to 0.1875
- w_out: bfloat16 [1024, 1024], replicated, may hold values from -0.375 to 0.375
- w_up: bfloat16 [1024, 4096], replicated, may hold values from -0.1875 to 0.1875
- w_down: bfloat16 [4096, 1024], replicated, may hold values from -0.09375 to 0.09375
Outputs:
- output: bfloat16 [4, 4, 1024, 1024], P(None, 'seq', 'head')
- input_grad: float32 [4, 4, 1024, 1024], P(None, 'seq', 'head')
- skip_grad: float32 [4, 4, 1024, 1024], P(None, 'seq', 'head')
- grad_skip: float32 [2048, 1024], P(('head', 'seq'))
- grad_time: float32 [256, 4096], P(('head', 'seq'))
- grad_qkv: float32 [1024, 3072], P(('head', 'seq'))
- grad_out: float32 [1024, 1024], P(('head', 'seq'))
- grad_up: float32 [1024, 4096], P(('head', 'seq'))
- grad_down: float32 [4096, 1024], P(('head', 'seq'))
Inputs may be any that keep to these rules, and one draw needn't show every extreme that they name: segment_ids never fall along a bucket, start at 0 and rise by 0 or 1 from frame to frame. frame_mask is 1 on a leading run of each bucket and 0 after it, with at most 64 zeros in a bucket. flow_time is equal on all frames of one segment.
All inputs are finite; a program needn't handle non-finite values.
Results may differ from a plain program's by a relative error of at most 0.015.
Values may be sent and summed in bfloat16 or wider, within the bound.
No kernel may reach another device: no remote copies, remote signals or barrier semaphores. Data moves between devices by JAX's collectives and lax.ppermute only.
A program may use at most 320 MiB of HBM per device.

v0:
```python
from functools import partial
import math

import jax
import jax.numpy as jnp
from jax import lax
from jax.sharding import PartitionSpec as P

HD = 64


eps_norm = 1e-06
neg_fill = -1e30


def modulated_norm(hidden, shift_term, scale_term):
    centre = jnp.mean(hidden, axis=-1, keepdims=True)
    centered = hidden - centre
    spread = jnp.mean(centered * centered, axis=-1, keepdims=True)
    return centered * lax.rsqrt(spread + eps_norm) * (1.0 + scale_term) + shift_term


def gelu_tanh(values):
    return jax.nn.gelu(values, approximate=True)


def time_features(times, feature_count):
    half_size = feature_count // 2
    freq_steps = jnp.exp(
        jnp.arange(half_size, dtype=jnp.float32) * (-math.log(10000.0) / (half_size - 1))
    )
    angles = 1000.0 * times[..., None] * freq_steps
    return jnp.concatenate([jnp.sin(angles), jnp.cos(angles)], axis=-1)


def rotate_mid(values, cos_table, sin_table):
    half_size = values.shape[1] // 2
    turned = jnp.concatenate([-values[:, half_size:], values[:, :half_size]], axis=1)
    return values * cos_table + turned * sin_table


def rotate_both(queries, key_rows, cos_table, sin_table):
    return (rotate_mid(queries, cos_table, sin_table), rotate_mid(key_rows, cos_table, sin_table))


def permitted_scores(q_block, key_rows, seg_row, mask_row, first_row, score_factor):
    block_rows = q_block.shape[2]
    bucket_len = key_rows.shape[2]
    raw_scores = (
        jnp.einsum("hdi,hdj->hij", q_block, key_rows, preferred_element_type=jnp.float32)
        * score_factor
    )
    seg_query = lax.dynamic_slice_in_dim(seg_row, first_row, block_rows)
    query_place = first_row + lax.broadcasted_iota(jnp.int32, (block_rows, 1), 0)
    key_place = lax.broadcasted_iota(jnp.int32, (1, bucket_len), 1)
    allowed = (seg_query[:, None] == seg_row[None, :]) & (
        (mask_row[None, :] == 1) | (query_place == key_place)
    )
    return jnp.where(allowed[None], raw_scores, neg_fill)


def attend(packed, seg_row, mask_row, block_rows, score_factor):
    queries, key_rows, values = (packed[0], packed[1], packed[2])
    local_heads, head_size, bucket_len = queries.shape

    def one_block(block_index, state_carry):
        attended, log_totals = state_carry
        first_row = block_index * block_rows
        q_block = lax.dynamic_slice_in_dim(queries, first_row, block_rows, axis=2)
        scores = permitted_scores(q_block, key_rows, seg_row, mask_row, first_row, score_factor)
        row_max = jnp.max(scores, axis=-1, keepdims=True)
        powered = jnp.exp(scores - row_max)
        row_total = jnp.sum(powered, axis=-1, keepdims=True)
        attn_probs = (powered / row_total).astype(jnp.bfloat16)
        out_block = jnp.einsum(
            "hij,hdj->hdi", attn_probs, values, preferred_element_type=jnp.float32
        )
        attended = lax.dynamic_update_slice_in_dim(
            attended, out_block.astype(jnp.bfloat16), first_row, axis=2
        )
        log_block = (row_max + jnp.log(row_total))[..., 0]
        log_totals = lax.dynamic_update_slice_in_dim(log_totals, log_block, first_row, axis=1)
        return (attended, log_totals)

    start_state = (
        jnp.zeros((local_heads, head_size, bucket_len), jnp.bfloat16),
        jnp.zeros((local_heads, bucket_len), jnp.float32),
    )
    return lax.fori_loop(0, bucket_len // block_rows, one_block, start_state)


def attend_back(packed, log_totals, grad_heads, seg_row, mask_row, block_rows, score_factor):
    queries, key_rows, values = (packed[0], packed[1], packed[2])
    bucket_len = queries.shape[2]

    def one_block(block_index, state_carry):
        grad_queries, grad_keys, grad_values = state_carry
        first_row = block_index * block_rows
        q_block = lax.dynamic_slice_in_dim(queries, first_row, block_rows, axis=2)
        grad_block = lax.dynamic_slice_in_dim(grad_heads, first_row, block_rows, axis=2)
        log_block = lax.dynamic_slice_in_dim(log_totals, first_row, block_rows, axis=1)
        scores = permitted_scores(q_block, key_rows, seg_row, mask_row, first_row, score_factor)
        soft_rows = jnp.exp(scores - log_block[..., None])
        grad_values = grad_values + jnp.einsum(
            "hij,hdi->hdj",
            soft_rows.astype(jnp.bfloat16),
            grad_block,
            preferred_element_type=jnp.float32,
        )
        grad_probs = jnp.einsum(
            "hdi,hdj->hij", grad_block, values, preferred_element_type=jnp.float32
        )
        centre = jnp.sum(soft_rows * grad_probs, axis=-1, keepdims=True)
        grad_scores = (soft_rows * (grad_probs - centre)).astype(jnp.bfloat16)
        query_grad_block = (
            jnp.einsum("hij,hdj->hdi", grad_scores, key_rows, preferred_element_type=jnp.float32)
            * score_factor
        )
        grad_queries = lax.dynamic_update_slice_in_dim(
            grad_queries, query_grad_block, first_row, axis=2
        )
        grad_keys = (
            grad_keys
            + jnp.einsum("hij,hdi->hdj", grad_scores, q_block, preferred_element_type=jnp.float32)
            * score_factor
        )
        return (grad_queries, grad_keys, grad_values)

    zero_grads = jnp.zeros(queries.shape, jnp.float32)
    grad_parts = lax.fori_loop(
        0, bucket_len // block_rows, one_block, (zero_grads, zero_grads, zero_grads)
    )
    return jnp.stack(grad_parts).astype(jnp.bfloat16)


def per_device(
    inputs,
    skips,
    flow_time,
    segment_ids,
    frame_mask,
    cotangent,
    w_skip,
    w_time,
    w_qkv,
    w_out,
    w_up,
    w_down,
):
    groups = lax.axis_size("head")
    micro_count, frame_rows, model_width = (inputs.shape[0], inputs.shape[2], inputs.shape[3])
    head_count = model_width // HD
    bucket_len = frame_rows * groups
    block_rows = min(512, bucket_len)
    score_factor = HD ** (-0.5)
    dims_first = (((0,), (0,)), ((), ()))
    dims_last = (((1,), (1,)), ((), ()))
    seg_rows, mask_rows = (
        lax.all_gather(segment_ids.reshape(micro_count, frame_rows), "head", axis=1, tiled=True),
        lax.all_gather(frame_mask.reshape(micro_count, frame_rows), "head", axis=1, tiled=True),
    )
    frame_place = lax.broadcasted_iota(jnp.int32, (micro_count, bucket_len), 1)
    boundary = jnp.concatenate(
        [jnp.ones((micro_count, 1), jnp.bool_), seg_rows[:, 1:] != seg_rows[:, :-1]], axis=1
    )
    starts = lax.cummax(jnp.where(boundary, frame_place, 0), axis=1)
    positions = lax.dynamic_slice_in_dim(
        frame_place - starts, lax.axis_index("head") * frame_rows, frame_rows, axis=1
    )
    inv_freq = jnp.exp(jnp.arange(HD // 2, dtype=jnp.float32) * (-2.0 * math.log(10000.0) / HD))
    weights = (w_skip, w_time, w_qkv, w_out, w_up, w_down)
    totals = tuple((jnp.zeros(weight.shape, jnp.float32) for weight in weights))
    outputs, input_grads, skip_grads = ([], [], [])
    for micro_index in range(micro_count):
        joined = jnp.concatenate([inputs[micro_index, 0], skips[micro_index, 0]], axis=1)
        resid_in = jnp.dot(joined, w_skip, preferred_element_type=jnp.float32)
        features = time_features(flow_time[micro_index, 0], w_time.shape[0]).astype(jnp.bfloat16)
        modulation = jnp.dot(features, w_time, preferred_element_type=jnp.float32)
        shift_first, scale_first, shift_second, scale_second = jnp.split(modulation, 4, axis=1)
        normed_attn, pull_first = jax.vjp(modulated_norm, resid_in, shift_first, scale_first)
        normed_attn = normed_attn.astype(jnp.bfloat16)
        projected = lax.dot_general(
            w_qkv, normed_attn, (((0,), (1,)), ((), ())), preferred_element_type=jnp.float32
        )
        projected = projected.reshape(3, head_count, HD, frame_rows)
        angles = inv_freq[:, None] * positions[micro_index].astype(jnp.float32)[None, :]
        cos_table = jnp.concatenate([jnp.cos(angles), jnp.cos(angles)], axis=0)
        sin_table = jnp.concatenate([jnp.sin(angles), jnp.sin(angles)], axis=0)
        rotated, pull_rotate = jax.vjp(
            partial(rotate_both, cos_table=cos_table, sin_table=sin_table),
            projected[0],
            projected[1],
        )
        packed = jnp.stack([rotated[0], rotated[1], projected[2]]).astype(jnp.bfloat16)
        heads_view = lax.all_to_all(packed, "head", split_axis=1, concat_axis=3, tiled=True)
        attended, log_totals = attend(
            heads_view, seg_rows[micro_index], mask_rows[micro_index], block_rows, score_factor
        )
        returned = lax.all_to_all(
            attended, "head", split_axis=2, concat_axis=0, tiled=True
        ).reshape(model_width, frame_rows)
        resid_mid = resid_in + lax.dot_general(
            returned, w_out, dims_first, preferred_element_type=jnp.float32
        )
        normed_ffn, pull_second = jax.vjp(modulated_norm, resid_mid, shift_second, scale_second)
        normed_ffn = normed_ffn.astype(jnp.bfloat16)
        up_proj = jnp.dot(normed_ffn, w_up, preferred_element_type=jnp.float32)
        activated, pull_gelu = jax.vjp(gelu_tanh, up_proj)
        hidden = activated.astype(jnp.bfloat16)
        outputs.append(
            (resid_mid + jnp.dot(hidden, w_down, preferred_element_type=jnp.float32)).astype(
                jnp.bfloat16
            )
        )
        cot_rows = cotangent[micro_index, 0]
        grad_down = lax.dot_general(
            hidden, cot_rows, dims_first, preferred_element_type=jnp.float32
        )
        grad_hidden = lax.dot_general(
            cot_rows, w_down, dims_last, preferred_element_type=jnp.float32
        )
        grad_up_proj = pull_gelu(grad_hidden)[0].astype(jnp.bfloat16)
        grad_up = lax.dot_general(
            normed_ffn, grad_up_proj, dims_first, preferred_element_type=jnp.float32
        )
        grad_normed_ffn = lax.dot_general(
            grad_up_proj, w_up, dims_last, preferred_element_type=jnp.float32
        )
        grad_mid_norm, grad_shift_second, grad_scale_second = pull_second(grad_normed_ffn)
        grad_mid = cot_rows.astype(jnp.float32) + grad_mid_norm
        grad_mid_low = grad_mid.astype(jnp.bfloat16)
        grad_out = lax.dot_general(
            returned, grad_mid_low, (((1,), (0,)), ((), ())), preferred_element_type=jnp.float32
        )
        grad_returned = lax.dot_general(
            w_out, grad_mid_low, dims_last, preferred_element_type=jnp.float32
        )
        grad_returned = grad_returned.astype(jnp.bfloat16).reshape(head_count, HD, frame_rows)
        grad_heads = lax.all_to_all(grad_returned, "head", split_axis=0, concat_axis=2, tiled=True)
        grad_packed = attend_back(
            heads_view,
            log_totals,
            grad_heads,
            seg_rows[micro_index],
            mask_rows[micro_index],
            block_rows,
            score_factor,
        )
        grad_frames = lax.all_to_all(grad_packed, "head", split_axis=3, concat_axis=1, tiled=True)
        grad_rot_query, grad_rot_key = pull_rotate(
            (grad_frames[0].astype(jnp.float32), grad_frames[1].astype(jnp.float32))
        )
        grad_proj = jnp.stack(
            [grad_rot_query, grad_rot_key, grad_frames[2].astype(jnp.float32)]
        ).astype(jnp.bfloat16)
        grad_proj = grad_proj.reshape(3 * model_width, frame_rows)
        grad_qkv = lax.dot_general(
            normed_attn, grad_proj, (((0,), (1,)), ((), ())), preferred_element_type=jnp.float32
        )
        grad_normed_attn = lax.dot_general(
            grad_proj, w_qkv, (((0,), (1,)), ((), ())), preferred_element_type=jnp.float32
        )
        grad_in_norm, grad_shift_first, grad_scale_first = pull_first(grad_normed_attn)
        grad_in_low = (grad_mid + grad_in_norm).astype(jnp.bfloat16)
        grad_skip = lax.dot_general(
            joined, grad_in_low, dims_first, preferred_element_type=jnp.float32
        )
        grad_joined = lax.dot_general(
            grad_in_low, w_skip, dims_last, preferred_element_type=jnp.float32
        )
        input_grads.append(grad_joined[:, :model_width])
        skip_grads.append(grad_joined[:, model_width:])
        grad_modulation = jnp.concatenate(
            [grad_shift_first, grad_scale_first, grad_shift_second, grad_scale_second], axis=1
        ).astype(jnp.bfloat16)
        grad_time = lax.dot_general(
            features, grad_modulation, dims_first, preferred_element_type=jnp.float32
        )
        local_grads = (grad_skip, grad_time, grad_qkv, grad_out, grad_up, grad_down)
        totals = jax.tree.map(jnp.add, totals, local_grads)
    totals = lax.psum_scatter(totals, ("head", "seq"), scatter_dimension=0, tiled=True)
    output = jnp.stack(outputs)[:, None]
    input_grad = jnp.stack(input_grads)[:, None]
    skip_grad = jnp.stack(skip_grads)[:, None]
    return (output, input_grad, skip_grad) + tuple(totals)


def solution(mesh):
    return jax.shard_map(
        per_device,
        mesh=mesh,
        in_specs=(
            P(None, "seq", "head", None),
            P(None, "seq", "head", None),
            P(None, "seq", "head"),
            P(None, "seq", "head"),
            P(None, "seq", "head"),
            P(None, "seq", "head", None),
            P(),
            P(),
            P(),
            P(),
            P(),
            P(),
        ),
        out_specs=(
            P(None, "seq", "head", None),
            P(None, "seq", "head", None),
            P(None, "seq", "head", None),
            P(("head", "seq"), None),
            P(("head", "seq"), None),
            P(("head", "seq"), None),
            P(("head", "seq"), None),
            P(("head", "seq"), None),
            P(("head", "seq"), None),
        ),
        check_vma=False,
    )
```

profile of v0, /device:TPU:0, one launch (start us, length us, event | category | flops | bytes accessed | tf_op | source)
XLA Modules:
  0.0 1828.7 jit_solution(14402305479708995776)
XLA Ops:
  20.1 10.3 all-gather
  81.8 9.3 all-gather.1
  95.9 9.2 while.132
  112.1 9.2 while.133
  130.6 9.2 while.134
  146.6 9.2 while.135
  168.3 4.3 all-to-all-done.3
  195.1 4.8 fusion.405
  199.9 7.7 fusion.168
  213.6 7.7 fusion.161
  227.6 7.7 fusion.154
  251.9 4.8 fusion.406
  256.7 7.8 fusion.175
  264.6 4.4 fusion.376
  270.7 4.3 all-to-all-start.8
  296.1 15.4 while.137
  320.8 4.4 all-to-all-start.11
  325.4 15.4 while.136
  350.1 4.7 all-to-all-start.9
  354.9 15.4 while.138
  377.6 4.2 all-to-all-start.13
  404.3 5.8 fusion.377
  435.9 7.4 add_add_fusion.4
  448.5 15.6 while.139
  473.7 4.2 all-to-all-start.15
  484.1 7.8 all-to-all-done.15
  501.3 5.3 fusion.375
  514.2 4.5 fusion.278
  519.0 8.4 add_add_fusion.3
  528.6 6.3 fusion.411
  534.9 6.4 fusion.412
  541.3 6.4 fusion.413
  547.7 17.8 add_add_fusion.2
  567.1 8.2 fusion.309
  575.3 8.3 fusion.303
  583.6 8.1 fusion.297
  591.7 23.2 %add_add_fusion = f32[4096,1024]{1,0:T(8,128)} fusion(f32[4096,1024]{1,0:T(8,128)} %fusion.297, f32[4096,1024]{1,0:T(8,128)} %fusion.309, f32[4096,1024]{1,0:T(8,128)} %fusion.303, bf16[4,1,128,1024]{3,2,1,0:T(8,128)(2,1)S(1)} %copy-done.66, f32[128,4096]{1,0:T(8,128)S(1)} %copy-done.84), kind=kOutput, calls=%fused_computation.200 | convolution fusion | flops 1091043328 | bytes 69468160 | tf_op jit(solution)/shard_map/dot_general | solution.py:216
  616.1 8.1 fusion.417
  624.3 8.2 fusion.418
  632.5 8.2 fusion.419
  640.7 23.5 %add_add_fusion.1 = f32[1024,4096]{1,0:T(8,128)} fusion(f32[1024,4096]{1,0:T(8,128)} %fusion.419, f32[1024,4096]{1,0:T(8,128)} %fusion.417, f32[1024,4096]{1,0:T(8,128)} %fusion.418, bf16[128,1024]{1,0:T(8,128)(2,1)S(1)} %copy-done.126, bf16[128,4096]{1,0:T(8,128)(2,1)S(1)} %copy-done.104), kind=kOutput, calls=%fused_computation.201 | convolution fusion | flops 1086324736 | bytes 68419584 | tf_op jit(solution)/shard_map/dot_general | solution.py:223
  665.2 5.7 fusion.184
  671.0 5.1 fusion.185
  692.2 50.7 %reduce-scatter.9.cloned.1.call-done = f32[8,4096]{1,0:T(8,128)} async-done(((f32[256,4096]{1,0:T(8,128)}), f32[8,4096]{1,0:T(8,128)}) %reduce-scatter.9.cloned.1.call-update) | async-done | bytes 131088 | tf_op jit(solution)/shard_map/reduce_scatter | solution.py:281
  743.0 187.6 %reduce-scatter.7.cloned.1.call-done = f32[64,1024]{1,0:T(8,128)} async-done(((f32[2048,1024]{1,0:T(8,128)}), f32[64,1024]{1,0:T(8,128)}) %reduce-scatter.7.cloned.1.call-update) | async-done | bytes 262160 | tf_op jit(solution)/shard_map/reduce_scatter | solution.py:281
  930.5 159.9 %reduce-scatter.11.cloned.1.call-done = f32[32,3072]{1,0:T(8,128)} async-done(((f32[1024,3072]{1,0:T(8,128)}), f32[32,3072]{1,0:T(8,128)}) %reduce-scatter.11.cloned.1.call-update) | async-done | bytes 393232 | tf_op jit(solution)/shard_map/reduce_scatter | solution.py:281
  1090.4 366.2 %reduce-scatter.17.cloned.1.call-done = f32[128,1024]{1,0:T(8,128)} async-done(((f32[4096,1024]{1,0:T(8,128)}), f32[128,1024]{1,0:T(8,128)}) %reduce-scatter.17.cloned.1.call-update) | async-done | bytes 524304 | tf_op jit(solution)/shard_map/reduce_scatter | solution.py:281
  1456.6 365.0 %reduce-scatter.15.cloned.1.call-done = f32[32,4096]{1,0:T(8,128)} async-done(((f32[1024,4096]{1,0:T(8,128)}), f32[32,4096]{1,0:T(8,128)}) %reduce-scatter.15.cloned.1.call-update) | async-done | bytes 524304 | tf_op jit(solution)/shard_map/reduce_scatter | solution.py:281
  (1156 shorter events, 405.4 us)
Async XLA Ops:
  10.3 50.0 %copy-start.132 = (bf16[128,1024]{1,0:T(8,128)(2,1)}, bf16[128,1024]{1,0:T(8,128)(2,1)S(1)}, u32[]{:S(2)}) copy-start(bf16[128,1024]{1,0:T(8,128)(2,1)S(1)} %get-tuple-element.1878) | copy-start | bytes 786436
  15.3 40.0 %copy-start.221 = (bf16[128,128]{1,0:T(8,128)(2,1)}, bf16[128,128]{1,0:T(8,128)(2,1)S(1)}, u32[]{:S(2)}) copy-start(bf16[128,128]{1,0:T(8,128)(2,1)S(1)} %get-tuple-element.2024) | copy-start | bytes 98308
  15.3 46.1 %copy-start.217 = (bf16[128,128]{1,0:T(8,128)(2,1)}, bf16[128,128]{1,0:T(8,128)(2,1)S(1)}, u32[]{:S(2)}) copy-start(bf16[128,128]{1,0:T(8,128)(2,1)S(1)} %get-tuple-element.2026) | copy-start | bytes 98308
  15.3 46.1 %copy-start.219 = (bf16[128,128]{1,0:T(8,128)(2,1)}, bf16[128,128]{1,0:T(8,128)(2,1)S(1)}, u32[]{:S(2)}) copy-start(bf16[128,128]{1,0:T(8,128)(2,1)S(1)} %get-tuple-element.2027) | copy-start | bytes 98308
  39.0 52.1 %all-to-all-start = ((bf16[3,16,64,128]{3,2,0,1:T(8,128)(2,1)}), bf16[3,16,64,128]{3,2,0,1:T(8,128)(2,1)S(1)}, u32[]{:S(2)}, u32[]{:S(2)}) async-start(bf16[3,16,64,128]{3,2,0,1:T(8,128)(2,1)} %copy.147), calls=%async_computation | async-start | bytes 1572864 | tf_op jit(solution)/shard_map/all_to_all | solution.py:195
  66.8 10.7 copy-start.215
  67.5 11.4 copy-start.209
  67.5 11.4 copy-start.229
  91.1 16.3 all-to-all-start.2
  107.4 16.1 all-to-all-start.4
  124.4 17.0 all-to-all-start.6
  141.4 19.9 %all-to-all-start.1 = ((bf16[8,2,8192]{2,1,0:T(2,128)(2,1)}), bf16[8,2,8192]{2,1,0:T(2,128)(2,1)S(1)}, u32[]{:S(2)}, u32[]{:S(2)}) async-start(bf16[8,2,8192]{2,1,0:T(2,128)(2,1)} %reshape.1545), calls=%async_computation.1 | async-start | bytes 524288 | tf_op jit(solution)/shard_map/all_to_all | solution.py:199
  161.3 11.3 all-to-all-start.3
  166.9 72.2 %copy-start.46 = (f32[128,1024]{1,0:T(8,128)}, f32[128,1024]{1,0:T(8,128)S(1)}, u32[]{:S(2)}) copy-start(f32[128,1024]{1,0:T(8,128)S(1)} %get-tuple-element.2043) | copy-start | bytes 1572868
  167.1 13.6 copy-start.40
  168.3 57.9 %copy-start.119 = (bf16[128,1024]{1,0:T(8,128)(2,1)}, bf16[128,1024]{1,0:T(8,128)(2,1)S(1)}, u32[]{:S(2)}) copy-start(bf16[128,1024]{1,0:T(8,128)(2,1)S(1)} %fusion.223) | copy-start | bytes 786436
  172.6 11.4 all-to-all-start.5
  184.0 61.3 %all-to-all-start.7 = ((bf16[8,2,8192]{2,1,0:T(2,128)(2,1)}), bf16[8,2,8192]{2,1,0:T(2,128)(2,1)}, u32[]{:S(2)}, u32[]{:S(2)}) async-start(bf16[8,2,8192]{2,1,0:T(2,128)(2,1)} %reshape.1539), calls=%async_computation.7 | async-start | bytes 524288 | tf_op jit(solution)/shard_map/all_to_all | solution.py:199
  193.9 17.4 copy-start.51
  195.1 12.6 slice-start
  212.3 27.7 %copy-start.93 = (f32[128,1024]{1,0:T(8,128)}, f32[128,1024]{1,0:T(8,128)S(1)}, u32[]{:S(2)}) copy-start(f32[128,1024]{1,0:T(8,128)S(1)} %get-tuple-element.1824) | copy-start | bytes 1572868
  212.3 27.7 %copy-start.272 = (f32[128]{0:T(128)}, f32[128]{0:T(128)S(1)}, u32[]{:S(2)}) copy-start(f32[128]{0:T(128)S(1)} %negate_multiply_fusion.3) | copy-start | bytes 1540
  226.3 13.8 copy-start.95
  226.3 13.8 copy-start.274
  249.7 14.9 copy-start.53
  249.7 14.9 copy-start.270
  251.9 12.7 slice-start.2
  270.7 11.4 all-to-all-start.8
  282.1 10.3 all-to-all-start.10
  285.5 10.5 copy-start.14
  285.5 10.5 copy-start.35
  285.5 10.5 copy-start.80
  285.6 10.5 copy-start.82
  292.4 28.5 %all-to-all-start.12 = ((bf16[16,64,128]{2,1,0:T(8,128)(2,1)}), bf16[16,64,128]{2,1,0:T(8,128)(2,1)S(1)}, u32[]{:S(2)}, u32[]{:S(2)}) async-start(bf16[16,64,128]{2,1,0:T(8,128)(2,1)} %bitcast.146), calls=%async_computation.12 | async-start | bytes 524288 | tf_op jit(solution)/shard_map/all_to_all | solution.py:239
  320.8 29.3 %all-to-all-start.11 = ((bf16[8,2,24576]{2,1,0:T(2,128)(2,1)}), bf16[8,2,24576]{2,1,0:T(2,128)(2,1)S(1)}, u32[]{:S(2)}, u32[]{:S(2)}) async-start(bf16[8,2,24576]{2,1,0:T(2,128)(2,1)} %reshape.1551), calls=%async_computation.11 | async-start | bytes 1572864 | tf_op jit(solution)/shard_map/all_to_all | solution.py:249
  350.1 27.4 %all-to-all-start.9 = ((bf16[8,2,24576]{2,1,0:T(2,128)(2,1)}), bf16[8,2,24576]{2,1,0:T(2,128)(2,1)}, u32[]{:S(2)}, u32[]{:S(2)}) async-start(bf16[8,2,24576]{2,1,0:T(2,128)(2,1)} %reshape.1553), calls=%async_computation.9 | async-start | bytes 1572864 | tf_op jit(solution)/shard_map/all_to_all | solution.py:249
  377.6 17.4 all-to-all-start.13
  412.7 13.1 copy-start.101
  431.6 16.6 all-to-all-start.14
  435.8 256.4 %reduce-scatter.13.cloned.1.call-start = ((), (), s32[]{:S(2)}) async-start(), calls=%async_computation.25 | async-start | bytes 4325376 | tf_op jit(solution)/shard_map/reduce_scatter | solution.py:281
  473.7 18.2 all-to-all-start.15
  477.9 265.0 %reduce-scatter.9.cloned.1.call-start = ((), (), s32[]{:S(2)}) async-start(), calls=%async_computation.23 | async-start | bytes 4325376 | tf_op jit(solution)/shard_map/reduce_scatter | solution.py:281
  510.5 420.0 %reduce-scatter.7.cloned.1.call-start = ((), (), s32[]{:S(2)}) async-start(), calls=%async_computation.22 | async-start | bytes 8650752 | tf_op jit(solution)/shard_map/reduce_scatter | solution.py:281
  527.4 562.9 %reduce-scatter.11.cloned.1.call-start = ((), (), s32[]{:S(2)}) async-start(), calls=%async_computation.24 | async-start | bytes 12976128 | tf_op jit(solution)/shard_map/reduce_scatter | solution.py:281
  565.6 891.0 %reduce-scatter.17.cloned.1.call-start = ((), (), s32[]{:S(2)}) async-start(), calls=%async_computation.27 | async-start | bytes 17301504 | tf_op jit(solution)/shard_map/reduce_scatter | solution.py:281
  614.9 1206.7 %reduce-scatter.15.cloned.1.call-start = ((), (), s32[]{:S(2)}) async-start(), calls=%async_computation.26 | async-start | bytes 17301504 | tf_op jit(solution)/shard_map/reduce_scatter | solution.py:281
  665.2 11.0 slice-start.10
  690.7 1130.9 %copy-start.1 = (bf16[256,4096]{1,0:T(8,128)(2,1)S(1)}, bf16[256,4096]{1,0:T(8,128)(2,1)}, u32[]{:S(2)}) copy-start(bf16[256,4096]{1,0:T(8,128)(2,1)} %param.35) | copy-start | bytes 6291460
  (295 other events, 1130.4 us)
Sparse Core Ops, SparseCore 0:
  443.5 150.0 reduce-scatter.12
  596.4 146.5 reduce-scatter.8
  745.8 184.6 reduce-scatter.6
  937.0 153.3 reduce-scatter.10
  1093.2 363.3 reduce-scatter.16
  1459.4 362.1 reduce-scatter.14
where the time goes:
time: 1840 us; the launch traced here: 1830 us
  waiting for transfers between devices  1150 us (62%)
  matrix products  358 us (19%)
  local copies, waits for them, and re-layouts  130 us (7%)
  other arithmetic  83.9 us (5%)
  starting transfers between devices  65.7 us (4%)
  blocking collectives  19.6 us (1%)
  between operations  19.2 us (1%)
    reduce_scatter x6, waiting for transfers between devices, per_device(): lax.psum_scatter(totals, ('head', 'seq'), scatter_dimension=0, tiled=True)  1130 us
    unnamed x641, local copies, waits for them, and re-layouts  69.2 us
    dot_general x4, matrix products, per_device(): lax.dot_general(normed_ffn, grad_up_proj, dims_first, preferred_element_t...  48 us
    dot_general x4, matrix products, per_device(): lax.dot_general(hidden, cot_rows, dims_first, preferred_element_type=jnp....  47.7 us
    dot_general x4, matrix products, per_device(): lax.dot_general(normed_attn, grad_proj, (((0,), (1,)), ((), ())), preferr...  36.9 us
  transfers between devices with their start and end apart: 22, of which 11 were waited for; matrix products, arithmetic and copies ran while one was open for 25% of the time, Pallas kernels for 0%

commit v1 on v0

v1 whole, which is shorter than its diff:
```python
import math

import jax
import jax.numpy as jnp
from jax import lax
from jax.experimental import pallas as pl
from jax.experimental.pallas import tpu as pltpu
from jax.sharding import PartitionSpec as P

HD = 64
PAIR = 2 * HD
eps_norm = 1e-06
neg_fill = -1e30
BF = jnp.bfloat16
F32 = jnp.float32
DIMS_FIRST = (((0,), (0,)), ((), ()))
DIMS_LAST = (((1,), (1,)), ((), ()))
VMEM_BYTES = 56 * 1024 * 1024


def dot(left, right, dims=(((1,), (0,)), ((), ()))):
    return lax.dot_general(left, right, dims, preferred_element_type=F32)


def swap(values, axis_name, bits):
    size = lax.axis_size(axis_name)
    return lax.ppermute(values, axis_name, [(i, i ^ bits) for i in range(size)])


def pick(values, index, axis):
    return lax.dynamic_index_in_dim(values, index, axis, keepdims=False)


def to_buckets(parts, span, mine):
    count = parts.shape[0]
    got = [pick(parts, mine, 0)]
    for step in range(1, count):
        got.append(swap(pick(parts, mine ^ step, 0), "head", step * span))
    return jnp.stack(got)


def from_buckets(parts, span, mine):
    count = parts.shape[0]
    got = [parts[0]]
    for step in range(1, count):
        got.append(swap(parts[step], "head", step * span))
    got = jnp.stack(got)
    return jnp.stack([pick(got, mine ^ micro, 0) for micro in range(count)])


def weight_grad(left, right, descending):
    groups = lax.axis_size("head")
    place = lax.axis_index("head")
    frames, rows = left.shape
    width = right.shape[1]
    chunk = rows // groups
    bits = groups.bit_length() - 1
    split = left.reshape(frames, groups // 2, 2, chunk)
    low_bit = place % 2
    away = pick(split, 1 - low_bit, 2).reshape(frames, rows // 2)
    keep = pick(split, low_bit, 2).reshape(frames, rows // 2)
    came = swap(dot(away, right, DIMS_FIRST).astype(BF), "head", 1)
    total = (dot(keep, right, DIMS_FIRST) + came.astype(F32)).astype(BF)
    left_bits = list(range(1, bits))
    if descending:
        left_bits = left_bits[::-1]
    remaining = list(range(1, bits))
    for bit in left_bits:
        after = 2 ** len([b for b in remaining if b < bit]) * chunk
        view = total.reshape(-1, 2, after, width)
        here = (place >> bit) % 2
        came = swap(pick(view, 1 - here, 1), "head", 2**bit)
        total = (pick(view, here, 1).astype(F32) + came.astype(F32)).astype(BF)
        remaining.remove(bit)
    total = total.reshape(chunk, width)
    return lax.psum_scatter(total, "seq", scatter_dimension=0, tiled=True).astype(F32)


def norm_stats(hidden):
    centred = hidden - jnp.mean(hidden, axis=-1, keepdims=True)
    rate = lax.rsqrt(jnp.mean(centred * centred, axis=-1, keepdims=True) + eps_norm)
    return centred * rate, rate


def norm_back(grad, normal, rate, scale_term):
    inner = grad * (1.0 + scale_term)
    return rate * (
        inner
        - jnp.mean(inner, axis=-1, keepdims=True)
        - normal * jnp.mean(inner * normal, axis=-1, keepdims=True)
    )


def turn(values):
    lanes = lax.broadcasted_iota(jnp.int32, values.shape, 1)
    low = lax.rem(lanes, HD) < HD // 2
    return jnp.where(low, pltpu.roll(values, PAIR - HD // 2, 1), pltpu.roll(values, HD // 2, 1))


def project_kernel(rotated_tiles, x_ref, w_ref, cos_ref, sin_ref, o_ref):
    raw = dot(x_ref[...], w_ref[...])

    @pl.when(pl.program_id(0) < rotated_tiles)
    def _():
        for first in range(0, raw.shape[1], PAIR):
            part = raw[:, first : first + PAIR]
            turned = part * cos_ref[...] + turn(part) * sin_ref[...]
            o_ref[:, first : first + PAIR] = turned.astype(BF)

    @pl.when(pl.program_id(0) >= rotated_tiles)
    def _():
        o_ref[...] = raw.astype(BF)


def project(normed, w_qkv, cos_table, sin_table):
    frames, width = normed.shape
    tile = 512
    return pl.pallas_call(
        lambda *refs: project_kernel(2 * width // tile, *refs),
        grid=(3 * width // tile,),
        in_specs=[
            pl.BlockSpec((frames, width), lambda i: (0, 0)),
            pl.BlockSpec((width, tile), lambda i: (0, i)),
            pl.BlockSpec((frames, PAIR), lambda i: (0, 0)),
            pl.BlockSpec((frames, PAIR), lambda i: (0, 0)),
        ],
        out_specs=pl.BlockSpec((frames, tile), lambda i: (0, i)),
        out_shape=jax.ShapeDtypeStruct((frames, 3 * width), BF),
        compiler_params=pltpu.CompilerParams(vmem_limit_bytes=VMEM_BYTES),
        cost_estimate=pl.CostEstimate(
            flops=6 * frames * width * width,
            bytes_accessed=6 * width * width + 8 * frames * width,
            transcendentals=0,
        ),
    )(normed, w_qkv, cos_table, sin_table)


def head_lanes(shape, which):
    lanes = lax.broadcasted_iota(jnp.int32, shape, 1)
    return (lanes >= which * HD) & (lanes < (which + 1) * HD)


def attend_kernel(span, block, q_ref, *refs):
    k_refs, v_refs = refs[:span], refs[span : 2 * span]
    sq_ref, sk_ref, o_ref, p_ref, bias_ref = refs[2 * span :]
    frames = q_ref.shape[0]

    @pl.when(pl.program_id(0) == 0)
    def _():
        seg_q, place_q = sq_ref[:, 0:1], sq_ref[:, 1:2]
        for first in range(0, bias_ref.shape[1], frames):
            here = slice(first, first + frames)
            seg_k, place_k, live_k = sk_ref[0:1, here], sk_ref[1:2, here], sk_ref[2:3, here]
            allowed = (seg_q == seg_k) & ((live_k == 1) | (place_q == place_k))
            bias_ref[:, here] = jnp.where(allowed, 0.0, neg_fill)

    for first in range(0, frames, block):
        rows = slice(first, first + block)
        queries = q_ref[rows, :] * jnp.asarray(HD ** (-0.5), BF)
        kept = None
        for which in range(2):
            mine = head_lanes(queries.shape, which)
            one = jnp.where(mine, queries, jnp.zeros_like(queries))
            scores = jnp.concatenate([dot(one, k[...], DIMS_LAST) for k in k_refs], axis=1)
            scores = scores + bias_ref[rows, :]
            powered = jnp.exp(scores - jnp.max(scores, axis=1, keepdims=True))
            probs = (powered * (1.0 / jnp.sum(powered, axis=1, keepdims=True))).astype(BF)
            p_ref[which, rows, :] = probs
            result = None
            for index, v in enumerate(v_refs):
                part = dot(probs[:, index * frames : (index + 1) * frames], v[...])
                result = part if result is None else result + part
            kept = result if kept is None else jnp.where(mine, result, kept)
        o_ref[rows, :] = kept.astype(BF)


def attend(packed, others, meta_q, meta_k):
    span = len(others) + 1
    frames, width = packed.shape[0], packed.shape[1] // 3
    pairs = width // PAIR
    keys = span * frames

    def column(start):
        return pl.BlockSpec((frames, PAIR), lambda i, start=start: (0, start + i))

    return pl.pallas_call(
        lambda *refs: attend_kernel(span, 128, *refs),
        grid=(pairs,),
        in_specs=[column(0), column(pairs)]
        + [column(0)] * (span - 1)
        + [column(2 * pairs)]
        + [column(pairs)] * (span - 1)
        + [
            pl.BlockSpec((frames, PAIR), lambda i: (0, 0)),
            pl.BlockSpec((8, keys), lambda i: (0, 0)),
        ],
        out_specs=[
            column(0),
            pl.BlockSpec((2, frames, keys), lambda i: (i, 0, 0)),
        ],
        out_shape=[
            jax.ShapeDtypeStruct((frames, width), BF),
            jax.ShapeDtypeStruct((2 * pairs, frames, keys), BF),
        ],
        scratch_shapes=[pltpu.VMEM((frames, keys), F32)],
        compiler_params=pltpu.CompilerParams(vmem_limit_bytes=VMEM_BYTES),
        cost_estimate=pl.CostEstimate(
            flops=16 * pairs * frames * keys * PAIR,
            bytes_accessed=4 * pairs * frames * keys,
            transcendentals=2 * pairs * frames * keys,
        ),
    )(packed, packed, *others, packed, *others, meta_q, meta_k)


def attend_back_kernel(span, block, q_ref, *refs):
    k_refs, v_refs = refs[:span], refs[span : 2 * span]
    p_ref, o_ref, g_ref, cos_ref, sin_ref = refs[2 * span : 2 * span + 5]
    dq_ref = refs[2 * span + 5]
    dk_refs = refs[2 * span + 6 : 3 * span + 6]
    dv_refs = refs[3 * span + 6 : 4 * span + 6]
    ds_ref = refs[4 * span + 6]
    frames = q_ref.shape[0]
    factor = jnp.asarray(HD ** (-0.5), BF)

    def unturn(grad, index):
        rows = slice(index * frames, (index + 1) * frames)
        return grad * cos_ref[rows, :] - turn(grad) * sin_ref[rows, :]

    dk, dv, dq = [None] * span, [None] * span, None
    for which in range(2):
        mine = head_lanes(g_ref.shape, which)
        grads = jnp.where(mine, g_ref[...], jnp.zeros(g_ref.shape, BF))
        queries = jnp.where(mine, q_ref[...] * factor, jnp.zeros(g_ref.shape, BF))
        centre = jnp.sum(grads.astype(F32) * o_ref[...].astype(F32), axis=1, keepdims=True)
        for first in range(0, frames, block):
            rows = slice(first, first + block)
            for index in range(span):
                columns = slice(index * frames, (index + 1) * frames)
                grad_probs = dot(grads[rows, :], v_refs[index][...], DIMS_LAST)
                soft = p_ref[which, rows, columns].astype(F32)
                ds_ref[rows, columns] = (soft * (grad_probs - centre[rows, :])).astype(BF)
        result = None
        for index in range(span):
            columns = slice(index * frames, (index + 1) * frames)
            grad_scores = ds_ref[:, columns]
            part = dot(grad_scores, k_refs[index][...])
            result = part if result is None else result + part
            part = dot(grad_scores, queries, DIMS_FIRST)
            dk[index] = part if dk[index] is None else dk[index] + part
            part = dot(p_ref[which, :, columns], grads, DIMS_FIRST)
            dv[index] = part if dv[index] is None else dv[index] + part
        dq = result if dq is None else jnp.where(mine, result, dq)
    dq_ref[...] = unturn(dq * HD ** (-0.5), 0).astype(BF)
    for index in range(span):
        dk_refs[index][...] = unturn(dk[index], index).astype(BF)
        dv_refs[index][...] = dv[index].astype(BF)


def attend_back(packed, others, probs, attended, grads, cos_keys, sin_keys):
    span = len(others) + 1
    frames, width = packed.shape[0], packed.shape[1] // 3
    pairs = width // PAIR
    keys = span * frames

    def column(start):
        return pl.BlockSpec((frames, PAIR), lambda i, start=start: (0, start + i))

    out = jax.ShapeDtypeStruct((frames, width), BF)
    results = pl.pallas_call(
        lambda *refs: attend_back_kernel(span, 128, *refs),
        grid=(pairs,),
        in_specs=[column(0), column(pairs)]
        + [column(0)] * (span - 1)
        + [column(2 * pairs)]
        + [column(pairs)] * (span - 1)
        + [
            pl.BlockSpec((2, frames, keys), lambda i: (i, 0, 0)),
            column(0),
            column(0),
            pl.BlockSpec((keys, PAIR), lambda i: (0, 0)),
            pl.BlockSpec((keys, PAIR), lambda i: (0, 0)),
        ],
        out_specs=[column(0)] * (2 * span + 1),
        out_shape=[out] * (2 * span + 1),
        scratch_shapes=[pltpu.VMEM((frames, keys), BF)],
        compiler_params=pltpu.CompilerParams(vmem_limit_bytes=VMEM_BYTES),
        cost_estimate=pl.CostEstimate(
            flops=32 * pairs * frames * keys * PAIR,
            bytes_accessed=4 * pairs * frames * keys,
            transcendentals=0,
        ),
    )(packed, packed, *others, packed, *others, probs, attended, grads, cos_keys, sin_keys)
    return results[0], results[1 : span + 1], results[span + 1 :]


def per_device(
    inputs,
    skips,
    flow_time,
    segment_ids,
    frame_mask,
    cotangent,
    w_skip,
    w_time,
    w_qkv,
    w_out,
    w_up,
    w_down,
):
    groups = lax.axis_size("head")
    micro_count, _, rows, width = inputs.shape
    span = groups // micro_count
    place = lax.axis_index("head")
    mine = place // span
    frames = micro_count * rows

    joined = jnp.concatenate([inputs[:, 0], skips[:, 0]], axis=2)
    resid_local = dot(joined.reshape(frames, 2 * width), w_skip).astype(BF)
    resid_in = to_buckets(resid_local.reshape(micro_count, rows, width), span, mine)
    resid_in = resid_in.reshape(frames, width).astype(F32)
    later = jnp.concatenate([cotangent[:, 0], joined], axis=2)
    later = to_buckets(later, span, mine).reshape(frames, 3 * width)
    cot_rows, joined = later[:, :width], later[:, width:]

    meta = jnp.stack(
        [segment_ids[:, 0].astype(F32), frame_mask[:, 0].astype(F32), flow_time[:, 0]]
    )
    meta = lax.all_gather(meta, "head", axis=0)
    meta = pick(meta, mine, 2)
    order = jnp.stack(
        [place ^ other ^ (step * span) for other in range(span) for step in range(micro_count)]
    )
    seg_bucket = meta[:, 0].reshape(-1)
    meta = jnp.take(meta, order, axis=0)
    seg_keys = meta[:, 0].reshape(-1)
    live_keys = meta[:, 1].reshape(-1)
    place_keys = (order[:, None] * rows + jnp.arange(rows)[None, :]).reshape(-1).astype(F32)
    starts = jnp.sum((seg_bucket[None, :] < seg_keys[:, None]).astype(F32), axis=1)
    positions = place_keys - starts
    times = meta[:micro_count, 2].reshape(-1)

    feature_count = w_time.shape[0]
    half = feature_count // 2
    steps = jnp.exp(jnp.arange(half, dtype=F32) * (-math.log(10000.0) / (half - 1)))
    angles = 1000.0 * times[:, None] * steps
    features = jnp.concatenate([jnp.sin(angles), jnp.cos(angles)], axis=-1).astype(BF)
    modulation = dot(features, w_time)
    shift_first, scale_first, shift_second, scale_second = jnp.split(modulation, 4, axis=1)

    inv_freq = jnp.exp(jnp.arange(HD // 2, dtype=F32) * (-2.0 * math.log(10000.0) / HD))
    turns = positions[:, None] * inv_freq
    cos_half, sin_half = jnp.cos(turns), jnp.sin(turns)
    cos_keys = jnp.concatenate([cos_half] * 4, axis=1)
    sin_keys = jnp.concatenate([-sin_half, sin_half] * 2, axis=1)

    normal_first, rate_first = norm_stats(resid_in)
    normed_attn = (normal_first * (1.0 + scale_first) + shift_first).astype(BF)
    packed = project(normed_attn, w_qkv, cos_keys[:frames], sin_keys[:frames])
    others = [swap(packed[:, width:], "head", other) for other in range(1, span)]
    meta_q = jnp.concatenate(
        [seg_keys[:frames, None], place_keys[:frames, None], jnp.zeros((frames, PAIR - 2), F32)],
        axis=1,
    )
    meta_k = jnp.stack([seg_keys, place_keys, live_keys] + [jnp.zeros_like(seg_keys)] * 5)
    attended, probs = attend(packed, others, meta_q, meta_k)
    resid_mid = resid_in + dot(attended, w_out)

    normal_second, rate_second = norm_stats(resid_mid)
    normed_ffn = (normal_second * (1.0 + scale_second) + shift_second).astype(BF)
    up_proj = dot(normed_ffn, w_up)
    activated, pull_gelu = jax.vjp(lambda v: jax.nn.gelu(v, approximate=True), up_proj)
    hidden = activated.astype(BF)
    output = (resid_mid + dot(hidden, w_down)).astype(BF)
    output = from_buckets(output.reshape(micro_count, rows, width), span, mine)

    total_down = weight_grad(hidden, cot_rows, False)
    grad_up_proj = pull_gelu(dot(cot_rows, w_down, DIMS_LAST))[0].astype(BF)
    total_up = weight_grad(normed_ffn, grad_up_proj, True)
    grad_normed_ffn = dot(grad_up_proj, w_up, DIMS_LAST)
    grad_mid = cot_rows.astype(F32) + norm_back(
        grad_normed_ffn, normal_second, rate_second, scale_second
    )
    grad_mid_low = grad_mid.astype(BF)
    total_out = weight_grad(attended, grad_mid_low, False)
    grad_attended = dot(grad_mid_low, w_out, DIMS_LAST).astype(BF)
    dq, dk, dv = attend_back(packed, others, probs, attended, grad_attended, cos_keys, sin_keys)
    key_sum, value_sum = dk[0].astype(F32), dv[0].astype(F32)
    for other in range(1, span):
        both = swap(jnp.concatenate([dk[other], dv[other]], axis=1), "head", other).astype(F32)
        key_sum, value_sum = key_sum + both[:, :width], value_sum + both[:, width:]
    grad_proj = jnp.concatenate([dq, key_sum.astype(BF), value_sum.astype(BF)], axis=1)
    total_qkv = weight_grad(normed_attn, grad_proj, True)
    grad_normed_attn = dot(grad_proj, w_qkv, DIMS_LAST)
    grad_in_low = (
        grad_mid + norm_back(grad_normed_attn, normal_first, rate_first, scale_first)
    ).astype(BF)
    total_skip = weight_grad(joined, grad_in_low, False)
    grad_modulation = jnp.concatenate(
        [
            grad_normed_attn,
            grad_normed_attn * normal_first,
            grad_normed_ffn,
            grad_normed_ffn * normal_second,
        ],
        axis=1,
    ).astype(BF)
    total_time = weight_grad(features, grad_modulation, False)
    grad_local = from_buckets(grad_in_low.reshape(micro_count, rows, width), span, mine)
    grad_local = grad_local.reshape(frames, width)
    shape = (micro_count, 1, rows, width)
    input_grad = dot(grad_local, w_skip[:width], DIMS_LAST).reshape(shape)
    skip_grad = dot(grad_local, w_skip[width:], DIMS_LAST).reshape(shape)
    return (
        output[:, None],
        input_grad,
        skip_grad,
        total_skip,
        total_time,
        total_qkv,
        total_out,
        total_up,
        total_down,
    )


def solution(mesh):
    frames_spec = P(None, "seq", "head", None)
    line_spec = P(None, "seq", "head")
    shard_spec = P(("head", "seq"), None)
    return jax.shard_map(
        per_device,
        mesh=mesh,
        in_specs=(frames_spec, frames_spec, line_spec, line_spec, line_spec, frames_spec)
        + (P(),) * 6,
        out_specs=(frames_spec,) * 3 + (shard_spec,) * 6,
        check_vma=False,
    )
```

time: 1840 us -> 605 us (0.33)
  waiting for transfers between devices: 1150 us -> 173 us
  matrix products: 358 us -> 115 us
  Pallas kernels: 0 us -> 70.6 us
  starting transfers between devices: 65.7 us -> 28.5 us
  other arithmetic: 83.9 us -> 58.2 us
    reduce_scatter x6, waiting for transfers between devices: 1130 us -> 0.01 us  [weight_grad(): lax.psum_scatter(total, 'seq', scatter_dimension=0, tiled=True).astype(F32)]
    dot_general x124 -> x23, matrix products: 358 us -> 115 us  [dot(): return lax.dot_general(left, right, dims, preferred_element_type=F32)]
    ppermute x0 -> x32, waiting for transfers between devices: none -> 173 us  [swap(): return lax.ppermute(values, axis_name, [(i, i ^ bits) for i in range(size)])]
    pallas_call x0 -> x3, Pallas kernels: none -> 70.6 us  [the longest x1 33.6 us: attend(): pl.pallas_call(lambda *refs: attend_kernel(span, 128, *refs), grid=(pairs...]
    all_to_all x16 -> x0, starting transfers between devices: 64.6 us -> none  [the longest x4 17.5 us: per_device(): lax.all_to_all(grad_packed, 'head', split_axis=3, concat_axis=1, tiled=True)]
    dynamic_slice x24 -> x11, local copies, waits for them, and re-layouts: 1.28 us -> 30.5 us  [pick(): return lax.dynamic_index_in_dim(values, index, axis, keepdims=False)]
    ppermute x0 -> x32, starting transfers between devices: none -> 28.2 us  [swap(): return lax.ppermute(values, axis_name, [(i, i ^ bits) for i in range(size)])]
    all_to_all x16 -> x0, waiting for transfers between devices: 21.3 us -> none  [the longest x4 7.79 us: per_device(): lax.all_to_all(grad_packed, 'head', split_axis=3, concat_axis=1, tiled=True)]
  transfers between devices with their start and end apart: 22 -> 38, of which waited for: 11 -> 12; matrix products, arithmetic and copies ran while one was open for 25% -> 37% of each run, Pallas kernels for 0% -> 0%
where the time goes in v1:
time: 605 us; the launch traced here: 598 us
  waiting for transfers between devices  173 us (29%)
  local copies, waits for them, and re-layouts  122 us (20%)
  matrix products  115 us (19%)
  Pallas kernels  70.6 us (12%)
  other arithmetic  58.2 us (10%)
  starting transfers between devices  28.5 us (5%)
  blocking collectives  16.1 us (3%)
  between operations  15.5 us (3%)
    ppermute x32, waiting for transfers between devices, swap(): return lax.ppermute(values, axis_name, [(i, i ^ bits) for i in range(size)])  173 us
    dot_general x23, matrix products, dot(): return lax.dot_general(left, right, dims, preferred_element_type=F32)  115 us
    unnamed x142, local copies, waits for them, and re-layouts  59.4 us
    pallas_call x1, Pallas kernels, attend(): pl.pallas_call(lambda *refs: attend_kernel(span, 128, *refs), grid=(pairs...  33.6 us
    dynamic_slice x11, local copies, waits for them, and re-layouts, pick(): return lax.dynamic_index_in_dim(values, index, axis, keepdims=False)  30.5 us
    ppermute x32, starting transfers between devices, swap(): return lax.ppermute(values, axis_name, [(i, i ^ bits) for i in range(size)])  28.2 us
    pallas_call x1, Pallas kernels, attend_back(): pl.pallas_call(lambda *refs: attend_back_kernel(span, 128, *refs), grid=(...  26.8 us
    reshape x5, local copies, waits for them, and re-layouts, weight_grad(): split = left.reshape(frames, groups // 2, 2, chunk)  16.5 us
  transfers between devices with their start and end apart: 38, of which 12 were waited for; matrix products, arithmetic and copies ran while one was open for 37% of the time, Pallas kernels for 0%

profile of v1, /device:TPU:0, one launch (start us, length us, event | category | flops | bytes accessed | tf_op | source)
XLA Modules:
  0.0 598.0 jit_solution(12339924894169746168)
XLA Ops:
  7.3 5.3 fusion.48
  13.4 3.9 collective-permute-start.2
  17.9 16.1 %all-gather = f32[24,4,128]{2,1,0:T(4,128)S(1)} all-gather(f32[3,4,128]{2,1,0:T(4,128)S(1)} %pad_maximum_fusion.17), channel_id=2, replica_groups=mesh['head'=8,'seq'=4] {'head'}, dimensions={0}, use_global_device_ids=true | all-gather | bytes 55296 | tf_op jit(solution)/shard_map/all_gather | solution.py:328
  47.7 10.1 %shard_map.187.refs_0_.refs_1_.refs_3_ = bf16[512,3072]{1,0:T(8,128)(2,1)} custom-call(bf16[512,1024]{1,0:T(8,128)(2,1)} %fusion.13.refs_0_, bf16[1024,3072]{1,0:T(8,128)(2,1)} %refs_1_.1, f32[512,128]{1,0:T(8,128)} %slice.114.refs_2_, f32[512,128]{1,0:T(8,128)} %slice.115.refs_3_), custom_call_target="tpu_custom_call" | custom-call | flops 3221225472 | bytes 10485760 | tf_op jit(solution)/shard_map/pallas_call | solution.py:118
  57.8 3.3 slice.116
  70.9 3.1 constant_dynamic-slice_fusion.9
  74.0 3.6 copy.147
  79.9 5.2 collective-permute-done.9
  85.1 16.1 %collective-permute-done.8 = bf16[128,3072]{1,0:T(8,128)(2,1)} collective-permute-done((bf16[128,3072]{1,0:T(8,128)(2,1)}, bf16[128,3072]{1,0:T(8,128)(2,1)}, u32[]{:S(2)}, u32[]{:S(2)}) %collective-permute-start.8) | collective-permute-done | bytes 786464 | tf_op jit(solution)/shard_map/ppermute | solution.py:27
  107.6 33.6 %shard_map.188 = (bf16[512,1024]{1,0:T(8,128)(2,1)}, bf16[16,512,1024]{2,1,0:T(8,128)(2,1)}) custom-call(bf16[512,3072]{1,0:T(8,128)(2,1)} %shard_map.187.refs_0_.refs_1_.refs_3_, bf16[512,3072]{1,0:T(8,128)(2,1)} %shard_map.187.refs_0_.refs_1_.refs_3_, bf16[512,2048]{1,0:T(8,128)(2,1)} %collective-permute-done.3.refs_2_.refs_4_, ...), custom_call_target="tpu_custom_call" | custom-call | flops 8589934592 | bytes 16777216 | tf_op jit(solution)/shard_map/pallas_call | solution.py:186
  146.9 3.7 fusion.12
  150.7 9.1 %multiply_convert_fusion = (bf16[512,4096]{1,0:T(8,128)(2,1)}, f32[512,4096]{1,0:T(8,128)}) fusion(bf16[512,1024]{1,0:T(8,128)(2,1)S(1)} %fusion.12, bf16[1024,4096]{1,0:T(8,128)(2,1)S(1)} %bitcast.303), kind=kOutput, calls=%fused_computation.12 | convolution fusion | flops 4313841664 | bytes 22020096 | tf_op jit(solution)/shard_map/dot_general | solution.py:22
  159.8 15.5 %fusion.6 = bf16[512,4096]{1,0:T(8,128)(2,1)} fusion(f32[512,4096]{1,0:T(8,128)} %get-tuple-element.145, bf16[4096,1024]{1,0:T(8,128)(2,1)} %param.23, bf16[512,3072]{1,0:T(8,128)(2,1)S(1)} %bitcast.247), kind=kOutput, calls=%fused_computation.9 | convolution fusion | flops 4336910336 | bytes 22020096 | tf_op jit(solution)/shard_map/dot_general | solution.py:22
  175.3 8.7 %fusion.96 = (f32[512]{0:T(512)S(1)}, f32[512]{0:T(512)S(1)}, f32[512,1024]{1,0:T(8,128)S(1)}) fusion(f32[512,4096]{1,0:T(8,128)S(1)} %bitcast.241, f32[512]{0:T(512)S(1)} %add_rsqrt_fusion, f32[512,1024]{1,0:T(8,128)S(1)} %get-tuple-element.142, f32[512]{0:T(512)S(1)} %broadcast_multiply_fusion.4, bf16[512,4096]{1,0:T(8,128)(2,1)} %fusion.6, ...), kind=kOutput, calls=%fused_computation.222 | convolution fusion | flops 4298636288 | bytes 18882560 | tf_op jit(solution)/shard_map/dot_general | solution.py:22
  188.5 26.8 %shard_map.189 = (bf16[512,1024]{1,0:T(8,128)(2,1)}, bf16[512,1024]{1,0:T(8,128)(2,1)}, bf16[512,1024]{1,0:T(8,128)(2,1)}, bf16[512,1024]{1,0:T(8,128)(2,1)}, bf16[512,1024]{1,0:T(8,128)(2,1)}) custom-call(bf16[512,3072]{1,0:T(8,128)(2,1)} %shard_map.187.refs_0_.refs_1_.refs_3_, bf16[512,3072]{1,0:T(8,128)(2,1)} %shard_map.187.refs_0_.refs_1_.refs_3_, ...), custom_call_target="tpu_custom_call" | custom-call | flops 17179869184 | bytes 16777216 | tf_op jit(solution)/shard_map/pallas_call | solution.py:269
  215.3 3.2 pad_maximum_fusion.4
  218.5 3.5 constant_dynamic-slice_fusion.7
  222.0 3.5 copy.149
  228.9 6.3 %constant_dynamic-slice_fusion.12 = (bf16[512,4,1,256]{3,2,1,0:T(2,128)(2,1)}, bf16[512,4,1,256]{3,2,1,0:T(2,128)(2,1)}) fusion(bf16[512,4,2,256]{3,2,1,0:T(2,128)(2,1)S(1)} %copy-done.6, s32[]{:T(128)S(6)} %select_n.171, s32[]{:T(128)S(6)} %select_n.170), kind=kLoop, calls=%fused_computation.167 | loop fusion | bytes 4194312 | tf_op jit(solution)/shard_map/jit(dynamic_index_in_dim)/dynamic_slice | solution.py:31
  235.2 5.8 copy.143
  241.0 5.8 copy.142
  249.4 3.5 copy.148
  252.9 5.0 constant_dynamic-slice_fusion.3
  257.9 3.7 copy.152
  261.6 6.7 %convolution_convert_fusion = bf16[512,4096]{1,0:T(8,128)(2,1)} fusion(bf16[512,512]{0,1:T(8,128)(2,1)} %bitcast.280, bf16[512,4096]{1,0:T(8,128)(2,1)} %fusion.6), kind=kOutput, calls=%fused_computation.14 | convolution fusion | flops 2149580800 | bytes 8912896 | tf_op jit(solution)/shard_map/dot_general | solution.py:22
  268.3 7.8 %reshape.868 = bf16[512,4,2,512]{3,2,1,0:T(2,128)(2,1)} reshape(bf16[512,4096]{1,0:T(8,128)(2,1)} %get-tuple-element.144) | data formatting | bytes 8388608 | tf_op jit(solution)/shard_map/reshape | solution.py:58
  284.4 7.0 %fusion.97 = (f32[512]{0:T(512)S(1)}, f32[512]{0:T(512)S(1)}, f32[512,1024]{1,0:T(8,128)S(1)}) fusion(f32[512,4096]{1,0:T(8,128)S(1)} %bitcast.243, f32[512]{0:T(512)S(1)} %rsqrt_bitcast_fusion, f32[512]{0:T(512)S(1)} %get-tuple-element.139, bf16[4,128,1024]{2,1,0:T(8,128)(2,1)S(1)} %get-tuple-element.82, bf16[1024,3072]{1,0:T(8,128)(2,1)} %refs_1_.1, ...), kind=kOutput, calls=%fused_computation.223 | convolution fusion | flops 3234855936 | bytes 14688256 | tf_op jit(solution)/shard_map/dot_general | solution.py:22
  293.5 3.8 convolution_convert_fusion.1
  297.5 9.8 %constant_dynamic-slice_fusion.2 = (bf16[512,4,1,512]{3,2,1,0:T(2,128)(2,1)}, bf16[512,4,1,512]{3,2,1,0:T(2,128)(2,1)}) fusion(bf16[512,4,2,512]{3,2,1,0:T(2,128)(2,1)S(1)} %copy-done.3, s32[]{:T(128)S(6)} %select_n.170, s32[]{:T(128)S(6)} %select_n.171), kind=kLoop, calls=%fused_computation.157 | loop fusion | bytes 8388616 | tf_op jit(solution)/shard_map/jit(dynamic_index_in_dim)/dynamic_slice | solution.py:31
  307.4 10.6 %copy.154 = bf16[512,4,1,512]{0,3,1,2:T(8,128)(2,1)} copy(bf16[512,4,1,512]{3,2,1,0:T(2,128)(2,1)} %get-tuple-element.86) | data formatting | bytes 4194304
  321.9 3.8 add_convert_fusion.6
  329.0 3.7 convolution_convert_fusion.2
  333.2 6.5 %collective-permute-done.18 = bf16[2,32,4096]{2,1,0:T(8,128)(2,1)S(1)} collective-permute-done((bf16[2,32,4096]{2,1,0:T(8,128)(2,1)S(1)}, bf16[2,32,4096]{2,1,0:T(8,128)(2,1)S(1)}, u32[]{:S(2)}, u32[]{:S(2)}) %collective-permute-start.18) | collective-permute-done | bytes 524320 | tf_op jit(solution)/shard_map/ppermute | solution.py:27
  341.0 5.7 convolution_convert_fusion.3
  349.0 10.6 %copy.153 = bf16[512,4,1,512]{0,3,1,2:T(8,128)(2,1)} copy(bf16[512,4,1,512]{3,2,1,0:T(2,128)(2,1)} %get-tuple-element.85) | data formatting | bytes 4194304
  368.2 4.8 add_convert_fusion.1
  373.1 5.5 add_convert_fusion.2
  383.4 8.5 %collective-permute-done.15 = bf16[2,256,1024]{2,1,0:T(8,128)(2,1)S(1)} collective-permute-done((bf16[2,256,1024]{2,1,0:T(8,128)(2,1)S(1)}, bf16[2,256,1024]{2,1,0:T(8,128)(2,1)S(1)}, u32[]{:S(2)}, u32[]{:S(2)}) %collective-permute-start.15) | collective-permute-done | bytes 1048608 | tf_op jit(solution)/shard_map/ppermute | solution.py:27
  394.1 4.9 add_convert_fusion
  403.0 69.9 %collective-permute-done.16 = bf16[1,256,1024]{2,1,0:T(8,128)(2,1)S(1)} collective-permute-done((bf16[1,256,1024]{2,1,0:T(8,128)(2,1)S(1)}, bf16[1,256,1024]{2,1,0:T(8,128)(2,1)S(1)}, u32[]{:S(2)}, u32[]{:S(2)}) %collective-permute-start.16) | collective-permute-done | bytes 524320 | tf_op jit(solution)/shard_map/ppermute | solution.py:27
  482.2 15.0 %collective-permute-done.22 = bf16[1,128,3072]{2,1,0:T(8,128)(2,1)S(1)} collective-permute-done((bf16[1,128,3072]{2,1,0:T(8,128)(2,1)S(1)}, bf16[1,128,3072]{2,1,0:T(8,128)(2,1)S(1)}, u32[]{:S(2)}, u32[]{:S(2)}) %collective-permute-start.22) | collective-permute-done | bytes 786464 | tf_op jit(solution)/shard_map/ppermute | solution.py:27
  498.3 19.8 %collective-permute-done.28 = bf16[1,128,4096]{2,1,0:T(8,128)(2,1)} collective-permute-done((bf16[1,128,4096]{2,1,0:T(8,128)(2,1)}, bf16[1,128,4096]{2,1,0:T(8,128)(2,1)}, u32[]{:S(2)}, u32[]{:S(2)}) %collective-permute-start.28) | collective-permute-done | bytes 1048608 | tf_op jit(solution)/shard_map/ppermute | solution.py:27
  520.7 3.4 fusion.7
  524.8 8.4 %add_convert_fusion.7 = bf16[512,1024]{1,0:T(8,128)(2,1)} fusion(f32[512,1024]{1,0:T(8,128)S(1)} %copy-done.5, bf16[512,4096]{1,0:T(8,128)(2,1)S(1)} %copy-done.16, bf16[4096,1024]{1,0:T(8,128)(2,1)} %param.23), kind=kOutput, calls=%fused_computation.80 | convolution fusion | flops 4296015872 | bytes 15728640 | tf_op jit(solution)/shard_map/dot_general | solution.py:22
  533.1 14.7 %collective-permute-done.31 = bf16[1,512,1024]{2,1,0:T(8,128)(2,1)S(1)} collective-permute-done((bf16[1,512,1024]{2,1,0:T(8,128)(2,1)S(1)}, bf16[1,512,1024]{2,1,0:T(8,128)(2,1)S(1)}, u32[]{:S(2)}, u32[]{:S(2)}) %collective-permute-start.31) | collective-permute-done | bytes 1048608 | tf_op jit(solution)/shard_map/ppermute | solution.py:27
  552.9 6.2 %collective-permute-done.6 = bf16[128,1024]{1,0:T(8,128)(2,1)S(1)} collective-permute-done((bf16[128,1024]{1,0:T(8,128)(2,1)S(1)}, bf16[128,1024]{1,0:T(8,128)(2,1)S(1)}, u32[]{:S(2)}, u32[]{:S(2)}) %collective-permute-start.6) | collective-permute-done | bytes 262176 | tf_op jit(solution)/shard_map/ppermute | solution.py:27
  569.1 4.1 collective-permute-done.13
  573.2 3.9 collective-permute-done.12
  (316 shorter events, 133.0 us)
Async XLA Ops:
  7.2 34.2 %copy-start = (bf16[256,4096]{1,0:T(8,128)(2,1)S(1)}, bf16[256,4096]{1,0:T(8,128)(2,1)}, u32[]{:S(2)}) copy-start(bf16[256,4096]{1,0:T(8,128)(2,1)} %param.19) | copy-start | bytes 6291460
  7.2 560.3 %reduce-scatter.13.cloned.1.call-start = ((), (), s32[]{:S(2)}) async-start(), calls=%async_computation.9 | async-start | bytes 327680 | tf_op jit(solution)/shard_map/reduce_scatter | solution.py:76
  13.4 29.3 %collective-permute-start.2 = (bf16[128,1024]{1,0:T(8,128)(2,1)}, bf16[128,1024]{1,0:T(8,128)(2,1)S(1)}, u32[]{:S(2)}, u32[]{:S(2)}) collective-permute-start(bf16[128,1024]{1,0:T(8,128)(2,1)} %get-tuple-element.122), channel_id=1, source_target_pairs={{0,24},{4,28},{8,16},{12,20},{16,8},{20,12},{24,0},{28,4},{1,25},{... | collective-permute-start | bytes 786440 | tf_op jit(solution)/shard_map/ppermute | solution.py:27
  17.3 25.4 %collective-permute-start.1 = (bf16[128,1024]{1,0:T(8,128)(2,1)S(1)}, bf16[128,1024]{1,0:T(8,128)(2,1)S(1)}, u32[]{:S(2)}, u32[]{:S(2)}) collective-permute-start(bf16[128,1024]{1,0:T(8,128)(2,1)S(1)} %get-tuple-element.123), channel_id=1, source_target_pairs={{0,16},{4,20},{8,24},{12,28},{16,0},{20,4},{24,8},{28,12},{1,17},{... | collective-permute-start | bytes 786440 | tf_op jit(solution)/shard_map/ppermute | solution.py:27
  17.8 24.9 %collective-permute-start = (bf16[128,1024]{1,0:T(8,128)(2,1)S(1)}, bf16[128,1024]{1,0:T(8,128)(2,1)}, u32[]{:S(2)}, u32[]{:S(2)}) collective-permute-start(bf16[128,1024]{1,0:T(8,128)(2,1)S(1)} %get-tuple-element.124), channel_id=1, source_target_pairs={{0,8},{4,12},{8,0},{12,4},{16,24},{20,28},{24,16},{28,20},{1,9},{5... | collective-permute-start | bytes 786440 | tf_op jit(solution)/shard_map/ppermute | solution.py:27
  61.1 46.5 %collective-permute-start.3 = (bf16[512,2048]{1,0:T(8,128)(2,1)}, bf16[512,2048]{1,0:T(8,128)(2,1)}, u32[]{:S(2)}, u32[]{:S(2)}) collective-permute-start(bf16[512,2048]{1,0:T(8,128)(2,1)} %slice.116), channel_id=1, source_target_pairs={{0,4},{4,0},{8,12},{12,8},{16,20},{20,16},{24,28},{28,24},{1,5},{5... | collective-permute-start | bytes 6291464 | tf_op jit(solution)/shard_map/ppermute | solution.py:27
  63.4 21.6 %collective-permute-start.9 = (bf16[128,3072]{1,0:T(8,128)(2,1)}, bf16[128,3072]{1,0:T(8,128)(2,1)}, u32[]{:S(2)}, u32[]{:S(2)}) collective-permute-start(bf16[128,3072]{1,0:T(8,128)(2,1)} %get-tuple-element.92), channel_id=1, source_target_pairs={{0,24},{4,28},{8,16},{12,20},{16,8},{20,12},{24,0},{28,4},{1,25},{... | collective-permute-start | bytes 2359304 | tf_op jit(solution)/shard_map/ppermute | solution.py:27
  64.8 36.3 %collective-permute-start.8 = (bf16[128,3072]{1,0:T(8,128)(2,1)}, bf16[128,3072]{1,0:T(8,128)(2,1)}, u32[]{:S(2)}, u32[]{:S(2)}) collective-permute-start(bf16[128,3072]{1,0:T(8,128)(2,1)} %get-tuple-element.93), channel_id=1, source_target_pairs={{0,16},{4,20},{8,24},{12,28},{16,0},{20,4},{24,8},{28,12},{1,17},{... | collective-permute-start | bytes 2359304 | tf_op jit(solution)/shard_map/ppermute | solution.py:27
  65.4 35.7 %collective-permute-start.7 = (bf16[128,3072]{1,0:T(8,128)(2,1)}, bf16[128,3072]{1,0:T(8,128)(2,1)}, u32[]{:S(2)}, u32[]{:S(2)}) collective-permute-start(bf16[128,3072]{1,0:T(8,128)(2,1)} %get-tuple-element.94), channel_id=1, source_target_pairs={{0,8},{4,12},{8,0},{12,4},{16,24},{20,28},{24,16},{28,20},{1,9},{5... | collective-permute-start | bytes 2359304 | tf_op jit(solution)/shard_map/ppermute | solution.py:27
  74.0 27.1 %copy-start.21 = (bf16[1,128,3072]{2,1,0:T(8,128)(2,1)S(1)}, bf16[1,128,3072]{2,1,0:T(8,128)(2,1)}, u32[]{:S(2)}) copy-start(bf16[1,128,3072]{2,1,0:T(8,128)(2,1)} %get-tuple-element.91) | copy-start | bytes 2359300
  107.6 36.2 %copy-start.53 = (bf16[1024,1024]{1,0:T(8,128)(2,1)S(1)}, bf16[1024,1024]{1,0:T(8,128)(2,1)}, u32[]{:S(2)}) copy-start(bf16[1024,1024]{1,0:T(8,128)(2,1)} %param.21) | copy-start | bytes 6291460
  146.5 37.5 %copy-start.4 = (f32[512,1024]{1,0:T(8,128)}, f32[512,1024]{1,0:T(8,128)S(1)}, u32[]{:S(2)}) copy-start(f32[512,1024]{1,0:T(8,128)S(1)} %get-tuple-element.142) | copy-start | bytes 6291460
  150.7 24.6 %slice-start = ((s8[8388608]{0:T(1024)(128)(4,1)}), s8[4194304]{0:T(1024)(128)(4,1)S(1)}, s32[]{:S(2)}) async-start(s8[8388608]{0:T(1024)(128)(4,1)} %bitcast.240), calls=%async_computation.12 | async-start | bytes 8388608
  159.8 15.5 %slice-start.1 = ((s8[8388608]{0:T(1024)(128)(4,1)}), s8[4194304]{0:T(1024)(128)(4,1)S(1)}, s32[]{:S(2)}) async-start(s8[8388608]{0:T(1024)(128)(4,1)} %bitcast.240), calls=%async_computation.13 | async-start | bytes 8388608
  218.5 62.3 %collective-permute-start.10 = (bf16[512,2048]{1,0:T(8,128)(2,1)}, bf16[512,2048]{1,0:T(8,128)(2,1)}, u32[]{:S(2)}, u32[]{:S(2)}) collective-permute-start(bf16[512,2048]{1,0:T(8,128)(2,1)} %pad_maximum_fusion.4), channel_id=1, source_target_pairs={{0,4},{4,0},{8,12},{12,8},{16,20},{20,16},{24,28},{28,24},{1,5},{5... | collective-permute-start | bytes 6291464 | tf_op jit(solution)/shard_map/ppermute | solution.py:27
  228.4 47.8 %collective-permute-start.23 = (bf16[512,1024]{1,0:T(8,128)(2,1)}, bf16[512,1024]{1,0:T(8,128)(2,1)}, u32[]{:S(2)}, u32[]{:S(2)}) collective-permute-start(bf16[512,1024]{1,0:T(8,128)(2,1)} %convolution_convert_fusion.6), channel_id=1, source_target_pairs={{0,4},{4,0},{8,12},{12,8},{16,20},{20,16},{24,28},{28,24},{1,5},{5... | collective-permute-start | bytes 3145736 | tf_op jit(solution)/shard_map/ppermute | solution.py:27
  268.3 99.9 %collective-permute-start.26 = (bf16[512,4096]{1,0:T(8,128)(2,1)}, bf16[512,4096]{1,0:T(8,128)(2,1)}, u32[]{:S(2)}, u32[]{:S(2)}) collective-permute-start(bf16[512,4096]{1,0:T(8,128)(2,1)} %convolution_convert_fusion), channel_id=1, source_target_pairs={{0,4},{4,0},{8,12},{12,8},{16,20},{20,16},{24,28},{28,24},{1,5},{5... | collective-permute-start | bytes 12582920 | tf_op jit(solution)/shard_map/ppermute | solution.py:27
  280.2 37.8 %collective-permute-start.24 = (bf16[2,128,1024]{2,1,0:T(8,128)(2,1)}, bf16[2,128,1024]{2,1,0:T(8,128)(2,1)}, u32[]{:S(2)}, u32[]{:S(2)}) collective-permute-start(bf16[2,128,1024]{2,1,0:T(8,128)(2,1)} %dynamic-slice_bitcast_fusion.9), channel_id=1, source_target_pairs={{0,8},{4,12},{8,0},{12,4},{16,24},{20,28},{24,16},{28,20},{1,9},{5... | collective-permute-start | bytes 1572872 | tf_op jit(solution)/shard_map/ppermute | solution.py:27
  297.3 23.6 %collective-permute-start.17 = (bf16[128,4096]{1,0:T(8,128)(2,1)}, bf16[128,4096]{1,0:T(8,128)(2,1)S(1)}, u32[]{:S(2)}, u32[]{:S(2)}) collective-permute-start(bf16[128,4096]{1,0:T(8,128)(2,1)} %convolution_convert_fusion.1), channel_id=1, source_target_pairs={{0,4},{4,0},{8,12},{12,8},{16,20},{20,16},{24,28},{28,24},{1,5},{5... | collective-permute-start | bytes 3145736 | tf_op jit(solution)/shard_map/ppermute | solution.py:27
  319.3 40.3 %collective-permute-start.25 = (bf16[1,128,1024]{2,1,0:T(8,128)(2,1)S(1)}, bf16[1,128,1024]{2,1,0:T(8,128)(2,1)}, u32[]{:S(2)}, u32[]{:S(2)}) collective-permute-start(bf16[1,128,1024]{2,1,0:T(8,128)(2,1)S(1)} %constant_dynamic-slice_fusion.5), channel_id=1, source_target_pairs={{0,16},{4,20},{8,24},{12,28},{16,0},{20,4},{24,8},{28,12},{1,17},{... | collective-permute-start | bytes 786440 | tf_op jit(solution)/shard_map/ppermute | solution.py:27
  325.7 14.1 %collective-permute-start.18 = (bf16[2,32,4096]{2,1,0:T(8,128)(2,1)S(1)}, bf16[2,32,4096]{2,1,0:T(8,128)(2,1)S(1)}, u32[]{:S(2)}, u32[]{:S(2)}) collective-permute-start(bf16[2,32,4096]{2,1,0:T(8,128)(2,1)S(1)} %dynamic-slice_bitcast_fusion.10), channel_id=1, source_target_pairs={{0,8},{4,12},{8,0},{12,4},{16,24},{20,28},{24,16},{28,20},{1,9},{5... | collective-permute-start | bytes 1572872 | tf_op jit(solution)/shard_map/ppermute | solution.py:27
  329.0 34.3 %collective-permute-start.14 = (bf16[1024,1024]{1,0:T(8,128)(2,1)}, bf16[1024,1024]{1,0:T(8,128)(2,1)}, u32[]{:S(2)}, u32[]{:S(2)}) collective-permute-start(bf16[1024,1024]{1,0:T(8,128)(2,1)} %convolution_convert_fusion.4), channel_id=1, source_target_pairs={{0,4},{4,0},{8,12},{12,8},{16,20},{20,16},{24,28},{28,24},{1,5},{5... | collective-permute-start | bytes 6291464 | tf_op jit(solution)/shard_map/ppermute | solution.py:27
  329.0 12.0 %copy-start.23 = (bf16[512,4,1,512]{0,3,1,2:T(8,128)(2,1)S(1)}, bf16[512,4,1,512]{0,3,1,2:T(8,128)(2,1)}, u32[]{:S(2)}) copy-start(bf16[512,4,1,512]{0,3,1,2:T(8,128)(2,1)} %copy.154) | copy-start | bytes 6291460
  332.7 40.3 %collective-permute-start.20 = (bf16[512,3072]{1,0:T(8,128)(2,1)}, bf16[512,3072]{1,0:T(8,128)(2,1)}, u32[]{:S(2)}, u32[]{:S(2)}) collective-permute-start(bf16[512,3072]{1,0:T(8,128)(2,1)} %convolution_convert_fusion.2), channel_id=1, source_target_pairs={{0,4},{4,0},{8,12},{12,8},{16,20},{20,16},{24,28},{28,24},{1,5},{5... | collective-permute-start | bytes 9437192 | tf_op jit(solution)/shard_map/ppermute | solution.py:27
  340.6 20.8 %collective-permute-start.19 = (bf16[1,32,4096]{2,1,0:T(8,128)(2,1)}, bf16[1,32,4096]{2,1,0:T(8,128)(2,1)}, u32[]{:S(2)}, u32[]{:S(2)}) collective-permute-start(bf16[1,32,4096]{2,1,0:T(8,128)(2,1)} %constant_dynamic-slice_fusion.10), channel_id=1, source_target_pairs={{0,16},{4,20},{8,24},{12,28},{16,0},{20,4},{24,8},{28,12},{1,17},{... | collective-permute-start | bytes 786440 | tf_op jit(solution)/shard_map/ppermute | solution.py:27
  349.0 14.2 %copy-start.26 = (bf16[512,4,1,256]{0,3,1,2:T(8,128)(2,1)S(1)}, bf16[512,4,1,256]{0,3,1,2:T(8,128)(2,1)}, u32[]{:S(2)}) copy-start(bf16[512,4,1,256]{0,3,1,2:T(8,128)(2,1)} %copy.142) | copy-start | bytes 3145732
  359.6 34.5 %collective-permute-start.29 = (bf16[2048,1024]{1,0:T(8,128)(2,1)}, bf16[2048,1024]{1,0:T(8,128)(2,1)}, u32[]{:S(2)}, u32[]{:S(2)}) collective-permute-start(bf16[2048,1024]{1,0:T(8,128)(2,1)} %convolution_convert_fusion.3), channel_id=1, source_target_pairs={{0,4},{4,0},{8,12},{12,8},{16,20},{20,16},{24,28},{28,24},{1,5},{5... | collective-permute-start | bytes 12582920 | tf_op jit(solution)/shard_map/ppermute | solution.py:27
  361.4 221.2 %reduce-scatter.9.cloned.1.call-start = ((), (), s32[]{:S(2)}) async-start(), calls=%async_computation.7 | async-start | bytes 327680 | tf_op jit(solution)/shard_map/reduce_scatter | solution.py:76
  363.2 220.9 %reduce-scatter.7.cloned.1.call-start = ((), (), s32[]{:S(2)}) async-start(), calls=%async_computation.6 | async-start | bytes 655360 | tf_op jit(solution)/shard_map/reduce_scatter | solution.py:76
  366.3 25.6 %collective-permute-start.15 = (bf16[2,256,1024]{2,1,0:T(8,128)(2,1)S(1)}, bf16[2,256,1024]{2,1,0:T(8,128)(2,1)S(1)}, u32[]{:S(2)}, u32[]{:S(2)}) collective-permute-start(bf16[2,256,1024]{2,1,0:T(8,128)(2,1)S(1)} %dynamic-slice_bitcast_fusion.4), channel_id=1, source_target_pairs={{0,8},{4,12},{8,0},{12,4},{16,24},{20,28},{24,16},{28,20},{1,9},{5... | collective-permute-start | bytes 3145736 | tf_op jit(solution)/shard_map/ppermute | solution.py:27
  380.0 94.0 %collective-permute-start.21 = (bf16[1,256,3072]{2,1,0:T(8,128)(2,1)}, bf16[1,256,3072]{2,1,0:T(8,128)(2,1)}, u32[]{:S(2)}, u32[]{:S(2)}) collective-permute-start(bf16[1,256,3072]{2,1,0:T(8,128)(2,1)} %dynamic-slice_bitcast_fusion.2), channel_id=1, source_target_pairs={{0,16},{4,20},{8,24},{12,28},{16,0},{20,4},{24,8},{28,12},{1,17},{... | collective-permute-start | bytes 4718600 | tf_op jit(solution)/shard_map/ppermute | solution.py:27
  381.8 12.4 %copy-start.22 = (bf16[512,4,1,512]{0,3,1,2:T(8,128)(2,1)S(1)}, bf16[512,4,1,512]{0,3,1,2:T(8,128)(2,1)}, u32[]{:S(2)}) copy-start(bf16[512,4,1,512]{0,3,1,2:T(8,128)(2,1)} %copy.153) | copy-start | bytes 6291460
  381.8 95.3 %collective-permute-start.27 = (bf16[1,256,4096]{2,1,0:T(8,128)(2,1)}, bf16[1,256,4096]{2,1,0:T(8,128)(2,1)}, u32[]{:S(2)}, u32[]{:S(2)}) collective-permute-start(bf16[1,256,4096]{2,1,0:T(8,128)(2,1)} %dynamic-slice_bitcast_fusion.1), channel_id=1, source_target_pairs={{0,16},{4,20},{8,24},{12,28},{16,0},{20,4},{24,8},{28,12},{1,17},{... | collective-permute-start | bytes 6291464 | tf_op jit(solution)/shard_map/ppermute | solution.py:27
  392.4 80.4 %collective-permute-start.16 = (bf16[1,256,1024]{2,1,0:T(8,128)(2,1)S(1)}, bf16[1,256,1024]{2,1,0:T(8,128)(2,1)S(1)}, u32[]{:S(2)}, u32[]{:S(2)}) collective-permute-start(bf16[1,256,1024]{2,1,0:T(8,128)(2,1)S(1)} %constant_dynamic-slice_fusion.11), channel_id=1, source_target_pairs={{0,16},{4,20},{8,24},{12,28},{16,0},{20,4},{24,8},{28,12},{1,17},{... | collective-permute-start | bytes 1572872 | tf_op jit(solution)/shard_map/ppermute | solution.py:27
  402.6 118.1 %collective-permute-start.30 = (bf16[2,512,1024]{2,1,0:T(8,128)(2,1)}, bf16[2,512,1024]{2,1,0:T(8,128)(2,1)}, u32[]{:S(2)}, u32[]{:S(2)}) collective-permute-start(bf16[2,512,1024]{2,1,0:T(8,128)(2,1)} %dynamic-slice_bitcast_fusion), channel_id=1, source_target_pairs={{0,8},{4,12},{8,0},{12,4},{16,24},{20,28},{24,16},{28,20},{1,9},{5... | collective-permute-start | bytes 6291464 | tf_op jit(solution)/shard_map/ppermute | solution.py:27
  473.9 111.8 %reduce-scatter.11.cloned.1.call-start = ((), (), s32[]{:S(2)}) async-start(), calls=%async_computation.8 | async-start | bytes 983040 | tf_op jit(solution)/shard_map/reduce_scatter | solution.py:76
  476.6 20.5 %collective-permute-start.22 = (bf16[1,128,3072]{2,1,0:T(8,128)(2,1)S(1)}, bf16[1,128,3072]{2,1,0:T(8,128)(2,1)S(1)}, u32[]{:S(2)}, u32[]{:S(2)}) collective-permute-start(bf16[1,128,3072]{2,1,0:T(8,128)(2,1)S(1)} %dynamic-slice_bitcast_fusion.5), channel_id=1, source_target_pairs={{0,8},{4,12},{8,0},{12,4},{16,24},{20,28},{24,16},{28,20},{1,9},{5... | collective-permute-start | bytes 2359304 | tf_op jit(solution)/shard_map/ppermute | solution.py:27
  480.5 37.6 %collective-permute-start.28 = (bf16[1,128,4096]{2,1,0:T(8,128)(2,1)}, bf16[1,128,4096]{2,1,0:T(8,128)(2,1)}, u32[]{:S(2)}, u32[]{:S(2)}) collective-permute-start(bf16[1,128,4096]{2,1,0:T(8,128)(2,1)} %dynamic-slice_bitcast_fusion.3), channel_id=1, source_target_pairs={{0,8},{4,12},{8,0},{12,4},{16,24},{20,28},{24,16},{28,20},{1,9},{5... | collective-permute-start | bytes 3145736 | tf_op jit(solution)/shard_map/ppermute | solution.py:27
  498.3 89.1 %reduce-scatter.15.cloned.1.call-start = ((), (), s32[]{:S(2)}) async-start(), calls=%async_computation.10 | async-start | bytes 1310720 | tf_op jit(solution)/shard_map/reduce_scatter | solution.py:76
  520.6 68.5 %reduce-scatter.17.cloned.1.call-start = ((), (), s32[]{:S(2)}) async-start(), calls=%async_computation.11 | async-start | bytes 1310720 | tf_op jit(solution)/shard_map/reduce_scatter | solution.py:76
  524.2 23.6 %collective-permute-start.31 = (bf16[1,512,1024]{2,1,0:T(8,128)(2,1)S(1)}, bf16[1,512,1024]{2,1,0:T(8,128)(2,1)S(1)}, u32[]{:S(2)}, u32[]{:S(2)}) collective-permute-start(bf16[1,512,1024]{2,1,0:T(8,128)(2,1)S(1)} %constant_dynamic-slice_fusion), channel_id=1, source_target_pairs={{0,16},{4,20},{8,24},{12,28},{16,0},{20,4},{24,8},{28,12},{1,17},{... | collective-permute-start | bytes 3145736 | tf_op jit(solution)/shard_map/ppermute | solution.py:27
  533.1 16.1 %copy-start.32 = (bf16[512,1024]{1,0:T(8,128)(2,1)S(1)}, bf16[512,1024]{1,0:T(8,128)(2,1)}, u32[]{:S(2)}) copy-start(bf16[512,1024]{1,0:T(8,128)(2,1)} %add_convert_fusion.7) | copy-start | bytes 3145732
  549.3 9.8 %collective-permute-start.6 = (bf16[128,1024]{1,0:T(8,128)(2,1)S(1)}, bf16[128,1024]{1,0:T(8,128)(2,1)S(1)}, u32[]{:S(2)}, u32[]{:S(2)}) collective-permute-start(bf16[128,1024]{1,0:T(8,128)(2,1)S(1)} %get-tuple-element.118), channel_id=1, source_target_pairs={{0,24},{4,28},{8,16},{12,20},{16,8},{20,12},{24,0},{28,4},{1,25},{... | collective-permute-start | bytes 786440 | tf_op jit(solution)/shard_map/ppermute | solution.py:27
  550.8 10.9 %collective-permute-start.5 = (bf16[128,1024]{1,0:T(8,128)(2,1)S(1)}, bf16[128,1024]{1,0:T(8,128)(2,1)S(1)}, u32[]{:S(2)}, u32[]{:S(2)}) collective-permute-start(bf16[128,1024]{1,0:T(8,128)(2,1)S(1)} %get-tuple-element.119), channel_id=1, source_target_pairs={{0,16},{4,20},{8,24},{12,28},{16,0},{20,4},{24,8},{28,12},{1,17},{... | collective-permute-start | bytes 786440 | tf_op jit(solution)/shard_map/ppermute | solution.py:27
  551.2 10.5 %collective-permute-start.4 = (bf16[128,1024]{1,0:T(8,128)(2,1)S(1)}, bf16[128,1024]{1,0:T(8,128)(2,1)S(1)}, u32[]{:S(2)}, u32[]{:S(2)}) collective-permute-start(bf16[128,1024]{1,0:T(8,128)(2,1)S(1)} %get-tuple-element.120), channel_id=1, source_target_pairs={{0,8},{4,12},{8,0},{12,4},{16,24},{20,28},{24,16},{28,20},{1,9},{5... | collective-permute-start | bytes 786440 | tf_op jit(solution)/shard_map/ppermute | solution.py:27
  562.8 10.4 %collective-permute-start.13 = (bf16[128,1024]{1,0:T(8,128)(2,1)}, bf16[128,1024]{1,0:T(8,128)(2,1)S(1)}, u32[]{:S(2)}, u32[]{:S(2)}) collective-permute-start(bf16[128,1024]{1,0:T(8,128)(2,1)} %get-tuple-element.110), channel_id=1, source_target_pairs={{0,24},{4,28},{8,16},{12,20},{16,8},{20,12},{24,0},{28,4},{1,25},{... | collective-permute-start | bytes 786440 | tf_op jit(solution)/shard_map/ppermute | solution.py:27
  564.2 12.8 %collective-permute-start.12 = (bf16[128,1024]{1,0:T(8,128)(2,1)}, bf16[128,1024]{1,0:T(8,128)(2,1)S(1)}, u32[]{:S(2)}, u32[]{:S(2)}) collective-permute-start(bf16[128,1024]{1,0:T(8,128)(2,1)} %get-tuple-element.111), channel_id=1, source_target_pairs={{0,16},{4,20},{8,24},{12,28},{16,0},{20,4},{24,8},{28,12},{1,17},{... | collective-permute-start | bytes 786440 | tf_op jit(solution)/shard_map/ppermute | solution.py:27
  564.8 12.2 %collective-permute-start.11 = (bf16[128,1024]{1,0:T(8,128)(2,1)}, bf16[128,1024]{1,0:T(8,128)(2,1)S(1)}, u32[]{:S(2)}, u32[]{:S(2)}) collective-permute-start(bf16[128,1024]{1,0:T(8,128)(2,1)} %get-tuple-element.112), channel_id=1, source_target_pairs={{0,8},{4,12},{8,0},{12,4},{16,24},{20,28},{24,16},{28,20},{1,9},{5... | collective-permute-start | bytes 786440 | tf_op jit(solution)/shard_map/ppermute | solution.py:27
  (56 other events, 262.3 us)
Sparse Core Ops, SparseCore 0:
  361.5 20.2 reduce-scatter.12
  384.2 17.8 reduce-scatter.8
  474.0 21.7 reduce-scatter.6
  498.4 23.4 reduce-scatter.10
  524.0 26.4 reduce-scatter.14
  552.7 25.7 reduce-scatter.16

commit v2 on v1

v2 whole, which is shorter than its diff:
```python
import functools
import math

import jax
import jax.numpy as jnp
from jax import lax
from jax.experimental import pallas as pl
from jax.experimental.pallas import tpu as pltpu
from jax.sharding import PartitionSpec as P

HD = 64
PAIR = 2 * HD
eps_norm = 1e-06
neg_fill = -1e30
BF = jnp.bfloat16
F32 = jnp.float32
DIMS_FIRST = (((0,), (0,)), ((), ()))
DIMS_LAST = (((1,), (1,)), ((), ()))
LOG2E = 1.4426950408889634
VMEM_BYTES = 56 * 1024 * 1024


def dot(left, right, dims=(((1,), (0,)), ((), ()))):
    return lax.dot_general(left, right, dims, preferred_element_type=F32)


def swap(values, axis_name, bits):
    size = lax.axis_size(axis_name)
    return lax.ppermute(values, axis_name, [(i, i ^ bits) for i in range(size)])


def pick(values, index, axis):
    return lax.dynamic_index_in_dim(values, index, axis, keepdims=False)


def after(value, *others):
    return lax.optimization_barrier((value, *others))[0]


def to_buckets(parts, span, mine):
    got = [pick(parts, mine, 0)]
    for step in range(1, parts.shape[0]):
        got.append(swap(pick(parts, mine ^ step, 0), "head", step * span))
    return got


def from_buckets(parts, span, mine):
    count = parts.shape[0]
    got = [parts[0]]
    for step in range(1, count):
        got.append(swap(parts[step], "head", step * span))
    got = jnp.stack(got)
    return jnp.stack([pick(got, mine ^ micro, 0) for micro in range(count)])


def core_sum(away, keep):
    return (keep.astype(F32) + swap(away, "head", 1).astype(F32)).astype(BF)


def scatter(total, descending):
    groups = lax.axis_size("head")
    place = lax.axis_index("head")
    width = total.shape[1]
    chunk = total.shape[0] // (groups // 2)
    remaining = list(range(1, groups.bit_length() - 1))
    for bit in remaining[::-1] if descending else list(remaining):
        tail = 2 ** len([b for b in remaining if b < bit]) * chunk
        view = total.reshape(-1, 2, tail, width)
        here = (place >> bit) % 2
        came = swap(pick(view, 1 - here, 1), "head", 2**bit)
        total = (pick(view, here, 1).astype(F32) + came.astype(F32)).astype(BF)
        remaining.remove(bit)
    total = total.reshape(chunk, width)
    return lax.psum_scatter(total, "seq", scatter_dimension=0, tiled=True).astype(F32)


def norm_stats(hidden):
    centred = hidden - jnp.mean(hidden, axis=-1, keepdims=True)
    rate = lax.rsqrt(jnp.mean(centred * centred, axis=-1, keepdims=True) + eps_norm)
    return centred * rate, rate


def norm_back(grad, normal, rate, scale_term):
    inner = grad * (1.0 + scale_term)
    return rate * (
        inner
        - jnp.mean(inner, axis=-1, keepdims=True)
        - normal * jnp.mean(inner * normal, axis=-1, keepdims=True)
    )


def time_features(times, feature_count):
    half = feature_count // 2
    steps = jnp.exp(jnp.arange(half, dtype=F32) * (-math.log(10000.0) / (half - 1)))
    angles = 1000.0 * times[:, None] * steps
    return jnp.concatenate([jnp.sin(angles), jnp.cos(angles)], axis=-1).astype(BF)


def params():
    return pltpu.CompilerParams(vmem_limit_bytes=VMEM_BYTES)


def cost(flops, moved, hard=0):
    return pl.CostEstimate(flops=int(flops), bytes_accessed=int(moved), transcendentals=int(hard))


def turn(values):
    lanes = lax.broadcasted_iota(jnp.int32, values.shape, 1)
    low = lax.rem(lanes, HD) < HD // 2
    return jnp.where(low, pltpu.roll(values, PAIR - HD // 2, 1), pltpu.roll(values, HD // 2, 1))


def project_kernel(tiles, x_ref, w_ref, cos_ref, sin_ref, o_ref):
    raw = dot(x_ref[...], w_ref[...])

    @pl.when(pl.program_id(0) < 2 * tiles)
    def _():
        factor = jnp.where(pl.program_id(0) < tiles, HD ** (-0.5) * LOG2E, 1.0)
        for first in range(0, raw.shape[1], PAIR):
            part = raw[:, first : first + PAIR]
            turned = part * cos_ref[...] + turn(part) * sin_ref[...]
            o_ref[:, first : first + PAIR] = (turned * factor).astype(BF)

    @pl.when(pl.program_id(0) >= 2 * tiles)
    def _():
        o_ref[...] = raw.astype(BF)


def project(normed, w_qkv, cos_table, sin_table):
    frames, width = normed.shape
    tile = 512
    return pl.pallas_call(
        functools.partial(project_kernel, width // tile),
        grid=(3 * width // tile,),
        in_specs=[
            pl.BlockSpec((frames, width), lambda i: (0, 0)),
            pl.BlockSpec((width, tile), lambda i: (0, i)),
            pl.BlockSpec((frames, PAIR), lambda i: (0, 0)),
            pl.BlockSpec((frames, PAIR), lambda i: (0, 0)),
        ],
        out_specs=pl.BlockSpec((frames, tile), lambda i: (0, i)),
        out_shape=jax.ShapeDtypeStruct((frames, 3 * width), BF),
        compiler_params=params(),
        cost_estimate=cost(6 * frames * width * width, 6 * width * width + 8 * frames * width),
    )(normed, w_qkv, cos_table, sin_table)


def only_head(values, which):
    lanes = lax.broadcasted_iota(jnp.int32, values.shape, 1)
    mine = (lanes >= which * HD) & (lanes < (which + 1) * HD)
    return jnp.where(mine, values, jnp.zeros_like(values))


def attend_kernel(span, q_ref, *refs):
    k_refs, v_refs = refs[:span], refs[span : 2 * span]
    mk_ref, mq_ref, o_ref, p_ref, l_ref, bias_ref = refs[2 * span :]
    frames = q_ref.shape[0]

    @pl.when(pl.program_id(0) == 0)
    def _():
        seg_q, place_q = mq_ref[0:1, :], mq_ref[1:2, :]
        for index in range(span):
            rows = slice(index * frames, (index + 1) * frames)
            seg_k, place_k, live_k = mk_ref[rows, 0:1], mk_ref[rows, 1:2], mk_ref[rows, 2:3]
            allowed = (seg_q == seg_k) & ((live_k == 1) | (place_q == place_k))
            bias_ref[rows, :] = jnp.where(allowed, 0.0, neg_fill)

    values_t = [v[...].T for v in v_refs]
    ones = jnp.ones((16, frames), BF)
    results, inverses = [], []
    for which in range(2):
        queries = only_head(q_ref[...], which)
        scores = [
            dot(k[...], queries, DIMS_LAST) + bias_ref[i * frames : (i + 1) * frames, :]
            for i, k in enumerate(k_refs)
        ]
        top = functools.reduce(jnp.maximum, [jnp.max(s, axis=0, keepdims=True) for s in scores])
        result = None
        for index, part in enumerate(scores):
            powered = jnp.exp2(part - top).astype(BF)
            p_ref[which, index * frames : (index + 1) * frames, :] = powered
            lanes = values_t[index][which * HD : (which + 1) * HD]
            part = dot(jnp.concatenate([lanes, ones], axis=0), powered)
            result = part if result is None else result + part
        inverse = 1.0 / result[HD : HD + 1]
        results.append(result[:HD] * inverse)
        inverses.append(inverse)
    o_ref[...] = jnp.concatenate(results, axis=0).T.astype(BF)
    l_ref[0] = jnp.concatenate(inverses + [jnp.zeros((6, frames), F32)], axis=0)


def columns(frames, start=0):
    return pl.BlockSpec((frames, PAIR), lambda i: (0, start + i))


def attend(packed, others, meta_k, meta_q):
    span = len(others) + 1
    frames, width = packed.shape[0], packed.shape[1] // 3
    pairs = width // PAIR
    keys = span * frames
    return pl.pallas_call(
        functools.partial(attend_kernel, span),
        grid=(pairs,),
        in_specs=[columns(frames), columns(frames, pairs)]
        + [columns(frames)] * (span - 1)
        + [columns(frames, 2 * pairs)]
        + [columns(frames, pairs)] * (span - 1)
        + [
            pl.BlockSpec((keys, PAIR), lambda i: (0, 0)),
            pl.BlockSpec((8, frames), lambda i: (0, 0)),
        ],
        out_specs=[
            columns(frames),
            pl.BlockSpec((2, keys, frames), lambda i: (i, 0, 0)),
            pl.BlockSpec((1, 8, frames), lambda i: (i, 0, 0)),
        ],
        out_shape=[
            jax.ShapeDtypeStruct((frames, width), BF),
            jax.ShapeDtypeStruct((2 * pairs, keys, frames), BF),
            jax.ShapeDtypeStruct((pairs, 8, frames), F32),
        ],
        scratch_shapes=[pltpu.VMEM((keys, frames), F32)],
        compiler_params=params(),
        cost_estimate=cost(
            16 * pairs * frames * keys * PAIR,
            4 * pairs * frames * keys,
            2 * pairs * frames * keys,
        ),
    )(packed, packed, *others, packed, *others, meta_k, meta_q)


def grad_heads_kernel(g_ref, w_ref, a_ref, l_ref, o_ref, c_ref):
    grads = dot(g_ref[...], w_ref[...], DIMS_LAST)
    for pair in range(l_ref.shape[0]):
        lanes = slice(pair * PAIR, (pair + 1) * PAIR)
        own = lax.broadcasted_iota(jnp.int32, (8, PAIR), 1) // HD
        own = (own == lax.broadcasted_iota(jnp.int32, (8, PAIR), 0)).astype(F32)
        spread = lax.dot_general(
            l_ref[pair], own, DIMS_FIRST, precision=lax.Precision.HIGHEST, preferred_element_type=F32
        )
        scaled = grads[:, lanes] * spread
        o_ref[:, lanes] = scaled.astype(BF)
        c_ref[pair] = lax.dot_general(
            own,
            scaled * a_ref[:, lanes].astype(F32),
            DIMS_LAST,
            precision=lax.Precision.HIGHEST,
            preferred_element_type=F32,
        )


def grad_heads(grad_low, w_out, attended, inverses):
    frames, width = grad_low.shape
    pairs = width // PAIR
    tile = 2
    return pl.pallas_call(
        grad_heads_kernel,
        grid=(pairs // tile,),
        in_specs=[
            pl.BlockSpec((frames, width), lambda i: (0, 0)),
            pl.BlockSpec((tile * PAIR, width), lambda i: (i, 0)),
            pl.BlockSpec((frames, tile * PAIR), lambda i: (0, i)),
            pl.BlockSpec((tile, 8, frames), lambda i: (i, 0, 0)),
        ],
        out_specs=[
            pl.BlockSpec((frames, tile * PAIR), lambda i: (0, i)),
            pl.BlockSpec((tile, 8, frames), lambda i: (i, 0, 0)),
        ],
        out_shape=[
            jax.ShapeDtypeStruct((frames, width), BF),
            jax.ShapeDtypeStruct((pairs, 8, frames), F32),
        ],
        compiler_params=params(),
        cost_estimate=cost(2 * frames * width * width, 2 * width * width + 6 * frames * width),
    )(grad_low, w_out, attended, inverses)


def attend_back_kernel(span, q_ref, *refs):
    k_refs, v_refs = refs[:span], refs[span : 2 * span]
    p_ref, c_ref, g_ref, cos_ref, sin_ref = refs[2 * span : 2 * span + 5]
    dq_ref = refs[2 * span + 5]
    dk_refs = refs[2 * span + 6 : 3 * span + 6]
    dv_refs = refs[3 * span + 6 : 4 * span + 6]
    ds_ref = refs[4 * span + 6]
    frames = q_ref.shape[0]

    def unturn(grad, index):
        rows = slice(index * frames, (index + 1) * frames)
        return grad * cos_ref[rows, :] - turn(grad) * sin_ref[rows, :]

    keys_t = [k[...].T for k in k_refs]
    dk, dv, dq = [None] * span, [None] * span, []
    for which in range(2):
        centre = c_ref[0, which : which + 1, :]
        grads = only_head(g_ref[...], which)
        queries = only_head(q_ref[...], which)
        result = None
        for index in range(span):
            rows = slice(index * frames, (index + 1) * frames)
            grad_probs = dot(v_refs[index][...], grads, DIMS_LAST)
            soft = p_ref[which, rows, :]
            ds_ref[rows, :] = (soft.astype(F32) * (grad_probs - centre)).astype(BF)
            part = dot(soft, grads)
            dv[index] = part if dv[index] is None else dv[index] + part
            part = dot(ds_ref[rows, :], queries)
            dk[index] = part if dk[index] is None else dk[index] + part
            part = dot(keys_t[index][which * HD : (which + 1) * HD], ds_ref[rows, :])
            result = part if result is None else result + part
        dq.append(result)
    dq = jnp.concatenate(dq, axis=0).T
    dq_ref[...] = unturn(dq * HD ** (-0.5), 0).astype(BF)
    for index in range(span):
        dk_refs[index][...] = unturn(dk[index] * (1.0 / LOG2E), index).astype(BF)
        dv_refs[index][...] = dv[index].astype(BF)


def attend_back(packed, others, probs, centres, grads, cos_keys, sin_keys):
    span = len(others) + 1
    frames, width = packed.shape[0], packed.shape[1] // 3
    pairs = width // PAIR
    keys = span * frames
    out = jax.ShapeDtypeStruct((frames, width), BF)
    results = pl.pallas_call(
        functools.partial(attend_back_kernel, span),
        grid=(pairs,),
        in_specs=[columns(frames), columns(frames, pairs)]
        + [columns(frames)] * (span - 1)
        + [columns(frames, 2 * pairs)]
        + [columns(frames, pairs)] * (span - 1)
        + [
            pl.BlockSpec((2, keys, frames), lambda i: (i, 0, 0)),
            pl.BlockSpec((1, 8, frames), lambda i: (i, 0, 0)),
            columns(frames),
            pl.BlockSpec((keys, PAIR), lambda i: (0, 0)),
            pl.BlockSpec((keys, PAIR), lambda i: (0, 0)),
        ],
        out_specs=[columns(frames)] * (2 * span + 1),
        out_shape=[out] * (2 * span + 1),
        scratch_shapes=[pltpu.VMEM((keys, frames), BF)],
        compiler_params=params(),
        cost_estimate=cost(32 * pairs * frames * keys * PAIR, 4 * pairs * frames * keys),
    )(packed, packed, *others, packed, *others, probs, centres, grads, cos_keys, sin_keys)
    return results[0], results[1 : span + 1], results[span + 1 :]


def split_rows(source, target, groups, low_bit):
    chunk = source.shape[0] // groups
    half = source.shape[0] // 2
    for index in range(groups // 2):
        for part, bit in ((0, 1 - low_bit), (1, low_bit)):
            first = pl.multiple_of((2 * index + bit) * chunk, chunk)
            start = part * half + index * chunk
            target[start : start + chunk, :] = source[pl.ds(first, chunk), :]


def feed_kernel(groups, x_ref, g_ref, up_ref, down_ref, *refs):
    acc_ref, gx_ref, da_ref, dk_ref, ua_ref, uk_ref, t_ref, xt_ref = refs
    step = pl.program_id(0)
    low_bit = lax.axis_index("head") % 2

    @pl.when(step == 0)
    def _():
        t_ref[...] = x_ref[...].T
        split_rows(t_ref, xt_ref, groups, low_bit)
        acc_ref[...] = jnp.zeros_like(acc_ref)
        gx_ref[...] = jnp.zeros_like(gx_ref)

    up = dot(x_ref[...], up_ref[...])
    grad_hidden = dot(g_ref[...], down_ref[...], DIMS_LAST)
    root = math.sqrt(2.0 / math.pi)
    square = up * up
    bent = jnp.tanh(root * up * (1.0 + 0.044715 * square))
    half = 0.5 + 0.5 * bent
    slope = half + 0.5 * up * (1.0 - bent * bent) * (root * (1.0 + 3 * 0.044715 * square))
    hidden = (up * half).astype(BF)
    grad_up = (grad_hidden * slope).astype(BF)
    acc_ref[...] += dot(hidden, down_ref[...])
    gx_ref[...] += dot(grad_up, up_ref[...], DIMS_LAST)
    rows = dot(hidden, g_ref[...], DIMS_FIRST).astype(BF)

    @pl.when(step % 2 == low_bit)
    def _():
        dk_ref[...] = rows

    @pl.when(step % 2 != low_bit)
    def _():
        da_ref[...] = rows

    depth = x_ref.shape[1] // 2
    ua_ref[...] = dot(xt_ref[:depth, :], grad_up).astype(BF)
    uk_ref[...] = dot(xt_ref[depth:, :], grad_up).astype(BF)


def feed(normed, grads, w_up, w_down):
    groups = lax.axis_size("head")
    frames, width = normed.shape
    inner = w_up.shape[1]
    tile = inner // groups
    whole = pl.BlockSpec((frames, width), lambda i: (0, 0))
    rows = pl.BlockSpec((tile, width), lambda i: (i // 2, 0))
    cols = pl.BlockSpec((width // 2, tile), lambda i: (0, i))
    total = jax.ShapeDtypeStruct((frames, width), F32)
    down = jax.ShapeDtypeStruct((inner // 2, width), BF)
    up = jax.ShapeDtypeStruct((width // 2, inner), BF)
    return pl.pallas_call(
        functools.partial(feed_kernel, groups),
        grid=(groups,),
        in_specs=[
            whole,
            whole,
            pl.BlockSpec((width, tile), lambda i: (0, i)),
            pl.BlockSpec((tile, width), lambda i: (i, 0)),
        ],
        out_specs=[whole, whole, rows, rows, cols, cols],
        out_shape=[total, total, down, down, up, up],
        scratch_shapes=[pltpu.VMEM((width, frames), BF), pltpu.VMEM((width, frames), BF)],
        compiler_params=params(),
        cost_estimate=cost(12 * frames * width * inner, 8 * width * inner, frames * inner),
    )(normed, grads, w_up, w_down)


def weight_kernel(groups, x_ref, g_ref, away_ref, keep_ref, t_ref, xt_ref):
    @pl.when(pl.program_id(0) == 0)
    def _():
        t_ref[...] = x_ref[...].T
        split_rows(t_ref, xt_ref, groups, lax.axis_index("head") % 2)

    half = x_ref.shape[1] // 2
    away_ref[...] = dot(xt_ref[:half, :], g_ref[...]).astype(BF)
    keep_ref[...] = dot(xt_ref[half:, :], g_ref[...]).astype(BF)


def weight_grad(left, right):
    groups = lax.axis_size("head")
    frames, rows = left.shape
    width = right.shape[1]
    tile = 512
    spec = pl.BlockSpec((rows // 2, tile), lambda i: (0, i))
    out = jax.ShapeDtypeStruct((rows // 2, width), BF)
    return pl.pallas_call(
        functools.partial(weight_kernel, groups),
        grid=(width // tile,),
        in_specs=[
            pl.BlockSpec((frames, rows), lambda i: (0, 0)),
            pl.BlockSpec((frames, tile), lambda i: (0, i)),
        ],
        out_specs=[spec, spec],
        out_shape=[out, out],
        scratch_shapes=[pltpu.VMEM((rows, frames), BF), pltpu.VMEM((rows, frames), BF)],
        compiler_params=params(),
        cost_estimate=cost(
            2 * frames * rows * width, 2 * rows * width + 2 * frames * (rows + width)
        ),
    )(left, right)


def per_device(
    inputs,
    skips,
    flow_time,
    segment_ids,
    frame_mask,
    cotangent,
    w_skip,
    w_time,
    w_qkv,
    w_out,
    w_up,
    w_down,
):
    groups = lax.axis_size("head")
    micro_count, _, rows, width = inputs.shape
    span = groups // micro_count
    place = lax.axis_index("head")
    mine = place // span
    frames = micro_count * rows
    feature_count = w_time.shape[0]
    inputs, skips, cotangent = inputs[:, 0], skips[:, 0], cotangent[:, 0]

    resid_own = dot(inputs.reshape(frames, width), w_skip[:width]) + dot(
        skips.reshape(frames, width), w_skip[width:]
    )
    own_mod = dot(time_features(flow_time.reshape(-1), feature_count), w_time[:, : 2 * width])
    normed_own = norm_stats(resid_own)[0] * (1.0 + own_mod[:, width:]) + own_mod[:, :width]
    normed_own = normed_own.astype(BF).reshape(micro_count, rows, width)

    meta = jnp.stack(
        [segment_ids[:, 0].astype(F32), frame_mask[:, 0].astype(F32), flow_time[:, 0]], axis=1
    )
    meta = [meta] + [swap(meta, "head", other) for other in range(1, span)]
    meta = jnp.stack(to_buckets(jnp.stack(meta, axis=1), span, mine))
    seg_keys, live_keys, times = [meta[:, :, i].swapaxes(0, 1).reshape(-1) for i in range(3)]
    order = jnp.stack(
        [place ^ other ^ (step * span) for other in range(span) for step in range(micro_count)]
    )
    place_keys = (order[:, None] * rows + jnp.arange(rows)[None, :]).reshape(-1).astype(F32)
    starts = jnp.sum((seg_keys[None, :] < seg_keys[:, None]).astype(F32), axis=1)
    positions = place_keys - starts
    inv_freq = jnp.exp(jnp.arange(HD // 2, dtype=F32) * (-2.0 * math.log(10000.0) / HD))
    turns = positions[:, None] * inv_freq
    cos_half, sin_half = jnp.cos(turns), jnp.sin(turns)
    cos_keys = jnp.concatenate([cos_half] * 4, axis=1)
    sin_keys = jnp.concatenate([-sin_half, sin_half] * 2, axis=1)
    meta_q = jnp.stack(
        [seg_keys[:frames], place_keys[:frames]] + [jnp.zeros((frames,), F32)] * 6
    )
    meta_k = jnp.stack([seg_keys, place_keys, live_keys], axis=1)
    meta_k = jnp.pad(meta_k, ((0, 0), (0, PAIR - 3)))
    features = time_features(times[:frames], feature_count)
    modulation = dot(features, w_time)
    scale_first = modulation[:, width : 2 * width]
    shift_second = modulation[:, 2 * width : 3 * width]
    scale_second = modulation[:, 3 * width :]

    normed_attn = jnp.concatenate(to_buckets(normed_own, span, mine))
    second = jnp.stack(
        [cotangent, resid_own.astype(BF).reshape(micro_count, rows, width)], axis=1
    )
    second = to_buckets(after(second, normed_attn), span, mine)
    cot_rows = jnp.concatenate([part[0] for part in second])
    resid_in = jnp.concatenate([part[1] for part in second])

    packed = project(normed_attn, w_qkv, cos_keys[:frames], sin_keys[:frames])
    others = [swap(packed[:, width:], "head", other) for other in range(1, span)]
    attended, probs, inverses = attend(packed, others, meta_k, meta_q)
    resid_in, cot_rows, attended = lax.optimization_barrier((resid_in, cot_rows, attended))
    joined = to_buckets(after(jnp.concatenate([inputs, skips], axis=2), resid_in), span, mine)
    joined = jnp.concatenate(joined)
    resid_in = resid_in.astype(F32)
    resid_mid = resid_in + dot(attended, w_out)
    normal_second, rate_second = norm_stats(resid_mid)
    normed_ffn = (normal_second * (1.0 + scale_second) + shift_second).astype(BF)
    fed, grad_normed_ffn, down_away, down_keep, up_away, up_keep = feed(
        normed_ffn, cot_rows, w_up, w_down
    )
    down_sum, up_sum = core_sum(down_away, down_keep), core_sum(up_away, up_keep)
    total_down, total_up = scatter(down_sum, False), scatter(up_sum, True)
    output = (resid_mid + fed).astype(BF)
    output = from_buckets(output.reshape(micro_count, rows, width), span, mine)

    grad_mid = cot_rows.astype(F32) + norm_back(
        grad_normed_ffn, normal_second, rate_second, scale_second
    )
    grad_mid_low = grad_mid.astype(BF)
    grads, centres = grad_heads(grad_mid_low, w_out, attended, inverses)
    out_away, out_keep = weight_grad(attended, grad_mid_low)
    grads, down_sum, up_sum, out_away = lax.optimization_barrier((grads, down_sum, up_sum, out_away))
    total_out = scatter(core_sum(out_away, out_keep), False)
    dq, dk, dv = attend_back(packed, others, probs, centres, grads, cos_keys, sin_keys)
    key_sum, value_sum = dk[0].astype(F32), dv[0].astype(F32)
    for other in range(1, span):
        both = swap(jnp.stack([dk[other], dv[other]]), "head", other).astype(F32)
        key_sum, value_sum = key_sum + both[0], value_sum + both[1]
    grad_proj = jnp.concatenate([dq, key_sum.astype(BF), value_sum.astype(BF)], axis=1)
    total_qkv = scatter(core_sum(*weight_grad(normed_attn, grad_proj)), True)
    grad_normed_attn = dot(grad_proj, w_qkv, DIMS_LAST)
    normal_first, rate_first = norm_stats(resid_in)
    grad_in_low = (
        grad_mid + norm_back(grad_normed_attn, normal_first, rate_first, scale_first)
    ).astype(BF)
    total_skip = scatter(core_sum(*weight_grad(joined, grad_in_low)), False)
    grad_modulation = jnp.concatenate(
        [
            grad_normed_attn,
            grad_normed_attn * normal_first,
            grad_normed_ffn,
            grad_normed_ffn * normal_second,
        ],
        axis=1,
    ).astype(BF)
    total_time = scatter(core_sum(*weight_grad(features, grad_modulation)), True)
    grad_local = from_buckets(grad_in_low.reshape(micro_count, rows, width), span, mine)
    grad_local = grad_local.reshape(frames, width)
    shape = (micro_count, 1, rows, width)
    input_grad = dot(grad_local, w_skip[:width], DIMS_LAST).reshape(shape)
    skip_grad = dot(grad_local, w_skip[width:], DIMS_LAST).reshape(shape)
    return (
        output[:, None],
        input_grad,
        skip_grad,
        total_skip,
        total_time,
        total_qkv,
        total_out,
        total_up,
        total_down,
    )


def solution(mesh):
    frames_spec = P(None, "seq", "head", None)
    line_spec = P(None, "seq", "head")
    shard_spec = P(("head", "seq"), None)
    return jax.shard_map(
        per_device,
        mesh=mesh,
        in_specs=(frames_spec, frames_spec, line_spec, line_spec, line_spec, frames_spec)
        + (P(),) * 6,
        out_specs=(frames_spec,) * 3 + (shard_spec,) * 6,
        check_vma=False,
    )
```

time: 605 us -> 489 us (0.81)
  local copies, waits for them, and re-layouts: 122 us -> 26.3 us
  matrix products: 115 us -> 27 us
  Pallas kernels: 70.6 us -> 129 us
  other arithmetic: 58.2 us -> 96.2 us
  blocking collectives: 16.1 us -> 0 us
  waiting for transfers between devices: 173 us -> 157 us
    dot_general x23 -> x8, matrix products: 115 us -> 27 us  [dot(): return lax.dot_general(left, right, dims, preferred_element_type=F32)]
    pallas_call x3 -> x9, Pallas kernels: 70.6 us -> 129 us  [the longest x1 37 us: feed(): pl.pallas_call(functools.partial(feed_kernel, groups), grid=(groups,), in...]
    unnamed x142 -> x76, local copies, waits for them, and re-layouts: 59.4 us -> 5.83 us
    dynamic_slice x11 -> x1, local copies, waits for them, and re-layouts: 30.5 us -> 0.21 us  [pick(): return lax.dynamic_index_in_dim(values, index, axis, keepdims=False)]
    convert_element_type x14 -> x22, other arithmetic: 24 us -> 47.6 us  [the longest x6 19.2 us: core_sum(): return (keep.astype(F32) + swap(away, 'head', 1).astype(F32)).astype(BF)]
    ppermute x32 -> x39, waiting for transfers between devices: 173 us -> 155 us  [swap(): return lax.ppermute(values, axis_name, [(i, i ^ bits) for i in range(size)])]
    reshape x5 -> x0, local copies, waits for them, and re-layouts: 16.5 us -> none  [weight_grad(): split = left.reshape(frames, groups // 2, 2, chunk)]
    all_gather x1 -> x0, blocking collectives: 16.1 us -> none  [per_device(): meta = lax.all_gather(meta, 'head', axis=0)]
  transfers between devices with their start and end apart: 38 -> 45, of which waited for: 12 -> 23; matrix products, arithmetic and copies ran while one was open for 37% -> 25% of each run, Pallas kernels for 0% -> 13%
where the time goes in v2:
time: 489 us; the launch traced here: 484 us
  waiting for transfers between devices  157 us (32%)
  Pallas kernels  129 us (26%)
  other arithmetic  96.2 us (20%)
  starting transfers between devices  34.1 us (7%)
  matrix products  27 us (6%)
  local copies, waits for them, and re-layouts  26.3 us (5%)
  between operations  15.1 us (3%)
    ppermute x39, waiting for transfers between devices, swap(): return lax.ppermute(values, axis_name, [(i, i ^ bits) for i in range(size)])  155 us
    pallas_call x1, Pallas kernels, feed(): pl.pallas_call(functools.partial(feed_kernel, groups), grid=(groups,), in...  37 us
    ppermute x39, starting transfers between devices, swap(): return lax.ppermute(values, axis_name, [(i, i ^ bits) for i in range(size)])  33.6 us
    dot_general x8, matrix products, dot(): return lax.dot_general(left, right, dims, preferred_element_type=F32)  27 us
    pallas_call x1, Pallas kernels, attend_back(): pl.pallas_call(functools.partial(attend_back_kernel, span), grid=(pairs,)...  25.8 us
    pallas_call x4, Pallas kernels, weight_grad(): pl.pallas_call(functools.partial(weight_kernel, groups), grid=(width // t...  25.6 us
    pallas_call x1, Pallas kernels, attend(): pl.pallas_call(functools.partial(attend_kernel, span), grid=(pairs,), in_...  20.7 us
    convert_element_type x6, other arithmetic, core_sum(): return (keep.astype(F32) + swap(away, 'head', 1).astype(F32)).astype(BF)  19.2 us
  transfers between devices with their start and end apart: 45, of which 23 were waited for; matrix products, arithmetic and copies ran while one was open for 25% of the time, Pallas kernels for 13%

profile of v2, /device:TPU:0, one launch (start us, length us, event | category | flops | bytes accessed | tf_op | source)
XLA Modules:
  0.0 484.5 jit_solution(618208408870253449)
XLA Ops:
  10.5 3.3 fusion.31
  15.9 2.6 collective-permute-start.7
  22.1 2.4 collective-permute-done.9
  24.5 2.4 fusion.57
  30.3 2.9 collective-permute-start.2
  38.9 3.6 collective-permute-done.1
  43.6 10.1 %shard_map.187.q_ref.refs_0_.refs_2_ = bf16[512,3072]{1,0:T(8,128)(2,1)} custom-call(bf16[512,1024]{1,0:T(8,128)(2,1)} %pad_maximum_fusion.6.x_ref, bf16[1024,3072]{1,0:T(8,128)(2,1)} %w_ref.2, f32[512,128]{1,0:T(8,128)} %slice.169.cos_ref, f32[512,128]{1,0:T(8,128)} %slice.170.sin_ref), custom_call_target="tpu_custom_call" | custom-call | flops 3221225472 | bytes 10485760 | tf_op jit(solution)/shard_map/pallas_call | solution.py:132
  53.7 3.2 slice.171
  59.5 4.6 fusion.77
  68.2 4.6 collective-permute-done.3
  73.9 16.8 %collective-permute-done.4 = bf16[2,128,1024]{2,1,0:T(8,128)(2,1)S(1)} collective-permute-done((bf16[2,128,1024]{2,1,0:T(8,128)(2,1)}, bf16[2,128,1024]{2,1,0:T(8,128)(2,1)S(1)}, u32[]{:S(2)}, u32[]{:S(2)}) %collective-permute-start.4) | collective-permute-done | bytes 524320 | tf_op jit(solution)/shard_map/ppermute | solution.py:29
  92.0 20.7 %shard_map.188 = (bf16[512,1024]{1,0:T(8,128)(2,1)}, bf16[16,1024,512]{2,1,0:T(8,128)(2,1)}, f32[8,8,512]{2,1,0:T(8,128)}) custom-call(bf16[512,3072]{1,0:T(8,128)(2,1)} %shard_map.187.q_ref.refs_0_.refs_2_, bf16[512,3072]{1,0:T(8,128)(2,1)} %shard_map.187.q_ref.refs_0_.refs_2_, bf16[512,2048]{1,0:T(8,128)(2,1)} %collective-permute-done.10.refs_1_.refs_3_, ...), custom_call_target="tpu_custom_call" | custom-call | flops 8589934592 | bytes 16777216 | tf_op jit(solution)/shard_map/pallas_call | solution.py:201
  112.7 2.6 fusion.83
  115.6 3.7 fusion.20.x_ref
  119.3 37.0 %shard_map.189 = (f32[512,1024]{1,0:T(8,128)}, f32[512,1024]{1,0:T(8,128)}, bf16[2048,1024]{1,0:T(8,128)(2,1)}, bf16[2048,1024]{1,0:T(8,128)(2,1)}, bf16[512,409...) custom-call(bf16[512,1024]{1,0:T(8,128)(2,1)} %fusion.20.x_ref, bf16[512,1024]{1,0:T(8,128)(2,1)} %pad_maximum_fusion.8.g_ref, ...), custom_call_target="tpu_custom_call" | custom-call | flops 25769803776 | bytes 33554432 | tf_op jit(solution)/shard_map/pallas_call | solution.py:405
  156.8 3.2 pad_maximum_fusion.4
  163.4 4.5 fusion.81
  167.8 4.1 shard_map.191
  171.9 9.5 %shard_map.190 = (bf16[512,1024]{1,0:T(8,128)(2,1)}, f32[8,8,512]{2,1,0:T(8,128)}) custom-call(bf16[512,1024]{1,0:T(8,128)(2,1)} %get-tuple-element.120.g_ref, bf16[1024,1024]{1,0:T(8,128)(2,1)} %w_ref.3, bf16[512,1024]{1,0:T(8,128)(2,1)} %get-tuple-element.43.a_ref.x_ref, f32[8,8,512]{2,1,0:T(8,128)} %get-tuple-element.48.l_ref), custom_call_target="tpu_custom_call" | custom-call | flops 1073741824 | bytes 5242880 | tf_op jit(solution)/shard_map/pallas_call | solution.py:256
  181.4 6.4 %add_convert_fusion.1 = bf16[2048,1024]{1,0:T(8,128)(2,1)} fusion(bf16[2048,1024]{1,0:T(8,128)(2,1)} %collective-permute-done.14, bf16[2048,1024]{1,0:T(8,128)(2,1)S(1)} %copy-done.12), kind=kLoop, calls=%fused_computation.1 | loop fusion | flops 8388608 | bytes 12582912 | tf_op jit(solution)/shard_map/convert_element_type | solution.py:57
  187.9 3.8 add_convert_fusion
  191.9 25.8 %shard_map.192 = (bf16[512,1024]{1,0:T(8,128)(2,1)}, bf16[512,1024]{1,0:T(8,128)(2,1)}, bf16[512,1024]{1,0:T(8,128)(2,1)}, bf16[512,1024]{1,0:T(8,128)(2,1)}, bf16[512,1024]{1,0:T(8,128)(2,1)}) custom-call(bf16[512,3072]{1,0:T(8,128)(2,1)} %shard_map.187.q_ref.refs_0_.refs_2_, bf16[512,3072]{1,0:T(8,128)(2,1)} %shard_map.187.q_ref.refs_0_.refs_2_, ...), custom_call_target="tpu_custom_call" | custom-call | flops 17179869184 | bytes 16777216 | tf_op jit(solution)/shard_map/pallas_call | solution.py:323
  225.4 9.6 %collective-permute-done.20 = bf16[128,2048]{1,0:T(8,128)(2,1)S(1)} collective-permute-done((bf16[128,2048]{1,0:T(8,128)(2,1)S(1)}, bf16[128,2048]{1,0:T(8,128)(2,1)S(1)}, u32[]{:S(2)}, u32[]{:S(2)}) %collective-permute-start.20) | collective-permute-done | bytes 524320 | tf_op jit(solution)/shard_map/ppermute | solution.py:29
  235.0 10.4 %collective-permute-done.21 = bf16[128,2048]{1,0:T(8,128)(2,1)S(1)} collective-permute-done((bf16[128,2048]{1,0:T(8,128)(2,1)S(1)}, bf16[128,2048]{1,0:T(8,128)(2,1)S(1)}, u32[]{:S(2)}, u32[]{:S(2)}) %collective-permute-start.21) | collective-permute-done | bytes 524320 | tf_op jit(solution)/shard_map/ppermute | solution.py:29
  252.0 5.5 %collective-permute-done.33 = bf16[2,128,1024]{2,1,0:T(8,128)(2,1)S(1)} collective-permute-done((bf16[2,128,1024]{2,1,0:T(8,128)(2,1)S(1)}, bf16[2,128,1024]{2,1,0:T(8,128)(2,1)S(1)}, u32[]{:S(2)}, u32[]{:S(2)}) %collective-permute-start.33) | collective-permute-done | bytes 524320 | tf_op jit(solution)/shard_map/ppermute | solution.py:29
  261.0 8.0 %fusion.79 = (f32[512]{0:T(512)S(1)}, f32[512]{0:T(512)S(1)}, f32[512,1024]{1,0:T(8,128)}) fusion(f32[512,4096]{1,0:T(8,128)S(1)} %bitcast.214, f32[512]{0:T(512)S(1)} %add_rsqrt_fusion, f32[512]{0:T(512)S(1)} %broadcast_multiply_fusion.3, bf16[512,1024]{1,0:T(8,128)(2,1)S(1)} %pad_maximum_fusion.7, bf16[1024,3072]{1,0:T(8,128)(2,1)} %w_ref.2, ...), kind=kOutput, calls=%fused_computation.205 | convolution fusion | flops 3234855936 | bytes 14688256 | tf_op jit(solution)/shard_map/dot_general | solution.py:24
  269.1 4.2 fusion.13
  275.5 7.2 %shard_map.194 = (bf16[128,4096]{1,0:T(8,128)(2,1)}, bf16[128,4096]{1,0:T(8,128)(2,1)}) custom-call(bf16[512,256]{1,0:T(8,128)(2,1)} %pad_maximum_fusion.14.x_ref, bf16[512,4096]{1,0:T(8,128)(2,1)} %pad_maximum_fusion.g_ref), custom_call_target="tpu_custom_call" | custom-call | flops 1073741824 | bytes 6553600 | tf_op jit(solution)/shard_map/pallas_call | solution.py:440
  286.7 15.1 %collective-permute-done.37 = bf16[2,512,1024]{2,1,0:T(8,128)(2,1)} collective-permute-done((bf16[2,512,1024]{2,1,0:T(8,128)(2,1)}, bf16[2,512,1024]{2,1,0:T(8,128)(2,1)}, u32[]{:S(2)}, u32[]{:S(2)}) %collective-permute-start.37) | collective-permute-done | bytes 2097184 | tf_op jit(solution)/shard_map/ppermute | solution.py:29
  301.8 3.2 fusion
  311.8 8.1 %shard_map.195 = (bf16[512,3072]{1,0:T(8,128)(2,1)}, bf16[512,3072]{1,0:T(8,128)(2,1)}) custom-call(bf16[512,1024]{1,0:T(8,128)(2,1)} %pad_maximum_fusion.6.x_ref, bf16[512,3072]{1,0:T(8,128)(2,1)} %pad_maximum_fusion.1.g_ref), custom_call_target="tpu_custom_call" | custom-call | flops 3221225472 | bytes 10485760 | tf_op jit(solution)/shard_map/pallas_call | solution.py:440
  319.9 6.2 %shard_map.193 = (bf16[1024,1024]{1,0:T(8,128)(2,1)}, bf16[1024,1024]{1,0:T(8,128)(2,1)}) custom-call(bf16[512,2048]{1,0:T(8,128)(2,1)} %pad_maximum_fusion.5.x_ref, bf16[512,1024]{1,0:T(8,128)(2,1)} %get-tuple-element.126.g_ref), custom_call_target="tpu_custom_call" | custom-call | flops 2147483648 | bytes 7340032 | tf_op jit(solution)/shard_map/pallas_call | solution.py:440
  326.6 17.6 %collective-permute-done.27 = bf16[1,64,4096]{2,1,0:T(8,128)(2,1)} collective-permute-done((bf16[1,64,4096]{2,1,0:T(8,128)(2,1)S(1)}, bf16[1,64,4096]{2,1,0:T(8,128)(2,1)}, u32[]{:S(2)}, u32[]{:S(2)}) %collective-permute-start.27) | collective-permute-done | bytes 524320 | tf_op jit(solution)/shard_map/ppermute | solution.py:29
  346.1 3.7 fusion.1
  349.8 3.2 collective-permute-done.28
  356.7 9.5 %collective-permute-done.38 = bf16[1,512,1024]{2,1,0:T(8,128)(2,1)} collective-permute-done((bf16[1,512,1024]{2,1,0:T(8,128)(2,1)}, bf16[1,512,1024]{2,1,0:T(8,128)(2,1)}, u32[]{:S(2)}, u32[]{:S(2)}) %collective-permute-start.38) | collective-permute-done | bytes 1048608 | tf_op jit(solution)/shard_map/ppermute | solution.py:29
  366.3 2.7 fusion.46
  369.1 3.3 add_convert_fusion.3
  372.4 3.8 add_convert_fusion.2
  380.4 2.5 fusion.47
  382.9 21.1 %collective-permute-done.24 = bf16[2,256,1024]{2,1,0:T(8,128)(2,1)} collective-permute-done((bf16[2,256,1024]{2,1,0:T(8,128)(2,1)}, bf16[2,256,1024]{2,1,0:T(8,128)(2,1)}, u32[]{:S(2)}, u32[]{:S(2)}) %collective-permute-start.24) | collective-permute-done | bytes 1048608 | tf_op jit(solution)/shard_map/ppermute | solution.py:29
  407.4 7.7 %collective-permute-done.30 = bf16[1,256,3072]{2,1,0:T(8,128)(2,1)} collective-permute-done((bf16[1,256,3072]{2,1,0:T(8,128)(2,1)}, bf16[1,256,3072]{2,1,0:T(8,128)(2,1)}, u32[]{:S(2)}, u32[]{:S(2)}) %collective-permute-start.30) | collective-permute-done | bytes 1572896 | tf_op jit(solution)/shard_map/ppermute | solution.py:29
  419.8 5.2 %collective-permute-done.25 = bf16[1,256,1024]{2,1,0:T(8,128)(2,1)S(1)} collective-permute-done((bf16[1,256,1024]{2,1,0:T(8,128)(2,1)S(1)}, bf16[1,256,1024]{2,1,0:T(8,128)(2,1)S(1)}, u32[]{:S(2)}, u32[]{:S(2)}) %collective-permute-start.25) | collective-permute-done | bytes 524320 | tf_op jit(solution)/shard_map/ppermute | solution.py:29
  430.7 9.3 %collective-permute-done.31 = bf16[1,128,3072]{2,1,0:T(8,128)(2,1)} collective-permute-done((bf16[1,128,3072]{2,1,0:T(8,128)(2,1)}, bf16[1,128,3072]{2,1,0:T(8,128)(2,1)}, u32[]{:S(2)}, u32[]{:S(2)}) %collective-permute-start.31) | collective-permute-done | bytes 786464 | tf_op jit(solution)/shard_map/ppermute | solution.py:29
  446.8 4.7 collective-permute-done.13
  456.1 2.8 collective-permute-done.19
  461.7 2.6 fusion.39
  464.3 2.6 fusion.36
  (253 shorter events, 111.5 us)
Async XLA Ops:
  7.2 445.5 %reduce-scatter.13.cloned.1.call-start = ((), (), s32[]{:S(2)}) async-start(), calls=%async_computation.9 | async-start | bytes 327680 | tf_op jit(solution)/shard_map/reduce_scatter | solution.py:74
  9.3 6.6 %collective-permute-start.6 = (f32[4,3,128]{2,1,0:T(4,128)S(1)}, f32[4,3,128]{2,1,0:T(4,128)S(1)}, u32[]{:S(2)}, u32[]{:S(2)}) collective-permute-start(f32[4,3,128]{2,1,0:T(4,128)S(1)} %get-tuple-element.174), channel_id=1, source_target_pairs={{0,4},{4,0},{8,12},{12,8},{16,20},{20,16},{24,28},{28,24},{1,5},{5... | collective-permute-start | bytes 18440 | tf_op jit(solution)/shard_map/ppermute | solution.py:29
  15.9 4.3 collective-permute-start.7
  18.5 3.6 collective-permute-start.8
  20.0 4.5 collective-permute-start.9
  29.6 9.3 %collective-permute-start = (bf16[128,1024]{1,0:T(8,128)(2,1)S(1)}, bf16[128,1024]{1,0:T(8,128)(2,1)S(1)}, u32[]{:S(2)}, u32[]{:S(2)}) collective-permute-start(bf16[128,1024]{1,0:T(8,128)(2,1)S(1)} %get-tuple-element.160), channel_id=1, source_target_pairs={{0,8},{4,12},{8,0},{12,4},{16,24},{20,28},{24,16},{28,20},{1,9},{5... | collective-permute-start | bytes 786440 | tf_op jit(solution)/shard_map/ppermute | solution.py:29
  30.2 12.3 %collective-permute-start.1 = (bf16[128,1024]{1,0:T(8,128)(2,1)S(1)}, bf16[128,1024]{1,0:T(8,128)(2,1)S(1)}, u32[]{:S(2)}, u32[]{:S(2)}) collective-permute-start(bf16[128,1024]{1,0:T(8,128)(2,1)S(1)} %get-tuple-element.159), channel_id=1, source_target_pairs={{0,16},{4,20},{8,24},{12,28},{16,0},{20,4},{24,8},{28,12},{1,17},{... | collective-permute-start | bytes 786440 | tf_op jit(solution)/shard_map/ppermute | solution.py:29
  30.3 12.3 %collective-permute-start.2 = (bf16[128,1024]{1,0:T(8,128)(2,1)S(1)}, bf16[128,1024]{1,0:T(8,128)(2,1)S(1)}, u32[]{:S(2)}, u32[]{:S(2)}) collective-permute-start(bf16[128,1024]{1,0:T(8,128)(2,1)S(1)} %get-tuple-element.158), channel_id=1, source_target_pairs={{0,24},{4,28},{8,16},{12,20},{16,8},{20,12},{24,0},{28,4},{1,25},{... | collective-permute-start | bytes 786440 | tf_op jit(solution)/shard_map/ppermute | solution.py:29
  56.9 35.1 %collective-permute-start.10 = (bf16[512,2048]{1,0:T(8,128)(2,1)}, bf16[512,2048]{1,0:T(8,128)(2,1)}, u32[]{:S(2)}, u32[]{:S(2)}) collective-permute-start(bf16[512,2048]{1,0:T(8,128)(2,1)} %slice.171), channel_id=1, source_target_pairs={{0,4},{4,0},{8,12},{12,8},{16,20},{20,16},{24,28},{28,24},{1,5},{5... | collective-permute-start | bytes 6291464 | tf_op jit(solution)/shard_map/ppermute | solution.py:29
  58.0 14.8 %collective-permute-start.3 = (bf16[2,128,1024]{2,1,0:T(8,128)(2,1)S(1)}, bf16[2,128,1024]{2,1,0:T(8,128)(2,1)}, u32[]{:S(2)}, u32[]{:S(2)}) collective-permute-start(bf16[2,128,1024]{2,1,0:T(8,128)(2,1)S(1)} %get-tuple-element.136), channel_id=1, source_target_pairs={{0,8},{4,12},{8,0},{12,4},{16,24},{20,28},{24,16},{28,20},{1,9},{5... | collective-permute-start | bytes 1572872 | tf_op jit(solution)/shard_map/ppermute | solution.py:29
  65.2 25.5 %collective-permute-start.4 = (bf16[2,128,1024]{2,1,0:T(8,128)(2,1)}, bf16[2,128,1024]{2,1,0:T(8,128)(2,1)S(1)}, u32[]{:S(2)}, u32[]{:S(2)}) collective-permute-start(bf16[2,128,1024]{2,1,0:T(8,128)(2,1)} %get-tuple-element.138), channel_id=1, source_target_pairs={{0,16},{4,20},{8,24},{12,28},{16,0},{20,4},{24,8},{28,12},{1,17},{... | collective-permute-start | bytes 1572872 | tf_op jit(solution)/shard_map/ppermute | solution.py:29
  66.4 24.3 %collective-permute-start.5 = (bf16[2,128,1024]{2,1,0:T(8,128)(2,1)}, bf16[2,128,1024]{2,1,0:T(8,128)(2,1)S(1)}, u32[]{:S(2)}, u32[]{:S(2)}) collective-permute-start(bf16[2,128,1024]{2,1,0:T(8,128)(2,1)} %get-tuple-element.137), channel_id=1, source_target_pairs={{0,24},{4,28},{8,16},{12,20},{16,8},{20,12},{24,0},{28,4},{1,25},{... | collective-permute-start | bytes 1572872 | tf_op jit(solution)/shard_map/ppermute | solution.py:29
  156.3 25.1 %collective-permute-start.14 = (bf16[2048,1024]{1,0:T(8,128)(2,1)}, bf16[2048,1024]{1,0:T(8,128)(2,1)}, u32[]{:S(2)}, u32[]{:S(2)}) collective-permute-start(bf16[2048,1024]{1,0:T(8,128)(2,1)} %get-tuple-element.52), channel_id=1, source_target_pairs={{0,4},{4,0},{8,12},{12,8},{16,20},{20,16},{24,28},{28,24},{1,5},{5... | collective-permute-start | bytes 12582920 | tf_op jit(solution)/shard_map/ppermute | solution.py:29
  156.3 31.5 %collective-permute-start.15 = (bf16[512,4096]{1,0:T(8,128)(2,1)}, bf16[512,4096]{1,0:T(8,128)(2,1)}, u32[]{:S(2)}, u32[]{:S(2)}) collective-permute-start(bf16[512,4096]{1,0:T(8,128)(2,1)} %get-tuple-element.54), channel_id=1, source_target_pairs={{0,4},{4,0},{8,12},{12,8},{16,20},{20,16},{24,28},{28,24},{1,5},{5... | collective-permute-start | bytes 12582920 | tf_op jit(solution)/shard_map/ppermute | solution.py:29
  191.7 91.0 %copy-start = (bf16[512,4096]{1,0:T(8,128)(2,1)}, bf16[512,4096]{1,0:T(8,128)(2,1)S(1)}, u32[]{:S(2)}) copy-start(bf16[512,4096]{1,0:T(8,128)(2,1)S(1)} %add_convert_fusion) | copy-start | bytes 12582916
  191.7 32.6 %collective-permute-start.32 = (bf16[512,1024]{1,0:T(8,128)(2,1)S(1)}, bf16[512,1024]{1,0:T(8,128)(2,1)S(1)}, u32[]{:S(2)}, u32[]{:S(2)}) collective-permute-start(bf16[512,1024]{1,0:T(8,128)(2,1)S(1)} %copy-done.35), channel_id=1, source_target_pairs={{0,4},{4,0},{8,12},{12,8},{16,20},{20,16},{24,28},{28,24},{1,5},{5... | collective-permute-start | bytes 3145736 | tf_op jit(solution)/shard_map/ppermute | solution.py:29
  219.6 38.7 %collective-permute-start.16 = (bf16[2,512,1024]{2,1,0:T(8,128)(2,1)S(1)}, bf16[2,512,1024]{2,1,0:T(8,128)(2,1)S(1)}, u32[]{:S(2)}, u32[]{:S(2)}) collective-permute-start(bf16[2,512,1024]{2,1,0:T(8,128)(2,1)S(1)} %pad_maximum_fusion.3), channel_id=1, source_target_pairs={{0,4},{4,0},{8,12},{12,8},{16,20},{20,16},{24,28},{28,24},{1,5},{5... | collective-permute-start | bytes 6291464 | tf_op jit(solution)/shard_map/ppermute | solution.py:29
  220.2 14.8 %collective-permute-start.20 = (bf16[128,2048]{1,0:T(8,128)(2,1)S(1)}, bf16[128,2048]{1,0:T(8,128)(2,1)S(1)}, u32[]{:S(2)}, u32[]{:S(2)}) collective-permute-start(bf16[128,2048]{1,0:T(8,128)(2,1)S(1)} %get-tuple-element.132), channel_id=1, source_target_pairs={{0,8},{4,12},{8,0},{12,4},{16,24},{20,28},{24,16},{28,20},{1,9},{5... | collective-permute-start | bytes 1572872 | tf_op jit(solution)/shard_map/ppermute | solution.py:29
  220.8 24.6 %collective-permute-start.21 = (bf16[128,2048]{1,0:T(8,128)(2,1)S(1)}, bf16[128,2048]{1,0:T(8,128)(2,1)S(1)}, u32[]{:S(2)}, u32[]{:S(2)}) collective-permute-start(bf16[128,2048]{1,0:T(8,128)(2,1)S(1)} %get-tuple-element.131), channel_id=1, source_target_pairs={{0,16},{4,20},{8,24},{12,28},{16,0},{20,4},{24,8},{28,12},{1,17},{... | collective-permute-start | bytes 1572872 | tf_op jit(solution)/shard_map/ppermute | solution.py:29
  222.0 24.2 %collective-permute-start.22 = (bf16[128,2048]{1,0:T(8,128)(2,1)S(1)}, bf16[128,2048]{1,0:T(8,128)(2,1)S(1)}, u32[]{:S(2)}, u32[]{:S(2)}) collective-permute-start(bf16[128,2048]{1,0:T(8,128)(2,1)S(1)} %get-tuple-element.130), channel_id=1, source_target_pairs={{0,24},{4,28},{8,16},{12,20},{16,8},{20,12},{24,0},{28,4},{1,25},{... | collective-permute-start | bytes 1572872 | tf_op jit(solution)/shard_map/ppermute | solution.py:29
  224.8 32.6 %collective-permute-start.33 = (bf16[2,128,1024]{2,1,0:T(8,128)(2,1)S(1)}, bf16[2,128,1024]{2,1,0:T(8,128)(2,1)S(1)}, u32[]{:S(2)}, u32[]{:S(2)}) collective-permute-start(bf16[2,128,1024]{2,1,0:T(8,128)(2,1)S(1)} %dynamic-slice_bitcast_fusion.6), channel_id=1, source_target_pairs={{0,8},{4,12},{8,0},{12,4},{16,24},{20,28},{24,16},{28,20},{1,9},{5... | collective-permute-start | bytes 1572872 | tf_op jit(solution)/shard_map/ppermute | solution.py:29
  250.7 51.1 %collective-permute-start.37 = (bf16[2,512,1024]{2,1,0:T(8,128)(2,1)}, bf16[2,512,1024]{2,1,0:T(8,128)(2,1)}, u32[]{:S(2)}, u32[]{:S(2)}) collective-permute-start(bf16[2,512,1024]{2,1,0:T(8,128)(2,1)} %dynamic-slice_bitcast_fusion), channel_id=1, source_target_pairs={{0,8},{4,12},{8,0},{12,4},{16,24},{20,28},{24,16},{28,20},{1,9},{5... | collective-permute-start | bytes 6291464 | tf_op jit(solution)/shard_map/ppermute | solution.py:29
  257.7 27.2 %collective-permute-start.34 = (bf16[1,128,1024]{2,1,0:T(8,128)(2,1)S(1)}, bf16[1,128,1024]{2,1,0:T(8,128)(2,1)}, u32[]{:S(2)}, u32[]{:S(2)}) collective-permute-start(bf16[1,128,1024]{2,1,0:T(8,128)(2,1)S(1)} %constant_dynamic-slice_fusion.1), channel_id=1, source_target_pairs={{0,16},{4,20},{8,24},{12,28},{16,0},{20,4},{24,8},{28,12},{1,17},{... | collective-permute-start | bytes 786440 | tf_op jit(solution)/shard_map/ppermute | solution.py:29
  282.7 24.4 %collective-permute-start.26 = (bf16[128,4096]{1,0:T(8,128)(2,1)}, bf16[128,4096]{1,0:T(8,128)(2,1)}, u32[]{:S(2)}, u32[]{:S(2)}) collective-permute-start(bf16[128,4096]{1,0:T(8,128)(2,1)} %get-tuple-element.66), channel_id=1, source_target_pairs={{0,4},{4,0},{8,12},{12,8},{16,20},{20,16},{24,28},{28,24},{1,5},{5... | collective-permute-start | bytes 3145736 | tf_op jit(solution)/shard_map/ppermute | solution.py:29
  284.2 61.8 %collective-permute-start.35 = (bf16[1,256,4096]{2,1,0:T(8,128)(2,1)}, bf16[1,256,4096]{2,1,0:T(8,128)(2,1)}, u32[]{:S(2)}, u32[]{:S(2)}) collective-permute-start(bf16[1,256,4096]{2,1,0:T(8,128)(2,1)} %dynamic-slice_bitcast_fusion.1), channel_id=1, source_target_pairs={{0,16},{4,20},{8,24},{12,28},{16,0},{20,4},{24,8},{28,12},{1,17},{... | collective-permute-start | bytes 6291464 | tf_op jit(solution)/shard_map/ppermute | solution.py:29
  286.7 180.3 %reduce-scatter.9.cloned.1.call-start = ((), (), s32[]{:S(2)}) async-start(), calls=%async_computation.7 | async-start | bytes 327680 | tf_op jit(solution)/shard_map/reduce_scatter | solution.py:74
  308.6 35.6 %collective-permute-start.27 = (bf16[1,64,4096]{2,1,0:T(8,128)(2,1)S(1)}, bf16[1,64,4096]{2,1,0:T(8,128)(2,1)}, u32[]{:S(2)}, u32[]{:S(2)}) collective-permute-start(bf16[1,64,4096]{2,1,0:T(8,128)(2,1)S(1)} %dynamic-slice_bitcast_fusion.7), channel_id=1, source_target_pairs={{0,16},{4,20},{8,24},{12,28},{16,0},{20,4},{24,8},{28,12},{1,17},{... | collective-permute-start | bytes 1572872 | tf_op jit(solution)/shard_map/ppermute | solution.py:29
  310.3 56.0 %collective-permute-start.38 = (bf16[1,512,1024]{2,1,0:T(8,128)(2,1)}, bf16[1,512,1024]{2,1,0:T(8,128)(2,1)}, u32[]{:S(2)}, u32[]{:S(2)}) collective-permute-start(bf16[1,512,1024]{2,1,0:T(8,128)(2,1)} %constant_dynamic-slice_fusion), channel_id=1, source_target_pairs={{0,16},{4,20},{8,24},{12,28},{16,0},{20,4},{24,8},{28,12},{1,17},{... | collective-permute-start | bytes 3145736 | tf_op jit(solution)/shard_map/ppermute | solution.py:29
  319.9 52.5 %collective-permute-start.29 = (bf16[512,3072]{1,0:T(8,128)(2,1)}, bf16[512,3072]{1,0:T(8,128)(2,1)}, u32[]{:S(2)}, u32[]{:S(2)}) collective-permute-start(bf16[512,3072]{1,0:T(8,128)(2,1)} %get-tuple-element.68), channel_id=1, source_target_pairs={{0,4},{4,0},{8,12},{12,8},{16,20},{20,16},{24,28},{28,24},{1,5},{5... | collective-permute-start | bytes 9437192 | tf_op jit(solution)/shard_map/ppermute | solution.py:29
  319.9 26.2 %copy-start.1 = (bf16[512,4096]{1,0:T(8,128)(2,1)S(1)}, bf16[512,4096]{1,0:T(8,128)(2,1)}, u32[]{:S(2)}) copy-start(bf16[512,4096]{1,0:T(8,128)(2,1)} %copy-done) | copy-start | bytes 12582916
  326.1 42.9 %collective-permute-start.23 = (bf16[1024,1024]{1,0:T(8,128)(2,1)}, bf16[1024,1024]{1,0:T(8,128)(2,1)}, u32[]{:S(2)}, u32[]{:S(2)}) collective-permute-start(bf16[1024,1024]{1,0:T(8,128)(2,1)} %get-tuple-element.64), channel_id=1, source_target_pairs={{0,4},{4,0},{8,12},{12,8},{16,20},{20,16},{24,28},{28,24},{1,5},{5... | collective-permute-start | bytes 6291464 | tf_op jit(solution)/shard_map/ppermute | solution.py:29
  345.4 7.6 %collective-permute-start.28 = (bf16[1,32,4096]{2,1,0:T(8,128)(2,1)S(1)}, bf16[1,32,4096]{2,1,0:T(8,128)(2,1)S(1)}, u32[]{:S(2)}, u32[]{:S(2)}) collective-permute-start(bf16[1,32,4096]{2,1,0:T(8,128)(2,1)S(1)} %dynamic-slice_bitcast_fusion.17), channel_id=1, source_target_pairs={{0,8},{4,12},{8,0},{12,4},{16,24},{20,28},{24,16},{28,20},{1,9},{5... | collective-permute-start | bytes 786440 | tf_op jit(solution)/shard_map/ppermute | solution.py:29
  353.8 114.6 %reduce-scatter.17.cloned.1.call-start = ((), (), s32[]{:S(2)}) async-start(), calls=%async_computation.11 | async-start | bytes 1310720 | tf_op jit(solution)/shard_map/reduce_scatter | solution.py:74
  356.2 24.2 %collective-permute-start.36 = (bf16[1,128,4096]{2,1,0:T(8,128)(2,1)}, bf16[1,128,4096]{2,1,0:T(8,128)(2,1)}, u32[]{:S(2)}, u32[]{:S(2)}) collective-permute-start(bf16[1,128,4096]{2,1,0:T(8,128)(2,1)} %dynamic-slice_bitcast_fusion.3), channel_id=1, source_target_pairs={{0,8},{4,12},{8,0},{12,4},{16,24},{20,28},{24,16},{28,20},{1,9},{5... | collective-permute-start | bytes 3145736 | tf_op jit(solution)/shard_map/ppermute | solution.py:29
  369.0 101.2 %reduce-scatter.15.cloned.1.call-start = ((), (), s32[]{:S(2)}) async-start(), calls=%async_computation.10 | async-start | bytes 1310720 | tf_op jit(solution)/shard_map/reduce_scatter | solution.py:74
  377.5 37.6 %collective-permute-start.30 = (bf16[1,256,3072]{2,1,0:T(8,128)(2,1)}, bf16[1,256,3072]{2,1,0:T(8,128)(2,1)}, u32[]{:S(2)}, u32[]{:S(2)}) collective-permute-start(bf16[1,256,3072]{2,1,0:T(8,128)(2,1)} %dynamic-slice_bitcast_fusion.2), channel_id=1, source_target_pairs={{0,16},{4,20},{8,24},{12,28},{16,0},{20,4},{24,8},{28,12},{1,17},{... | collective-permute-start | bytes 4718600 | tf_op jit(solution)/shard_map/ppermute | solution.py:29
  379.2 24.8 %collective-permute-start.24 = (bf16[2,256,1024]{2,1,0:T(8,128)(2,1)}, bf16[2,256,1024]{2,1,0:T(8,128)(2,1)}, u32[]{:S(2)}, u32[]{:S(2)}) collective-permute-start(bf16[2,256,1024]{2,1,0:T(8,128)(2,1)} %dynamic-slice_bitcast_fusion.4), channel_id=1, source_target_pairs={{0,8},{4,12},{8,0},{12,4},{16,24},{20,28},{24,16},{28,20},{1,9},{5... | collective-permute-start | bytes 3145736 | tf_op jit(solution)/shard_map/ppermute | solution.py:29
  382.9 89.2 %reduce-scatter.7.cloned.1.call-start = ((), (), s32[]{:S(2)}) async-start(), calls=%async_computation.6 | async-start | bytes 655360 | tf_op jit(solution)/shard_map/reduce_scatter | solution.py:74
  406.0 19.0 %collective-permute-start.25 = (bf16[1,256,1024]{2,1,0:T(8,128)(2,1)S(1)}, bf16[1,256,1024]{2,1,0:T(8,128)(2,1)S(1)}, u32[]{:S(2)}, u32[]{:S(2)}) collective-permute-start(bf16[1,256,1024]{2,1,0:T(8,128)(2,1)S(1)} %constant_dynamic-slice_fusion.2), channel_id=1, source_target_pairs={{0,16},{4,20},{8,24},{12,28},{16,0},{20,4},{24,8},{28,12},{1,17},{... | collective-permute-start | bytes 1572872 | tf_op jit(solution)/shard_map/ppermute | solution.py:29
  419.2 20.8 %copy-start.9 = (bf16[1,256,3072]{2,1,0:T(8,128)(2,1)S(1)}, bf16[1,256,3072]{2,1,0:T(8,128)(2,1)}, u32[]{:S(2)}) copy-start(bf16[1,256,3072]{2,1,0:T(8,128)(2,1)} %copy-done.8) | copy-start | bytes 4718596
  419.2 20.8 %collective-permute-start.31 = (bf16[1,128,3072]{2,1,0:T(8,128)(2,1)}, bf16[1,128,3072]{2,1,0:T(8,128)(2,1)}, u32[]{:S(2)}, u32[]{:S(2)}) collective-permute-start(bf16[1,128,3072]{2,1,0:T(8,128)(2,1)} %dynamic-slice_bitcast_fusion.5), channel_id=1, source_target_pairs={{0,8},{4,12},{8,0},{12,4},{16,24},{20,28},{24,16},{28,20},{1,9},{5... | collective-permute-start | bytes 2359304 | tf_op jit(solution)/shard_map/ppermute | solution.py:29
  426.0 49.6 %reduce-scatter.11.cloned.1.call-start = ((), (), s32[]{:S(2)}) async-start(), calls=%async_computation.8 | async-start | bytes 983040 | tf_op jit(solution)/shard_map/reduce_scatter | solution.py:74
  427.2 18.3 %collective-permute-start.11 = (bf16[128,1024]{1,0:T(8,128)(2,1)}, bf16[128,1024]{1,0:T(8,128)(2,1)S(1)}, u32[]{:S(2)}, u32[]{:S(2)}) collective-permute-start(bf16[128,1024]{1,0:T(8,128)(2,1)} %get-tuple-element.156), channel_id=1, source_target_pairs={{0,8},{4,12},{8,0},{12,4},{16,24},{20,28},{24,16},{28,20},{1,9},{5... | collective-permute-start | bytes 786440 | tf_op jit(solution)/shard_map/ppermute | solution.py:29
  427.8 19.0 %collective-permute-start.12 = (bf16[128,1024]{1,0:T(8,128)(2,1)}, bf16[128,1024]{1,0:T(8,128)(2,1)}, u32[]{:S(2)}, u32[]{:S(2)}) collective-permute-start(bf16[128,1024]{1,0:T(8,128)(2,1)} %get-tuple-element.155), channel_id=1, source_target_pairs={{0,16},{4,20},{8,24},{12,28},{16,0},{20,4},{24,8},{28,12},{1,17},{... | collective-permute-start | bytes 786440 | tf_op jit(solution)/shard_map/ppermute | solution.py:29
  429.0 22.5 %collective-permute-start.13 = (bf16[128,1024]{1,0:T(8,128)(2,1)S(1)}, bf16[128,1024]{1,0:T(8,128)(2,1)}, u32[]{:S(2)}, u32[]{:S(2)}) collective-permute-start(bf16[128,1024]{1,0:T(8,128)(2,1)S(1)} %get-tuple-element.154), channel_id=1, source_target_pairs={{0,24},{4,28},{8,16},{12,20},{16,8},{20,12},{24,0},{28,4},{1,25},{... | collective-permute-start | bytes 786440 | tf_op jit(solution)/shard_map/ppermute | solution.py:29
  443.1 13.0 %collective-permute-start.17 = (bf16[128,1024]{1,0:T(8,128)(2,1)}, bf16[128,1024]{1,0:T(8,128)(2,1)S(1)}, u32[]{:S(2)}, u32[]{:S(2)}) collective-permute-start(bf16[128,1024]{1,0:T(8,128)(2,1)} %get-tuple-element.148), channel_id=1, source_target_pairs={{0,8},{4,12},{8,0},{12,4},{16,24},{20,28},{24,16},{28,20},{1,9},{5... | collective-permute-start | bytes 786440 | tf_op jit(solution)/shard_map/ppermute | solution.py:29
  443.7 12.4 %collective-permute-start.18 = (bf16[128,1024]{1,0:T(8,128)(2,1)}, bf16[128,1024]{1,0:T(8,128)(2,1)S(1)}, u32[]{:S(2)}, u32[]{:S(2)}) collective-permute-start(bf16[128,1024]{1,0:T(8,128)(2,1)} %get-tuple-element.147), channel_id=1, source_target_pairs={{0,16},{4,20},{8,24},{12,28},{16,0},{20,4},{24,8},{28,12},{1,17},{... | collective-permute-start | bytes 786440 | tf_op jit(solution)/shard_map/ppermute | solution.py:29
  445.5 13.5 %collective-permute-start.19 = (bf16[128,1024]{1,0:T(8,128)(2,1)S(1)}, bf16[128,1024]{1,0:T(8,128)(2,1)S(1)}, u32[]{:S(2)}, u32[]{:S(2)}) collective-permute-start(bf16[128,1024]{1,0:T(8,128)(2,1)S(1)} %get-tuple-element.146), channel_id=1, source_target_pairs={{0,24},{4,28},{8,16},{12,20},{16,8},{20,12},{24,0},{28,4},{1,25},{... | collective-permute-start | bytes 786440 | tf_op jit(solution)/shard_map/ppermute | solution.py:29
  (35 other events, 197.6 us)
Sparse Core Ops, SparseCore 0:
  286.8 19.7 reduce-scatter.12
  353.9 19.6 reduce-scatter.8
  375.9 25.3 reduce-scatter.16
  403.5 25.8 reduce-scatter.14
  431.5 20.2 reduce-scatter.6
  453.9 21.6 reduce-scatter.10

commit v3 on v2

v3 whole, which is shorter than its diff:
```python
import functools
import math

import jax
import jax.numpy as jnp
from jax import lax
from jax.experimental import pallas as pl
from jax.experimental.pallas import tpu as pltpu
from jax.sharding import PartitionSpec as P

HD = 64
PAIR = 2 * HD
eps_norm = 1e-06
neg_fill = -1e30
BF = jnp.bfloat16
F32 = jnp.float32
DIMS_FIRST = (((0,), (0,)), ((), ()))
DIMS_LAST = (((1,), (1,)), ((), ()))
LOG2E = 1.4426950408889634
VMEM_BYTES = 52 * 1024 * 1024


def dot(left, right, dims=(((1,), (0,)), ((), ()))):
    return lax.dot_general(left, right, dims, preferred_element_type=F32)


def swap(values, axis_name, bits):
    size = lax.axis_size(axis_name)
    return lax.ppermute(values, axis_name, [(i, i ^ bits) for i in range(size)])


def pick(values, index, axis):
    return lax.dynamic_index_in_dim(values, index, axis, keepdims=False)


def together(*values):
    return lax.optimization_barrier(values)


def cut_parts(values, mine):
    return [pick(values, mine ^ step, 0) for step in range(values.shape[0])]


def send_parts(parts, span):
    return parts[:1] + [
        swap(part, "head", step * span) for step, part in enumerate(parts) if step > 0
    ]


def from_buckets(parts, span, mine):
    count = parts.shape[0]
    got = [parts[0]]
    for step in range(1, count):
        got.append(swap(parts[step], "head", step * span))
    got = jnp.stack(got)
    return jnp.stack([pick(got, mine ^ micro, 0) for micro in range(count)])


def add_low(terms):
    return functools.reduce(jnp.add, [term.astype(F32) for term in terms]).astype(BF)


class Rows:
    def __init__(self, arrays, bits, before=1, cols=None):
        self.order = sorted(bits, reverse=True)
        self.before, self.arrays = before, []
        self.start, self.size = cols or (0, arrays[0].shape[-1])
        self.chunk = arrays[0].size // arrays[0].shape[-1] // before // 2 ** len(bits)
        for array in arrays:
            self.join(array, self.start)

    def join(self, array, start=0):
        shape = [self.before] + [2] * len(self.order) + [self.chunk, array.shape[-1]]
        self.arrays.append((array.reshape(shape), tuple(self.order), {}, start))

    def read(self, bit=None, index=None):
        terms = []
        for array, bits, picks, start in self.arrays:
            picks = picks if bit is None else {**picks, bit: index}
            starts = [0] + [picks.get(b, 0) for b in bits] + [0, start]
            sizes = [self.before] + [1 if b in picks else 2 for b in bits] + [self.chunk, self.size]
            terms.append(lax.dynamic_slice(array, starts, sizes).reshape(-1, self.size))
        return add_low(terms)

    def away(self, bit):
        here = (place_of() >> bit) % 2
        sent = self.read(bit, 1 - here)
        self.order.remove(bit)
        for _, _, picks, _ in self.arrays:
            picks[bit] = here
        return sent


def place_of():
    return lax.axis_index("head") * lax.axis_size("seq") + lax.axis_index("seq")


def cross(rows, bit):
    seq_bits = lax.axis_size("seq").bit_length() - 1
    if bit < seq_bits:
        return swap(rows, "seq", 2**bit)
    return swap(rows, "head", 2 ** (bit - seq_bits))


def away_all(parts, bit):
    return jnp.concatenate([part.away(bit) for part in parts])


def join_all(parts, came):
    start = 0
    for part in parts:
        height = part.before * part.chunk * 2 ** len(part.order)
        part.join(came[start : start + height])
        start += height


def step_all(parts, bit):
    join_all(parts, cross(away_all(parts, bit), bit))


def last_sum(*rows):
    size = lax.axis_size("seq")
    narrow = min(part.shape[1] for part in rows)
    blocks, counts = [], []
    for part in rows:
        part = part.reshape(size, -1, part.shape[1])
        counts.append((part.shape[1], part.shape[2] // narrow))
        blocks += [part[:, :, i * narrow : (i + 1) * narrow] for i in range(counts[-1][1])]
    joint = jnp.concatenate(blocks, axis=1) if len(blocks) > 1 else blocks[0]
    joint = joint.reshape(-1, narrow)
    total = lax.psum_scatter(joint, "seq", scatter_dimension=0, tiled=True).astype(F32)
    results, start = [], 0
    for height, count in counts:
        parts = [total[start + i * height : start + (i + 1) * height] for i in range(count)]
        results.append(jnp.concatenate(parts, axis=1) if count > 1 else parts[0])
        start += height * count
    return results


def norm_stats(hidden):
    centred = hidden - jnp.mean(hidden, axis=-1, keepdims=True)
    rate = lax.rsqrt(jnp.mean(centred * centred, axis=-1, keepdims=True) + eps_norm)
    return centred * rate, rate


def norm_back(grad, normal, rate, scale_term):
    inner = grad * (1.0 + scale_term)
    return rate * (
        inner
        - jnp.mean(inner, axis=-1, keepdims=True)
        - normal * jnp.mean(inner * normal, axis=-1, keepdims=True)
    )


def time_features(times, feature_count):
    half = feature_count // 2
    steps = jnp.exp(jnp.arange(half, dtype=F32) * (-math.log(10000.0) / (half - 1)))
    angles = 1000.0 * times[:, None] * steps
    return jnp.concatenate([jnp.sin(angles), jnp.cos(angles)], axis=-1).astype(BF)


def params():
    return pltpu.CompilerParams(vmem_limit_bytes=VMEM_BYTES)


def cost(flops, moved, hard=0):
    return pl.CostEstimate(flops=int(flops), bytes_accessed=int(moved), transcendentals=int(hard))


def turn(values):
    lanes = lax.broadcasted_iota(jnp.int32, values.shape, 1)
    low = lax.rem(lanes, HD) < HD // 2
    return jnp.where(low, pltpu.roll(values, PAIR - HD // 2, 1), pltpu.roll(values, HD // 2, 1))


def project_kernel(tiles, x_ref, w_ref, cos_ref, sin_ref, q_ref, kv_ref):
    raw = dot(x_ref[...], w_ref[...])
    step = pl.program_id(0)

    def rotated(o_ref, factor):
        for first in range(0, raw.shape[1], PAIR):
            part = raw[:, first : first + PAIR]
            turned = part * cos_ref[...] + turn(part) * sin_ref[...]
            o_ref[:, first : first + PAIR] = (turned * factor).astype(BF)

    @pl.when(step < tiles)
    def _():
        rotated(q_ref, HD ** (-0.5) * LOG2E)

    @pl.when((step >= tiles) & (step < 2 * tiles))
    def _():
        rotated(kv_ref, 1.0)

    @pl.when(step >= 2 * tiles)
    def _():
        kv_ref[...] = raw.astype(BF)


def project(normed, w_qkv, cos_table, sin_table):
    frames, width = normed.shape
    tile = 512
    tiles = width // tile
    return pl.pallas_call(
        functools.partial(project_kernel, tiles),
        grid=(3 * tiles,),
        in_specs=[
            pl.BlockSpec((frames, width), lambda i: (0, 0)),
            pl.BlockSpec((width, tile), lambda i: (0, i)),
            pl.BlockSpec((frames, PAIR), lambda i: (0, 0)),
            pl.BlockSpec((frames, PAIR), lambda i: (0, 0)),
        ],
        out_specs=[
            pl.BlockSpec((frames, tile), lambda i: (0, jnp.minimum(i, tiles - 1))),
            pl.BlockSpec((frames, tile), lambda i: (0, jnp.maximum(i - tiles, 0))),
        ],
        out_shape=[
            jax.ShapeDtypeStruct((frames, width), BF),
            jax.ShapeDtypeStruct((frames, 2 * width), BF),
        ],
        compiler_params=params(),
        cost_estimate=cost(6 * frames * width * width, 6 * width * width + 8 * frames * width),
    )(normed, w_qkv, cos_table, sin_table)


def only_head(values, which):
    lanes = lax.broadcasted_iota(jnp.int32, values.shape, 1)
    mine = (lanes >= which * HD) & (lanes < (which + 1) * HD)
    return jnp.where(mine, values, jnp.zeros_like(values))


def attend_kernel(span, q_ref, *refs):
    k_refs, v_refs = refs[:span], refs[span : 2 * span]
    mk_ref, mq_ref, o_ref, p_ref, l_ref, bias_ref = refs[2 * span :]
    frames = q_ref.shape[0]

    @pl.when(pl.program_id(0) == 0)
    def _():
        seg_q, place_q = mq_ref[0:1, :], mq_ref[1:2, :]
        for index in range(span):
            rows = slice(index * frames, (index + 1) * frames)
            seg_k, place_k, live_k = mk_ref[rows, 0:1], mk_ref[rows, 1:2], mk_ref[rows, 2:3]
            allowed = (seg_q == seg_k) & ((live_k == 1) | (place_q == place_k))
            bias_ref[rows, :] = jnp.where(allowed, 0.0, neg_fill)

    values_t = [v[...].T for v in v_refs]
    ones = jnp.ones((16, frames), BF)
    results, inverses = [], []
    for which in range(2):
        queries = only_head(q_ref[...], which)
        scores = [
            dot(k[...], queries, DIMS_LAST) + bias_ref[i * frames : (i + 1) * frames, :]
            for i, k in enumerate(k_refs)
        ]
        top = functools.reduce(jnp.maximum, [jnp.max(s, axis=0, keepdims=True) for s in scores])
        result = None
        for index, part in enumerate(scores):
            powered = jnp.exp2(part - top).astype(BF)
            p_ref[which, index * frames : (index + 1) * frames, :] = powered
            lanes = values_t[index][which * HD : (which + 1) * HD]
            part = dot(jnp.concatenate([lanes, ones], axis=0), powered)
            result = part if result is None else result + part
        inverse = 1.0 / result[HD : HD + 1]
        results.append(result[:HD] * inverse)
        inverses.append(inverse)
    o_ref[...] = jnp.concatenate(results, axis=0).T.astype(BF)
    l_ref[0] = jnp.concatenate(inverses + [jnp.zeros((6, frames), F32)], axis=0)


def columns(frames, start=0):
    return pl.BlockSpec((frames, PAIR), lambda i: (0, start + i))


def attend(queries, pairs_kv, meta_k, meta_q):
    span = len(pairs_kv)
    frames, width = queries.shape
    pairs = width // PAIR
    keys = span * frames
    return pl.pallas_call(
        functools.partial(attend_kernel, span),
        grid=(pairs,),
        in_specs=[columns(frames)]
        + [columns(frames)] * span
        + [columns(frames, pairs)] * span
        + [
            pl.BlockSpec((keys, PAIR), lambda i: (0, 0)),
            pl.BlockSpec((8, frames), lambda i: (0, 0)),
        ],
        out_specs=[
            columns(frames),
            pl.BlockSpec((2, keys, frames), lambda i: (i, 0, 0)),
            pl.BlockSpec((1, 8, frames), lambda i: (i, 0, 0)),
        ],
        out_shape=[
            jax.ShapeDtypeStruct((frames, width), BF),
            jax.ShapeDtypeStruct((2 * pairs, keys, frames), BF),
            jax.ShapeDtypeStruct((pairs, 8, frames), F32),
        ],
        scratch_shapes=[pltpu.VMEM((keys, frames), F32)],
        compiler_params=params(),
        cost_estimate=cost(
            16 * pairs * frames * keys * PAIR,
            4 * pairs * frames * keys,
            2 * pairs * frames * keys,
        ),
    )(queries, *pairs_kv, *pairs_kv, meta_k, meta_q)


def middle_kernel(*refs):
    fed_ref, mid_ref, gx_ref, cot_ref, scale_ref, w_ref, a_ref, l_ref = refs[:8]
    out_ref, gm_ref, gl_ref, gs_ref, gc_ref, o_ref, c_ref = refs[8:]
    frames = mid_ref.shape[0]
    out_ref[...] = (mid_ref[...] + fed_ref[...]).astype(BF)
    normal, rate = norm_stats(mid_ref[...])
    grad = gx_ref[...]
    grad_mid = cot_ref[...].astype(F32) + norm_back(grad, normal, rate, scale_ref[...])
    gm_ref[...] = grad_mid
    gl_ref[...] = grad_mid.astype(BF)
    gs_ref[...] = grad.astype(BF)
    gc_ref[...] = (grad * normal).astype(BF)
    grads = dot(w_ref[...], grad_mid.astype(BF), DIMS_LAST)
    for pair in range(l_ref.shape[0]):
        lanes = slice(pair * PAIR, (pair + 1) * PAIR)
        scaled, centres = [], []
        results = a_ref[:, lanes].T
        for which in range(2):
            rows = slice(pair * PAIR + which * HD, pair * PAIR + (which + 1) * HD)
            scaled.append(grads[rows] * l_ref[pair, which : which + 1, :])
            product = scaled[-1] * results[which * HD : (which + 1) * HD].astype(F32)
            centres.append(jnp.sum(product, axis=0, keepdims=True))
        o_ref[:, lanes] = jnp.concatenate(scaled, axis=0).astype(BF).T
        c_ref[pair] = jnp.concatenate(centres + [jnp.zeros((6, frames), F32)], axis=0)


def middle(fed, resid_mid, grad_normed, cot_rows, modulation, w_out, attended, inverses):
    frames, width = resid_mid.shape
    pairs = width // PAIR
    tile = 256
    rows = pl.BlockSpec((tile, width), lambda i: (i, 0))
    heads = pl.BlockSpec((pairs, 8, tile), lambda i: (0, 0, i))
    low = jax.ShapeDtypeStruct((frames, width), BF)
    return pl.pallas_call(
        middle_kernel,
        grid=(frames // tile,),
        in_specs=[
            rows,
            rows,
            rows,
            rows,
            pl.BlockSpec((tile, width), lambda i: (i, 2)),
            pl.BlockSpec((width, width), lambda i: (0, 0)),
            rows,
            heads,
        ],
        out_specs=[rows] * 6 + [heads],
        out_shape=[low, jax.ShapeDtypeStruct((frames, width), F32), low, low, low, low]
        + [jax.ShapeDtypeStruct((pairs, 8, frames), F32)],
        compiler_params=params(),
        cost_estimate=cost(2 * frames * width * width, 2 * width * width + 30 * frames * width),
    )(fed, resid_mid, grad_normed, cot_rows, modulation, w_out, attended, inverses)


def attend_back_kernel(span, q_ref, *refs):
    k_refs, v_refs = refs[:span], refs[span : 2 * span]
    p_ref, c_ref, g_ref, cos_ref, sin_ref = refs[2 * span : 2 * span + 5]
    dq_ref, dkv_refs, ds_ref = refs[2 * span + 5], refs[2 * span + 6 : -1], refs[-1]
    frames = q_ref.shape[0]

    def unturn(grad, index):
        rows = slice(index * frames, (index + 1) * frames)
        return grad * cos_ref[rows, :] - turn(grad) * sin_ref[rows, :]

    keys_t = [k[...].T for k in k_refs]
    dk, dv, dq = [None] * span, [None] * span, []
    for which in range(2):
        centre = c_ref[0, which : which + 1, :]
        grads = only_head(g_ref[...], which)
        queries = only_head(q_ref[...], which)
        result = None
        for index in range(span):
            rows = slice(index * frames, (index + 1) * frames)
            grad_probs = dot(v_refs[index][...], grads, DIMS_LAST)
            soft = p_ref[which, rows, :]
            ds_ref[rows, :] = (soft.astype(F32) * (grad_probs - centre)).astype(BF)
            part = dot(soft, grads)
            dv[index] = part if dv[index] is None else dv[index] + part
            part = dot(ds_ref[rows, :], queries)
            dk[index] = part if dk[index] is None else dk[index] + part
            part = dot(keys_t[index][which * HD : (which + 1) * HD], ds_ref[rows, :])
            result = part if result is None else result + part
        dq.append(result)
    dq = jnp.concatenate(dq, axis=0).T
    dq_ref[...] = unturn(dq * HD ** (-0.5), 0).astype(BF)
    for index in range(span):
        dkv_refs[index][0] = unturn(dk[index] * (1.0 / LOG2E), index).astype(BF)
        dkv_refs[index][1] = dv[index].astype(BF)


def attend_back(queries, pairs_kv, probs, centres, grads, cos_keys, sin_keys):
    span = len(pairs_kv)
    frames, width = queries.shape
    pairs = width // PAIR
    keys = span * frames
    results = pl.pallas_call(
        functools.partial(attend_back_kernel, span),
        grid=(pairs,),
        in_specs=[columns(frames)]
        + [columns(frames)] * span
        + [columns(frames, pairs)] * span
        + [
            pl.BlockSpec((2, keys, frames), lambda i: (i, 0, 0)),
            pl.BlockSpec((1, 8, frames), lambda i: (i, 0, 0)),
            columns(frames),
            pl.BlockSpec((keys, PAIR), lambda i: (0, 0)),
            pl.BlockSpec((keys, PAIR), lambda i: (0, 0)),
        ],
        out_specs=[columns(frames)]
        + [pl.BlockSpec((2, frames, PAIR), lambda i: (0, 0, i))] * span,
        out_shape=[jax.ShapeDtypeStruct((frames, width), BF)]
        + [jax.ShapeDtypeStruct((2, frames, width), BF)] * span,
        scratch_shapes=[pltpu.VMEM((keys, frames), BF)],
        compiler_params=params(),
        cost_estimate=cost(32 * pairs * frames * keys * PAIR, 4 * pairs * frames * keys),
    )(queries, *pairs_kv, *pairs_kv, probs, centres, grads, cos_keys, sin_keys)
    return results[0], results[1:]


def split_rows(source, target, groups, low_bit):
    chunk = source.shape[0] // groups
    half = source.shape[0] // 2
    for index in range(groups // 2):
        for part, bit in ((0, 1 - low_bit), (1, low_bit)):
            first = pl.multiple_of((2 * index + bit) * chunk, chunk)
            start = part * half + index * chunk
            target[start : start + chunk, :] = source[pl.ds(first, chunk), :]


def feed_kernel(groups, started, x_ref, g_ref, up_ref, down_ref, *refs):
    if started:
        before_acc, before_gx, *refs = refs
    acc_ref, gx_ref, da_ref, dk_ref, ua_ref, uk_ref, t_ref, xt_ref = refs
    step = pl.program_id(0)
    low_bit = lax.axis_index("head") % 2

    @pl.when(step == 0)
    def _():
        t_ref[...] = x_ref[...].T
        split_rows(t_ref, xt_ref, groups, low_bit)
        acc_ref[...] = before_acc[...] if started else jnp.zeros_like(acc_ref)
        gx_ref[...] = before_gx[...] if started else jnp.zeros_like(gx_ref)

    up = dot(x_ref[...], up_ref[...])
    grad_hidden = dot(g_ref[...], down_ref[...], DIMS_LAST)
    root = math.sqrt(2.0 / math.pi)
    square = up * up
    bent = jnp.tanh(root * up * (1.0 + 0.044715 * square))
    half = 0.5 + 0.5 * bent
    slope = half + 0.5 * up * (1.0 - bent * bent) * (root * (1.0 + 3 * 0.044715 * square))
    hidden = (up * half).astype(BF)
    grad_up = (grad_hidden * slope).astype(BF)
    acc_ref[...] += dot(hidden, down_ref[...])
    gx_ref[...] += dot(grad_up, up_ref[...], DIMS_LAST)
    rows = dot(hidden, g_ref[...], DIMS_FIRST).astype(BF)

    @pl.when(step % 2 == low_bit)
    def _():
        dk_ref[...] = rows

    @pl.when(step % 2 != low_bit)
    def _():
        da_ref[...] = rows

    depth = x_ref.shape[1] // 2
    ua_ref[...] = dot(xt_ref[:depth, :], grad_up).astype(BF)
    uk_ref[...] = dot(xt_ref[depth:, :], grad_up).astype(BF)


def feed(normed, grads, w_up, w_down, first, count, *sums):
    groups = lax.axis_size("head")
    frames, width = normed.shape
    tile = w_up.shape[1] // groups
    inner = count * tile
    whole = pl.BlockSpec((frames, width), lambda i: (0, 0))
    rows = pl.BlockSpec((tile, width), lambda i: (i // 2, 0))
    cols = pl.BlockSpec((width // 2, tile), lambda i: (0, i))
    total = jax.ShapeDtypeStruct((frames, width), F32)
    down = jax.ShapeDtypeStruct((inner // 2, width), BF)
    up = jax.ShapeDtypeStruct((width // 2, inner), BF)
    return pl.pallas_call(
        functools.partial(feed_kernel, groups, bool(sums)),
        grid=(count,),
        in_specs=[
            whole,
            whole,
            pl.BlockSpec((width, tile), lambda i: (0, first + i)),
            pl.BlockSpec((tile, width), lambda i: (first + i, 0)),
        ]
        + [whole] * len(sums),
        out_specs=[whole, whole, rows, rows, cols, cols],
        out_shape=[total, total, down, down, up, up],
        scratch_shapes=[pltpu.VMEM((width, frames), BF), pltpu.VMEM((width, frames), BF)],
        compiler_params=params(),
        cost_estimate=cost(12 * frames * width * inner, 8 * width * inner, frames * inner),
    )(normed, grads, w_up, w_down, *sums)


def near_kernel(groups, span, *refs):
    dq_ref, dkv_refs, refs = refs[0], refs[1 : span + 1], refs[span + 1 :]
    w_ref, x_ref, a_ref, gl_ref, r_ref, scale_ref, gm_ref = refs[:7]
    away_ref, keep_ref, gi_ref, gs_ref, gc_ref = refs[7:12]
    t_ref, xt_ref, at_ref, acc_ref = refs[12:]
    step = pl.program_id(0)
    tiles = x_ref.shape[1] // dq_ref.shape[1]
    low_bit = lax.axis_index("head") % 2
    half = x_ref.shape[1] // 2

    @pl.when(step == 0)
    def _():
        for source, target in ((x_ref, xt_ref), (a_ref, at_ref)):
            t_ref[...] = source[...].T
            split_rows(t_ref, target, groups, low_bit)

    def one(left_ref, grads):
        away_ref[...] = dot(left_ref[:half, :], grads).astype(BF)
        keep_ref[...] = dot(left_ref[half:, :], grads).astype(BF)

    def projected(grads, first):
        one(xt_ref, grads)
        part = dot(grads, w_ref[...], DIMS_LAST)
        acc_ref[...] = part if first else acc_ref[...] + part

    @pl.when(step == 0)
    def _():
        projected(dq_ref[...], True)

    @pl.when((step > 0) & (step < tiles))
    def _():
        projected(dq_ref[...], False)

    @pl.when((step >= tiles) & (step < 3 * tiles))
    def _():
        grads = functools.reduce(jnp.add, [ref[0].astype(F32) for ref in dkv_refs])
        projected(grads.astype(BF), False)

    @pl.when(step >= 3 * tiles)
    def _():
        one(at_ref, gl_ref[...])

    @pl.when(step == 4 * tiles - 1)
    def _():
        normal, rate = norm_stats(r_ref[...].astype(F32))
        grad = acc_ref[...]
        gi_ref[...] = (gm_ref[...] + norm_back(grad, normal, rate, scale_ref[...])).astype(BF)
        gs_ref[...] = grad.astype(BF)
        gc_ref[...] = (grad * normal).astype(BF)


def near(dq, dkv, w_qkv, normed, attended, grad_low, resid_in, modulation, grad_mid):
    groups = lax.axis_size("head")
    frames, width = dq.shape
    tile = 512
    tiles = width // tile
    whole = pl.BlockSpec((frames, width), lambda i: (0, 0))

    def pair(i):
        index = jnp.clip(i - tiles, 0, 2 * tiles - 1)
        return (index // tiles, 0, index % tiles)

    grads = pl.BlockSpec((width // 2, tile), lambda i: (0, i))
    out = jax.ShapeDtypeStruct((width // 2, 4 * width), BF)
    low = jax.ShapeDtypeStruct((frames, width), BF)
    return pl.pallas_call(
        functools.partial(near_kernel, groups, len(dkv)),
        grid=(4 * tiles,),
        in_specs=[pl.BlockSpec((frames, tile), lambda i: (0, jnp.minimum(i, tiles - 1)))]
        + [pl.BlockSpec((1, frames, tile), pair)] * len(dkv)
        + [
            pl.BlockSpec((width, tile), lambda i: (0, jnp.minimum(i, 3 * tiles - 1))),
            whole,
            whole,
            pl.BlockSpec((frames, tile), lambda i: (0, jnp.maximum(i - 3 * tiles, 0))),
            whole,
            whole,
            whole,
        ],
        out_specs=[grads, grads, whole, whole, whole],
        out_shape=[out, out, low, low, low],
        scratch_shapes=[pltpu.VMEM((width, frames), BF)] * 3 + [pltpu.VMEM((frames, width), F32)],
        compiler_params=params(),
        cost_estimate=cost(14 * frames * width * width, 14 * width * width + 30 * frames * width),
    )(dq, *dkv, w_qkv, normed, attended, grad_low, resid_in, modulation, grad_mid)


def far_kernel(groups, count, *refs):
    pieces, refs = refs[:count], refs[count:]
    f_ref, gi_ref, m_refs = refs[0], refs[1], refs[2:6]
    sa_ref, sk_ref, ta_ref, tk_ref, t_ref, st_ref, u_ref, ft_ref = refs[6:]
    low_bit = lax.axis_index("head") % 2
    rows, width = pieces[0].shape[1], pieces[0].shape[2]

    @pl.when(pl.program_id(0) == 0)
    def _():
        for index, piece in enumerate(pieces):
            here = slice(index * rows, (index + 1) * rows)
            t_ref[:width, here] = piece[0].T
            t_ref[width:, here] = piece[1].T
        split_rows(t_ref, st_ref, groups, low_bit)
        u_ref[...] = f_ref[...].T
        split_rows(u_ref, ft_ref, groups, low_bit)

    half, few = width, u_ref.shape[0] // 2
    sa_ref[...] = dot(st_ref[:half, :], gi_ref[...]).astype(BF)
    sk_ref[...] = dot(st_ref[half:, :], gi_ref[...]).astype(BF)
    for index, m_ref in enumerate(m_refs):
        ta_ref[index] = dot(ft_ref[:few, :], m_ref[...]).astype(BF)
        tk_ref[index] = dot(ft_ref[few:, :], m_ref[...]).astype(BF)


def far(pieces, features, grad_in, grad_mods):
    groups = lax.axis_size("head")
    frames, width = grad_in.shape
    few = features.shape[1]
    tile = 512
    cols = pl.BlockSpec((frames, tile), lambda i: (0, i))
    big = pl.BlockSpec((width, tile), lambda i: (0, i))
    small = pl.BlockSpec((4, few // 2, tile), lambda i: (0, 0, i))
    return pl.pallas_call(
        functools.partial(far_kernel, groups, len(pieces)),
        grid=(width // tile,),
        in_specs=[pl.BlockSpec(piece.shape, lambda i: (0, 0, 0)) for piece in pieces]
        + [pl.BlockSpec((frames, few), lambda i: (0, 0))]
        + [cols] * 5,
        out_specs=[big, big, small, small],
        out_shape=[jax.ShapeDtypeStruct((width, width), BF)] * 2
        + [jax.ShapeDtypeStruct((4, few // 2, width), BF)] * 2,
        scratch_shapes=[pltpu.VMEM((2 * width, frames), BF)] * 2
        + [pltpu.VMEM((few, frames), BF)] * 2,
        compiler_params=params(),
        cost_estimate=cost(6 * frames * width * width, 6 * width * width + 20 * frames * width),
    )(*pieces, features, grad_in, *grad_mods)


def per_device(
    inputs,
    skips,
    flow_time,
    segment_ids,
    frame_mask,
    cotangent,
    w_skip,
    w_time,
    w_qkv,
    w_out,
    w_up,
    w_down,
):
    groups = lax.axis_size("head")
    micro_count, _, rows, width = inputs.shape
    span = groups // micro_count
    place = lax.axis_index("head")
    mine = place // span
    frames = micro_count * rows
    feature_count = w_time.shape[0]
    inputs, skips, cotangent = inputs[:, 0], skips[:, 0], cotangent[:, 0]

    resid_own = dot(inputs.reshape(frames, width), w_skip[:width]) + dot(
        skips.reshape(frames, width), w_skip[width:]
    )
    own_mod = dot(time_features(flow_time.reshape(-1), feature_count), w_time[:, : 2 * width])
    normed_own = norm_stats(resid_own)[0] * (1.0 + own_mod[:, width:]) + own_mod[:, :width]
    normed_own = cut_parts(normed_own.astype(BF).reshape(micro_count, rows, width), mine)

    meta = jnp.stack(
        [segment_ids[:, 0].astype(F32), frame_mask[:, 0].astype(F32), flow_time[:, 0]], axis=1
    )[None]
    for bit in range(groups.bit_length() - 1):
        meta = jnp.concatenate([meta, swap(meta, "head", 2**bit)])
    meta = pick(meta, mine, 1).reshape(micro_count, span, 3, rows)
    seg_keys, live_keys, times = [meta[:, :, i].swapaxes(0, 1).reshape(-1) for i in range(3)]
    order = jnp.stack(
        [place ^ other ^ (step * span) for other in range(span) for step in range(micro_count)]
    )
    place_keys = (order[:, None] * rows + jnp.arange(rows)[None, :]).reshape(-1).astype(F32)
    starts = jnp.sum((seg_keys[None, :] < seg_keys[:, None]).astype(F32), axis=1)
    positions = place_keys - starts
    inv_freq = jnp.exp(jnp.arange(HD // 2, dtype=F32) * (-2.0 * math.log(10000.0) / HD))
    turns = positions[:, None] * inv_freq
    cos_half, sin_half = jnp.cos(turns), jnp.sin(turns)
    cos_keys = jnp.concatenate([cos_half] * 4, axis=1)
    sin_keys = jnp.concatenate([-sin_half, sin_half] * 2, axis=1)
    meta_q = jnp.stack(
        [seg_keys[:frames], place_keys[:frames]] + [jnp.zeros((frames,), F32)] * 6
    )
    meta_k = jnp.stack([seg_keys, place_keys, live_keys], axis=1)
    meta_k = jnp.pad(meta_k, ((0, 0), (0, PAIR - 3)))
    features = time_features(times[:frames], feature_count)
    modulation = dot(features, w_time[:, width:])

    normed_attn = send_parts(normed_own, span)
    modulation, *normed_attn = together(modulation, *normed_attn)
    normed_attn = jnp.concatenate(normed_attn)
    second = jnp.stack(
        [cotangent, resid_own.astype(BF).reshape(micro_count, rows, width)], axis=1
    )
    second = cut_parts(second, mine)
    joined = cut_parts(jnp.stack([inputs, skips], axis=1), mine)
    normed_attn, *second = together(normed_attn, *second)
    second = send_parts(second, span)

    queries, keys_values = project(normed_attn, w_qkv, cos_keys[:frames], sin_keys[:frames])
    pairs_kv = [keys_values] + [swap(keys_values, "head", other) for other in range(1, span)]
    queries, *joined = together(queries, *joined)
    attended, probs, inverses = attend(queries, pairs_kv, meta_k, meta_q)
    attended, *second = together(attended, *second)
    cot_rows = jnp.concatenate([part[0] for part in second])
    resid_in = jnp.concatenate([part[1] for part in second])
    resid_mid = resid_in.astype(F32) + dot(attended, w_out)
    normal_second = norm_stats(resid_mid)[0]
    normed_ffn = (
        normal_second * (1.0 + modulation[:, 2 * width :]) + modulation[:, width : 2 * width]
    ).astype(BF)

    normed_ffn, *joined = together(normed_ffn, *joined)
    joined = send_parts(joined, span)
    half = groups // 2
    *sums, down_away, down_keep, up_away, up_keep = feed(
        normed_ffn, cot_rows, w_up, w_down, 0, half
    )
    down_away, up_away, normed_ffn, *rest = together(down_away, up_away, normed_ffn, *sums, *joined)
    sums, joined = rest[:2], rest[2:]
    down_came, up_came = swap(down_away, "head", 1), swap(up_away, "head", 1)
    *sums, down_away, down_keep_b, up_away_b, up_keep_b = feed(
        normed_ffn, cot_rows, w_up, w_down, half, half, *sums
    )
    *sums, down_came, up_came, down_away_b, up_away_b = together(
        *sums, down_came, up_came, down_away, up_away_b
    )
    seq_bits = lax.axis_size("seq").bit_length() - 1
    bits = list(range(seq_bits + 1, seq_bits + groups.bit_length() - 1))
    first, top = bits[0], bits[-1]
    down_a, up_a = Rows([down_keep, down_came], bits[:-1]), Rows([up_keep, up_came], bits)
    down_go, up_go, *sums = together(down_a.away(first), up_a.away(top), *sums)

    down_came, up_came = cross(down_go, first), cross(up_go, top)
    down_came_b, up_came_b = swap(down_away_b, "head", 1), swap(up_away_b, "head", 1)
    output, grad_mid, grad_mid_low, mod_shift, mod_scale, grads, centres = middle(
        sums[0], resid_mid, sums[1], cot_rows, modulation, w_out, attended, inverses
    )
    dq, dkv = attend_back(queries, pairs_kv, probs, centres, grads, cos_keys, sin_keys)
    dq, down_came, up_came, down_came_b, up_came_b, *dkv = together(
        dq, down_came, up_came, down_came_b, up_came_b, *dkv
    )
    down_a.join(down_came)
    up_a.join(up_came)
    down_b, up_b = Rows([down_keep_b, down_came_b], bits[:-1]), Rows([up_keep_b, up_came_b], bits)

    dkv[1:] = [swap(part, "head", other) for other, part in enumerate(dkv) if other > 0]
    dq, down_go, up_go = together(dq, down_b.away(first), up_b.away(top))
    down_came, up_came = cross(down_go, first), cross(up_go, top)
    near_away, near_keep, grad_in_low, first_shift, first_scale = near(
        dq, dkv, w_qkv, normed_attn, attended, grad_mid_low, resid_in, modulation, grad_mid
    )
    near_away, grad_in_low, down_came, up_came = together(
        near_away, grad_in_low, down_came, up_came
    )
    down_b.join(down_came)
    up_b.join(up_came)

    near_came = swap(near_away, "head", 1)
    for bit in bits[1:-1]:
        step_all([down_a, down_b], bit)
        step_all([up_a, up_b], bit)
    down_a, down_b = down_a.read(), down_b.read()
    upper = (place_of() >> top) % 2 == 1
    down_keep = jnp.where(upper, down_b, down_a)
    grad_in_low, down_go, up_go, up_go_b = together(
        grad_in_low, jnp.where(upper, down_a, down_b), up_a.away(first), up_b.away(first)
    )
    down_came = cross(down_go, top)
    up_came, up_came_b = cross(up_go, first), cross(up_go_b, first)
    skip_away, skip_keep, time_away, time_keep = far(
        joined, features, grad_in_low, [first_shift, first_scale, mod_shift, mod_scale]
    )
    skip_away, time_away, near_came, down_came, up_came, up_came_b = together(
        skip_away, time_away, near_came, down_came, up_came, up_came_b
    )
    up_a.join(up_came)
    up_b.join(up_came_b)

    skip_came, time_came = swap(skip_away, "head", 1), swap(time_away, "head", 1)
    middle_col = near_keep.shape[1] // 2
    wide = [[Rows([near_keep, near_came], bits, 1, (i * middle_col, middle_col))] for i in range(2)]

    def both_ways(pairs, index):
        return [(parts, order[index]) for parts, order in zip(pairs, (bits, bits[::-1]), strict=True)]

    def stage(steps, *values):
        sent = [cross(away_all(parts, bit), bit) for parts, bit in steps]
        *sent, values = together(*sent, values)
        for (parts, _), came in zip(steps, sent, strict=True):
            join_all(parts, came)
        return values

    total_down, total_up = last_sum(
        add_low([down_keep, down_came]), jnp.concatenate([up_a.read(), up_b.read()], axis=1)
    )
    skip_came, time_came = stage(both_ways(wide, 0), skip_came, time_came)
    narrow = [
        [
            Rows([skip_keep, skip_came], list(range(seq_bits)) + bits, 1, cols),
            Rows([time_keep, time_came], list(range(seq_bits)) + bits, 4, cols),
        ]
        for cols in ((0, width // 2), (width // 2, width // 2))
    ]
    for index in range(1, len(bits)):
        stage(both_ways(wide, index) + both_ways(narrow, index - 1))
    wide_sum = jnp.concatenate([wide[0][0].read(), wide[1][0].read()], axis=1)
    (near_sum,) = last_sum(wide_sum)
    wide_sum, output, grad_in_low = together(wide_sum, output, grad_in_low)
    output = from_buckets(output.reshape(micro_count, rows, width), span, mine)
    output, grad_in_low = stage(both_ways(narrow, len(bits) - 1), output, grad_in_low)
    grad_local = from_buckets(grad_in_low.reshape(micro_count, rows, width), span, mine)
    grad_local = grad_local.reshape(frames, width)
    total_qkv, total_out = near_sum[:, : 3 * width], near_sum[:, 3 * width :]
    for bit in range(seq_bits):
        for parts in narrow:
            step_all(parts, bit)
    total_skip = jnp.concatenate([parts[0].read() for parts in narrow], axis=1).astype(F32)
    total_time = jnp.concatenate([parts[1].read() for parts in narrow], axis=1).astype(F32)
    total_time = total_time.reshape(4, -1, width).swapaxes(0, 1).reshape(-1, 4 * width)
    shape = (micro_count, 1, rows, width)
    input_grad = dot(grad_local, w_skip[:width], DIMS_LAST).reshape(shape)
    skip_grad = dot(grad_local, w_skip[width:], DIMS_LAST).reshape(shape)
    return (
        output[:, None],
        input_grad,
        skip_grad,
        total_skip,
        total_time,
        total_qkv,
        total_out,
        total_up,
        total_down,
    )


def solution(mesh):
    frames_spec = P(None, "seq", "head", None)
    line_spec = P(None, "seq", "head")
    shard_spec = P(("head", "seq"), None)
    return jax.shard_map(
        per_device,
        mesh=mesh,
        in_specs=(frames_spec, frames_spec, line_spec, line_spec, line_spec, frames_spec)
        + (P(),) * 6,
        out_specs=(frames_spec,) * 3 + (shard_spec,) * 6,
        check_vma=False,
    )
```

time: 489 us -> 404 us (0.83)
  waiting for transfers between devices: 157 us -> 74.9 us
  other arithmetic: 96.2 us -> 75 us
  starting transfers between devices: 34.1 us -> 47.4 us
  local copies, waits for them, and re-layouts: 26.3 us -> 37.7 us
  matrix products: 27 us -> 16.5 us
    ppermute x39 -> x46, waiting for transfers between devices: 155 us -> 74.8 us  [swap(): return lax.ppermute(values, axis_name, [(i, i ^ bits) for i in range(size)])]
    ppermute x39 -> x46, starting transfers between devices: 33.6 us -> 47.1 us  [swap(): return lax.ppermute(values, axis_name, [(i, i ^ bits) for i in range(size)])]
    convert_element_type x23 -> x32, other arithmetic: 51.5 us -> 38.5 us  [the longest x29 36.7 us: add_low(): functools.reduce(jnp.add, [term.astype(F32) for term in terms]).astype(BF)]
    squeeze x15 -> x1, local copies, waits for them, and re-layouts: 11.3 us -> 0.1 us  [pick(): return lax.dynamic_index_in_dim(values, index, axis, keepdims=False)]
    slice x4 -> x18, local copies, waits for them, and re-layouts: 4.7 us -> 15.7 us  [the longest x12 9.71 us: join_all(): part.join(came[start:start + height])]
    dot_general x8 -> x7, matrix products: 27 us -> 16.5 us  [dot(): return lax.dot_general(left, right, dims, preferred_element_type=F32)]
    reshape x6 -> x1, other arithmetic: 10.9 us -> 0.67 us  [per_device(): total_time.reshape(4, -1, width).swapaxes(0, 1).reshape(-1, 4 * width)]
    unnamed x76 -> x113, local copies, waits for them, and re-layouts: 5.83 us -> 14.9 us
  transfers between devices with their start and end apart: 45 -> 48, of which waited for: 23 -> 17; matrix products, arithmetic and copies ran while one was open for 25% -> 24% of each run, Pallas kernels for 13% -> 31%
where the time goes in v3:
time: 404 us; the launch traced here: 399 us
  Pallas kernels  132 us (33%)
  other arithmetic  75 us (19%)
  waiting for transfers between devices  74.9 us (19%)
  starting transfers between devices  47.4 us (12%)
  local copies, waits for them, and re-layouts  37.7 us (9%)
  matrix products  16.5 us (4%)
  between operations  15.4 us (4%)
    ppermute x46, waiting for transfers between devices, swap(): return lax.ppermute(values, axis_name, [(i, i ^ bits) for i in range(size)])  74.8 us
    ppermute x46, starting transfers between devices, swap(): return lax.ppermute(values, axis_name, [(i, i ^ bits) for i in range(size)])  47.1 us
    pallas_call x2, Pallas kernels, feed(): pl.pallas_call(functools.partial(feed_kernel, groups, bool(sums)), grid=(...  42.8 us
    convert_element_type x29, other arithmetic, add_low(): functools.reduce(jnp.add, [term.astype(F32) for term in terms]).astype(BF)  36.7 us
    pallas_call x1, Pallas kernels, attend_back(): pl.pallas_call(functools.partial(attend_back_kernel, span), grid=(pairs,)...  23.4 us
    pallas_call x1, Pallas kernels, attend(): pl.pallas_call(functools.partial(attend_kernel, span), grid=(pairs,), in_...  20.5 us
    pallas_call x1, Pallas kernels, near(): pl.pallas_call(functools.partial(near_kernel, groups, len(dkv)), grid=(4...  19.8 us
    dot_general x7, matrix products, dot(): return lax.dot_general(left, right, dims, preferred_element_type=F32)  16.5 us
  transfers between devices with their start and end apart: 48, of which 17 were waited for; matrix products, arithmetic and copies ran while one was open for 24% of the time, Pallas kernels for 31%

profile of v3, /device:TPU:0, one launch (start us, length us, event | category | flops | bytes accessed | tf_op | source)
XLA Modules:
  0.0 399.1 jit_solution(14321005867398787883)
XLA Ops:
  10.6 2.3 constant_dynamic-update-slice_fusion.1
  12.9 3.0 fusion.9
  18.9 2.6 collective-permute-start.1
  23.1 2.1 collective-permute-start.2
  25.3 1.8 collective-permute-done.2
  27.1 2.8 fusion.53
  29.9 1.9 fusion.39
  32.6 2.1 collective-permute-start.3
  36.8 3.6 fusion.20.refs_4_.refs_8_
  40.4 1.9 fusion.62
  44.2 1.9 fusion.42
  47.4 10.1 %shard_map.187 = (bf16[512,1024]{1,0:T(8,128)(2,1)S(1)}, bf16[512,2048]{1,0:T(8,128)(2,1)}) custom-call(bf16[512,1024]{1,0:T(8,128)(2,1)} %pad_maximum_fusion.x_ref.refs_4_, bf16[1024,3072]{1,0:T(8,128)(2,1)} %refs_3_.1, f32[512,128]{1,0:T(8,128)S(1)} %slice.260.cos_ref, f32[512,128]{1,0:T(8,128)S(1)} %slice.261.sin_ref), custom_call_target="tpu_custom_call" | custom-call | flops 3221225472 | bytes 10485760 | tf_op jit(solution)/shard_map/pallas_call | solution.py:203
  63.5 20.5 %shard_map.188 = (bf16[512,1024]{1,0:T(8,128)(2,1)S(1)}, bf16[16,1024,512]{2,1,0:T(8,128)(2,1)}, f32[8,8,512]{2,1,0:T(8,128)S(1)}) custom-call(bf16[512,1024]{1,0:T(8,128)(2,1)} %copy-done.5, bf16[512,2048]{1,0:T(8,128)(2,1)} %get-tuple-element.134.refs_0_.refs_2_, bf16[512,2048]{1,0:T(8,128)(2,1)} %collective-permute-done.6.refs_1_.refs_3_, ...), custom_call_target="tpu_custom_call" | custom-call | flops 8589934592 | bytes 16777216 | tf_op jit(solution)/shard_map/pallas_call | solution.py:278
  84.0 3.1 collective-permute-done.8
  96.8 20.7 %shard_map.189 = (f32[512,1024]{1,0:T(8,128)}, f32[512,1024]{1,0:T(8,128)}, bf16[1024,1024]{1,0:T(8,128)(2,1)}, bf16[1024,1024]{1,0:T(8,128)(2,1)}, bf16[512,204...) custom-call(bf16[512,1024]{1,0:T(8,128)(2,1)S(1)} %add_convert_fusion.7.x_ref, ...), custom_call_target="tpu_custom_call" | custom-call | flops 12884901888 | bytes 16777216 | tf_op jit(solution)/shard_map/pallas_call | solution.py:488
  120.1 22.1 %shard_map.190 = (f32[512,1024]{1,0:T(8,128)}, f32[512,1024]{1,0:T(8,128)}, bf16[1024,1024]{1,0:T(8,128)(2,1)}, bf16[1024,1024]{1,0:T(8,128)(2,1)}, bf16[512,204...) custom-call(bf16[512,1024]{1,0:T(8,128)(2,1)S(1)} %add_convert_fusion.7.x_ref, ...), custom_call_target="tpu_custom_call" | custom-call | flops 12884901888 | bytes 16777216 | tf_op jit(solution)/shard_map/pallas_call | solution.py:488
  142.8 2.7 fusion.25
  145.4 2.6 add_convert_fusion.5
  150.0 7.8 %shard_map.191 = (bf16[512,1024]{1,0:T(8,128)(2,1)S(1)}, f32[512,1024]{1,0:T(8,128)}, bf16[512,1024]{1,0:T(8,128)(2,1)}, bf16[512,1024]{1,0:T(8,128)(2,1)}, bf16...) custom-call(f32[512,1024]{1,0:T(8,128)} %get-tuple-element.179.refs_0_, ...), custom_call_target="tpu_custom_call" | custom-call | flops 1073741824 | bytes 17825792 | tf_op jit(solution)/shard_map/pallas_call | solution.py:341
  157.8 23.4 %shard_map.192 = (bf16[512,1024]{1,0:T(8,128)(2,1)}, bf16[2,512,1024]{2,1,0:T(8,128)(2,1)}, bf16[2,512,1024]{2,1,0:T(8,128)(2,1)}) custom-call(bf16[512,1024]{1,0:T(8,128)(2,1)} %copy-done.5, bf16[512,2048]{1,0:T(8,128)(2,1)} %get-tuple-element.134.refs_0_.refs_2_, bf16[512,2048]{1,0:T(8,128)(2,1)} %collective-permute-done.6.refs_1_.refs_3_, ...), custom_call_target="tpu_custom_call" | custom-call | flops 17179869184 | bytes 16777216 | tf_op jit(solution)/shard_map/pallas_call | solution.py:403
  189.1 19.8 %shard_map.193 = (bf16[512,4096]{1,0:T(8,128)(2,1)}, bf16[512,4096]{1,0:T(8,128)(2,1)}, bf16[512,1024]{1,0:T(8,128)(2,1)S(1)}, bf16[512,1024]{1,0:T(8,128)(2,1)}, bf16[512,1024]{1,0:T(8,128)(2,1)}) custom-call(bf16[512,1024]{1,0:T(8,128)(2,1)} %get-tuple-element.196.refs_0_, bf16[2,512,1024]{2,1,0:T(8,128)(2,1)} %get-tuple-element.197.refs_1_, ...), custom_call_target="tpu_custom_call" | custom-call | flops 7516192768 | bytes 30408704 | tf_op jit(solution)/shard_map/pallas_call | solution.py:571
  210.1 2.6 fusion.38
  212.7 2.4 fusion.37
  215.1 3.9 broadcast_select_fusion
  222.1 8.1 %shard_map.194 = (bf16[1024,1024]{1,0:T(8,128)(2,1)}, bf16[1024,1024]{1,0:T(8,128)(2,1)}, bf16[4,128,1024]{2,1,0:T(8,128)(2,1)}, bf16[4,128,1024]{2,1,0:T(8,128)(2,1)}) custom-call(bf16[2,128,1024]{2,1,0:T(8,128)(2,1)S(1)} %get-tuple-element.159.refs_0_, bf16[2,128,1024]{2,1,0:T(8,128)(2,1)S(1)} %collective-permute-done.10.refs_1_, ...), custom_call_target="tpu_custom_call" | custom-call | flops 3221225472 | bytes 16777216 | tf_op jit(solution)/shard_map/pallas_call | solution.py:626
  230.2 4.8 %collective-permute-done.24 = bf16[128,2048]{1,0:T(8,128)(2,1)S(1)} collective-permute-done((bf16[128,2048]{1,0:T(8,128)(2,1)}, bf16[128,2048]{1,0:T(8,128)(2,1)S(1)}, u32[]{:S(2)}, u32[]{:S(2)}) %collective-permute-start.24) | collective-permute-done | bytes 524320 | tf_op jit(solution)/shard_map/ppermute | solution.py:29
  234.9 10.6 %collective-permute-done.25 = bf16[128,2048]{1,0:T(8,128)(2,1)} collective-permute-done((bf16[128,2048]{1,0:T(8,128)(2,1)}, bf16[128,2048]{1,0:T(8,128)(2,1)}, u32[]{:S(2)}, u32[]{:S(2)}) %collective-permute-start.25) | collective-permute-done | bytes 524320 | tf_op jit(solution)/shard_map/ppermute | solution.py:29
  245.6 2.6 add_convert_fusion.2
  248.2 2.6 add_convert_fusion.1
  253.3 1.8 fusion.28
  259.4 16.2 %collective-permute-done.26 = bf16[256,2048]{1,0:T(8,128)(2,1)} collective-permute-done((bf16[256,2048]{1,0:T(8,128)(2,1)}, bf16[256,2048]{1,0:T(8,128)(2,1)}, u32[]{:S(2)}, u32[]{:S(2)}) %collective-permute-start.26) | collective-permute-done | bytes 1048608 | tf_op jit(solution)/shard_map/ppermute | solution.py:29
  285.3 3.4 fusion.35
  292.1 1.9 convert_add_fusion.21
  295.7 2.0 convert_add_fusion.11
  297.7 15.5 %collective-permute-done.30 = bf16[128,2048]{1,0:T(8,128)(2,1)} collective-permute-done((bf16[128,2048]{1,0:T(8,128)(2,1)}, bf16[128,2048]{1,0:T(8,128)(2,1)}, u32[]{:S(2)}, u32[]{:S(2)}) %collective-permute-start.30) | collective-permute-done | bytes 524320 | tf_op jit(solution)/shard_map/ppermute | solution.py:29
  315.4 1.9 slice.221
  317.2 1.9 slice.220
  321.2 2.8 fusion.34
  333.6 2.8 collective-permute-done.38
  336.5 3.2 collective-permute-done.37
  339.7 2.0 collective-permute-done.36
  355.9 8.0 %collective-permute-done.42 = bf16[192,512]{1,0:T(8,128)(2,1)S(1)} collective-permute-done((bf16[192,512]{1,0:T(8,128)(2,1)S(1)}, bf16[192,512]{1,0:T(8,128)(2,1)S(1)}, u32[]{:S(2)}, u32[]{:S(2)}) %collective-permute-start.42) | collective-permute-done | bytes 196640 | tf_op jit(solution)/shard_map/ppermute | solution.py:29
  365.6 3.8 collective-permute-start.43
  369.7 1.9 copy-done.49
  371.7 2.6 fusion.14
  377.7 2.6 fusion.17
  380.3 1.9 collective-permute-done.45
  385.3 1.8 slice.282
  (318 shorter events, 109.7 us)
Async XLA Ops:
  7.2 378.1 %reduce-scatter.5.cloned.1.call-start = ((), (), s32[]{:S(2)}) async-start(), calls=%async_computation.3 | async-start | bytes 2621440 | tf_op jit(solution)/shard_map/reduce_scatter | solution.py:131
  9.4 9.5 %collective-permute-start = (f32[1,4,3,128]{3,1,2,0:T(4,128)S(1)}, f32[1,4,3,128]{3,1,2,0:T(4,128)S(1)}, u32[]{:S(2)}, u32[]{:S(2)}) collective-permute-start(f32[1,4,3,128]{3,1,2,0:T(4,128)S(1)} %bitcast.489), channel_id=1, source_target_pairs={{0,4},{4,0},{8,12},{12,8},{16,20},{20,16},{24,28},{28,24},{1,5},{5... | collective-permute-start | bytes 18440 | tf_op jit(solution)/shard_map/ppermute | solution.py:29
  18.9 4.2 %collective-permute-start.1 = (f32[2,4,3,128]{3,1,2,0:T(4,128)S(1)}, f32[2,4,3,128]{3,1,2,0:T(4,128)S(1)}, u32[]{:S(2)}, u32[]{:S(2)}) collective-permute-start(f32[2,4,3,128]{3,1,2,0:T(4,128)S(1)} %pad_maximum_fusion.25), channel_id=1, source_target_pairs={{0,8},{4,12},{8,0},{12,4},{16,24},{20,28},{24,16},{28,20},{1,9},{5... | collective-permute-start | bytes 36872 | tf_op jit(solution)/shard_map/ppermute | solution.py:29
  23.1 3.9 collective-permute-start.2
  32.6 13.5 %collective-permute-start.3 = (bf16[128,1024]{1,0:T(8,128)(2,1)S(1)}, bf16[128,1024]{1,0:T(8,128)(2,1)S(1)}, u32[]{:S(2)}, u32[]{:S(2)}) collective-permute-start(bf16[128,1024]{1,0:T(8,128)(2,1)S(1)} %get-tuple-element.346), channel_id=1, source_target_pairs={{0,8},{4,12},{8,0},{12,4},{16,24},{20,28},{24,16},{28,20},{1,9},{5... | collective-permute-start | bytes 786440 | tf_op jit(solution)/shard_map/ppermute | solution.py:29
  34.7 11.7 %collective-permute-start.4 = (bf16[128,1024]{1,0:T(8,128)(2,1)S(1)}, bf16[128,1024]{1,0:T(8,128)(2,1)S(1)}, u32[]{:S(2)}, u32[]{:S(2)}) collective-permute-start(bf16[128,1024]{1,0:T(8,128)(2,1)S(1)} %get-tuple-element.345), channel_id=1, source_target_pairs={{0,16},{4,20},{8,24},{12,28},{16,0},{20,4},{24,8},{28,12},{1,17},{... | collective-permute-start | bytes 786440 | tf_op jit(solution)/shard_map/ppermute | solution.py:29
  36.2 10.2 %collective-permute-start.5 = (bf16[128,1024]{1,0:T(8,128)(2,1)S(1)}, bf16[128,1024]{1,0:T(8,128)(2,1)S(1)}, u32[]{:S(2)}, u32[]{:S(2)}) collective-permute-start(bf16[128,1024]{1,0:T(8,128)(2,1)S(1)} %get-tuple-element.344), channel_id=1, source_target_pairs={{0,24},{4,28},{8,16},{12,20},{16,8},{20,12},{24,0},{28,4},{1,25},{... | collective-permute-start | bytes 786440 | tf_op jit(solution)/shard_map/ppermute | solution.py:29
  57.5 6.0 %collective-permute-start.6 = (bf16[512,2048]{1,0:T(8,128)(2,1)}, bf16[512,2048]{1,0:T(8,128)(2,1)}, u32[]{:S(2)}, u32[]{:S(2)}) collective-permute-start(bf16[512,2048]{1,0:T(8,128)(2,1)} %get-tuple-element.134.refs_0_.refs_2_), channel_id=1, source_target_pairs={{0,4},{4,0},{8,12},{12,8},{16,20},{20,16},{24,28},{28,24},{1,5},{5... | collective-permute-start | bytes 6291464 | tf_op jit(solution)/shard_map/ppermute | solution.py:29
  60.0 24.0 %collective-permute-start.7 = (bf16[2,128,1024]{2,1,0:T(8,128)(2,1)}, bf16[2,128,1024]{2,1,0:T(8,128)(2,1)S(1)}, u32[]{:S(2)}, u32[]{:S(2)}) collective-permute-start(bf16[2,128,1024]{2,1,0:T(8,128)(2,1)} %get-tuple-element.137), channel_id=1, source_target_pairs={{0,8},{4,12},{8,0},{12,4},{16,24},{20,28},{24,16},{28,20},{1,9},{5... | collective-permute-start | bytes 1572872 | tf_op jit(solution)/shard_map/ppermute | solution.py:29
  61.6 25.5 %collective-permute-start.8 = (bf16[2,128,1024]{2,1,0:T(8,128)(2,1)}, bf16[2,128,1024]{2,1,0:T(8,128)(2,1)S(1)}, u32[]{:S(2)}, u32[]{:S(2)}) collective-permute-start(bf16[2,128,1024]{2,1,0:T(8,128)(2,1)} %get-tuple-element.138), channel_id=1, source_target_pairs={{0,16},{4,20},{8,24},{12,28},{16,0},{20,4},{24,8},{28,12},{1,17},{... | collective-permute-start | bytes 1572872 | tf_op jit(solution)/shard_map/ppermute | solution.py:29
  63.1 24.0 %collective-permute-start.9 = (bf16[2,128,1024]{2,1,0:T(8,128)(2,1)}, bf16[2,128,1024]{2,1,0:T(8,128)(2,1)S(1)}, u32[]{:S(2)}, u32[]{:S(2)}) collective-permute-start(bf16[2,128,1024]{2,1,0:T(8,128)(2,1)} %get-tuple-element.139), channel_id=1, source_target_pairs={{0,24},{4,28},{8,16},{12,20},{16,8},{20,12},{24,0},{28,4},{1,25},{... | collective-permute-start | bytes 1572872 | tf_op jit(solution)/shard_map/ppermute | solution.py:29
  92.2 25.3 %collective-permute-start.10 = (bf16[2,128,1024]{2,1,0:T(8,128)(2,1)S(1)}, bf16[2,128,1024]{2,1,0:T(8,128)(2,1)S(1)}, u32[]{:S(2)}, u32[]{:S(2)}) collective-permute-start(bf16[2,128,1024]{2,1,0:T(8,128)(2,1)S(1)} %copy-done.44), channel_id=1, source_target_pairs={{0,8},{4,12},{8,0},{12,4},{16,24},{20,28},{24,16},{28,20},{1,9},{5... | collective-permute-start | bytes 1572872 | tf_op jit(solution)/shard_map/ppermute | solution.py:29
  93.5 24.5 %collective-permute-start.11 = (bf16[2,128,1024]{2,1,0:T(8,128)(2,1)S(1)}, bf16[2,128,1024]{2,1,0:T(8,128)(2,1)S(1)}, u32[]{:S(2)}, u32[]{:S(2)}) collective-permute-start(bf16[2,128,1024]{2,1,0:T(8,128)(2,1)S(1)} %copy-done.43), channel_id=1, source_target_pairs={{0,16},{4,20},{8,24},{12,28},{16,0},{20,4},{24,8},{28,12},{1,17},{... | collective-permute-start | bytes 1572872 | tf_op jit(solution)/shard_map/ppermute | solution.py:29
  94.3 24.5 %collective-permute-start.12 = (bf16[2,128,1024]{2,1,0:T(8,128)(2,1)S(1)}, bf16[2,128,1024]{2,1,0:T(8,128)(2,1)S(1)}, u32[]{:S(2)}, u32[]{:S(2)}) collective-permute-start(bf16[2,128,1024]{2,1,0:T(8,128)(2,1)S(1)} %copy-done.42), channel_id=1, source_target_pairs={{0,24},{4,28},{8,16},{12,20},{16,8},{20,12},{24,0},{28,4},{1,25},{... | collective-permute-start | bytes 1572872 | tf_op jit(solution)/shard_map/ppermute | solution.py:29
  119.6 22.6 %collective-permute-start.13 = (bf16[1024,1024]{1,0:T(8,128)(2,1)}, bf16[1024,1024]{1,0:T(8,128)(2,1)}, u32[]{:S(2)}, u32[]{:S(2)}) collective-permute-start(bf16[1024,1024]{1,0:T(8,128)(2,1)} %get-tuple-element.170), channel_id=1, source_target_pairs={{0,4},{4,0},{8,12},{12,8},{16,20},{20,16},{24,28},{28,24},{1,5},{5... | collective-permute-start | bytes 6291464 | tf_op jit(solution)/shard_map/ppermute | solution.py:29
  119.6 22.6 %collective-permute-start.14 = (bf16[512,2048]{1,0:T(8,128)(2,1)}, bf16[512,2048]{1,0:T(8,128)(2,1)}, u32[]{:S(2)}, u32[]{:S(2)}) collective-permute-start(bf16[512,2048]{1,0:T(8,128)(2,1)} %get-tuple-element.171), channel_id=1, source_target_pairs={{0,4},{4,0},{8,12},{12,8},{16,20},{20,16},{24,28},{28,24},{1,5},{5... | collective-permute-start | bytes 6291464 | tf_op jit(solution)/shard_map/ppermute | solution.py:29
  142.2 39.0 %collective-permute-start.17 = (bf16[1024,1024]{1,0:T(8,128)(2,1)}, bf16[1024,1024]{1,0:T(8,128)(2,1)S(1)}, u32[]{:S(2)}, u32[]{:S(2)}) collective-permute-start(bf16[1024,1024]{1,0:T(8,128)(2,1)} %get-tuple-element.187), channel_id=1, source_target_pairs={{0,4},{4,0},{8,12},{12,8},{16,20},{20,16},{24,28},{28,24},{1,5},{5... | collective-permute-start | bytes 6291464 | tf_op jit(solution)/shard_map/ppermute | solution.py:29
  142.3 38.9 %collective-permute-start.18 = (bf16[512,2048]{1,0:T(8,128)(2,1)}, bf16[512,2048]{1,0:T(8,128)(2,1)S(1)}, u32[]{:S(2)}, u32[]{:S(2)}) collective-permute-start(bf16[512,2048]{1,0:T(8,128)(2,1)} %get-tuple-element.188), channel_id=1, source_target_pairs={{0,4},{4,0},{8,12},{12,8},{16,20},{20,16},{24,28},{28,24},{1,5},{5... | collective-permute-start | bytes 6291464 | tf_op jit(solution)/shard_map/ppermute | solution.py:29
  148.0 33.1 %collective-permute-start.15 = (bf16[512,1024]{1,0:T(8,128)(2,1)}, bf16[512,1024]{1,0:T(8,128)(2,1)}, u32[]{:S(2)}, u32[]{:S(2)}) collective-permute-start(bf16[512,1024]{1,0:T(8,128)(2,1)} %fusion.25), channel_id=1, source_target_pairs={{0,8},{4,12},{8,0},{12,4},{16,24},{20,28},{24,16},{28,20},{1,9},{5... | collective-permute-start | bytes 3145736 | tf_op jit(solution)/shard_map/ppermute | solution.py:29
  148.8 32.3 %collective-permute-start.16 = (bf16[256,2048]{1,0:T(8,128)(2,1)}, bf16[256,2048]{1,0:T(8,128)(2,1)}, u32[]{:S(2)}, u32[]{:S(2)}) collective-permute-start(bf16[256,2048]{1,0:T(8,128)(2,1)} %bitcast.56), channel_id=1, source_target_pairs={{0,16},{4,20},{8,24},{12,28},{16,0},{20,4},{24,8},{28,12},{1,17},{... | collective-permute-start | bytes 3145736 | tf_op jit(solution)/shard_map/ppermute | solution.py:29
  181.2 6.6 %collective-permute-start.19 = (bf16[2,512,1024]{2,1,0:T(8,128)(2,1)}, bf16[2,512,1024]{2,1,0:T(8,128)(2,1)S(1)}, u32[]{:S(2)}, u32[]{:S(2)}) collective-permute-start(bf16[2,512,1024]{2,1,0:T(8,128)(2,1)} %get-tuple-element.198), channel_id=1, source_target_pairs={{0,4},{4,0},{8,12},{12,8},{16,20},{20,16},{24,28},{28,24},{1,5},{5... | collective-permute-start | bytes 6291464 | tf_op jit(solution)/shard_map/ppermute | solution.py:29
  184.6 25.3 %collective-permute-start.20 = (bf16[512,1024]{1,0:T(8,128)(2,1)}, bf16[512,1024]{1,0:T(8,128)(2,1)}, u32[]{:S(2)}, u32[]{:S(2)}) collective-permute-start(bf16[512,1024]{1,0:T(8,128)(2,1)} %fusion.26), channel_id=1, source_target_pairs={{0,8},{4,12},{8,0},{12,4},{16,24},{20,28},{24,16},{28,20},{1,9},{5... | collective-permute-start | bytes 3145736 | tf_op jit(solution)/shard_map/ppermute | solution.py:29
  185.7 24.4 %collective-permute-start.21 = (bf16[256,2048]{1,0:T(8,128)(2,1)S(1)}, bf16[256,2048]{1,0:T(8,128)(2,1)}, u32[]{:S(2)}, u32[]{:S(2)}) collective-permute-start(bf16[256,2048]{1,0:T(8,128)(2,1)S(1)} %bitcast.450), channel_id=1, source_target_pairs={{0,16},{4,20},{8,24},{12,28},{16,0},{20,4},{24,8},{28,12},{1,17},{... | collective-permute-start | bytes 3145736 | tf_op jit(solution)/shard_map/ppermute | solution.py:29
  210.1 35.5 %collective-permute-start.22 = (bf16[512,4096]{1,0:T(8,128)(2,1)}, bf16[512,4096]{1,0:T(8,128)(2,1)}, u32[]{:S(2)}, u32[]{:S(2)}) collective-permute-start(bf16[512,4096]{1,0:T(8,128)(2,1)} %get-tuple-element.219), channel_id=1, source_target_pairs={{0,4},{4,0},{8,12},{12,8},{16,20},{20,16},{24,28},{28,24},{1,5},{5... | collective-permute-start | bytes 12582920 | tf_op jit(solution)/shard_map/ppermute | solution.py:29
  219.0 26.6 %collective-permute-start.23 = (bf16[512,1024]{1,0:T(8,128)(2,1)S(1)}, bf16[512,1024]{1,0:T(8,128)(2,1)S(1)}, u32[]{:S(2)}, u32[]{:S(2)}) collective-permute-start(bf16[512,1024]{1,0:T(8,128)(2,1)S(1)} %get-tuple-element.220), channel_id=1, source_target_pairs={{0,16},{4,20},{8,24},{12,28},{16,0},{20,4},{24,8},{28,12},{1,17},{... | collective-permute-start | bytes 3145736 | tf_op jit(solution)/shard_map/ppermute | solution.py:29
  220.0 15.0 %collective-permute-start.24 = (bf16[128,2048]{1,0:T(8,128)(2,1)}, bf16[128,2048]{1,0:T(8,128)(2,1)S(1)}, u32[]{:S(2)}, u32[]{:S(2)}) collective-permute-start(bf16[128,2048]{1,0:T(8,128)(2,1)} %fusion.38), channel_id=1, source_target_pairs={{0,8},{4,12},{8,0},{12,4},{16,24},{20,28},{24,16},{28,20},{1,9},{5... | collective-permute-start | bytes 1572872 | tf_op jit(solution)/shard_map/ppermute | solution.py:29
  220.8 24.8 %collective-permute-start.25 = (bf16[128,2048]{1,0:T(8,128)(2,1)}, bf16[128,2048]{1,0:T(8,128)(2,1)}, u32[]{:S(2)}, u32[]{:S(2)}) collective-permute-start(bf16[128,2048]{1,0:T(8,128)(2,1)} %fusion.37), channel_id=1, source_target_pairs={{0,8},{4,12},{8,0},{12,4},{16,24},{20,28},{24,16},{28,20},{1,9},{5... | collective-permute-start | bytes 1572872 | tf_op jit(solution)/shard_map/ppermute | solution.py:29
  250.8 24.8 %collective-permute-start.26 = (bf16[256,2048]{1,0:T(8,128)(2,1)}, bf16[256,2048]{1,0:T(8,128)(2,1)}, u32[]{:S(2)}, u32[]{:S(2)}) collective-permute-start(bf16[256,2048]{1,0:T(8,128)(2,1)} %bitcast.74), channel_id=1, source_target_pairs={{0,8},{4,12},{8,0},{12,4},{16,24},{20,28},{24,16},{28,20},{1,9},{5... | collective-permute-start | bytes 3145736 | tf_op jit(solution)/shard_map/ppermute | solution.py:29
  251.6 24.5 %collective-permute-start.27 = (bf16[256,2048]{1,0:T(8,128)(2,1)}, bf16[256,2048]{1,0:T(8,128)(2,1)}, u32[]{:S(2)}, u32[]{:S(2)}) collective-permute-start(bf16[256,2048]{1,0:T(8,128)(2,1)} %bitcast.75), channel_id=1, source_target_pairs={{0,16},{4,20},{8,24},{12,28},{16,0},{20,4},{24,8},{28,12},{1,17},{... | collective-permute-start | bytes 3145736 | tf_op jit(solution)/shard_map/ppermute | solution.py:29
  252.8 23.3 %collective-permute-start.28 = (bf16[1024,1024]{1,0:T(8,128)(2,1)}, bf16[1024,1024]{1,0:T(8,128)(2,1)}, u32[]{:S(2)}, u32[]{:S(2)}) collective-permute-start(bf16[1024,1024]{1,0:T(8,128)(2,1)} %get-tuple-element.224), channel_id=1, source_target_pairs={{0,4},{4,0},{8,12},{12,8},{16,20},{20,16},{24,28},{28,24},{1,5},{5... | collective-permute-start | bytes 6291464 | tf_op jit(solution)/shard_map/ppermute | solution.py:29
  252.8 23.3 %collective-permute-start.29 = (bf16[4,128,1024]{2,1,0:T(8,128)(2,1)}, bf16[4,128,1024]{2,1,0:T(8,128)(2,1)}, u32[]{:S(2)}, u32[]{:S(2)}) collective-permute-start(bf16[4,128,1024]{2,1,0:T(8,128)(2,1)} %get-tuple-element.225), channel_id=1, source_target_pairs={{0,4},{4,0},{8,12},{12,8},{16,20},{20,16},{24,28},{28,24},{1,5},{5... | collective-permute-start | bytes 3145736 | tf_op jit(solution)/shard_map/ppermute | solution.py:29
  259.2 129.7 %reduce-scatter.3.cloned.1.call-start = ((), (), s32[]{:S(2)}) async-start(), calls=%async_computation.2 | async-start | bytes 1310720 | tf_op jit(solution)/shard_map/reduce_scatter | solution.py:131
  280.8 32.4 %collective-permute-start.32 = (bf16[768,512]{1,0:T(8,128)(2,1)}, bf16[768,512]{1,0:T(8,128)(2,1)}, u32[]{:S(2)}, u32[]{:S(2)}) collective-permute-start(bf16[768,512]{1,0:T(8,128)(2,1)} %pad_maximum_fusion.9), channel_id=1, source_target_pairs={{0,8},{4,12},{8,0},{12,4},{16,24},{20,28},{24,16},{28,20},{1,9},{5... | collective-permute-start | bytes 2359304 | tf_op jit(solution)/shard_map/ppermute | solution.py:29
  284.3 28.9 %collective-permute-start.33 = (bf16[768,512]{1,0:T(8,128)(2,1)}, bf16[768,512]{1,0:T(8,128)(2,1)}, u32[]{:S(2)}, u32[]{:S(2)}) collective-permute-start(bf16[768,512]{1,0:T(8,128)(2,1)} %pad_maximum_fusion.10), channel_id=1, source_target_pairs={{0,16},{4,20},{8,24},{12,28},{16,0},{20,4},{24,8},{28,12},{1,17},{... | collective-permute-start | bytes 2359304 | tf_op jit(solution)/shard_map/ppermute | solution.py:29
  288.8 24.4 %collective-permute-start.30 = (bf16[128,2048]{1,0:T(8,128)(2,1)}, bf16[128,2048]{1,0:T(8,128)(2,1)}, u32[]{:S(2)}, u32[]{:S(2)}) collective-permute-start(bf16[128,2048]{1,0:T(8,128)(2,1)} %get-tuple-element.305), channel_id=1, source_target_pairs={{0,16},{4,20},{8,24},{12,28},{16,0},{20,4},{24,8},{28,12},{1,17},{... | collective-permute-start | bytes 1572872 | tf_op jit(solution)/shard_map/ppermute | solution.py:29
  289.7 23.5 %collective-permute-start.31 = (bf16[128,2048]{1,0:T(8,128)(2,1)}, bf16[128,2048]{1,0:T(8,128)(2,1)}, u32[]{:S(2)}, u32[]{:S(2)}) collective-permute-start(bf16[128,2048]{1,0:T(8,128)(2,1)} %get-tuple-element.304), channel_id=1, source_target_pairs={{0,8},{4,12},{8,0},{12,4},{16,24},{20,28},{24,16},{28,20},{1,9},{5... | collective-permute-start | bytes 1572872 | tf_op jit(solution)/shard_map/ppermute | solution.py:29
  320.1 24.1 %collective-permute-start.34 = (bf16[384,512]{1,0:T(8,128)(2,1)}, bf16[384,512]{1,0:T(8,128)(2,1)}, u32[]{:S(2)}, u32[]{:S(2)}) collective-permute-start(bf16[384,512]{1,0:T(8,128)(2,1)} %pad_maximum_fusion.14), channel_id=1, source_target_pairs={{0,16},{4,20},{8,24},{12,28},{16,0},{20,4},{24,8},{28,12},{1,17},{... | collective-permute-start | bytes 1179656 | tf_op jit(solution)/shard_map/ppermute | solution.py:29
  326.0 10.5 %collective-permute-start.38 = (bf16[128,1024]{1,0:T(8,128)(2,1)}, bf16[128,1024]{1,0:T(8,128)(2,1)}, u32[]{:S(2)}, u32[]{:S(2)}) collective-permute-start(bf16[128,1024]{1,0:T(8,128)(2,1)} %get-tuple-element.341), channel_id=1, source_target_pairs={{0,24},{4,28},{8,16},{12,20},{16,8},{20,12},{24,0},{28,4},{1,25},{... | collective-permute-start | bytes 786440 | tf_op jit(solution)/shard_map/ppermute | solution.py:29
  327.1 12.5 %collective-permute-start.37 = (bf16[128,1024]{1,0:T(8,128)(2,1)}, bf16[128,1024]{1,0:T(8,128)(2,1)}, u32[]{:S(2)}, u32[]{:S(2)}) collective-permute-start(bf16[128,1024]{1,0:T(8,128)(2,1)} %get-tuple-element.342), channel_id=1, source_target_pairs={{0,16},{4,20},{8,24},{12,28},{16,0},{20,4},{24,8},{28,12},{1,17},{... | collective-permute-start | bytes 786440 | tf_op jit(solution)/shard_map/ppermute | solution.py:29
  328.4 13.2 %collective-permute-start.36 = (bf16[128,1024]{1,0:T(8,128)(2,1)}, bf16[128,1024]{1,0:T(8,128)(2,1)}, u32[]{:S(2)}, u32[]{:S(2)}) collective-permute-start(bf16[128,1024]{1,0:T(8,128)(2,1)} %get-tuple-element.343), channel_id=1, source_target_pairs={{0,8},{4,12},{8,0},{12,4},{16,24},{20,28},{24,16},{28,20},{1,9},{5... | collective-permute-start | bytes 786440 | tf_op jit(solution)/shard_map/ppermute | solution.py:29
  332.6 13.2 %collective-permute-start.35 = (bf16[384,512]{1,0:T(8,128)(2,1)}, bf16[384,512]{1,0:T(8,128)(2,1)}, u32[]{:S(2)}, u32[]{:S(2)}) collective-permute-start(bf16[384,512]{1,0:T(8,128)(2,1)} %pad_maximum_fusion.15), channel_id=1, source_target_pairs={{0,8},{4,12},{8,0},{12,4},{16,24},{20,28},{24,16},{28,20},{1,9},{5... | collective-permute-start | bytes 1179656 | tf_op jit(solution)/shard_map/ppermute | solution.py:29
  349.8 19.7 %collective-permute-start.41 = (bf16[128,1024]{1,0:T(8,128)(2,1)S(1)}, bf16[128,1024]{1,0:T(8,128)(2,1)S(1)}, u32[]{:S(2)}, u32[]{:S(2)}) collective-permute-start(bf16[128,1024]{1,0:T(8,128)(2,1)S(1)} %get-tuple-element.333), channel_id=1, source_target_pairs={{0,24},{4,28},{8,16},{12,20},{16,8},{20,12},{24,0},{28,4},{1,25},{... | collective-permute-start | bytes 786440 | tf_op jit(solution)/shard_map/ppermute | solution.py:29
  351.2 18.3 %collective-permute-start.40 = (bf16[128,1024]{1,0:T(8,128)(2,1)S(1)}, bf16[128,1024]{1,0:T(8,128)(2,1)S(1)}, u32[]{:S(2)}, u32[]{:S(2)}) collective-permute-start(bf16[128,1024]{1,0:T(8,128)(2,1)S(1)} %get-tuple-element.334), channel_id=1, source_target_pairs={{0,16},{4,20},{8,24},{12,28},{16,0},{20,4},{24,8},{28,12},{1,17},{... | collective-permute-start | bytes 786440 | tf_op jit(solution)/shard_map/ppermute | solution.py:29
  351.9 17.6 %collective-permute-start.39 = (bf16[128,1024]{1,0:T(8,128)(2,1)S(1)}, bf16[128,1024]{1,0:T(8,128)(2,1)S(1)}, u32[]{:S(2)}, u32[]{:S(2)}) collective-permute-start(bf16[128,1024]{1,0:T(8,128)(2,1)S(1)} %get-tuple-element.335), channel_id=1, source_target_pairs={{0,8},{4,12},{8,0},{12,4},{16,24},{20,28},{24,16},{28,20},{1,9},{5... | collective-permute-start | bytes 786440 | tf_op jit(solution)/shard_map/ppermute | solution.py:29
  353.5 10.3 %collective-permute-start.42 = (bf16[192,512]{1,0:T(8,128)(2,1)S(1)}, bf16[192,512]{1,0:T(8,128)(2,1)S(1)}, u32[]{:S(2)}, u32[]{:S(2)}) collective-permute-start(bf16[192,512]{1,0:T(8,128)(2,1)S(1)} %pad_maximum_fusion.17), channel_id=1, source_target_pairs={{0,1},{1,0},{2,3},{3,2},{4,5},{5,4},{6,7},{7,6},{8,9},{9,8},{10,11... | collective-permute-start | bytes 589832 | tf_op jit(solution)/shard_map/ppermute | solution.py:29
  355.3 14.2 %collective-permute-start.44 = (bf16[192,512]{1,0:T(8,128)(2,1)S(1)}, bf16[192,512]{1,0:T(8,128)(2,1)S(1)}, u32[]{:S(2)}, u32[]{:S(2)}) collective-permute-start(bf16[192,512]{1,0:T(8,128)(2,1)S(1)} %pad_maximum_fusion.18), channel_id=1, source_target_pairs={{0,1},{1,0},{2,3},{3,2},{4,5},{5,4},{6,7},{7,6},{8,9},{9,8},{10,11... | collective-permute-start | bytes 589832 | tf_op jit(solution)/shard_map/ppermute | solution.py:29
  365.6 8.7 %collective-permute-start.43 = (bf16[96,512]{1,0:T(8,128)(2,1)S(1)}, bf16[96,512]{1,0:T(8,128)(2,1)S(1)}, u32[]{:S(2)}, u32[]{:S(2)}) collective-permute-start(bf16[96,512]{1,0:T(8,128)(2,1)S(1)} %pad_maximum_fusion.21), channel_id=1, source_target_pairs={{0,2},{1,3},{2,0},{3,1},{4,6},{5,7},{6,4},{7,5},{8,10},{9,11},{10,... | collective-permute-start | bytes 294920 | tf_op jit(solution)/shard_map/ppermute | solution.py:29
  376.2 6.0 %collective-permute-start.45 = (bf16[96,512]{1,0:T(8,128)(2,1)S(1)}, bf16[96,512]{1,0:T(8,128)(2,1)S(1)}, u32[]{:S(2)}, u32[]{:S(2)}) collective-permute-start(bf16[96,512]{1,0:T(8,128)(2,1)S(1)} %pad_maximum_fusion.22), channel_id=1, source_target_pairs={{0,2},{1,3},{2,0},{3,1},{4,6},{5,7},{6,4},{7,5},{8,10},{9,11},{10,... | collective-permute-start | bytes 294920 | tf_op jit(solution)/shard_map/ppermute | solution.py:29
  (54 other events, 264.4 us)
Sparse Core Ops, SparseCore 0:
  259.3 44.1 reduce-scatter.4
  333.7 32.5 reduce-scatter.2

commit v4 on v3

v4 whole, which is shorter than its diff:
```python
import functools
import math

import jax
import jax.numpy as jnp
from jax import lax
from jax.experimental import pallas as pl
from jax.experimental.pallas import tpu as pltpu
from jax.sharding import PartitionSpec as P

HD = 64
PAIR = 2 * HD
eps_norm = 1e-06
neg_fill = -1e30
BF = jnp.bfloat16
F32 = jnp.float32
DIMS_FIRST = (((0,), (0,)), ((), ()))
DIMS_LAST = (((1,), (1,)), ((), ()))
LOG2E = 1.4426950408889634


def dot(left, right, dims=(((1,), (0,)), ((), ()))):
    return lax.dot_general(left, right, dims, preferred_element_type=F32)


def swap(values, axis_name, bits):
    size = lax.axis_size(axis_name)
    return lax.ppermute(values, axis_name, [(i, i ^ bits) for i in range(size)])


def pick(values, index, axis):
    return lax.dynamic_index_in_dim(values, index, axis, keepdims=False)


def together(*values):
    return lax.optimization_barrier(values)


def cut_parts(values, mine):
    return [pick(values, mine ^ step, 0) for step in range(values.shape[0])]


def cut_pairs(left, right, mine):
    pairs = zip(cut_parts(left, mine), cut_parts(right, mine), strict=True)
    return [jnp.stack(pair) for pair in pairs]


def send_parts(parts, span):
    return parts[:1] + [
        swap(part, "head", step * span) for step, part in enumerate(parts) if step > 0
    ]


def by_micro(parts, mine):
    parts = jnp.stack(parts)
    return jnp.stack([pick(parts, mine ^ micro, 0) for micro in range(parts.shape[0])])


def add_low(terms):
    return functools.reduce(jnp.add, [term.astype(F32) for term in terms]).astype(BF)


class Rows:
    def __init__(self, arrays, bits, before=1, cols=None):
        self.order = sorted(bits, reverse=True)
        self.before, self.arrays = before, []
        self.start, self.size = cols or (0, arrays[0].shape[-1])
        self.chunk = arrays[0].size // arrays[0].shape[-1] // before // 2 ** len(bits)
        for array in arrays:
            self.join(array, self.start)

    def join(self, array, start=0):
        shape = [self.before] + [2] * len(self.order) + [self.chunk, array.shape[-1]]
        self.arrays.append((array.reshape(shape), tuple(self.order), {}, start))

    def read(self, bit=None, index=None):
        terms = []
        for array, bits, picks, start in self.arrays:
            picks = picks if bit is None else {**picks, bit: index}
            starts = [0] + [picks.get(b, 0) for b in bits] + [0, start]
            sizes = [self.before] + [1 if b in picks else 2 for b in bits] + [self.chunk, self.size]
            terms.append(lax.dynamic_slice(array, starts, sizes).reshape(-1, self.size))
        return add_low(terms)

    def away(self, bit):
        here = (place_of() >> bit) % 2
        sent = self.read(bit, 1 - here)
        self.order.remove(bit)
        for _, _, picks, _ in self.arrays:
            picks[bit] = here
        return sent


def place_of():
    return lax.axis_index("head") * lax.axis_size("seq") + lax.axis_index("seq")


def cross(rows, bit):
    seq_bits = lax.axis_size("seq").bit_length() - 1
    if bit < seq_bits:
        return swap(rows, "seq", 2**bit)
    return swap(rows, "head", 2 ** (bit - seq_bits))


def away_all(parts, bit):
    return jnp.concatenate([part.away(bit) for part in parts])


def join_all(parts, came):
    start = 0
    for part in parts:
        height = part.before * part.chunk * 2 ** len(part.order)
        part.join(came[start : start + height])
        start += height


def step_all(parts, bit):
    join_all(parts, cross(away_all(parts, bit), bit))


def seq_first(rows):
    size = lax.axis_size("seq")
    if seq_blocks(2 * rows.shape[0]) == 1:
        rows = rows.reshape(-1, size, rows.shape[0] * 2 // lax.axis_size("head") // size, rows.shape[1])
        rows = rows.swapaxes(0, 1).reshape(-1, rows.shape[-1])
    return lax.psum_scatter(rows, "seq", scatter_dimension=0, tiled=True)


def last_sum(*rows):
    size = lax.axis_size("seq")
    narrow = min(part.shape[1] for part in rows)
    blocks, counts = [], []
    for part in rows:
        part = part.reshape(size, -1, part.shape[1])
        counts.append((part.shape[1], part.shape[2] // narrow))
        blocks += [part[:, :, i * narrow : (i + 1) * narrow] for i in range(counts[-1][1])]
    joint = jnp.concatenate(blocks, axis=1) if len(blocks) > 1 else blocks[0]
    joint = joint.reshape(-1, narrow)
    total = lax.psum_scatter(joint, "seq", scatter_dimension=0, tiled=True)
    results, start = [], 0
    for height, count in counts:
        parts = [total[start + i * height : start + (i + 1) * height] for i in range(count)]
        results.append(jnp.concatenate(parts, axis=1) if count > 1 else parts[0])
        start += height * count
    return results


def norm_stats(hidden):
    centred = hidden - jnp.mean(hidden, axis=-1, keepdims=True)
    rate = lax.rsqrt(jnp.mean(centred * centred, axis=-1, keepdims=True) + eps_norm)
    return centred * rate, rate


def norm_back(grad, normal, rate, scale_term):
    inner = grad * (1.0 + scale_term)
    return rate * (
        inner
        - jnp.mean(inner, axis=-1, keepdims=True)
        - normal * jnp.mean(inner * normal, axis=-1, keepdims=True)
    )


def time_features(times, feature_count):
    half = feature_count // 2
    steps = jnp.exp(jnp.arange(half, dtype=F32) * (-math.log(10000.0) / (half - 1)))
    angles = 1000.0 * times[:, None] * steps
    return jnp.concatenate([jnp.sin(angles), jnp.cos(angles)], axis=-1).astype(BF)


def params(mebibytes):
    return pltpu.CompilerParams(vmem_limit_bytes=mebibytes * 1024 * 1024)


def once(shape, index_map=None):
    fixed = index_map or (lambda i: (0,) * len(shape))
    return pl.BlockSpec(shape, fixed, pipeline_mode=pl.Buffered(1))


def in_hbm(value):
    return pltpu.with_memory_space_constraint(value, pltpu.HBM)


def cost(flops, moved, hard=0):
    return pl.CostEstimate(flops=int(flops), bytes_accessed=int(moved), transcendentals=int(hard))


def turn(values):
    lanes = lax.broadcasted_iota(jnp.int32, values.shape, 1)
    low = lax.rem(lanes, HD) < HD // 2
    return jnp.where(low, pltpu.roll(values, PAIR - HD // 2, 1), pltpu.roll(values, HD // 2, 1))


def project_kernel(tiles, x_ref, w_ref, cos_ref, sin_ref, q_ref, kv_ref):
    raw = dot(x_ref[...], w_ref[...])
    step = pl.program_id(0)

    def rotated(o_ref, factor):
        for first in range(0, raw.shape[1], PAIR):
            part = raw[:, first : first + PAIR]
            turned = part * cos_ref[...] + turn(part) * sin_ref[...]
            o_ref[:, first : first + PAIR] = (turned * factor).astype(BF)

    @pl.when(step < tiles)
    def _():
        rotated(q_ref, HD ** (-0.5) * LOG2E)

    @pl.when((step >= tiles) & (step < 2 * tiles))
    def _():
        rotated(kv_ref, 1.0)

    @pl.when(step >= 2 * tiles)
    def _():
        kv_ref[...] = raw.astype(BF)


def project(normed, w_qkv, cos_table, sin_table):
    frames, width = normed.shape
    tile = 512
    tiles = width // tile
    return pl.pallas_call(
        functools.partial(project_kernel, tiles),
        grid=(3 * tiles,),
        in_specs=[
            once((frames, width)),
            pl.BlockSpec((width, tile), lambda i: (0, i)),
            once((frames, PAIR)),
            once((frames, PAIR)),
        ],
        out_specs=[
            pl.BlockSpec((frames, tile), lambda i: (0, jnp.minimum(i, tiles - 1))),
            pl.BlockSpec((frames, tile), lambda i: (0, jnp.maximum(i - tiles, 0))),
        ],
        out_shape=[
            jax.ShapeDtypeStruct((frames, width), BF),
            jax.ShapeDtypeStruct((frames, 2 * width), BF),
        ],
        compiler_params=params(52),
        cost_estimate=cost(6 * frames * width * width, 6 * width * width + 8 * frames * width),
    )(normed, w_qkv, cos_table, sin_table)


def only_head(values, which):
    lanes = lax.broadcasted_iota(jnp.int32, values.shape, 1)
    mine = (lanes >= which * HD) & (lanes < (which + 1) * HD)
    return jnp.where(mine, values, jnp.zeros_like(values))


def attend_kernel(span, q_ref, *refs):
    k_refs, v_refs = refs[:span], refs[span : 2 * span]
    mk_ref, mq_ref, o_ref, p_ref, l_ref, bias_ref = refs[2 * span :]
    frames = q_ref.shape[0]

    @pl.when(pl.program_id(0) == 0)
    def _():
        seg_q, place_q = mq_ref[0:1, :], mq_ref[1:2, :]
        for index in range(span):
            rows = slice(index * frames, (index + 1) * frames)
            seg_k, place_k, live_k = mk_ref[rows, 0:1], mk_ref[rows, 1:2], mk_ref[rows, 2:3]
            allowed = (seg_q == seg_k) & ((live_k == 1) | (place_q == place_k))
            bias_ref[rows, :] = jnp.where(allowed, 0.0, neg_fill)

    values_t = [v[...].T for v in v_refs]
    ones = jnp.ones((16, frames), BF)
    results, inverses = [], []
    for which in range(2):
        queries = only_head(q_ref[...], which)
        scores = [
            dot(k[...], queries, DIMS_LAST) + bias_ref[i * frames : (i + 1) * frames, :]
            for i, k in enumerate(k_refs)
        ]
        top = functools.reduce(jnp.maximum, [jnp.max(s, axis=0, keepdims=True) for s in scores])
        result = None
        for index, part in enumerate(scores):
            powered = jnp.exp2(part - top).astype(BF)
            p_ref[which, index * frames : (index + 1) * frames, :] = powered
            lanes = values_t[index][which * HD : (which + 1) * HD]
            part = dot(jnp.concatenate([lanes, ones], axis=0), powered)
            result = part if result is None else result + part
        inverse = 1.0 / result[HD : HD + 1]
        results.append(result[:HD] * inverse)
        inverses.append(inverse)
    o_ref[...] = jnp.concatenate(results, axis=0).T.astype(BF)
    l_ref[0] = jnp.concatenate(inverses + [jnp.zeros((6, frames), F32)], axis=0)


def columns(frames, start=0):
    return pl.BlockSpec((frames, PAIR), lambda i: (0, start + i))


def attend(queries, pairs_kv, meta_k, meta_q):
    span = len(pairs_kv)
    frames, width = queries.shape
    pairs = width // PAIR
    keys = span * frames
    return pl.pallas_call(
        functools.partial(attend_kernel, span),
        grid=(pairs,),
        in_specs=[columns(frames)]
        + [columns(frames)] * span
        + [columns(frames, pairs)] * span
        + [
            once((keys, PAIR)),
            once((8, frames)),
        ],
        out_specs=[
            columns(frames),
            pl.BlockSpec((2, keys, frames), lambda i: (i, 0, 0)),
            pl.BlockSpec((1, 8, frames), lambda i: (i, 0, 0)),
        ],
        out_shape=[
            jax.ShapeDtypeStruct((frames, width), BF),
            pltpu.HBM((2 * pairs, keys, frames), BF),
            jax.ShapeDtypeStruct((pairs, 8, frames), F32),
        ],
        scratch_shapes=[pltpu.VMEM((keys, frames), F32)],
        compiler_params=params(52),
        cost_estimate=cost(
            16 * pairs * frames * keys * PAIR,
            4 * pairs * frames * keys,
            2 * pairs * frames * keys,
        ),
    )(queries, *pairs_kv, *pairs_kv, meta_k, meta_q)


def attend_back_kernel(span, q_ref, *refs):
    k_refs, v_refs = refs[:span], refs[span : 2 * span]
    p_ref, c_ref, g_ref, cos_ref, sin_ref = refs[2 * span : 2 * span + 5]
    dq_ref, dkv_refs, ds_ref = refs[2 * span + 5], refs[2 * span + 6 : -1], refs[-1]
    frames = q_ref.shape[0]

    def unturn(grad, index):
        rows = slice(index * frames, (index + 1) * frames)
        return grad * cos_ref[rows, :] - turn(grad) * sin_ref[rows, :]

    keys_t = [k[...].T for k in k_refs]
    dk, dv, dq = [None] * span, [None] * span, []
    for which in range(2):
        centre = c_ref[0, which : which + 1, :]
        grads = only_head(g_ref[...], which)
        queries = only_head(q_ref[...], which)
        result = None
        for index in range(span):
            rows = slice(index * frames, (index + 1) * frames)
            grad_probs = dot(v_refs[index][...], grads, DIMS_LAST)
            soft = p_ref[which, rows, :]
            ds_ref[rows, :] = (soft.astype(F32) * (grad_probs - centre)).astype(BF)
            part = dot(soft, grads)
            dv[index] = part if dv[index] is None else dv[index] + part
            part = dot(ds_ref[rows, :], queries)
            dk[index] = part if dk[index] is None else dk[index] + part
            part = dot(keys_t[index][which * HD : (which + 1) * HD], ds_ref[rows, :])
            result = part if result is None else result + part
        dq.append(result)
    dq = jnp.concatenate(dq, axis=0).T
    dq_ref[...] = unturn(dq * HD ** (-0.5), 0).astype(BF)
    for index in range(span):
        dkv_refs[index][0] = unturn(dk[index] * (1.0 / LOG2E), index).astype(BF)
        dkv_refs[index][1] = dv[index].astype(BF)


def attend_back(queries, pairs_kv, probs, centres, grads, cos_keys, sin_keys):
    span = len(pairs_kv)
    frames, width = queries.shape
    pairs = width // PAIR
    keys = span * frames
    results = pl.pallas_call(
        functools.partial(attend_back_kernel, span),
        grid=(pairs,),
        in_specs=[columns(frames)]
        + [columns(frames)] * span
        + [columns(frames, pairs)] * span
        + [
            pl.BlockSpec((2, keys, frames), lambda i: (i, 0, 0)),
            pl.BlockSpec((1, 8, frames), lambda i: (i, 0, 0)),
            columns(frames),
            once((keys, PAIR)),
            once((keys, PAIR)),
        ],
        out_specs=[columns(frames)]
        + [pl.BlockSpec((2, frames, PAIR), lambda i: (0, 0, i))] * span,
        out_shape=[jax.ShapeDtypeStruct((frames, width), BF)]
        + [jax.ShapeDtypeStruct((2, frames, width), BF)] * span,
        scratch_shapes=[pltpu.VMEM((keys, frames), BF)],
        compiler_params=params(52),
        cost_estimate=cost(32 * pairs * frames * keys * PAIR, 4 * pairs * frames * keys),
    )(queries, *pairs_kv, *pairs_kv, in_hbm(probs), centres, grads, cos_keys, sin_keys)
    return results[0], results[1:]


def seq_blocks(rows):
    size = lax.axis_size("seq")
    return size if rows // lax.axis_size("head") // size % 16 == 0 else 1


def split_rows(source, target, groups, low_bit, blocks=1):
    chunk = source.shape[0] // groups // blocks
    half = source.shape[0] // 2
    for index in range(groups // 2):
        for part, bit in ((0, 1 - low_bit), (1, low_bit)):
            for block in range(blocks):
                first = pl.multiple_of(((2 * index + bit) * blocks + block) * chunk, chunk)
                start = part * half + (block * (groups // 2) + index) * chunk
                target[start : start + chunk, :] = source[pl.ds(first, chunk), :]


def fetches(pairs, sems):
    return [
        pltpu.make_async_copy(source, target, sems.at[index])
        for index, (source, target) in enumerate(pairs)
    ]


def feed_kernel(groups, blocks, x_ref, g_ref, up_ref, down_ref, l_ref, *refs):
    later, refs = refs[:4], refs[4:]
    da_ref, dk_ref, ua_ref, uk_ref = refs[:4]
    out_ref, gl_ref, gs_ref, gc_ref, o_ref, c_ref = refs[4:10]
    acc_ref, gx_ref, t_ref, xt_ref, mid_ref, scale_ref, w_ref, a_ref, sems = refs[10:]
    step = pl.program_id(0)
    low_bit = lax.axis_index("head") % 2
    copies = fetches(zip(later, (mid_ref, scale_ref, w_ref, a_ref), strict=True), sems)

    @pl.when(step == 0)
    def _():
        for copy in copies:
            copy.start()
        t_ref[...] = x_ref[...].T
        split_rows(t_ref, xt_ref, groups, low_bit, blocks)
        acc_ref[...] = jnp.zeros_like(acc_ref)
        gx_ref[...] = jnp.zeros_like(gx_ref)

    @pl.when(step < groups)
    def _():
        up = dot(x_ref[...], up_ref[...])
        grad_hidden = dot(g_ref[...], down_ref[...], DIMS_LAST)
        root = math.sqrt(2.0 / math.pi)
        square = up * up
        bent = jnp.tanh(root * up * (1.0 + 0.044715 * square))
        half = 0.5 + 0.5 * bent
        slope = half + 0.5 * up * (1.0 - bent * bent) * (root * (1.0 + 3 * 0.044715 * square))
        hidden = (up * half).astype(BF)
        grad_up = (grad_hidden * slope).astype(BF)
        acc_ref[...] += dot(hidden, down_ref[...])
        gx_ref[...] += dot(grad_up, up_ref[...], DIMS_LAST)
        rows = dot(hidden, g_ref[...], DIMS_FIRST).astype(BF)

        @pl.when(step % 2 == low_bit)
        def _():
            dk_ref[...] = rows

        @pl.when(step % 2 != low_bit)
        def _():
            da_ref[...] = rows

        depth = x_ref.shape[1] // 2
        ua_ref[...] = dot(xt_ref[:depth, :], grad_up).astype(BF)
        uk_ref[...] = dot(xt_ref[depth:, :], grad_up).astype(BF)

    @pl.when(step == groups)
    def _():
        for copy in copies:
            copy.wait()

    @pl.when(step >= groups)
    def _():
        few = out_ref.shape[0]
        here = pl.ds(pl.multiple_of((step - groups) * few, few), few)
        mid, grad = mid_ref[here, :], gx_ref[here, :]
        out_ref[...] = (mid + acc_ref[here, :]).astype(BF)
        normal, rate = norm_stats(mid)
        grad_mid = g_ref[here, :].astype(F32) + norm_back(grad, normal, rate, scale_ref[here, :])
        grad_low = grad_mid.astype(BF)
        gl_ref[...] = grad_low
        gs_ref[...] = grad.astype(BF)
        gc_ref[...] = (grad * normal).astype(BF)
        heads = dot(w_ref[...], grad_low, DIMS_LAST)
        for pair in range(l_ref.shape[0]):
            lanes = slice(pair * PAIR, (pair + 1) * PAIR)
            scaled, centres = [], []
            results = a_ref[here, lanes].T
            for which in range(2):
                rows = slice(pair * PAIR + which * HD, pair * PAIR + (which + 1) * HD)
                scaled.append(heads[rows] * l_ref[pair, which : which + 1, :])
                product = scaled[-1] * results[which * HD : (which + 1) * HD].astype(F32)
                centres.append(jnp.sum(product, axis=0, keepdims=True))
            o_ref[:, lanes] = jnp.concatenate(scaled, axis=0).astype(BF).T
            c_ref[pair] = jnp.concatenate(centres + [jnp.zeros((6, few), F32)], axis=0)


def feed(normed, cot_resid, w_up, w_down, resid_mid, scale, w_out, attended, inverses):
    groups = lax.axis_size("head")
    frames, width = normed.shape
    pairs = width // PAIR
    tile = w_up.shape[1] // groups
    inner = groups * tile
    few = 128
    whole = once((frames, width))
    last = groups - 1
    rows = pl.BlockSpec((tile, width), lambda i: (jnp.minimum(i, last) // 2, 0))
    cols = pl.BlockSpec((width // 2, tile), lambda i: (0, jnp.minimum(i, last)))
    part = pl.BlockSpec((few, width), lambda i: (jnp.maximum(i - groups, 0), 0))
    heads = pl.BlockSpec((pairs, 8, few), lambda i: (0, 0, jnp.maximum(i - groups, 0)))
    low = jax.ShapeDtypeStruct((frames, width), BF)
    anywhere = pl.BlockSpec(memory_space=pl.ANY)
    return pl.pallas_call(
        functools.partial(feed_kernel, groups, seq_blocks(width)),
        grid=(groups + frames // few,),
        in_specs=[
            whole,
            whole,
            pl.BlockSpec((width, tile), lambda i: (0, jnp.minimum(i, last))),
            pl.BlockSpec((tile, width), lambda i: (jnp.minimum(i, last), 0)),
            heads,
        ]
        + [anywhere] * 4,
        out_specs=[rows, rows, cols, cols] + [part] * 5 + [heads],
        out_shape=[
            jax.ShapeDtypeStruct((inner // 2, width), BF),
            pltpu.HBM((inner // 2, width), BF),
            jax.ShapeDtypeStruct((width // 2, inner), BF),
            pltpu.HBM((width // 2, inner), BF),
        ]
        + [low] * 5
        + [jax.ShapeDtypeStruct((pairs, 8, frames), F32)],
        scratch_shapes=[
            pltpu.VMEM((frames, width), F32),
            pltpu.VMEM((frames, width), F32),
            pltpu.VMEM((width, frames), BF),
            pltpu.VMEM((width, frames), BF),
            pltpu.VMEM((frames, width), F32),
            pltpu.VMEM((frames, width), F32),
            pltpu.VMEM((width, width), BF),
            pltpu.VMEM((frames, width), BF),
            pltpu.SemaphoreType.DMA((4,)),
        ],
        compiler_params=params(52),
        cost_estimate=cost(12 * frames * width * inner, 8 * width * inner, frames * inner),
    )(
        normed,
        cot_resid,
        in_hbm(w_up),
        in_hbm(w_down),
        inverses,
        resid_mid,
        scale,
        w_out,
        attended,
    )


def near_kernel(groups, span, *refs):
    dq_ref, dkv_refs, refs = refs[0], refs[1 : span + 1], refs[span + 1 :]
    w_ref, x_ref, gl_ref = refs[:3]
    attended, second, scale, grad_mid = refs[3:7]
    away_ref, keep_ref, gi_ref, gs_ref, gc_ref = refs[7:12]
    t_ref, xt_ref, acc_ref, a_ref, r_ref, scale_ref, gm_ref, sems = refs[12:]
    step = pl.program_id(0)
    tiles = x_ref.shape[1] // dq_ref.shape[1]
    low_bit = lax.axis_index("head") % 2
    width = x_ref.shape[1]
    half = width // 2
    first, *rest = fetches(
        [
            (attended, a_ref),
            (second.at[:, pl.ds(width, width)], r_ref),
            (scale, scale_ref),
            (grad_mid, gm_ref),
        ],
        sems,
    )

    @pl.when(step == 0)
    def _():
        for copy in (first, *rest):
            copy.start()
        t_ref[...] = x_ref[...].T
        split_rows(t_ref, xt_ref, groups, low_bit)

    @pl.when(step == 3 * tiles)
    def _():
        first.wait()
        t_ref[...] = a_ref[...].T
        split_rows(t_ref, xt_ref, groups, low_bit)

    def one(grads):
        away_ref[...] = dot(xt_ref[:half, :], grads).astype(BF)
        keep_ref[...] = dot(xt_ref[half:, :], grads).astype(BF)

    def projected(grads, start):
        one(grads)
        part = dot(grads, w_ref[...], DIMS_LAST)
        acc_ref[...] = part if start else acc_ref[...] + part

    @pl.when(step == 0)
    def _():
        projected(dq_ref[...], True)

    @pl.when((step > 0) & (step < tiles))
    def _():
        projected(dq_ref[...], False)

    @pl.when((step >= tiles) & (step < 3 * tiles))
    def _():
        grads = functools.reduce(jnp.add, [ref[0].astype(F32) for ref in dkv_refs])
        projected(grads.astype(BF), False)

    @pl.when((step >= 3 * tiles) & (step < 4 * tiles))
    def _():
        one(gl_ref[...])

    @pl.when(step == 4 * tiles)
    def _():
        for copy in rest:
            copy.wait()

    @pl.when(step >= 4 * tiles)
    def _():
        few = gi_ref.shape[0]
        here = pl.ds(pl.multiple_of((step - 4 * tiles) * few, few), few)
        normal, rate = norm_stats(r_ref[here, :].astype(F32))
        grad = acc_ref[here, :]
        grad_in = gm_ref[here, :].astype(F32) + norm_back(grad, normal, rate, scale_ref[here, :])
        gi_ref[...] = grad_in.astype(BF)
        gs_ref[...] = grad.astype(BF)
        gc_ref[...] = (grad * normal).astype(BF)


def near(dq, dkv, w_qkv, normed, attended, grad_low, cot_resid, scale):
    groups = lax.axis_size("head")
    frames, width = dq.shape
    tile = 512
    few = 128
    tiles = width // tile

    def pair(i):
        index = jnp.clip(i - tiles, 0, 2 * tiles - 1)
        return (index // tiles, 0, index % tiles)

    grads = pl.BlockSpec((width // 2, tile), lambda i: (0, jnp.minimum(i, 4 * tiles - 1)))
    part = pl.BlockSpec((few, width), lambda i: (jnp.maximum(i - 4 * tiles, 0), 0))
    out = pltpu.HBM((width // 2, 4 * width), BF)
    low = jax.ShapeDtypeStruct((frames, width), BF)
    return pl.pallas_call(
        functools.partial(near_kernel, groups, len(dkv)),
        grid=(4 * tiles + frames // few,),
        in_specs=[pl.BlockSpec((frames, tile), lambda i: (0, jnp.minimum(i, tiles - 1)))]
        + [pl.BlockSpec((1, frames, tile), pair)] * len(dkv)
        + [
            pl.BlockSpec((width, tile), lambda i: (0, jnp.minimum(i, 3 * tiles - 1))),
            once((frames, width)),
            pl.BlockSpec((frames, tile), lambda i: (0, jnp.clip(i - 3 * tiles, 0, tiles - 1))),
        ]
        + [pl.BlockSpec(memory_space=pl.ANY)] * 4,
        out_specs=[grads, grads, part, part, part],
        out_shape=[out, out, low, low, low],
        scratch_shapes=[
            pltpu.VMEM((width, frames), BF),
            pltpu.VMEM((width, frames), BF),
            pltpu.VMEM((frames, width), F32),
            pltpu.VMEM((frames, width), BF),
            pltpu.VMEM((frames, width), BF),
            pltpu.VMEM((frames, width), F32),
            pltpu.VMEM((frames, width), BF),
            pltpu.SemaphoreType.DMA((4,)),
        ],
        compiler_params=params(52),
        cost_estimate=cost(14 * frames * width * width, 14 * width * width + 30 * frames * width),
    )(dq, *dkv, w_qkv, normed, grad_low, attended, cot_resid, scale, grad_low)


def far_kernel(groups, count, *refs):
    pieces, refs = refs[:count], refs[count:]
    f_ref, gi_ref, m_refs = refs[0], refs[1], refs[2:6]
    away_ref, keep_ref, t_ref, st_ref, u_ref, ft_ref = refs[6:]
    low_bit = lax.axis_index("head") % 2
    rows, width = pieces[0].shape[1], pieces[0].shape[2]

    @pl.when(pl.program_id(0) == 0)
    def _():
        for index, piece in enumerate(pieces):
            here = slice(index * rows, (index + 1) * rows)
            t_ref[:width, here] = piece[0].T
            t_ref[width:, here] = piece[1].T
        split_rows(t_ref, st_ref, groups, low_bit)
        u_ref[...] = f_ref[...].T
        split_rows(u_ref, ft_ref, groups, low_bit)

    many, few = 2 * width // groups, u_ref.shape[0] // groups
    for part, out_ref in enumerate((away_ref, keep_ref)):
        big = dot(st_ref[part * width : (part + 1) * width, :], gi_ref[...]).astype(BF)
        half = u_ref.shape[0] // 2
        here = ft_ref[part * half : (part + 1) * half, :]
        small = [dot(here, m_ref[...]).astype(BF) for m_ref in m_refs]
        for index in range(groups // 2):
            start = index * (many + 4 * few)
            out_ref[start : start + many, :] = big[index * many : (index + 1) * many]
            for block in range(4):
                first = start + many + block * few
                out_ref[first : first + few, :] = small[block][index * few : (index + 1) * few]


def far(pieces, features, grad_in, grad_mods):
    groups = lax.axis_size("head")
    frames, width = grad_in.shape
    few = features.shape[1]
    tile = 512
    cols = pl.BlockSpec((frames, tile), lambda i: (0, i))
    out = pl.BlockSpec((width + 2 * few, tile), lambda i: (0, i))
    return pl.pallas_call(
        functools.partial(far_kernel, groups, len(pieces)),
        grid=(width // tile,),
        in_specs=[once(piece.shape) for piece in pieces] + [once((frames, few))] + [cols] * 5,
        out_specs=[out, out],
        out_shape=[pltpu.HBM((width + 2 * few, width), BF)] * 2,
        scratch_shapes=[pltpu.VMEM((2 * width, frames), BF)] * 2
        + [pltpu.VMEM((few, frames), BF)] * 2,
        compiler_params=params(52),
        cost_estimate=cost(6 * frames * width * width, 6 * width * width + 20 * frames * width),
    )(*pieces, features, grad_in, *grad_mods)


def per_device(
    inputs,
    skips,
    flow_time,
    segment_ids,
    frame_mask,
    cotangent,
    w_skip,
    w_time,
    w_qkv,
    w_out,
    w_up,
    w_down,
):
    groups = lax.axis_size("head")
    micro_count, _, rows, width = inputs.shape
    span = groups // micro_count
    place = lax.axis_index("head")
    mine = place // span
    frames = micro_count * rows
    feature_count = w_time.shape[0]
    inputs, skips, cotangent = inputs[:, 0], skips[:, 0], cotangent[:, 0]

    resid_own = dot(inputs.reshape(frames, width), w_skip[:width]) + dot(
        skips.reshape(frames, width), w_skip[width:]
    )
    own_mod = dot(time_features(flow_time.reshape(-1), feature_count), w_time[:, : 2 * width])
    normed_own = norm_stats(resid_own)[0] * (1.0 + own_mod[:, width:]) + own_mod[:, :width]
    normed_own = cut_parts(normed_own.astype(BF).reshape(micro_count, rows, width), mine)

    meta = jnp.stack(
        [segment_ids[:, 0].astype(F32), frame_mask[:, 0].astype(F32), flow_time[:, 0]], axis=1
    )[None]
    meta = jnp.concatenate([meta, swap(meta, "head", 1)])
    meta, *normed_own = together(meta, *normed_own)
    normed_attn = send_parts(normed_own, span)
    for bit in range(1, groups.bit_length() - 1):
        meta = jnp.concatenate([meta, swap(meta, "head", 2**bit)])
    resid_low = resid_own.astype(BF).reshape(micro_count, rows, width)
    second = [
        jnp.concatenate(pair, axis=1)
        for pair in zip(cut_parts(cotangent, mine), cut_parts(resid_low, mine), strict=True)
    ]
    meta, *rest = together(meta, *normed_attn, *second)
    normed_attn, second = jnp.concatenate(rest[:micro_count]), rest[micro_count:]
    meta = pick(meta, mine, 1).reshape(micro_count, span, 3, rows)
    seg_keys, live_keys, times = [meta[:, :, i].swapaxes(0, 1).reshape(-1) for i in range(3)]
    order = jnp.stack(
        [place ^ other ^ (step * span) for other in range(span) for step in range(micro_count)]
    )
    place_keys = (order[:, None] * rows + jnp.arange(rows)[None, :]).reshape(-1).astype(F32)
    starts = jnp.sum((seg_keys[None, :] < seg_keys[:, None]).astype(F32), axis=1)
    positions = place_keys - starts
    inv_freq = jnp.exp(jnp.arange(HD // 2, dtype=F32) * (-2.0 * math.log(10000.0) / HD))
    turns = positions[:, None] * inv_freq
    cos_half, sin_half = jnp.cos(turns), jnp.sin(turns)
    cos_keys = jnp.concatenate([cos_half] * 4, axis=1)
    sin_keys = jnp.concatenate([-sin_half, sin_half] * 2, axis=1)

    queries, keys_values = project(normed_attn, w_qkv, cos_keys[:frames], sin_keys[:frames])
    keys_values, seg_keys, live_keys, place_keys, times = together(
        keys_values, seg_keys, live_keys, place_keys, times
    )
    features = time_features(times[:frames], feature_count)
    scale_first, shift_second, scale_second = [
        dot(features, w_time[:, i * width : (i + 1) * width]) for i in range(1, 4)
    ]
    pairs_kv = [keys_values] + [swap(keys_values, "head", other) for other in range(1, span)]
    meta_q = jnp.stack(
        [seg_keys[:frames], place_keys[:frames]] + [jnp.zeros((frames,), F32)] * 6
    )
    meta_k = jnp.stack([seg_keys, place_keys, live_keys], axis=1)
    meta_k = jnp.pad(meta_k, ((0, 0), (0, PAIR - 3)))
    queries, meta_k, meta_q, scale_first, shift_second, scale_second, *pairs_kv = together(
        queries, meta_k, meta_q, scale_first, shift_second, scale_second, *pairs_kv
    )

    second = send_parts(second, span)
    attended, probs, inverses = attend(queries, pairs_kv, meta_k, meta_q)
    attended, inputs, skips = together(attended, inputs, skips)
    joined = cut_pairs(inputs, skips, mine)
    attended, *rest = together(attended, *second, *joined)
    second, joined = rest[:micro_count], rest[micro_count:]
    second = jnp.concatenate(second)
    resid_mid = second[:, width:].astype(F32) + dot(attended, w_out)
    normal_second = norm_stats(resid_mid)[0]
    normed_ffn = (normal_second * (1.0 + scale_second) + shift_second).astype(BF)

    normed_ffn, *joined = together(normed_ffn, *joined)
    joined = send_parts(joined, span)
    (
        down_away, down_keep, up_away, up_keep, output, grad_mid, mod_shift, mod_scale, grads, centres
    ) = feed(
        normed_ffn, second, w_up, w_down, resid_mid, scale_second, w_out, attended, inverses
    )
    grads, down_away, up_away, output, *joined = together(
        grads, down_away, up_away, output, *joined
    )
    seq_bits = lax.axis_size("seq").bit_length() - 1
    bits = list(range(seq_bits + 1, seq_bits + groups.bit_length() - 1))
    orders = (bits, bits[::-1])

    def two_ways(*arrays):
        middle_col = arrays[0].shape[1] // 2
        return [Rows(list(arrays), bits, 1, (i * middle_col, middle_col)) for i in range(2)]

    def begin(*pairs, index):
        return [
            away_all([pair[side] for pair in pairs], order[index])
            for side, order in enumerate(orders)
        ]

    def send(away, index):
        return [cross(rows, order[index]) for rows, order in zip(away, orders, strict=True)]

    def end(*pairs, came):
        for side, rows in enumerate(came):
            join_all([pair[side] for pair in pairs], rows)

    down_came, up_came = swap(down_away, "head", 1), swap(up_away, "head", 1)
    output = send_parts(list(output.reshape(micro_count, rows, width)), span)
    dq, dkv = attend_back(queries, pairs_kv, probs, centres, grads, cos_keys, sin_keys)
    dq, down_came, up_came, *rest = together(dq, down_came, up_came, *dkv, *output)
    dkv, output = rest[:span], rest[span:]

    dkv[1:] = [swap(part, "head", other) for other, part in enumerate(dkv) if other > 0]
    down = two_ways(down_keep, down_came)
    half = up_keep.shape[1] // 2
    up_0 = add_low([up_keep[:, :half], up_came[:, :half]])
    up_1 = add_low([up_keep[:, half:], up_came[:, half:]])
    dq, up_0, up_1, *rest = together(dq, up_0, up_1, *begin(down, index=0), *dkv)
    away, dkv = rest[:2], rest[2:]
    up_0 = seq_first(up_0)
    came = send(away, 0)
    near_away, near_keep, grad_in_low, first_shift, first_scale = near(
        dq, dkv, w_qkv, normed_attn, attended, grad_mid, second, scale_first
    )
    near_away, grad_in_low, *came = together(near_away, grad_in_low, *came)
    end(down, came=came)

    near_came = swap(near_away, "head", 1)
    for index in range(1, len(bits) - 1):
        end(down, came=send(begin(down, index=index), index))
    last_index = len(bits) - 1
    grad_in_low, *away = together(grad_in_low, *begin(down, index=last_index))
    came = send(away, last_index)
    far_away, far_keep = far(
        joined, features, grad_in_low, [first_shift, first_scale, mod_shift, mod_scale]
    )
    wide = two_ways(near_keep, near_came)
    far_away, up_0, *rest = together(far_away, up_0, *begin(wide, index=0), *came)
    wide_away, came = rest[:2], rest[2:]
    end(down, came=came)

    far_came = swap(far_away, "head", 1)
    wide_came = send(wide_away, 0)
    grad_local = send_parts(list(grad_in_low.reshape(micro_count, rows, width)), span)
    narrow = two_ways(far_keep, far_came)
    up_1 = seq_first(up_1)
    down_rows = jnp.concatenate([part.read() for part in down], axis=1)
    rest = together(*begin(narrow, index=0), up_1, *wide_came, down_rows, *grad_local)
    narrow_away, up_1, wide_came = rest[:2], rest[2], rest[3:5]
    down_rows, grad_local = rest[5], rest[6:]
    end(wide, came=wide_came)
    (down_sum,) = last_sum(down_rows)
    narrow_came = send(narrow_away, 0)
    for index in range(1, len(bits)):
        wide_came = send(begin(wide, index=index), index)
        if index < last_index:
            rest = together(*narrow_came, *wide_came)
            end(narrow, came=rest[:2])
            end(wide, came=rest[2:])
            narrow_came = send(begin(narrow, index=index), index)
    end(wide, came=wide_came)
    ups = [Rows([up_0], bits), Rows([up_1], bits)]
    wide_sum = jnp.concatenate([wide[0].read(), wide[1].read()], axis=1)
    wide_sum, down_sum, *rest = together(
        wide_sum, down_sum, *begin(ups, index=0), *narrow_came
    )
    up_away = rest[:2]
    end(narrow, came=rest[2:])
    narrow_came = send(begin(narrow, index=last_index), last_index)
    (near_sum,) = last_sum(wide_sum)
    end(narrow, came=together(*narrow_came))
    far_sum = jnp.concatenate([narrow[0].read(), narrow[1].read()], axis=1)
    many = w_skip.shape[0] // groups
    last = [
        Rows([far_sum[:many]], list(range(seq_bits))),
        Rows([far_sum[many:]], list(range(seq_bits)), 4),
    ]
    for index in range(max(seq_bits, len(bits))):
        came, up_came = [], []
        if index < seq_bits:
            came = [cross(away_all(last, index), index)]
        if index < len(bits):
            up_came = send(up_away, index)
        near_sum, *rest = together(near_sum, *came, *up_came)
        if index < seq_bits:
            join_all(last, rest[0])
        if index < len(bits):
            end(ups, came=rest[len(came) :])
        if index + 1 < len(bits):
            up_away = begin(ups, index=index + 1)
    output = by_micro(output, mine)
    grad_local = by_micro(grad_local, mine).reshape(frames, width)
    total_down, near_sum = down_sum.astype(F32), near_sum.astype(F32)
    total_up = jnp.concatenate([part.read() for part in ups], axis=1).astype(F32)
    total_qkv, total_out = near_sum[:, : 3 * width], near_sum[:, 3 * width :]
    total_skip = last[0].read().astype(F32)
    total_time = last[1].read().astype(F32)
    total_time = total_time.reshape(4, -1, width).swapaxes(0, 1).reshape(-1, 4 * width)
    shape = (micro_count, 1, rows, width)
    input_grad = dot(grad_local, w_skip[:width], DIMS_LAST).reshape(shape)
    skip_grad = dot(grad_local, w_skip[width:], DIMS_LAST).reshape(shape)
    return (
        output[:, None],
        input_grad,
        skip_grad,
        total_skip,
        total_time,
        total_qkv,
        total_out,
        total_up,
        total_down,
    )


def solution(mesh):
    frames_spec = P(None, "seq", "head", None)
    line_spec = P(None, "seq", "head")
    shard_spec = P(("head", "seq"), None)
    return jax.shard_map(
        per_device,
        mesh=mesh,
        in_specs=(frames_spec, frames_spec, line_spec, line_spec, line_spec, frames_spec)
        + (P(),) * 6,
        out_specs=(frames_spec,) * 3 + (shard_spec,) * 6,
        check_vma=False,
    )
```

time: 404 us -> 370 us (0.916)
  local copies, waits for them, and re-layouts: 37.7 us -> 19.4 us
  other arithmetic: 75 us -> 63.4 us
  waiting for transfers between devices: 74.9 us -> 84.3 us
  Pallas kernels: 132 us -> 123 us
    reduce_scatter x2 -> x4, waiting for transfers between devices: 0.01 us -> 9.11 us  [the longest x2 9.1 us: seq_first(): return lax.psum_scatter(rows, 'seq', scatter_dimension=0, tiled=True)]
    pallas_call x3 -> x1, Pallas kernels: 50.6 us -> 42.6 us  [feed(): pl.pallas_call(functools.partial(feed_kernel, groups, seq_blocks(width)),...]
    slice x12 -> x2, local copies, waits for them, and re-layouts: 9.71 us -> 1.92 us  [join_all(): part.join(came[start:start + height])]
    add x4 -> x0, other arithmetic: 7.25 us -> none  [add_low(): functools.reduce(jnp.add, [term.astype(F32) for term in terms]).astype(BF)]
    unnamed x113 -> x72, local copies, waits for them, and re-layouts: 14.9 us -> 7.8 us
    ppermute x46 -> x42, starting transfers between devices: 47.1 us -> 44.2 us  [swap(): return lax.ppermute(values, axis_name, [(i, i ^ bits) for i in range(size)])]
    convert_element_type x29 -> x18, other arithmetic: 36.7 us -> 37.8 us  [add_low(): functools.reduce(jnp.add, [term.astype(F32) for term in terms]).astype(BF)]
    dot_general x7 -> x9, matrix products: 16.5 us -> 16.9 us  [dot(): return lax.dot_general(left, right, dims, preferred_element_type=F32)]
  transfers between devices with their start and end apart: 48 -> 46, of which waited for: 17 -> 16; matrix products, arithmetic and copies ran while one was open for 24% -> 20% of each run, Pallas kernels for 31% -> 31%
where the time goes in v4:
time: 370 us; the launch traced here: 367 us
  Pallas kernels  123 us (33%)
  waiting for transfers between devices  84.3 us (23%)
  other arithmetic  63.4 us (17%)
  starting transfers between devices  44.3 us (12%)
  local copies, waits for them, and re-layouts  19.4 us (5%)
  matrix products  16.9 us (5%)
  between operations  15 us (4%)
    ppermute x42, waiting for transfers between devices, swap(): return lax.ppermute(values, axis_name, [(i, i ^ bits) for i in range(size)])  75.1 us
    ppermute x42, starting transfers between devices, swap(): return lax.ppermute(values, axis_name, [(i, i ^ bits) for i in range(size)])  44.2 us
    pallas_call x1, Pallas kernels, feed(): pl.pallas_call(functools.partial(feed_kernel, groups, seq_blocks(width)),...  42.6 us
    convert_element_type x18, other arithmetic, add_low(): functools.reduce(jnp.add, [term.astype(F32) for term in terms]).astype(BF)  37.8 us
    pallas_call x1, Pallas kernels, attend_back(): pl.pallas_call(functools.partial(attend_back_kernel, span), grid=(pairs,)...  23.4 us
    pallas_call x1, Pallas kernels, attend(): pl.pallas_call(functools.partial(attend_kernel, span), grid=(pairs,), in_...  20.6 us
    pallas_call x1, Pallas kernels, near(): pl.pallas_call(functools.partial(near_kernel, groups, len(dkv)), grid=(4...  18.3 us
    dot_general x9, matrix products, dot(): return lax.dot_general(left, right, dims, preferred_element_type=F32)  16.9 us
  transfers between devices with their start and end apart: 46, of which 16 were waited for; matrix products, arithmetic and copies ran while one was open for 20% of the time, Pallas kernels for 31%

profile of v4, /device:TPU:0, one launch (start us, length us, event | category | flops | bytes accessed | tf_op | source)
XLA Modules:
  0.0 366.5 jit_solution(17225088948828915101)
XLA Ops:
  10.5 3.3 fusion.7
  15.7 1.7 fusion.48
  17.4 2.0 fusion.33
  25.7 2.6 collective-permute-start.1
  28.4 2.0 collective-permute-start.4
  31.9 1.6 collective-permute-start.2
  33.5 8.7 %collective-permute-done.2 = f32[4,4,3,128]{3,1,2,0:T(4,128)S(1)} collective-permute-done((f32[4,4,3,128]{3,1,2,0:T(4,128)S(1)}, f32[4,4,3,128]{3,1,2,0:T(4,128)S(1)}, u32[]{:S(2)}, u32[]{:S(2)}) %collective-permute-start.2) | collective-permute-done | bytes 24608 | tf_op jit(solution)/shard_map/ppermute | solution.py:28
  44.0 1.9 fusion.64
  48.0 10.1 %shard_map.187 = (bf16[512,1024]{1,0:T(8,128)(2,1)S(1)}, bf16[512,2048]{1,0:T(8,128)(2,1)}) custom-call(bf16[512,1024]{1,0:T(8,128)(2,1)} %copy-done.28, bf16[1024,3072]{1,0:T(8,128)(2,1)} %refs_3_.1, f32[512,128]{1,0:T(8,128)S(1)} %slice.129.cos_ref, f32[512,128]{1,0:T(8,128)S(1)} %slice.130.sin_ref), custom_call_target="tpu_custom_call" | custom-call | flops 3221225472 | bytes 10485760 | tf_op jit(solution)/shard_map/pallas_call | solution.py:220
  66.2 1.7 fusion.46.refs_8_
  68.0 20.6 %shard_map.188 = (bf16[512,1024]{1,0:T(8,128)(2,1)S(1)}, bf16[16,1024,512]{2,1,0:T(8,128)(2,1)}, f32[8,8,512]{2,1,0:T(8,128)S(1)}) custom-call(bf16[512,1024]{1,0:T(8,128)(2,1)} %copy-done.3, bf16[512,2048]{1,0:T(8,128)(2,1)} %get-tuple-element.159.refs_0_.refs_2_, bf16[512,2048]{1,0:T(8,128)(2,1)} %collective-permute-done.6.refs_1_.refs_3_, ...), custom_call_target="tpu_custom_call" | custom-call | flops 8589934592 | bytes 16777216 | tf_op jit(solution)/shard_map/pallas_call | solution.py:295
  100.4 42.6 %shard_map.189 = (bf16[2048,1024]{1,0:T(8,128)(2,1)}, bf16[2048,1024]{1,0:T(8,128)(2,1)}, bf16[512,4096]{1,0:T(8,128)(2,1)}, bf16[512,4096]{1,0:T(8,128)(2,1)}, ...) custom-call(bf16[512,1024]{1,0:T(8,128)(2,1)} %add_convert_fusion.6., ...), custom_call_target="tpu_custom_call" | custom-call | flops 25769803776 | bytes 33554432 | tf_op jit(solution)/shard_map/pallas_call | solution.py:504
  147.5 23.4 %shard_map.190 = (bf16[512,1024]{1,0:T(8,128)(2,1)}, bf16[2,512,1024]{2,1,0:T(8,128)(2,1)}, bf16[2,512,1024]{2,1,0:T(8,128)(2,1)}) custom-call(bf16[512,1024]{1,0:T(8,128)(2,1)} %copy-done.3, bf16[512,2048]{1,0:T(8,128)(2,1)} %get-tuple-element.159.refs_0_.refs_2_, bf16[512,2048]{1,0:T(8,128)(2,1)} %collective-permute-done.6.refs_1_.refs_3_, ...), custom_call_target="tpu_custom_call" | custom-call | flops 17179869184 | bytes 16777216 | tf_op jit(solution)/shard_map/pallas_call | solution.py:366
  171.1 2.0 add_convert_fusion.4
  173.1 2.8 add_convert_fusion.5
  175.9 4.5 %add_convert_fusion = (bf16[512,2048]{1,0:T(8,128)(2,1)}, bf16[512,2048]{1,0:T(8,128)(2,1)}) fusion(bf16[512,4096]{1,0:T(8,128)(2,1)} %collective-permute-done.14, bf16[512,4096]{1,0:T(8,128)(2,1)S(1)} %copy-done.6), kind=kLoop, calls=%fused_computation | loop fusion | flops 8388608 | bytes 12582912 | tf_op jit(solution)/shard_map/convert_element_type | solution.py:60
  183.3 18.3 %shard_map.191 = (bf16[512,4096]{1,0:T(8,128)(2,1)}, bf16[512,4096]{1,0:T(8,128)(2,1)}, bf16[512,1024]{1,0:T(8,128)(2,1)S(1)}, bf16[512,1024]{1,0:T(8,128)(2,1)}, bf16[512,1024]{1,0:T(8,128)(2,1)}) custom-call(bf16[512,1024]{1,0:T(8,128)(2,1)} %get-tuple-element.216.refs_0_, bf16[2,512,1024]{2,1,0:T(8,128)(2,1)} %get-tuple-element.217.refs_1_, ...), custom_call_target="tpu_custom_call" | custom-call | flops 7516192768 | bytes 30408704 | tf_op jit(solution)/shard_map/pallas_call | solution.py:642
  202.6 3.6 collective-permute-done.19
  207.2 2.3 fusion.31
  209.4 1.6 collective-permute-start.22
  211.6 8.5 %shard_map.192 = (bf16[1536,1024]{1,0:T(8,128)(2,1)}, bf16[1536,1024]{1,0:T(8,128)(2,1)}) custom-call(bf16[2,128,1024]{2,1,0:T(8,128)(2,1)S(1)} %pad_maximum_fusion.11.refs_0_, bf16[2,128,1024]{2,1,0:T(8,128)(2,1)S(1)} %collective-permute-done.10.refs_1_, bf16[2,128,1024]{2,1,0:T(8,128)(2,1)S(1)} %collective-permute-done.11.refs_2_, ...), custom_call_target="tpu_custom_call" | custom-call | flops 3221225472 | bytes 16777216 | tf_op jit(solution)/shard_map/pallas_call | solution.py:708
  220.1 2.6 add_convert_fusion.2
  222.8 2.7 add_convert_fusion.3
  231.8 2.9 fusion.30
  235.8 2.3 collective-permute-start.29
  238.1 2.3 add_convert_fusion.7
  240.4 2.3 add_convert_fusion.8
  242.7 15.9 %collective-permute-done.27 = bf16[128,1024]{1,0:T(8,128)(2,1)} collective-permute-done((bf16[128,1024]{1,0:T(8,128)(2,1)}, bf16[128,1024]{1,0:T(8,128)(2,1)}, u32[]{:S(2)}, u32[]{:S(2)}) %collective-permute-start.27) | collective-permute-done | bytes 262176 | tf_op jit(solution)/shard_map/ppermute | solution.py:28
  258.6 6.4 %collective-permute-done.28 = bf16[128,1024]{1,0:T(8,128)(2,1)} collective-permute-done((bf16[128,1024]{1,0:T(8,128)(2,1)}, bf16[128,1024]{1,0:T(8,128)(2,1)}, u32[]{:S(2)}, u32[]{:S(2)}) %collective-permute-start.28) | collective-permute-done | bytes 262176 | tf_op jit(solution)/shard_map/ppermute | solution.py:28
  265.0 7.9 %reduce-scatter.7.cloned.1.call-done = bf16[128,2048]{1,0:T(8,128)(2,1)} async-done(((bf16[512,2048]{1,0:T(8,128)(2,1)}), bf16[128,2048]{1,0:T(8,128)(2,1)}) %reduce-scatter.7.cloned.1.call-update) | async-done | bytes 524304 | tf_op jit(solution)/shard_map/reduce_scatter | solution.py:126
  273.0 3.4 fusion.24
  279.3 1.7 constant_dynamic-slice_fusion.1
  282.1 1.7 constant_dynamic-slice_fusion
  283.7 7.8 %collective-permute-done.30 = bf16[128,2048]{1,0:T(8,128)(2,1)} collective-permute-done((bf16[128,2048]{1,0:T(8,128)(2,1)}, bf16[128,2048]{1,0:T(8,128)(2,1)}, u32[]{:S(2)}, u32[]{:S(2)}) %collective-permute-start.30) | collective-permute-done | bytes 524320 | tf_op jit(solution)/shard_map/ppermute | solution.py:28
  293.0 2.9 fusion.26
  296.9 11.3 %collective-permute-done.32 = bf16[768,512]{1,0:T(8,128)(2,1)} collective-permute-done((bf16[768,512]{1,0:T(8,128)(2,1)}, bf16[768,512]{1,0:T(8,128)(2,1)}, u32[]{:S(2)}, u32[]{:S(2)}) %collective-permute-start.32) | collective-permute-done | bytes 786464 | tf_op jit(solution)/shard_map/ppermute | solution.py:28
  311.8 2.4 fusion.37
  316.1 2.6 fusion.15
  319.3 1.7 collective-permute-start.38
  320.9 5.4 %collective-permute-done.34 = bf16[384,512]{1,0:T(8,128)(2,1)S(1)} collective-permute-done((bf16[384,512]{1,0:T(8,128)(2,1)S(1)}, bf16[384,512]{1,0:T(8,128)(2,1)S(1)}, u32[]{:S(2)}, u32[]{:S(2)}) %collective-permute-start.34) | collective-permute-done | bytes 393248 | tf_op jit(solution)/shard_map/ppermute | solution.py:28
  326.7 1.8 fusion.40
  328.7 2.6 fusion.12
  331.4 9.0 %collective-permute-done.36 = bf16[192,1024]{1,0:T(8,128)(2,1)} collective-permute-done((bf16[192,1024]{1,0:T(8,128)(2,1)S(1)}, bf16[192,1024]{1,0:T(8,128)(2,1)}, u32[]{:S(2)}, u32[]{:S(2)}) %collective-permute-start.36) | collective-permute-done | bytes 393248 | tf_op jit(solution)/shard_map/ppermute | solution.py:28
  343.3 1.5 collective-permute-start.41
  344.9 2.5 collective-permute-start.39
  348.4 1.5 collective-permute-start.40
  351.9 1.5 collective-permute-done.40
  353.4 1.6 collective-permute-done.39
  (240 shorter events, 77.9 us)
Async XLA Ops:
  7.2 219.5 %reduce-scatter.5.cloned.1.call-start = ((), (), s32[]{:S(2)}) async-start(), calls=%async_computation.4 | async-start | bytes 2621440 | tf_op jit(solution)/shard_map/reduce_scatter | solution.py:126
  9.3 16.4 %collective-permute-start = (f32[1,4,3,128]{3,1,2,0:T(4,128)S(1)}, f32[1,4,3,128]{3,1,2,0:T(4,128)S(1)}, u32[]{:S(2)}, u32[]{:S(2)}) collective-permute-start(f32[1,4,3,128]{3,1,2,0:T(4,128)S(1)} %bitcast.304), channel_id=1, source_target_pairs={{0,4},{4,0},{8,12},{12,8},{16,20},{20,16},{24,28},{28,24},{1,5},{5... | collective-permute-start | bytes 18440 | tf_op jit(solution)/shard_map/ppermute | solution.py:28
  25.7 6.2 %collective-permute-start.1 = (f32[2,4,3,128]{3,1,2,0:T(4,128)S(1)}, f32[2,4,3,128]{3,1,2,0:T(4,128)S(1)}, u32[]{:S(2)}, u32[]{:S(2)}) collective-permute-start(f32[2,4,3,128]{3,1,2,0:T(4,128)S(1)} %pad_maximum_fusion.24), channel_id=1, source_target_pairs={{0,8},{4,12},{8,0},{12,4},{16,24},{20,28},{24,16},{28,20},{1,9},{5... | collective-permute-start | bytes 36872 | tf_op jit(solution)/shard_map/ppermute | solution.py:28
  28.4 13.8 %collective-permute-start.3 = (bf16[128,1024]{1,0:T(8,128)(2,1)S(1)}, bf16[128,1024]{1,0:T(8,128)(2,1)S(1)}, u32[]{:S(2)}, u32[]{:S(2)}) collective-permute-start(bf16[128,1024]{1,0:T(8,128)(2,1)S(1)} %get-tuple-element.143), channel_id=1, source_target_pairs={{0,8},{4,12},{8,0},{12,4},{16,24},{20,28},{24,16},{28,20},{1,9},{5... | collective-permute-start | bytes 786440 | tf_op jit(solution)/shard_map/ppermute | solution.py:28
  28.4 13.8 %collective-permute-start.4 = (bf16[128,1024]{1,0:T(8,128)(2,1)S(1)}, bf16[128,1024]{1,0:T(8,128)(2,1)S(1)}, u32[]{:S(2)}, u32[]{:S(2)}) collective-permute-start(bf16[128,1024]{1,0:T(8,128)(2,1)S(1)} %get-tuple-element.144), channel_id=1, source_target_pairs={{0,16},{4,20},{8,24},{12,28},{16,0},{20,4},{24,8},{28,12},{1,17},{... | collective-permute-start | bytes 786440 | tf_op jit(solution)/shard_map/ppermute | solution.py:28
  30.4 12.9 %collective-permute-start.5 = (bf16[128,1024]{1,0:T(8,128)(2,1)S(1)}, bf16[128,1024]{1,0:T(8,128)(2,1)S(1)}, u32[]{:S(2)}, u32[]{:S(2)}) collective-permute-start(bf16[128,1024]{1,0:T(8,128)(2,1)S(1)} %get-tuple-element.145), channel_id=1, source_target_pairs={{0,24},{4,28},{8,16},{12,20},{16,8},{20,12},{24,0},{28,4},{1,25},{... | collective-permute-start | bytes 786440 | tf_op jit(solution)/shard_map/ppermute | solution.py:28
  31.9 10.3 %collective-permute-start.2 = (f32[4,4,3,128]{3,1,2,0:T(4,128)S(1)}, f32[4,4,3,128]{3,1,2,0:T(4,128)S(1)}, u32[]{:S(2)}, u32[]{:S(2)}) collective-permute-start(f32[4,4,3,128]{3,1,2,0:T(4,128)S(1)} %pad_maximum_fusion.22), channel_id=1, source_target_pairs={{0,16},{4,20},{8,24},{12,28},{16,0},{20,4},{24,8},{28,12},{1,17},{... | collective-permute-start | bytes 73736 | tf_op jit(solution)/shard_map/ppermute | solution.py:28
  59.1 8.9 %collective-permute-start.6 = (bf16[512,2048]{1,0:T(8,128)(2,1)}, bf16[512,2048]{1,0:T(8,128)(2,1)}, u32[]{:S(2)}, u32[]{:S(2)}) collective-permute-start(bf16[512,2048]{1,0:T(8,128)(2,1)} %get-tuple-element.159.refs_0_.refs_2_), channel_id=1, source_target_pairs={{0,4},{4,0},{8,12},{12,8},{16,20},{20,16},{24,28},{28,24},{1,5},{5... | collective-permute-start | bytes 6291464 | tf_op jit(solution)/shard_map/ppermute | solution.py:28
  59.5 31.8 %collective-permute-start.7 = (bf16[128,2048]{1,0:T(8,128)(2,1)}, bf16[128,2048]{1,0:T(8,128)(2,1)S(1)}, u32[]{:S(2)}, u32[]{:S(2)}) collective-permute-start(bf16[128,2048]{1,0:T(8,128)(2,1)} %pad_maximum_fusion.6), channel_id=1, source_target_pairs={{0,8},{4,12},{8,0},{12,4},{16,24},{20,28},{24,16},{28,20},{1,9},{5... | collective-permute-start | bytes 1572872 | tf_op jit(solution)/shard_map/ppermute | solution.py:28
  61.0 30.3 %collective-permute-start.8 = (bf16[128,2048]{1,0:T(8,128)(2,1)}, bf16[128,2048]{1,0:T(8,128)(2,1)}, u32[]{:S(2)}, u32[]{:S(2)}) collective-permute-start(bf16[128,2048]{1,0:T(8,128)(2,1)} %pad_maximum_fusion.7), channel_id=1, source_target_pairs={{0,16},{4,20},{8,24},{12,28},{16,0},{20,4},{24,8},{28,12},{1,17},{... | collective-permute-start | bytes 1572872 | tf_op jit(solution)/shard_map/ppermute | solution.py:28
  62.5 28.8 %collective-permute-start.9 = (bf16[128,2048]{1,0:T(8,128)(2,1)}, bf16[128,2048]{1,0:T(8,128)(2,1)}, u32[]{:S(2)}, u32[]{:S(2)}) collective-permute-start(bf16[128,2048]{1,0:T(8,128)(2,1)} %pad_maximum_fusion.8), channel_id=1, source_target_pairs={{0,24},{4,28},{8,16},{12,20},{16,8},{20,12},{24,0},{28,4},{1,25},{... | collective-permute-start | bytes 1572872 | tf_op jit(solution)/shard_map/ppermute | solution.py:28
  65.8 29.7 %copy-start.4 = (f32[512,1024]{1,0:T(8,128)}, f32[512,1024]{1,0:T(8,128)S(1)}, u32[]{:S(2)}) copy-start(f32[512,1024]{1,0:T(8,128)S(1)} %fusion.42.refs_1_) | copy-start | bytes 6291460
  68.0 20.6 %copy-start.12 = (bf16[4,1,128,1024]{3,2,1,0:T(8,128)(2,1)S(1)}, bf16[4,1,128,1024]{3,2,1,0:T(8,128)(2,1)}, u32[]{:S(2)}) copy-start(bf16[4,1,128,1024]{3,2,1,0:T(8,128)(2,1)} %param.12) | copy-start | bytes 3145732
  97.0 46.1 %collective-permute-start.10 = (bf16[2,128,1024]{2,1,0:T(8,128)(2,1)}, bf16[2,128,1024]{2,1,0:T(8,128)(2,1)S(1)}, u32[]{:S(2)}, u32[]{:S(2)}) collective-permute-start(bf16[2,128,1024]{2,1,0:T(8,128)(2,1)} %pad_maximum_fusion.12), channel_id=1, source_target_pairs={{0,8},{4,12},{8,0},{12,4},{16,24},{20,28},{24,16},{28,20},{1,9},{5... | collective-permute-start | bytes 1572872 | tf_op jit(solution)/shard_map/ppermute | solution.py:28
  98.3 44.7 %collective-permute-start.11 = (bf16[2,128,1024]{2,1,0:T(8,128)(2,1)S(1)}, bf16[2,128,1024]{2,1,0:T(8,128)(2,1)S(1)}, u32[]{:S(2)}, u32[]{:S(2)}) collective-permute-start(bf16[2,128,1024]{2,1,0:T(8,128)(2,1)S(1)} %pad_maximum_fusion.13), channel_id=1, source_target_pairs={{0,16},{4,20},{8,24},{12,28},{16,0},{20,4},{24,8},{28,12},{1,17},{... | collective-permute-start | bytes 1572872 | tf_op jit(solution)/shard_map/ppermute | solution.py:28
  99.8 43.2 %collective-permute-start.12 = (bf16[2,128,1024]{2,1,0:T(8,128)(2,1)S(1)}, bf16[2,128,1024]{2,1,0:T(8,128)(2,1)S(1)}, u32[]{:S(2)}, u32[]{:S(2)}) collective-permute-start(bf16[2,128,1024]{2,1,0:T(8,128)(2,1)S(1)} %pad_maximum_fusion.14), channel_id=1, source_target_pairs={{0,24},{4,28},{8,16},{12,20},{16,8},{20,12},{24,0},{28,4},{1,25},{... | collective-permute-start | bytes 1572872 | tf_op jit(solution)/shard_map/ppermute | solution.py:28
  143.1 27.8 %collective-permute-start.13 = (bf16[2048,1024]{1,0:T(8,128)(2,1)}, bf16[2048,1024]{1,0:T(8,128)(2,1)}, u32[]{:S(2)}, u32[]{:S(2)}) collective-permute-start(bf16[2048,1024]{1,0:T(8,128)(2,1)} %get-tuple-element.196), channel_id=1, source_target_pairs={{0,4},{4,0},{8,12},{12,8},{16,20},{20,16},{24,28},{28,24},{1,5},{5... | collective-permute-start | bytes 12582920 | tf_op jit(solution)/shard_map/ppermute | solution.py:28
  143.9 27.1 %collective-permute-start.14 = (bf16[512,4096]{1,0:T(8,128)(2,1)}, bf16[512,4096]{1,0:T(8,128)(2,1)}, u32[]{:S(2)}, u32[]{:S(2)}) collective-permute-start(bf16[512,4096]{1,0:T(8,128)(2,1)} %get-tuple-element.197), channel_id=1, source_target_pairs={{0,4},{4,0},{8,12},{12,8},{16,20},{20,16},{24,28},{28,24},{1,5},{5... | collective-permute-start | bytes 12582920 | tf_op jit(solution)/shard_map/ppermute | solution.py:28
  144.0 26.9 %collective-permute-start.15 = (bf16[128,1024]{1,0:T(8,128)(2,1)S(1)}, bf16[128,1024]{1,0:T(8,128)(2,1)S(1)}, u32[]{:S(2)}, u32[]{:S(2)}) collective-permute-start(bf16[128,1024]{1,0:T(8,128)(2,1)S(1)} %get-tuple-element.366), channel_id=1, source_target_pairs={{0,8},{4,12},{8,0},{12,4},{16,24},{20,28},{24,16},{28,20},{1,9},{5... | collective-permute-start | bytes 786440 | tf_op jit(solution)/shard_map/ppermute | solution.py:28
  145.4 25.5 %collective-permute-start.16 = (bf16[128,1024]{1,0:T(8,128)(2,1)S(1)}, bf16[128,1024]{1,0:T(8,128)(2,1)}, u32[]{:S(2)}, u32[]{:S(2)}) collective-permute-start(bf16[128,1024]{1,0:T(8,128)(2,1)S(1)} %get-tuple-element.365), channel_id=1, source_target_pairs={{0,16},{4,20},{8,24},{12,28},{16,0},{20,4},{24,8},{28,12},{1,17},{... | collective-permute-start | bytes 786440 | tf_op jit(solution)/shard_map/ppermute | solution.py:28
  146.9 24.0 %collective-permute-start.17 = (bf16[128,1024]{1,0:T(8,128)(2,1)S(1)}, bf16[128,1024]{1,0:T(8,128)(2,1)}, u32[]{:S(2)}, u32[]{:S(2)}) collective-permute-start(bf16[128,1024]{1,0:T(8,128)(2,1)S(1)} %get-tuple-element.364), channel_id=1, source_target_pairs={{0,24},{4,28},{8,16},{12,20},{16,8},{20,12},{24,0},{28,4},{1,25},{... | collective-permute-start | bytes 786440 | tf_op jit(solution)/shard_map/ppermute | solution.py:28
  170.9 9.4 %collective-permute-start.18 = (bf16[2,512,1024]{2,1,0:T(8,128)(2,1)}, bf16[2,512,1024]{2,1,0:T(8,128)(2,1)}, u32[]{:S(2)}, u32[]{:S(2)}) collective-permute-start(bf16[2,512,1024]{2,1,0:T(8,128)(2,1)} %get-tuple-element.215), channel_id=1, source_target_pairs={{0,4},{4,0},{8,12},{12,8},{16,20},{20,16},{24,28},{28,24},{1,5},{5... | collective-permute-start | bytes 6291464 | tf_op jit(solution)/shard_map/ppermute | solution.py:28
  180.4 25.8 %collective-permute-start.19 = (bf16[1024,512]{1,0:T(8,128)(2,1)}, bf16[1024,512]{1,0:T(8,128)(2,1)}, u32[]{:S(2)}, u32[]{:S(2)}) collective-permute-start(bf16[1024,512]{1,0:T(8,128)(2,1)} %bitcast.278), channel_id=1, source_target_pairs={{0,8},{4,12},{8,0},{12,4},{16,24},{20,28},{24,16},{28,20},{1,9},{5... | collective-permute-start | bytes 3145736 | tf_op jit(solution)/shard_map/ppermute | solution.py:28
  181.7 25.3 %collective-permute-start.20 = (bf16[1024,512]{1,0:T(8,128)(2,1)S(1)}, bf16[1024,512]{1,0:T(8,128)(2,1)}, u32[]{:S(2)}, u32[]{:S(2)}) collective-permute-start(bf16[1024,512]{1,0:T(8,128)(2,1)S(1)} %bitcast.277), channel_id=1, source_target_pairs={{0,16},{4,20},{8,24},{12,28},{16,0},{20,4},{24,8},{28,12},{1,17},{... | collective-permute-start | bytes 3145736 | tf_op jit(solution)/shard_map/ppermute | solution.py:28
  183.3 89.6 %reduce-scatter.7.cloned.1.call-start = ((), (), s32[]{:S(2)}) async-start(), calls=%async_computation.5 | async-start | bytes 2621440 | tf_op jit(solution)/shard_map/reduce_scatter | solution.py:126
  207.1 13.0 %collective-permute-start.21 = (bf16[512,4096]{1,0:T(8,128)(2,1)}, bf16[512,4096]{1,0:T(8,128)(2,1)}, u32[]{:S(2)}, u32[]{:S(2)}) collective-permute-start(bf16[512,4096]{1,0:T(8,128)(2,1)} %get-tuple-element.237), channel_id=1, source_target_pairs={{0,4},{4,0},{8,12},{12,8},{16,20},{20,16},{24,28},{28,24},{1,5},{5... | collective-permute-start | bytes 12582920 | tf_op jit(solution)/shard_map/ppermute | solution.py:28
  207.1 101.1 %reduce-scatter.9.cloned.1.call-start = ((), (), s32[]{:S(2)}) async-start(), calls=%async_computation.6 | async-start | bytes 1310720 | tf_op jit(solution)/shard_map/reduce_scatter | solution.py:139
  209.4 16.0 %collective-permute-start.22 = (bf16[512,512]{1,0:T(8,128)(2,1)S(1)}, bf16[512,512]{1,0:T(8,128)(2,1)S(1)}, u32[]{:S(2)}, u32[]{:S(2)}) collective-permute-start(bf16[512,512]{1,0:T(8,128)(2,1)S(1)} %get-tuple-element.238), channel_id=1, source_target_pairs={{0,16},{4,20},{8,24},{12,28},{16,0},{20,4},{24,8},{28,12},{1,17},{... | collective-permute-start | bytes 1572872 | tf_op jit(solution)/shard_map/ppermute | solution.py:28
  211.0 14.4 %collective-permute-start.23 = (bf16[512,512]{1,0:T(8,128)(2,1)S(1)}, bf16[512,512]{1,0:T(8,128)(2,1)S(1)}, u32[]{:S(2)}, u32[]{:S(2)}) collective-permute-start(bf16[512,512]{1,0:T(8,128)(2,1)S(1)} %get-tuple-element.239), channel_id=1, source_target_pairs={{0,8},{4,12},{8,0},{12,4},{16,24},{20,28},{24,16},{28,20},{1,9},{5... | collective-permute-start | bytes 1572872 | tf_op jit(solution)/shard_map/ppermute | solution.py:28
  226.7 9.1 %collective-permute-start.24 = (bf16[1536,1024]{1,0:T(8,128)(2,1)}, bf16[1536,1024]{1,0:T(8,128)(2,1)}, u32[]{:S(2)}, u32[]{:S(2)}) collective-permute-start(bf16[1536,1024]{1,0:T(8,128)(2,1)} %get-tuple-element.240), channel_id=1, source_target_pairs={{0,4},{4,0},{8,12},{12,8},{16,20},{20,16},{24,28},{28,24},{1,5},{5... | collective-permute-start | bytes 9437192 | tf_op jit(solution)/shard_map/ppermute | solution.py:28
  226.7 46.2 %collective-permute-start.25 = (bf16[256,2048]{1,0:T(8,128)(2,1)}, bf16[256,2048]{1,0:T(8,128)(2,1)}, u32[]{:S(2)}, u32[]{:S(2)}) collective-permute-start(bf16[256,2048]{1,0:T(8,128)(2,1)} %bitcast.63), channel_id=1, source_target_pairs={{0,8},{4,12},{8,0},{12,4},{16,24},{20,28},{24,16},{28,20},{1,9},{5... | collective-permute-start | bytes 3145736 | tf_op jit(solution)/shard_map/ppermute | solution.py:28
  228.1 44.7 %collective-permute-start.26 = (bf16[256,2048]{1,0:T(8,128)(2,1)}, bf16[256,2048]{1,0:T(8,128)(2,1)}, u32[]{:S(2)}, u32[]{:S(2)}) collective-permute-start(bf16[256,2048]{1,0:T(8,128)(2,1)} %bitcast.64), channel_id=1, source_target_pairs={{0,16},{4,20},{8,24},{12,28},{16,0},{20,4},{24,8},{28,12},{1,17},{... | collective-permute-start | bytes 3145736 | tf_op jit(solution)/shard_map/ppermute | solution.py:28
  230.6 28.0 %collective-permute-start.27 = (bf16[128,1024]{1,0:T(8,128)(2,1)}, bf16[128,1024]{1,0:T(8,128)(2,1)}, u32[]{:S(2)}, u32[]{:S(2)}) collective-permute-start(bf16[128,1024]{1,0:T(8,128)(2,1)} %get-tuple-element.358), channel_id=1, source_target_pairs={{0,8},{4,12},{8,0},{12,4},{16,24},{20,28},{24,16},{28,20},{1,9},{5... | collective-permute-start | bytes 786440 | tf_op jit(solution)/shard_map/ppermute | solution.py:28
  231.2 33.8 %collective-permute-start.28 = (bf16[128,1024]{1,0:T(8,128)(2,1)}, bf16[128,1024]{1,0:T(8,128)(2,1)}, u32[]{:S(2)}, u32[]{:S(2)}) collective-permute-start(bf16[128,1024]{1,0:T(8,128)(2,1)} %get-tuple-element.357), channel_id=1, source_target_pairs={{0,16},{4,20},{8,24},{12,28},{16,0},{20,4},{24,8},{28,12},{1,17},{... | collective-permute-start | bytes 786440 | tf_op jit(solution)/shard_map/ppermute | solution.py:28
  235.8 29.2 %collective-permute-start.29 = (bf16[128,1024]{1,0:T(8,128)(2,1)}, bf16[128,1024]{1,0:T(8,128)(2,1)}, u32[]{:S(2)}, u32[]{:S(2)}) collective-permute-start(bf16[128,1024]{1,0:T(8,128)(2,1)} %get-tuple-element.356), channel_id=1, source_target_pairs={{0,24},{4,28},{8,16},{12,20},{16,8},{20,12},{24,0},{28,4},{1,25},{... | collective-permute-start | bytes 786440 | tf_op jit(solution)/shard_map/ppermute | solution.py:28
  272.9 67.5 %reduce-scatter.11.cloned.1.call-start = ((), (), s32[]{:S(2)}) async-start(), calls=%async_computation.7 | async-start | bytes 1310720 | tf_op jit(solution)/shard_map/reduce_scatter | solution.py:139
  276.3 15.2 %collective-permute-start.30 = (bf16[128,2048]{1,0:T(8,128)(2,1)}, bf16[128,2048]{1,0:T(8,128)(2,1)}, u32[]{:S(2)}, u32[]{:S(2)}) collective-permute-start(bf16[128,2048]{1,0:T(8,128)(2,1)} %get-tuple-element.338), channel_id=1, source_target_pairs={{0,16},{4,20},{8,24},{12,28},{16,0},{20,4},{24,8},{28,12},{1,17},{... | collective-permute-start | bytes 1572872 | tf_op jit(solution)/shard_map/ppermute | solution.py:28
  277.8 15.2 %collective-permute-start.31 = (bf16[128,2048]{1,0:T(8,128)(2,1)}, bf16[128,2048]{1,0:T(8,128)(2,1)}, u32[]{:S(2)}, u32[]{:S(2)}) collective-permute-start(bf16[128,2048]{1,0:T(8,128)(2,1)} %get-tuple-element.339), channel_id=1, source_target_pairs={{0,8},{4,12},{8,0},{12,4},{16,24},{20,28},{24,16},{28,20},{1,9},{5... | collective-permute-start | bytes 1572872 | tf_op jit(solution)/shard_map/ppermute | solution.py:28
  281.0 27.3 %collective-permute-start.32 = (bf16[768,512]{1,0:T(8,128)(2,1)}, bf16[768,512]{1,0:T(8,128)(2,1)}, u32[]{:S(2)}, u32[]{:S(2)}) collective-permute-start(bf16[768,512]{1,0:T(8,128)(2,1)} %bitcast.285), channel_id=1, source_target_pairs={{0,8},{4,12},{8,0},{12,4},{16,24},{20,28},{24,16},{28,20},{1,9},{5... | collective-permute-start | bytes 2359304 | tf_op jit(solution)/shard_map/ppermute | solution.py:28
  281.5 26.7 %collective-permute-start.33 = (bf16[768,512]{1,0:T(8,128)(2,1)}, bf16[768,512]{1,0:T(8,128)(2,1)}, u32[]{:S(2)}, u32[]{:S(2)}) collective-permute-start(bf16[768,512]{1,0:T(8,128)(2,1)} %bitcast.284), channel_id=1, source_target_pairs={{0,16},{4,20},{8,24},{12,28},{16,0},{20,4},{24,8},{28,12},{1,17},{... | collective-permute-start | bytes 2359304 | tf_op jit(solution)/shard_map/ppermute | solution.py:28
  314.2 12.1 %collective-permute-start.34 = (bf16[384,512]{1,0:T(8,128)(2,1)S(1)}, bf16[384,512]{1,0:T(8,128)(2,1)S(1)}, u32[]{:S(2)}, u32[]{:S(2)}) collective-permute-start(bf16[384,512]{1,0:T(8,128)(2,1)S(1)} %get-tuple-element.349), channel_id=1, source_target_pairs={{0,16},{4,20},{8,24},{12,28},{16,0},{20,4},{24,8},{28,12},{1,17},{... | collective-permute-start | bytes 1179656 | tf_op jit(solution)/shard_map/ppermute | solution.py:28
  314.6 12.1 %collective-permute-start.35 = (bf16[384,512]{1,0:T(8,128)(2,1)S(1)}, bf16[384,512]{1,0:T(8,128)(2,1)S(1)}, u32[]{:S(2)}, u32[]{:S(2)}) collective-permute-start(bf16[384,512]{1,0:T(8,128)(2,1)S(1)} %get-tuple-element.348), channel_id=1, source_target_pairs={{0,8},{4,12},{8,0},{12,4},{16,24},{20,28},{24,16},{28,20},{1,9},{5... | collective-permute-start | bytes 1179656 | tf_op jit(solution)/shard_map/ppermute | solution.py:28
  318.7 12.6 %collective-permute-start.37 = (bf16[64,2048]{1,0:T(8,128)(2,1)S(1)}, bf16[64,2048]{1,0:T(8,128)(2,1)}, u32[]{:S(2)}, u32[]{:S(2)}) collective-permute-start(bf16[64,2048]{1,0:T(8,128)(2,1)S(1)} %bitcast.295), channel_id=1, source_target_pairs={{0,8},{4,12},{8,0},{12,4},{16,24},{20,28},{24,16},{28,20},{1,9},{5... | collective-permute-start | bytes 786440 | tf_op jit(solution)/shard_map/ppermute | solution.py:28
  319.3 12.1 %collective-permute-start.38 = (bf16[64,2048]{1,0:T(8,128)(2,1)S(1)}, bf16[64,2048]{1,0:T(8,128)(2,1)}, u32[]{:S(2)}, u32[]{:S(2)}) collective-permute-start(bf16[64,2048]{1,0:T(8,128)(2,1)S(1)} %bitcast.296), channel_id=1, source_target_pairs={{0,16},{4,20},{8,24},{12,28},{16,0},{20,4},{24,8},{28,12},{1,17},{... | collective-permute-start | bytes 786440 | tf_op jit(solution)/shard_map/ppermute | solution.py:28
  328.6 11.8 %collective-permute-start.36 = (bf16[192,1024]{1,0:T(8,128)(2,1)S(1)}, bf16[192,1024]{1,0:T(8,128)(2,1)}, u32[]{:S(2)}, u32[]{:S(2)}) collective-permute-start(bf16[192,1024]{1,0:T(8,128)(2,1)S(1)} %pad_maximum_fusion.15), channel_id=1, source_target_pairs={{0,1},{1,0},{2,3},{3,2},{4,5},{5,4},{6,7},{7,6},{8,9},{9,8},{10,11... | collective-permute-start | bytes 1179656 | tf_op jit(solution)/shard_map/ppermute | solution.py:28
  343.3 8.6 %collective-permute-start.41 = (bf16[32,2048]{1,0:T(8,128)(2,1)S(1)}, bf16[32,2048]{1,0:T(8,128)(2,1)S(1)}, u32[]{:S(2)}, u32[]{:S(2)}) collective-permute-start(bf16[32,2048]{1,0:T(8,128)(2,1)S(1)} %fusion.59), channel_id=1, source_target_pairs={{0,8},{4,12},{8,0},{12,4},{16,24},{20,28},{24,16},{28,20},{1,9},{5... | collective-permute-start | bytes 393224 | tf_op jit(solution)/shard_map/ppermute | solution.py:28
  344.9 10.0 %collective-permute-start.39 = (bf16[96,1024]{1,0:T(8,128)(2,1)S(1)}, bf16[96,1024]{1,0:T(8,128)(2,1)S(1)}, u32[]{:S(2)}, u32[]{:S(2)}) collective-permute-start(bf16[96,1024]{1,0:T(8,128)(2,1)S(1)} %pad_maximum_fusion.18), channel_id=1, source_target_pairs={{0,2},{1,3},{2,0},{3,1},{4,6},{5,7},{6,4},{7,5},{8,10},{9,11},{10,... | collective-permute-start | bytes 589832 | tf_op jit(solution)/shard_map/ppermute | solution.py:28
  348.4 5.0 %collective-permute-start.40 = (bf16[32,2048]{1,0:T(8,128)(2,1)S(1)}, bf16[32,2048]{1,0:T(8,128)(2,1)S(1)}, u32[]{:S(2)}, u32[]{:S(2)}) collective-permute-start(bf16[32,2048]{1,0:T(8,128)(2,1)S(1)} %fusion.60), channel_id=1, source_target_pairs={{0,16},{4,20},{8,24},{12,28},{16,0},{20,4},{24,8},{28,12},{1,17},{... | collective-permute-start | bytes 393224 | tf_op jit(solution)/shard_map/ppermute | solution.py:28
  (31 other events, 190.0 us)
Sparse Core Ops, SparseCore 0:
  183.4 43.2 reduce-scatter.4
  229.7 43.1 reduce-scatter.6
  275.2 26.4 reduce-scatter.8
  308.4 29.0 reduce-scatter.10

commit v5 on v4

--- a/solution.py
+++ b/solution.py
@@ -12,6 +12,8 @@
 PAIR = 2 * HD
 eps_norm = 1e-06
 neg_fill = -1e30
+SEGMENTS = 8
+PADDING = 64
 BF = jnp.bfloat16
 F32 = jnp.float32
 DIMS_FIRST = (((0,), (0,)), ((), ()))
@@ -234,9 +236,9 @@
             jax.ShapeDtypeStruct((frames, width), BF),
             jax.ShapeDtypeStruct((frames, 2 * width), BF),
         ],
-        compiler_params=params(52),
+        compiler_params=params(20),
         cost_estimate=cost(6 * frames * width * width, 6 * width * width + 8 * frames * width),
-    )(normed, w_qkv, cos_table, sin_table)
+    )(normed, pltpu.with_memory_space_constraint(w_qkv, pltpu.VMEM), cos_table, sin_table)
 
 
 def only_head(values, which):
@@ -247,27 +249,20 @@
 
 def attend_kernel(span, q_ref, *refs):
     k_refs, v_refs = refs[:span], refs[span : 2 * span]
-    mk_ref, mq_ref, o_ref, p_ref, l_ref, bias_ref = refs[2 * span :]
+    mk_ref, mq_ref, o_ref, p_ref, l_ref = refs[2 * span :]
     frames = q_ref.shape[0]
-
-    @pl.when(pl.program_id(0) == 0)
-    def _():
-        seg_q, place_q = mq_ref[0:1, :], mq_ref[1:2, :]
-        for index in range(span):
-            rows = slice(index * frames, (index + 1) * frames)
-            seg_k, place_k, live_k = mk_ref[rows, 0:1], mk_ref[rows, 1:2], mk_ref[rows, 2:3]
-            allowed = (seg_q == seg_k) & ((live_k == 1) | (place_q == place_k))
-            bias_ref[rows, :] = jnp.where(allowed, 0.0, neg_fill)
-
     values_t = [v[...].T for v in v_refs]
     ones = jnp.ones((16, frames), BF)
+    keys = [
+        jnp.concatenate([k[...], mk_ref[i * frames : (i + 1) * frames, :]], axis=1)
+        for i, k in enumerate(k_refs)
+    ]
+    both = []
+    for which in range(2):
+        queries = jnp.concatenate([only_head(q_ref[...], which), mq_ref[...]], axis=1)
+        both.append([dot(k, queries, DIMS_LAST) for k in keys])
     results, inverses = [], []
-    for which in range(2):
-        queries = only_head(q_ref[...], which)
-        scores = [
-            dot(k[...], queries, DIMS_LAST) + bias_ref[i * frames : (i + 1) * frames, :]
-            for i, k in enumerate(k_refs)
-        ]
+    for which, scores in enumerate(both):
         top = functools.reduce(jnp.maximum, [jnp.max(s, axis=0, keepdims=True) for s in scores])
         result = None
         for index, part in enumerate(scores):
@@ -283,11 +278,21 @@
     l_ref[0] = jnp.concatenate(inverses + [jnp.zeros((6, frames), F32)], axis=0)
 
 
+def mask_lanes(segments, live, places, bucket_len):
+    lanes = jnp.arange(PAIR)[None, :]
+    segment = (lanes < SEGMENTS) & (segments[:, None] == lanes)
+    place = places[:, None] - (bucket_len - PADDING) == lanes - SEGMENTS
+    place = place & (lanes >= SEGMENTS) & (lanes < SEGMENTS + PADDING)
+    keys = (segment | (place & (live[:, None] == 0))).astype(BF)
+    fill = (lanes < SEGMENTS + PADDING) & ~(segment | place)
+    return keys, jnp.where(fill, neg_fill, 0.0).astype(BF)
+
+
 def columns(frames, start=0):
     return pl.BlockSpec((frames, PAIR), lambda i: (0, start + i))
 
 
-def attend(queries, pairs_kv, meta_k, meta_q):
+def attend(queries, pairs_kv, mask_keys, mask_queries):
     span = len(pairs_kv)
     frames, width = queries.shape
     pairs = width // PAIR
@@ -300,7 +305,7 @@
         + [columns(frames, pairs)] * span
         + [
             once((keys, PAIR)),
-            once((8, frames)),
+            once((frames, PAIR)),
         ],
         out_specs=[
             columns(frames),
@@ -312,14 +317,13 @@
             pltpu.HBM((2 * pairs, keys, frames), BF),
             jax.ShapeDtypeStruct((pairs, 8, frames), F32),
         ],
-        scratch_shapes=[pltpu.VMEM((keys, frames), F32)],
-        compiler_params=params(52),
+        compiler_params=params(28),
         cost_estimate=cost(
             16 * pairs * frames * keys * PAIR,
             4 * pairs * frames * keys,
             2 * pairs * frames * keys,
         ),
-    )(queries, *pairs_kv, *pairs_kv, meta_k, meta_q)
+    )(queries, *pairs_kv, *pairs_kv, mask_keys, mask_queries)
 
 
 def attend_back_kernel(span, q_ref, *refs):
@@ -667,19 +671,15 @@
     )(dq, *dkv, w_qkv, normed, grad_low, attended, cot_resid, scale, grad_low)
 
 
-def far_kernel(groups, count, *refs):
-    pieces, refs = refs[:count], refs[count:]
-    f_ref, gi_ref, m_refs = refs[0], refs[1], refs[2:6]
-    away_ref, keep_ref, t_ref, st_ref, u_ref, ft_ref = refs[6:]
+def far_kernel(groups, x_ref, y_ref, f_ref, gi_ref, *refs):
+    m_refs, (away_ref, keep_ref, t_ref, st_ref, u_ref, ft_ref) = refs[:4], refs[4:]
     low_bit = lax.axis_index("head") % 2
-    rows, width = pieces[0].shape[1], pieces[0].shape[2]
+    width = x_ref.shape[1]
 
     @pl.when(pl.program_id(0) == 0)
     def _():
-        for index, piece in enumerate(pieces):
-            here = slice(index * rows, (index + 1) * rows)
-            t_ref[:width, here] = piece[0].T
-            t_ref[width:, here] = piece[1].T
+        t_ref[:width, :] = x_ref[...].T
+        t_ref[width:, :] = y_ref[...].T
         split_rows(t_ref, st_ref, groups, low_bit)
         u_ref[...] = f_ref[...].T
         split_rows(u_ref, ft_ref, groups, low_bit)
@@ -698,7 +698,7 @@
                 out_ref[first : first + few, :] = small[block][index * few : (index + 1) * few]
 
 
-def far(pieces, features, grad_in, grad_mods):
+def far(inputs, skips, features, grad_in, grad_mods):
     groups = lax.axis_size("head")
     frames, width = grad_in.shape
     few = features.shape[1]
@@ -706,16 +706,16 @@
     cols = pl.BlockSpec((frames, tile), lambda i: (0, i))
     out = pl.BlockSpec((width + 2 * few, tile), lambda i: (0, i))
     return pl.pallas_call(
-        functools.partial(far_kernel, groups, len(pieces)),
+        functools.partial(far_kernel, groups),
         grid=(width // tile,),
-        in_specs=[once(piece.shape) for piece in pieces] + [once((frames, few))] + [cols] * 5,
+        in_specs=[once((frames, width)), once((frames, width)), once((frames, few))] + [cols] * 5,
         out_specs=[out, out],
         out_shape=[pltpu.HBM((width + 2 * few, width), BF)] * 2,
         scratch_shapes=[pltpu.VMEM((2 * width, frames), BF)] * 2
         + [pltpu.VMEM((few, frames), BF)] * 2,
         compiler_params=params(52),
         cost_estimate=cost(6 * frames * width * width, 6 * width * width + 20 * frames * width),
-    )(*pieces, features, grad_in, *grad_mods)
+    )(inputs, skips, features, grad_in, *grad_mods)
 
 
 def per_device(
@@ -781,41 +781,33 @@
     keys_values, seg_keys, live_keys, place_keys, times = together(
         keys_values, seg_keys, live_keys, place_keys, times
     )
+    pairs_kv = [keys_values] + [swap(keys_values, "head", other) for other in range(1, span)]
+    mask_keys, mask_queries = mask_lanes(seg_keys, live_keys, place_keys, groups * rows)
+    queries, mask_keys, mask_queries, *pairs_kv = together(
+        queries, mask_keys, mask_queries[:frames], *pairs_kv
+    )
+
+    second = send_parts(second, span)
+    attended, probs, inverses = attend(queries, pairs_kv, mask_keys, mask_queries)
+    attended, times = together(attended, times)
     features = time_features(times[:frames], feature_count)
     scale_first, shift_second, scale_second = [
         dot(features, w_time[:, i * width : (i + 1) * width]) for i in range(1, 4)
     ]
-    pairs_kv = [keys_values] + [swap(keys_values, "head", other) for other in range(1, span)]
-    meta_q = jnp.stack(
-        [seg_keys[:frames], place_keys[:frames]] + [jnp.zeros((frames,), F32)] * 6
-    )
-    meta_k = jnp.stack([seg_keys, place_keys, live_keys], axis=1)
-    meta_k = jnp.pad(meta_k, ((0, 0), (0, PAIR - 3)))
-    queries, meta_k, meta_q, scale_first, shift_second, scale_second, *pairs_kv = together(
-        queries, meta_k, meta_q, scale_first, shift_second, scale_second, *pairs_kv
-    )
-
-    second = send_parts(second, span)
-    attended, probs, inverses = attend(queries, pairs_kv, meta_k, meta_q)
-    attended, inputs, skips = together(attended, inputs, skips)
-    joined = cut_pairs(inputs, skips, mine)
-    attended, *rest = together(attended, *second, *joined)
-    second, joined = rest[:micro_count], rest[micro_count:]
+    attended, scale_first, shift_second, scale_second, *second = together(
+        attended, scale_first, shift_second, scale_second, *second
+    )
     second = jnp.concatenate(second)
     resid_mid = second[:, width:].astype(F32) + dot(attended, w_out)
     normal_second = norm_stats(resid_mid)[0]
     normed_ffn = (normal_second * (1.0 + scale_second) + shift_second).astype(BF)
 
-    normed_ffn, *joined = together(normed_ffn, *joined)
-    joined = send_parts(joined, span)
     (
         down_away, down_keep, up_away, up_keep, output, grad_mid, mod_shift, mod_scale, grads, centres
     ) = feed(
         normed_ffn, second, w_up, w_down, resid_mid, scale_second, w_out, attended, inverses
     )
-    grads, down_away, up_away, output, *joined = together(
-        grads, down_away, up_away, output, *joined
-    )
+    grads, down_away, up_away, output = together(grads, down_away, up_away, output)
     seq_bits = lax.axis_size("seq").bit_length() - 1
     bits = list(range(seq_bits + 1, seq_bits + groups.bit_length() - 1))
     orders = (bits, bits[::-1])
@@ -848,9 +840,10 @@
     half = up_keep.shape[1] // 2
     up_0 = add_low([up_keep[:, :half], up_came[:, :half]])
     up_1 = add_low([up_keep[:, half:], up_came[:, half:]])
-    dq, up_0, up_1, *rest = together(dq, up_0, up_1, *begin(down, index=0), *dkv)
-    away, dkv = rest[:2], rest[2:]
+    dq, up_0, up_1, down_came, *dkv = together(dq, up_0, up_1, down_came, *dkv)
     up_0 = seq_first(up_0)
+    down = two_ways(down_keep, down_came)
+    dq, *away = together(dq, *begin(down, index=0))
     came = send(away, 0)
     near_away, near_keep, grad_in_low, first_shift, first_scale = near(
         dq, dkv, w_qkv, normed_attn, attended, grad_mid, second, scale_first
@@ -864,44 +857,47 @@
     last_index = len(bits) - 1
     grad_in_low, *away = together(grad_in_low, *begin(down, index=last_index))
     came = send(away, last_index)
+    grad_local = send_parts(list(grad_in_low.reshape(micro_count, rows, width)), span)
+    wide = two_ways(near_keep, near_came)
+    up_0, *rest = together(up_0, *begin(wide, index=0), *came, *grad_local)
+    wide_away, came, grad_local = rest[:2], rest[2:4], rest[4:]
+    end(down, came=came)
+
+    wide_came = send(wide_away, 0)
+    grad_local = by_micro(grad_local, mine).reshape(frames, width)
     far_away, far_keep = far(
-        joined, features, grad_in_low, [first_shift, first_scale, mod_shift, mod_scale]
-    )
-    wide = two_ways(near_keep, near_came)
-    far_away, up_0, *rest = together(far_away, up_0, *begin(wide, index=0), *came)
-    wide_away, came = rest[:2], rest[2:]
-    end(down, came=came)
-
-    far_came = swap(far_away, "head", 1)
-    wide_came = send(wide_away, 0)
-    grad_local = send_parts(list(grad_in_low.reshape(micro_count, rows, width)), span)
-    narrow = two_ways(far_keep, far_came)
+        inputs.reshape(frames, width),
+        skips.reshape(frames, width),
+        features,
+        grad_local,
+        [first_shift, first_scale, mod_shift, mod_scale],
+    )
     up_1 = seq_first(up_1)
     down_rows = jnp.concatenate([part.read() for part in down], axis=1)
-    rest = together(*begin(narrow, index=0), up_1, *wide_came, down_rows, *grad_local)
-    narrow_away, up_1, wide_came = rest[:2], rest[2], rest[3:5]
-    down_rows, grad_local = rest[5], rest[6:]
+    far_away, down_rows, *wide_came = together(far_away, down_rows, *wide_came)
     end(wide, came=wide_came)
-    (down_sum,) = last_sum(down_rows)
-    narrow_came = send(narrow_away, 0)
+
+    far_came = swap(far_away, "head", 1)
+    narrow = two_ways(far_keep, far_came)
     for index in range(1, len(bits)):
         wide_came = send(begin(wide, index=index), index)
         if index < last_index:
-            rest = together(*narrow_came, *wide_came)
-            end(narrow, came=rest[:2])
-            end(wide, came=rest[2:])
-            narrow_came = send(begin(narrow, index=index), index)
+            end(wide, came=together(*wide_came))
+    (down_sum,) = last_sum(down_rows)
+    up_1, *rest = together(up_1, *begin(narrow, index=0), *wide_came)
+    narrow_away, wide_came = rest[:2], rest[2:]
     end(wide, came=wide_came)
+
+    narrow_came = send(narrow_away, 0)
+    wide_sum = jnp.concatenate([wide[0].read(), wide[1].read()], axis=1)
     ups = [Rows([up_0], bits), Rows([up_1], bits)]
-    wide_sum = jnp.concatenate([wide[0].read(), wide[1].read()], axis=1)
-    wide_sum, down_sum, *rest = together(
-        wide_sum, down_sum, *begin(ups, index=0), *narrow_came
-    )
-    up_away = rest[:2]
-    end(narrow, came=rest[2:])
-    narrow_came = send(begin(narrow, index=last_index), last_index)
+    rest = together(wide_sum, down_sum, *begin(ups, index=0), *narrow_came)
+    wide_sum, down_sum, up_away = rest[0], rest[1], rest[2:4]
+    end(narrow, came=rest[4:])
+
     (near_sum,) = last_sum(wide_sum)
-    end(narrow, came=together(*narrow_came))
+    for index in range(1, len(bits)):
+        end(narrow, came=together(*send(begin(narrow, index=index), index)))
     far_sum = jnp.concatenate([narrow[0].read(), narrow[1].read()], axis=1)
     many = w_skip.shape[0] // groups
     last = [
@@ -914,18 +910,24 @@
             came = [cross(away_all(last, index), index)]
         if index < len(bits):
             up_came = send(up_away, index)
-        near_sum, *rest = together(near_sum, *came, *up_came)
+        if index == 0:
+            near_sum, *rest = together(near_sum, *came, *up_came)
+            done = [
+                by_micro(output, mine),
+                near_sum[:, : 3 * width].astype(F32),
+                near_sum[:, 3 * width :].astype(F32),
+                down_sum.astype(F32),
+            ]
+        else:
+            *done, rest = together(*done, [*came, *up_came])
         if index < seq_bits:
             join_all(last, rest[0])
         if index < len(bits):
             end(ups, came=rest[len(came) :])
         if index + 1 < len(bits):
             up_away = begin(ups, index=index + 1)
-    output = by_micro(output, mine)
-    grad_local = by_micro(grad_local, mine).reshape(frames, width)
-    total_down, near_sum = down_sum.astype(F32), near_sum.astype(F32)
+    output, total_qkv, total_out, total_down = done
     total_up = jnp.concatenate([part.read() for part in ups], axis=1).astype(F32)
-    total_qkv, total_out = near_sum[:, : 3 * width], near_sum[:, 3 * width :]
     total_skip = last[0].read().astype(F32)
     total_time = last[1].read().astype(F32)
     total_time = total_time.reshape(4, -1, width).swapaxes(0, 1).reshape(-1, 4 * width)

time: 370 us -> 351 us (0.949)
  Pallas kernels: 123 us -> 117 us
  waiting for transfers between devices: 84.3 us -> 78.5 us
  local copies, waits for them, and re-layouts: 19.4 us -> 14.2 us
    reduce_scatter x2, waiting for transfers between devices: 0.01 us -> 12.4 us  [last_sum(): total = lax.psum_scatter(joint, 'seq', scatter_dimension=0, tiled=True)]
    ppermute x42 -> x39, waiting for transfers between devices: 75.1 us -> 66 us  [swap(): return lax.ppermute(values, axis_name, [(i, i ^ bits) for i in range(size)])]
    reduce_scatter x2, waiting for transfers between devices: 9.1 us -> 0.04 us  [seq_first(): return lax.psum_scatter(rows, 'seq', scatter_dimension=0, tiled=True)]
    ppermute x42 -> x39, starting transfers between devices: 44.2 us -> 41.6 us  [swap(): return lax.ppermute(values, axis_name, [(i, i ^ bits) for i in range(size)])]
    convert_element_type x18 -> x19, other arithmetic: 37.8 us -> 35.8 us  [add_low(): functools.reduce(jnp.add, [term.astype(F32) for term in terms]).astype(BF)]
    unnamed x72 -> x112, local copies, waits for them, and re-layouts: 7.8 us -> 7.96 us
  transfers between devices with their start and end apart: 46 -> 43, of which waited for: 16 -> 21; matrix products, arithmetic and copies ran while one was open for 20% -> 20% of each run, Pallas kernels for 31% -> 19%
where the time goes in v5:
time: 351 us; the launch traced here: 347 us
  Pallas kernels  117 us (33%)
  waiting for transfers between devices  78.5 us (22%)
  other arithmetic  64.2 us (18%)
  starting transfers between devices  42 us (12%)
  matrix products  16.1 us (5%)
  between operations  15 us (4%)
  local copies, waits for them, and re-layouts  14.2 us (4%)
    ppermute x39, waiting for transfers between devices, swap(): return lax.ppermute(values, axis_name, [(i, i ^ bits) for i in range(size)])  66 us
    pallas_call x1, Pallas kernels, feed(): pl.pallas_call(functools.partial(feed_kernel, groups, seq_blocks(width)),...  42.6 us
    ppermute x39, starting transfers between devices, swap(): return lax.ppermute(values, axis_name, [(i, i ^ bits) for i in range(size)])  41.6 us
    convert_element_type x19, other arithmetic, add_low(): functools.reduce(jnp.add, [term.astype(F32) for term in terms]).astype(BF)  35.8 us
    pallas_call x1, Pallas kernels, attend_back(): pl.pallas_call(functools.partial(attend_back_kernel, span), grid=(pairs,)...  23.2 us
    pallas_call x1, Pallas kernels, near(): pl.pallas_call(functools.partial(near_kernel, groups, len(dkv)), grid=(4...  18.1 us
    pallas_call x1, Pallas kernels, attend(): pl.pallas_call(functools.partial(attend_kernel, span), grid=(pairs,), in_...  17.1 us
    dot_general x9, matrix products, dot(): return lax.dot_general(left, right, dims, preferred_element_type=F32)  16.1 us
  transfers between devices with their start and end apart: 43, of which 21 were waited for; matrix products, arithmetic and copies ran while one was open for 20% of the time, Pallas kernels for 19%

profile of v5, /device:TPU:0, one launch (start us, length us, event | category | flops | bytes accessed | tf_op | source)
XLA Modules:
  0.0 347.0 jit_solution(17742252616405691408)
XLA Ops:
  10.5 3.3 fusion.7
  23.2 2.6 collective-permute-start.1
  25.9 2.0 collective-permute-start.4
  29.3 1.6 collective-permute-start.2
  30.9 8.8 %collective-permute-done.2 = f32[4,4,3,128]{3,1,2,0:T(4,128)S(1)} collective-permute-done((f32[4,4,3,128]{3,1,2,0:T(4,128)S(1)}, f32[4,4,3,128]{3,1,2,0:T(4,128)S(1)}, u32[]{:S(2)}, u32[]{:S(2)}) %collective-permute-start.2) | collective-permute-done | bytes 24608 | tf_op jit(solution)/shard_map/ppermute | solution.py:30
  41.5 1.9 fusion.66
  44.6 2.8 copy-done.1
  47.4 7.6 %shard_map.187 = (bf16[512,1024]{1,0:T(8,128)(2,1)S(1)}, bf16[512,2048]{1,0:T(8,128)(2,1)S(1)}) custom-call(bf16[512,1024]{1,0:T(8,128)(2,1)S(1)} %constant_dynamic-update-slice_fusion.x_ref.refs_4_, bf16[1024,3072]{1,0:T(8,128)(2,1)S(1)} %copy-done.1, f32[512,128]{1,0:T(8,128)S(1)} %slice.125.cos_ref, f32[512,128]{1,0:T(8,128)S(1)} %slice.126.sin_ref), custom_call_target="tpu_custom_call" | custom-call | flops 3221225472 | bytes 10485760 | tf_op jit(solution)/shard_map/pallas_call | solution.py:222
  56.6 1.5 collective-permute-start.8
  59.7 17.1 %shard_map.188 = (bf16[512,1024]{1,0:T(8,128)(2,1)S(1)}, bf16[16,1024,512]{2,1,0:T(8,128)(2,1)}, f32[8,8,512]{2,1,0:T(8,128)S(1)}) custom-call(bf16[512,1024]{1,0:T(8,128)(2,1)S(1)} %get-tuple-element.150.q_ref, bf16[512,2048]{1,0:T(8,128)(2,1)S(1)} %get-tuple-element.151.refs_0_.refs_2_, bf16[512,2048]{1,0:T(8,128)(2,1)S(1)} %collective-permute-done.6.refs_1_.refs_3_, ...), custom_call_target="tpu_custom_call" | custom-call | flops 8589934592 | bytes 16777216 | tf_op jit(solution)/shard_map/pallas_call | solution.py:300
  78.3 1.7 fusion.46.refs_8_
  86.4 42.6 %shard_map.189 = (bf16[2048,1024]{1,0:T(8,128)(2,1)}, bf16[2048,1024]{1,0:T(8,128)(2,1)}, bf16[512,4096]{1,0:T(8,128)(2,1)}, bf16[512,4096]{1,0:T(8,128)(2,1)}, ...) custom-call(bf16[512,1024]{1,0:T(8,128)(2,1)} %add_convert_fusion.6., ...), custom_call_target="tpu_custom_call" | custom-call | flops 25769803776 | bytes 33554432 | tf_op jit(solution)/shard_map/pallas_call | solution.py:508
  131.7 1.5 collective-permute-start.13
  133.8 23.2 %shard_map.190 = (bf16[512,1024]{1,0:T(8,128)(2,1)}, bf16[2,512,1024]{2,1,0:T(8,128)(2,1)}, bf16[2,512,1024]{2,1,0:T(8,128)(2,1)}) custom-call(bf16[512,1024]{1,0:T(8,128)(2,1)} %copy-done.6, bf16[512,2048]{1,0:T(8,128)(2,1)} %copy-done.2, bf16[512,2048]{1,0:T(8,128)(2,1)} %copy-done.3, bf16[512,2048]{1,0:T(8,128)(2,1)} %copy-done.2, ...), custom_call_target="tpu_custom_call" | custom-call | flops 17179869184 | bytes 16777216 | tf_op jit(solution)/shard_map/pallas_call | solution.py:370
  157.2 6.1 %add_convert_fusion = (bf16[512,2048]{1,0:T(8,128)(2,1)}, bf16[512,2048]{1,0:T(8,128)(2,1)}) fusion(bf16[512,4096]{1,0:T(8,128)(2,1)} %collective-permute-done.11, bf16[512,4096]{1,0:T(8,128)(2,1)} %get-tuple-element.189), kind=kLoop, calls=%fused_computation | loop fusion | flops 8388608 | bytes 12582912 | tf_op jit(solution)/shard_map/convert_element_type | solution.py:62
  163.3 2.9 add_convert_fusion.5
  166.2 2.9 add_convert_fusion.4
  172.1 18.1 %shard_map.191 = (bf16[512,4096]{1,0:T(8,128)(2,1)}, bf16[512,4096]{1,0:T(8,128)(2,1)}, bf16[512,1024]{1,0:T(8,128)(2,1)S(1)}, bf16[512,1024]{1,0:T(8,128)(2,1)}, bf16[512,1024]{1,0:T(8,128)(2,1)}) custom-call(bf16[512,1024]{1,0:T(8,128)(2,1)} %get-tuple-element.197.refs_0_, bf16[2,512,1024]{2,1,0:T(8,128)(2,1)} %get-tuple-element.198.refs_1_, ...), custom_call_target="tpu_custom_call" | custom-call | flops 7516192768 | bytes 30408704 | tf_op jit(solution)/shard_map/pallas_call | solution.py:646
  190.2 4.6 %collective-permute-done.16 = bf16[1024,512]{1,0:T(8,128)(2,1)} collective-permute-done((bf16[1024,512]{1,0:T(8,128)(2,1)}, bf16[1024,512]{1,0:T(8,128)(2,1)}, u32[]{:S(2)}, u32[]{:S(2)}) %collective-permute-start.16) | collective-permute-done | bytes 1048608 | tf_op jit(solution)/shard_map/ppermute | solution.py:30
  197.4 2.5 fusion.31
  199.9 1.5 collective-permute-start.19
  202.8 1.5 collective-permute-start.21
  206.3 2.6 add_convert_fusion.3
  208.9 2.6 add_convert_fusion.2
  211.5 10.4 %collective-permute-done.21 = bf16[128,1024]{1,0:T(8,128)(2,1)S(1)} collective-permute-done((bf16[128,1024]{1,0:T(8,128)(2,1)S(1)}, bf16[128,1024]{1,0:T(8,128)(2,1)S(1)}, u32[]{:S(2)}, u32[]{:S(2)}) %collective-permute-start.21) | collective-permute-done | bytes 262176 | tf_op jit(solution)/shard_map/ppermute | solution.py:30
  221.9 4.8 %collective-permute-done.23 = bf16[128,1024]{1,0:T(8,128)(2,1)S(1)} collective-permute-done((bf16[128,1024]{1,0:T(8,128)(2,1)S(1)}, bf16[128,1024]{1,0:T(8,128)(2,1)S(1)}, u32[]{:S(2)}, u32[]{:S(2)}) %collective-permute-start.23) | collective-permute-done | bytes 262176 | tf_op jit(solution)/shard_map/ppermute | solution.py:30
  228.9 2.7 fusion.30
  237.0 8.4 %shard_map.192 = (bf16[1536,1024]{1,0:T(8,128)(2,1)}, bf16[1536,1024]{1,0:T(8,128)(2,1)}) custom-call(bf16[512,1024]{1,0:T(8,128)(2,1)S(1)} %bitcast.247, bf16[512,1024]{1,0:T(8,128)(2,1)} %bitcast.310, bf16[512,256]{1,0:T(8,128)(2,1)S(1)} %pad_maximum_fusion.14.f_ref, bf16[512,1024]{1,0:T(8,128)(2,1)} %bitcast.269, ...), custom_call_target="tpu_custom_call" | custom-call | flops 3221225472 | bytes 16777216 | tf_op jit(solution)/shard_map/pallas_call | solution.py:708
  245.4 6.1 %collective-permute-done.24 = bf16[256,2048]{1,0:T(8,128)(2,1)} collective-permute-done((bf16[256,2048]{1,0:T(8,128)(2,1)}, bf16[256,2048]{1,0:T(8,128)(2,1)}, u32[]{:S(2)}, u32[]{:S(2)}) %collective-permute-start.24) | collective-permute-done | bytes 1048608 | tf_op jit(solution)/shard_map/ppermute | solution.py:30
  252.4 3.6 %fusion.23 = (bf16[128,2048]{1,0:T(8,128)(2,1)}, bf16[128,2048]{1,0:T(8,128)(2,1)}) fusion(bf16[1,2,128,2048]{3,2,1,0:T(8,128)(2,1)} %bitcast.74, s32[]{:T(128)S(6)} %select_n.213, bf16[1,2,2,128,4096]{4,3,2,1,0:T(8,128)(2,1)} %bitcast.46, s32[]{:T(128)S(6)} %select_n.216, bf16[1,2,2,128,4096]{4,3,2,1,0:T(8,128)(2,1)} %bitcast.252, ...), kind=kLoop, calls=%fused_computation.40 | loop fusion | flops 3145728 | bytes 4194320 | tf_op jit(solution)/shard_map/convert_element_type | solution.py:62
  256.0 1.5 collective-permute-start.27
  262.3 8.2 %collective-permute-done.27 = bf16[128,2048]{1,0:T(8,128)(2,1)S(1)} collective-permute-done((bf16[128,2048]{1,0:T(8,128)(2,1)}, bf16[128,2048]{1,0:T(8,128)(2,1)S(1)}, u32[]{:S(2)}, u32[]{:S(2)}) %collective-permute-start.27) | collective-permute-done | bytes 524320 | tf_op jit(solution)/shard_map/ppermute | solution.py:30
  274.3 2.9 fusion.26
  279.0 11.5 %reduce-scatter.9.cloned.1.call-done = bf16[128,1024]{1,0:T(8,128)(2,1)} async-done(((bf16[512,1024]{1,0:T(8,128)(2,1)}), bf16[128,1024]{1,0:T(8,128)(2,1)}) %reduce-scatter.9.cloned.1.call-update) | async-done | bytes 262160 | tf_op jit(solution)/shard_map/reduce_scatter | solution.py:141
  292.4 1.9 fusion.37
  295.8 4.2 %fusion.12 = f32[4,1,128,1024]{3,2,1,0:T(8,128)} fusion(bf16[2048,1024]{1,0:T(8,128)(2,1)} %param.18, bf16[1,128,1024]{2,1,0:T(8,128)(2,1)S(1)} %copy-done.25, bf16[1,128,1024]{2,1,0:T(8,128)(2,1)S(1)} %copy-done.27, bf16[1,128,1024]{2,1,0:T(8,128)(2,1)S(1)} %copy-done.29, bf16[1,128,1024]{2,1,0:T(8,128)(2,1)S(1)} %copy-done.23), kind=kOutput, calls=%fused_computation.25 | convolution fusion | flops 1075314688 | bytes 5242880 | tf_op jit(solution)/shard_map/dot_general | solution.py:25
  302.7 2.8 collective-permute-done.31
  305.4 1.7 collective-permute-done.32
  307.1 2.1 fusion.40
  309.4 1.7 collective-permute-start.33
  311.0 2.6 fusion.15
  317.0 8.6 %collective-permute-done.33 = bf16[192,1024]{1,0:T(8,128)(2,1)S(1)} collective-permute-done((bf16[192,1024]{1,0:T(8,128)(2,1)S(1)}, bf16[192,1024]{1,0:T(8,128)(2,1)S(1)}, u32[]{:S(2)}, u32[]{:S(2)}) %collective-permute-start.33) | collective-permute-done | bytes 393248 | tf_op jit(solution)/shard_map/ppermute | solution.py:30
  326.6 1.7 slice_convert_fusion
  328.4 1.6 collective-permute-start.36
  330.0 1.5 collective-permute-start.37
  331.6 1.7 collective-permute-start.38
  333.4 1.5 slice_convert_fusion.1
  335.1 1.6 collective-permute-done.38
  (269 shorter events, 73.2 us)
Async XLA Ops:
  7.2 219.6 %reduce-scatter.5.cloned.1.call-start = ((), (), s32[]{:S(2)}) async-start(), calls=%async_computation.4 | async-start | bytes 2621440 | tf_op jit(solution)/shard_map/reduce_scatter | solution.py:128
  9.3 13.9 %collective-permute-start = (f32[1,4,3,128]{3,1,2,0:T(4,128)S(1)}, f32[1,4,3,128]{3,1,2,0:T(4,128)S(1)}, u32[]{:S(2)}, u32[]{:S(2)}) collective-permute-start(f32[1,4,3,128]{3,1,2,0:T(4,128)S(1)} %bitcast.304), channel_id=1, source_target_pairs={{0,4},{4,0},{8,12},{12,8},{16,20},{20,16},{24,28},{28,24},{1,5},{5... | collective-permute-start | bytes 18440 | tf_op jit(solution)/shard_map/ppermute | solution.py:30
  23.2 6.1 %collective-permute-start.1 = (f32[2,4,3,128]{3,1,2,0:T(4,128)S(1)}, f32[2,4,3,128]{3,1,2,0:T(4,128)S(1)}, u32[]{:S(2)}, u32[]{:S(2)}) collective-permute-start(f32[2,4,3,128]{3,1,2,0:T(4,128)S(1)} %pad_maximum_fusion.18), channel_id=1, source_target_pairs={{0,8},{4,12},{8,0},{12,4},{16,24},{20,28},{24,16},{28,20},{1,9},{5... | collective-permute-start | bytes 36872 | tf_op jit(solution)/shard_map/ppermute | solution.py:30
  25.8 13.9 %collective-permute-start.3 = (bf16[128,1024]{1,0:T(8,128)(2,1)S(1)}, bf16[128,1024]{1,0:T(8,128)(2,1)S(1)}, u32[]{:S(2)}, u32[]{:S(2)}) collective-permute-start(bf16[128,1024]{1,0:T(8,128)(2,1)S(1)} %get-tuple-element.136), channel_id=1, source_target_pairs={{0,8},{4,12},{8,0},{12,4},{16,24},{20,28},{24,16},{28,20},{1,9},{5... | collective-permute-start | bytes 786440 | tf_op jit(solution)/shard_map/ppermute | solution.py:30
  25.9 13.9 %collective-permute-start.4 = (bf16[128,1024]{1,0:T(8,128)(2,1)S(1)}, bf16[128,1024]{1,0:T(8,128)(2,1)S(1)}, u32[]{:S(2)}, u32[]{:S(2)}) collective-permute-start(bf16[128,1024]{1,0:T(8,128)(2,1)S(1)} %get-tuple-element.137), channel_id=1, source_target_pairs={{0,16},{4,20},{8,24},{12,28},{16,0},{20,4},{24,8},{28,12},{1,17},{... | collective-permute-start | bytes 786440 | tf_op jit(solution)/shard_map/ppermute | solution.py:30
  27.9 12.9 %collective-permute-start.5 = (bf16[128,1024]{1,0:T(8,128)(2,1)S(1)}, bf16[128,1024]{1,0:T(8,128)(2,1)S(1)}, u32[]{:S(2)}, u32[]{:S(2)}) collective-permute-start(bf16[128,1024]{1,0:T(8,128)(2,1)S(1)} %get-tuple-element.138), channel_id=1, source_target_pairs={{0,24},{4,28},{8,16},{12,20},{16,8},{20,12},{24,0},{28,4},{1,25},{... | collective-permute-start | bytes 786440 | tf_op jit(solution)/shard_map/ppermute | solution.py:30
  29.3 10.4 %collective-permute-start.2 = (f32[4,4,3,128]{3,1,2,0:T(4,128)S(1)}, f32[4,4,3,128]{3,1,2,0:T(4,128)S(1)}, u32[]{:S(2)}, u32[]{:S(2)}) collective-permute-start(f32[4,4,3,128]{3,1,2,0:T(4,128)S(1)} %pad_maximum_fusion.17), channel_id=1, source_target_pairs={{0,16},{4,20},{8,24},{12,28},{16,0},{20,4},{24,8},{28,12},{1,17},{... | collective-permute-start | bytes 73736 | tf_op jit(solution)/shard_map/ppermute | solution.py:30
  55.0 21.9 %copy-start.2 = (bf16[512,2048]{1,0:T(8,128)(2,1)}, bf16[512,2048]{1,0:T(8,128)(2,1)S(1)}, u32[]{:S(2)}) copy-start(bf16[512,2048]{1,0:T(8,128)(2,1)S(1)} %get-tuple-element.151.refs_0_.refs_2_) | copy-start | bytes 6291460
  55.0 21.9 %copy-start.6 = (bf16[512,1024]{1,0:T(8,128)(2,1)}, bf16[512,1024]{1,0:T(8,128)(2,1)S(1)}, u32[]{:S(2)}) copy-start(bf16[512,1024]{1,0:T(8,128)(2,1)S(1)} %get-tuple-element.150.q_ref) | copy-start | bytes 3145732
  55.0 4.7 %collective-permute-start.6 = (bf16[512,2048]{1,0:T(8,128)(2,1)S(1)}, bf16[512,2048]{1,0:T(8,128)(2,1)S(1)}, u32[]{:S(2)}, u32[]{:S(2)}) collective-permute-start(bf16[512,2048]{1,0:T(8,128)(2,1)S(1)} %get-tuple-element.151.refs_0_.refs_2_), channel_id=1, source_target_pairs={{0,4},{4,0},{8,12},{12,8},{16,20},{20,16},{24,28},{28,24},{1,5},{5... | collective-permute-start | bytes 6291464 | tf_op jit(solution)/shard_map/ppermute | solution.py:30
  55.2 25.7 %collective-permute-start.7 = (bf16[128,2048]{1,0:T(8,128)(2,1)S(1)}, bf16[128,2048]{1,0:T(8,128)(2,1)S(1)}, u32[]{:S(2)}, u32[]{:S(2)}) collective-permute-start(bf16[128,2048]{1,0:T(8,128)(2,1)S(1)} %pad_maximum_fusion.7), channel_id=1, source_target_pairs={{0,8},{4,12},{8,0},{12,4},{16,24},{20,28},{24,16},{28,20},{1,9},{5... | collective-permute-start | bytes 1572872 | tf_op jit(solution)/shard_map/ppermute | solution.py:30
  56.6 25.3 %collective-permute-start.8 = (bf16[128,2048]{1,0:T(8,128)(2,1)S(1)}, bf16[128,2048]{1,0:T(8,128)(2,1)S(1)}, u32[]{:S(2)}, u32[]{:S(2)}) collective-permute-start(bf16[128,2048]{1,0:T(8,128)(2,1)S(1)} %pad_maximum_fusion.8), channel_id=1, source_target_pairs={{0,16},{4,20},{8,24},{12,28},{16,0},{20,4},{24,8},{28,12},{1,17},{... | collective-permute-start | bytes 1572872 | tf_op jit(solution)/shard_map/ppermute | solution.py:30
  58.1 23.8 %collective-permute-start.9 = (bf16[128,2048]{1,0:T(8,128)(2,1)S(1)}, bf16[128,2048]{1,0:T(8,128)(2,1)S(1)}, u32[]{:S(2)}, u32[]{:S(2)}) collective-permute-start(bf16[128,2048]{1,0:T(8,128)(2,1)S(1)} %pad_maximum_fusion.9), channel_id=1, source_target_pairs={{0,24},{4,28},{8,16},{12,20},{16,8},{20,12},{24,0},{28,4},{1,25},{... | collective-permute-start | bytes 1572872 | tf_op jit(solution)/shard_map/ppermute | solution.py:30
  59.7 17.2 %copy-start.3 = (bf16[512,2048]{1,0:T(8,128)(2,1)}, bf16[512,2048]{1,0:T(8,128)(2,1)S(1)}, u32[]{:S(2)}) copy-start(bf16[512,2048]{1,0:T(8,128)(2,1)S(1)} %collective-permute-done.6.refs_1_.refs_3_) | copy-start | bytes 6291460
  59.7 18.5 %copy-start.11 = (bf16[256,4096]{1,0:T(8,128)(2,1)S(1)}, bf16[256,4096]{1,0:T(8,128)(2,1)}, u32[]{:S(2)}) copy-start(bf16[256,4096]{1,0:T(8,128)(2,1)} %param.19) | copy-start | bytes 6291460
  129.0 28.1 %collective-permute-start.10 = (bf16[2048,1024]{1,0:T(8,128)(2,1)}, bf16[2048,1024]{1,0:T(8,128)(2,1)}, u32[]{:S(2)}, u32[]{:S(2)}) collective-permute-start(bf16[2048,1024]{1,0:T(8,128)(2,1)} %get-tuple-element.179), channel_id=1, source_target_pairs={{0,4},{4,0},{8,12},{12,8},{16,20},{20,16},{24,28},{28,24},{1,5},{5... | collective-permute-start | bytes 12582920 | tf_op jit(solution)/shard_map/ppermute | solution.py:30
  129.0 28.0 %collective-permute-start.11 = (bf16[512,4096]{1,0:T(8,128)(2,1)}, bf16[512,4096]{1,0:T(8,128)(2,1)}, u32[]{:S(2)}, u32[]{:S(2)}) collective-permute-start(bf16[512,4096]{1,0:T(8,128)(2,1)} %get-tuple-element.180), channel_id=1, source_target_pairs={{0,4},{4,0},{8,12},{12,8},{16,20},{20,16},{24,28},{28,24},{1,5},{5... | collective-permute-start | bytes 12582920 | tf_op jit(solution)/shard_map/ppermute | solution.py:30
  130.3 26.7 %collective-permute-start.12 = (bf16[128,1024]{1,0:T(8,128)(2,1)S(1)}, bf16[128,1024]{1,0:T(8,128)(2,1)S(1)}, u32[]{:S(2)}, u32[]{:S(2)}) collective-permute-start(bf16[128,1024]{1,0:T(8,128)(2,1)S(1)} %get-tuple-element.343), channel_id=1, source_target_pairs={{0,8},{4,12},{8,0},{12,4},{16,24},{20,28},{24,16},{28,20},{1,9},{5... | collective-permute-start | bytes 786440 | tf_op jit(solution)/shard_map/ppermute | solution.py:30
  131.7 25.3 %collective-permute-start.13 = (bf16[128,1024]{1,0:T(8,128)(2,1)S(1)}, bf16[128,1024]{1,0:T(8,128)(2,1)S(1)}, u32[]{:S(2)}, u32[]{:S(2)}) collective-permute-start(bf16[128,1024]{1,0:T(8,128)(2,1)S(1)} %get-tuple-element.342), channel_id=1, source_target_pairs={{0,16},{4,20},{8,24},{12,28},{16,0},{20,4},{24,8},{28,12},{1,17},{... | collective-permute-start | bytes 786440 | tf_op jit(solution)/shard_map/ppermute | solution.py:30
  133.2 23.8 %collective-permute-start.14 = (bf16[128,1024]{1,0:T(8,128)(2,1)S(1)}, bf16[128,1024]{1,0:T(8,128)(2,1)S(1)}, u32[]{:S(2)}, u32[]{:S(2)}) collective-permute-start(bf16[128,1024]{1,0:T(8,128)(2,1)S(1)} %get-tuple-element.341), channel_id=1, source_target_pairs={{0,24},{4,28},{8,16},{12,20},{16,8},{20,12},{24,0},{28,4},{1,25},{... | collective-permute-start | bytes 786440 | tf_op jit(solution)/shard_map/ppermute | solution.py:30
  157.1 6.3 %collective-permute-start.15 = (bf16[2,512,1024]{2,1,0:T(8,128)(2,1)}, bf16[2,512,1024]{2,1,0:T(8,128)(2,1)}, u32[]{:S(2)}, u32[]{:S(2)}) collective-permute-start(bf16[2,512,1024]{2,1,0:T(8,128)(2,1)} %get-tuple-element.193), channel_id=1, source_target_pairs={{0,4},{4,0},{8,12},{12,8},{16,20},{20,16},{24,28},{28,24},{1,5},{5... | collective-permute-start | bytes 6291464 | tf_op jit(solution)/shard_map/ppermute | solution.py:30
  169.1 25.8 %collective-permute-start.16 = (bf16[1024,512]{1,0:T(8,128)(2,1)}, bf16[1024,512]{1,0:T(8,128)(2,1)}, u32[]{:S(2)}, u32[]{:S(2)}) collective-permute-start(bf16[1024,512]{1,0:T(8,128)(2,1)} %bitcast.43), channel_id=1, source_target_pairs={{0,8},{4,12},{8,0},{12,4},{16,24},{20,28},{24,16},{28,20},{1,9},{5... | collective-permute-start | bytes 3145736 | tf_op jit(solution)/shard_map/ppermute | solution.py:30
  170.5 25.5 %collective-permute-start.17 = (bf16[1024,512]{1,0:T(8,128)(2,1)}, bf16[1024,512]{1,0:T(8,128)(2,1)}, u32[]{:S(2)}, u32[]{:S(2)}) collective-permute-start(bf16[1024,512]{1,0:T(8,128)(2,1)} %bitcast.44), channel_id=1, source_target_pairs={{0,16},{4,20},{8,24},{12,28},{16,0},{20,4},{24,8},{28,12},{1,17},{... | collective-permute-start | bytes 3145736 | tf_op jit(solution)/shard_map/ppermute | solution.py:30
  172.0 90.3 %reduce-scatter.7.cloned.1.call-start = ((), (), s32[]{:S(2)}) async-start(), calls=%async_computation.5 | async-start | bytes 2621440 | tf_op jit(solution)/shard_map/reduce_scatter | solution.py:128
  196.0 8.9 %collective-permute-start.18 = (bf16[512,4096]{1,0:T(8,128)(2,1)}, bf16[512,4096]{1,0:T(8,128)(2,1)}, u32[]{:S(2)}, u32[]{:S(2)}) collective-permute-start(bf16[512,4096]{1,0:T(8,128)(2,1)} %get-tuple-element.207), channel_id=1, source_target_pairs={{0,4},{4,0},{8,12},{12,8},{16,20},{20,16},{24,28},{28,24},{1,5},{5... | collective-permute-start | bytes 12582920 | tf_op jit(solution)/shard_map/ppermute | solution.py:30
  197.4 93.1 %reduce-scatter.9.cloned.1.call-start = ((), (), s32[]{:S(2)}) async-start(), calls=%async_computation.6 | async-start | bytes 1310720 | tf_op jit(solution)/shard_map/reduce_scatter | solution.py:141
  199.9 26.8 %collective-permute-start.19 = (bf16[512,512]{1,0:T(8,128)(2,1)S(1)}, bf16[512,512]{1,0:T(8,128)(2,1)}, u32[]{:S(2)}, u32[]{:S(2)}) collective-permute-start(bf16[512,512]{1,0:T(8,128)(2,1)S(1)} %get-tuple-element.212), channel_id=1, source_target_pairs={{0,16},{4,20},{8,24},{12,28},{16,0},{20,4},{24,8},{28,12},{1,17},{... | collective-permute-start | bytes 1572872 | tf_op jit(solution)/shard_map/ppermute | solution.py:30
  201.5 25.2 %collective-permute-start.20 = (bf16[512,512]{1,0:T(8,128)(2,1)S(1)}, bf16[512,512]{1,0:T(8,128)(2,1)}, u32[]{:S(2)}, u32[]{:S(2)}) collective-permute-start(bf16[512,512]{1,0:T(8,128)(2,1)S(1)} %get-tuple-element.213), channel_id=1, source_target_pairs={{0,8},{4,12},{8,0},{12,4},{16,24},{20,28},{24,16},{28,20},{1,9},{5... | collective-permute-start | bytes 1572872 | tf_op jit(solution)/shard_map/ppermute | solution.py:30
  202.8 19.1 %collective-permute-start.21 = (bf16[128,1024]{1,0:T(8,128)(2,1)S(1)}, bf16[128,1024]{1,0:T(8,128)(2,1)S(1)}, u32[]{:S(2)}, u32[]{:S(2)}) collective-permute-start(bf16[128,1024]{1,0:T(8,128)(2,1)S(1)} %get-tuple-element.335), channel_id=1, source_target_pairs={{0,8},{4,12},{8,0},{12,4},{16,24},{20,28},{24,16},{28,20},{1,9},{5... | collective-permute-start | bytes 786440 | tf_op jit(solution)/shard_map/ppermute | solution.py:30
  204.3 17.6 %collective-permute-start.22 = (bf16[128,1024]{1,0:T(8,128)(2,1)S(1)}, bf16[128,1024]{1,0:T(8,128)(2,1)S(1)}, u32[]{:S(2)}, u32[]{:S(2)}) collective-permute-start(bf16[128,1024]{1,0:T(8,128)(2,1)S(1)} %get-tuple-element.334), channel_id=1, source_target_pairs={{0,16},{4,20},{8,24},{12,28},{16,0},{20,4},{24,8},{28,12},{1,17},{... | collective-permute-start | bytes 786440 | tf_op jit(solution)/shard_map/ppermute | solution.py:30
  204.9 21.9 %collective-permute-start.23 = (bf16[128,1024]{1,0:T(8,128)(2,1)S(1)}, bf16[128,1024]{1,0:T(8,128)(2,1)S(1)}, u32[]{:S(2)}, u32[]{:S(2)}) collective-permute-start(bf16[128,1024]{1,0:T(8,128)(2,1)S(1)} %get-tuple-element.333), channel_id=1, source_target_pairs={{0,24},{4,28},{8,16},{12,20},{16,8},{20,12},{24,0},{28,4},{1,25},{... | collective-permute-start | bytes 786440 | tf_op jit(solution)/shard_map/ppermute | solution.py:30
  226.7 24.8 %collective-permute-start.24 = (bf16[256,2048]{1,0:T(8,128)(2,1)}, bf16[256,2048]{1,0:T(8,128)(2,1)}, u32[]{:S(2)}, u32[]{:S(2)}) collective-permute-start(bf16[256,2048]{1,0:T(8,128)(2,1)} %bitcast.48), channel_id=1, source_target_pairs={{0,8},{4,12},{8,0},{12,4},{16,24},{20,28},{24,16},{28,20},{1,9},{5... | collective-permute-start | bytes 3145736 | tf_op jit(solution)/shard_map/ppermute | solution.py:30
  227.5 24.7 %collective-permute-start.25 = (bf16[256,2048]{1,0:T(8,128)(2,1)}, bf16[256,2048]{1,0:T(8,128)(2,1)}, u32[]{:S(2)}, u32[]{:S(2)}) collective-permute-start(bf16[256,2048]{1,0:T(8,128)(2,1)} %bitcast.49), channel_id=1, source_target_pairs={{0,16},{4,20},{8,24},{12,28},{16,0},{20,4},{24,8},{28,12},{1,17},{... | collective-permute-start | bytes 3145736 | tf_op jit(solution)/shard_map/ppermute | solution.py:30
  252.2 7.3 %collective-permute-start.26 = (bf16[1536,1024]{1,0:T(8,128)(2,1)}, bf16[1536,1024]{1,0:T(8,128)(2,1)}, u32[]{:S(2)}, u32[]{:S(2)}) collective-permute-start(bf16[1536,1024]{1,0:T(8,128)(2,1)} %get-tuple-element.231), channel_id=1, source_target_pairs={{0,4},{4,0},{8,12},{12,8},{16,20},{20,16},{24,28},{28,24},{1,5},{5... | collective-permute-start | bytes 9437192 | tf_op jit(solution)/shard_map/ppermute | solution.py:30
  252.2 74.4 %reduce-scatter.11.cloned.1.call-start = ((), (), s32[]{:S(2)}) async-start(), calls=%async_computation.7 | async-start | bytes 1310720 | tf_op jit(solution)/shard_map/reduce_scatter | solution.py:141
  256.0 14.5 %collective-permute-start.27 = (bf16[128,2048]{1,0:T(8,128)(2,1)}, bf16[128,2048]{1,0:T(8,128)(2,1)S(1)}, u32[]{:S(2)}, u32[]{:S(2)}) collective-permute-start(bf16[128,2048]{1,0:T(8,128)(2,1)} %get-tuple-element.316), channel_id=1, source_target_pairs={{0,16},{4,20},{8,24},{12,28},{16,0},{20,4},{24,8},{28,12},{1,17},{... | collective-permute-start | bytes 1572872 | tf_op jit(solution)/shard_map/ppermute | solution.py:30
  257.5 14.2 %collective-permute-start.28 = (bf16[128,2048]{1,0:T(8,128)(2,1)}, bf16[128,2048]{1,0:T(8,128)(2,1)S(1)}, u32[]{:S(2)}, u32[]{:S(2)}) collective-permute-start(bf16[128,2048]{1,0:T(8,128)(2,1)} %get-tuple-element.315), channel_id=1, source_target_pairs={{0,8},{4,12},{8,0},{12,4},{16,24},{20,28},{24,16},{28,20},{1,9},{5... | collective-permute-start | bytes 1572872 | tf_op jit(solution)/shard_map/ppermute | solution.py:30
  272.5 18.8 %collective-permute-start.29 = (bf16[768,512]{1,0:T(8,128)(2,1)S(1)}, bf16[768,512]{1,0:T(8,128)(2,1)S(1)}, u32[]{:S(2)}, u32[]{:S(2)}) collective-permute-start(bf16[768,512]{1,0:T(8,128)(2,1)S(1)} %bitcast.276), channel_id=1, source_target_pairs={{0,8},{4,12},{8,0},{12,4},{16,24},{20,28},{24,16},{28,20},{1,9},{5... | collective-permute-start | bytes 2359304 | tf_op jit(solution)/shard_map/ppermute | solution.py:30
  273.7 18.6 %collective-permute-start.30 = (bf16[768,512]{1,0:T(8,128)(2,1)S(1)}, bf16[768,512]{1,0:T(8,128)(2,1)}, u32[]{:S(2)}, u32[]{:S(2)}) collective-permute-start(bf16[768,512]{1,0:T(8,128)(2,1)S(1)} %bitcast.275), channel_id=1, source_target_pairs={{0,16},{4,20},{8,24},{12,28},{16,0},{20,4},{24,8},{28,12},{1,17},{... | collective-permute-start | bytes 2359304 | tf_op jit(solution)/shard_map/ppermute | solution.py:30
  294.3 11.1 %collective-permute-start.31 = (bf16[384,512]{1,0:T(8,128)(2,1)S(1)}, bf16[384,512]{1,0:T(8,128)(2,1)S(1)}, u32[]{:S(2)}, u32[]{:S(2)}) collective-permute-start(bf16[384,512]{1,0:T(8,128)(2,1)S(1)} %get-tuple-element.326), channel_id=1, source_target_pairs={{0,16},{4,20},{8,24},{12,28},{16,0},{20,4},{24,8},{28,12},{1,17},{... | collective-permute-start | bytes 1179656 | tf_op jit(solution)/shard_map/ppermute | solution.py:30
  295.0 12.1 %collective-permute-start.32 = (bf16[384,512]{1,0:T(8,128)(2,1)S(1)}, bf16[384,512]{1,0:T(8,128)(2,1)S(1)}, u32[]{:S(2)}, u32[]{:S(2)}) collective-permute-start(bf16[384,512]{1,0:T(8,128)(2,1)S(1)} %get-tuple-element.325), channel_id=1, source_target_pairs={{0,8},{4,12},{8,0},{12,4},{16,24},{20,28},{24,16},{28,20},{1,9},{5... | collective-permute-start | bytes 1179656 | tf_op jit(solution)/shard_map/ppermute | solution.py:30
  300.0 15.6 %collective-permute-start.34 = (bf16[64,2048]{1,0:T(8,128)(2,1)S(1)}, bf16[64,2048]{1,0:T(8,128)(2,1)S(1)}, u32[]{:S(2)}, u32[]{:S(2)}) collective-permute-start(bf16[64,2048]{1,0:T(8,128)(2,1)S(1)} %bitcast.288), channel_id=1, source_target_pairs={{0,8},{4,12},{8,0},{12,4},{16,24},{20,28},{24,16},{28,20},{1,9},{5... | collective-permute-start | bytes 786440 | tf_op jit(solution)/shard_map/ppermute | solution.py:30
  301.3 14.4 %collective-permute-start.35 = (bf16[64,2048]{1,0:T(8,128)(2,1)S(1)}, bf16[64,2048]{1,0:T(8,128)(2,1)S(1)}, u32[]{:S(2)}, u32[]{:S(2)}) collective-permute-start(bf16[64,2048]{1,0:T(8,128)(2,1)S(1)} %bitcast.289), channel_id=1, source_target_pairs={{0,16},{4,20},{8,24},{12,28},{16,0},{20,4},{24,8},{28,12},{1,17},{... | collective-permute-start | bytes 786440 | tf_op jit(solution)/shard_map/ppermute | solution.py:30
  309.4 16.3 %collective-permute-start.33 = (bf16[192,1024]{1,0:T(8,128)(2,1)S(1)}, bf16[192,1024]{1,0:T(8,128)(2,1)S(1)}, u32[]{:S(2)}, u32[]{:S(2)}) collective-permute-start(bf16[192,1024]{1,0:T(8,128)(2,1)S(1)} %pad_maximum_fusion.12), channel_id=1, source_target_pairs={{0,1},{1,0},{2,3},{3,2},{4,5},{5,4},{6,7},{7,6},{8,9},{9,8},{10,11... | collective-permute-start | bytes 1179656 | tf_op jit(solution)/shard_map/ppermute | solution.py:30
  314.8 16.8 %copy-start.33 = (bf16[128,2048]{1,0:T(8,128)(2,1)S(1)}, bf16[128,2048]{1,0:T(8,128)(2,1)}, u32[]{:S(2)}) copy-start(bf16[128,2048]{1,0:T(8,128)(2,1)} %reduce-scatter.7.cloned.1.call-done) | copy-start | bytes 1572868
  328.4 9.6 %collective-permute-start.36 = (bf16[96,1024]{1,0:T(8,128)(2,1)S(1)}, bf16[96,1024]{1,0:T(8,128)(2,1)S(1)}, u32[]{:S(2)}, u32[]{:S(2)}) collective-permute-start(bf16[96,1024]{1,0:T(8,128)(2,1)S(1)} %pad_maximum_fusion.15), channel_id=1, source_target_pairs={{0,2},{1,3},{2,0},{3,1},{4,6},{5,7},{6,4},{7,5},{8,10},{9,11},{10,... | collective-permute-start | bytes 589832 | tf_op jit(solution)/shard_map/ppermute | solution.py:30
  330.0 5.0 %collective-permute-start.37 = (bf16[32,2048]{1,0:T(8,128)(2,1)S(1)}, bf16[32,2048]{1,0:T(8,128)(2,1)S(1)}, u32[]{:S(2)}, u32[]{:S(2)}) collective-permute-start(bf16[32,2048]{1,0:T(8,128)(2,1)S(1)} %fusion.62), channel_id=1, source_target_pairs={{0,16},{4,20},{8,24},{12,28},{16,0},{20,4},{24,8},{28,12},{1,17},{... | collective-permute-start | bytes 393224 | tf_op jit(solution)/shard_map/ppermute | solution.py:30
  331.6 5.0 %collective-permute-start.38 = (bf16[32,2048]{1,0:T(8,128)(2,1)S(1)}, bf16[32,2048]{1,0:T(8,128)(2,1)S(1)}, u32[]{:S(2)}, u32[]{:S(2)}) collective-permute-start(bf16[32,2048]{1,0:T(8,128)(2,1)S(1)} %fusion.61), channel_id=1, source_target_pairs={{0,8},{4,12},{8,0},{12,4},{16,24},{20,28},{24,16},{28,20},{1,9},{5... | collective-permute-start | bytes 393224 | tf_op jit(solution)/shard_map/ppermute | solution.py:30
  (48 other events, 185.7 us)
Sparse Core Ops, SparseCore 0:
  172.2 43.1 reduce-scatter.4
  218.3 43.2 reduce-scatter.6
  264.0 26.4 reduce-scatter.8
  292.7 33.7 reduce-scatter.10

commit v6 on v5

--- a/solution.py
+++ b/solution.py
@@ -523,7 +523,9 @@
             jax.ShapeDtypeStruct((width // 2, inner), BF),
             pltpu.HBM((width // 2, inner), BF),
         ]
-        + [low] * 5
+        + [low]
+        + [pltpu.HBM((frames, width), BF)] * 3
+        + [low]
         + [jax.ShapeDtypeStruct((pairs, 8, frames), F32)],
         scratch_shapes=[
             pltpu.VMEM((frames, width), F32),
@@ -536,7 +538,7 @@
             pltpu.VMEM((frames, width), BF),
             pltpu.SemaphoreType.DMA((4,)),
         ],
-        compiler_params=params(52),
+        compiler_params=params(40),
         cost_estimate=cost(12 * frames * width * inner, 8 * width * inner, frames * inner),
     )(
         normed,
@@ -754,9 +756,11 @@
     meta = jnp.concatenate([meta, swap(meta, "head", 1)])
     meta, *normed_own = together(meta, *normed_own)
     normed_attn = send_parts(normed_own, span)
+    resid_low = resid_own.astype(BF).reshape(micro_count, rows, width)
     for bit in range(1, groups.bit_length() - 1):
         meta = jnp.concatenate([meta, swap(meta, "head", 2**bit)])
-    resid_low = resid_own.astype(BF).reshape(micro_count, rows, width)
+        if bit == 1:
+            meta, cotangent, resid_low = together(meta, cotangent, resid_low)
     second = [
         jnp.concatenate(pair, axis=1)
         for pair in zip(cut_parts(cotangent, mine), cut_parts(resid_low, mine), strict=True)
@@ -859,8 +863,9 @@
     came = send(away, last_index)
     grad_local = send_parts(list(grad_in_low.reshape(micro_count, rows, width)), span)
     wide = two_ways(near_keep, near_came)
-    up_0, *rest = together(up_0, *begin(wide, index=0), *came, *grad_local)
-    wide_away, came, grad_local = rest[:2], rest[2:4], rest[4:]
+    up_0, *rest = together(up_0, *begin(wide, index=0), *came, *grad_local, *output)
+    wide_away, came, rest = rest[:2], rest[2:4], rest[4:]
+    grad_local, output = rest[:micro_count], rest[micro_count:]
     end(down, came=came)
 
     wide_came = send(wide_away, 0)

time: 351 us -> 343 us (0.977)
  local copies, waits for them, and re-layouts: 14.2 us -> 6.86 us
  other arithmetic: 64.2 us -> 60.2 us
    unnamed x112 -> x72, local copies, waits for them, and re-layouts: 7.96 us -> 2.88 us
  transfers between devices with their start and end apart: 43 -> 43, of which waited for: 21 -> 21; matrix products, arithmetic and copies ran while one was open for 20% -> 19% of each run, Pallas kernels for 19% -> 20%
where the time goes in v6:
time: 343 us; the launch traced here: 340 us
  Pallas kernels  117 us (34%)
  waiting for transfers between devices  80.6 us (23%)
  other arithmetic  60.2 us (18%)
  starting transfers between devices  42.7 us (12%)
  matrix products  17.8 us (5%)
  between operations  15 us (4%)
  local copies, waits for them, and re-layouts  6.86 us (2%)
    ppermute x39, waiting for transfers between devices, swap(): return lax.ppermute(values, axis_name, [(i, i ^ bits) for i in range(size)])  66.8 us
    ppermute x39, starting transfers between devices, swap(): return lax.ppermute(values, axis_name, [(i, i ^ bits) for i in range(size)])  42.3 us
    pallas_call x1, Pallas kernels, feed(): pl.pallas_call(functools.partial(feed_kernel, groups, seq_blocks(width)),...  42.1 us
    convert_element_type x19, other arithmetic, add_low(): functools.reduce(jnp.add, [term.astype(F32) for term in terms]).astype(BF)  34.6 us
    pallas_call x1, Pallas kernels, attend_back(): pl.pallas_call(functools.partial(attend_back_kernel, span), grid=(pairs,)...  23.2 us
    pallas_call x1, Pallas kernels, near(): pl.pallas_call(functools.partial(near_kernel, groups, len(dkv)), grid=(4...  18.3 us
    dot_general x9, matrix products, dot(): return lax.dot_general(left, right, dims, preferred_element_type=F32)  17.8 us
    pallas_call x1, Pallas kernels, attend(): pl.pallas_call(functools.partial(attend_kernel, span), grid=(pairs,), in_...  17.1 us
  transfers between devices with their start and end apart: 43, of which 21 were waited for; matrix products, arithmetic and copies ran while one was open for 19% of the time, Pallas kernels for 20%

profile of v6, /device:TPU:0, one launch (start us, length us, event | category | flops | bytes accessed | tf_op | source)
XLA Modules:
  0.0 340.0 jit_solution(2332152898908243575)
XLA Ops:
  10.5 3.3 fusion.7
  15.9 1.6 fusion.48
  17.5 2.0 fusion.33
  19.5 1.6 fusion.75
  21.2 2.6 collective-permute-start.1
  23.9 2.0 collective-permute-start.4
  27.3 1.6 collective-permute-start.2
  29.3 8.4 %collective-permute-done.2 = f32[4,4,3,128]{3,1,2,0:T(4,128)S(1)} collective-permute-done((f32[4,4,3,128]{3,1,2,0:T(4,128)S(1)}, f32[4,4,3,128]{3,1,2,0:T(4,128)S(1)}, u32[]{:S(2)}, u32[]{:S(2)}) %collective-permute-start.2) | collective-permute-done | bytes 24608 | tf_op jit(solution)/shard_map/ppermute | solution.py:30
  39.5 1.9 fusion.66
  42.6 7.7 %shard_map.187 = (bf16[512,1024]{1,0:T(8,128)(2,1)S(1)}, bf16[512,2048]{1,0:T(8,128)(2,1)S(1)}) custom-call(bf16[512,1024]{1,0:T(8,128)(2,1)S(1)} %constant_dynamic-update-slice_fusion.x_ref.refs_4_, bf16[1024,3072]{1,0:T(8,128)(2,1)S(1)} %bitcast.248, f32[512,128]{1,0:T(8,128)S(1)} %slice.125.cos_ref, f32[512,128]{1,0:T(8,128)S(1)} %slice.126.sin_ref), custom_call_target="tpu_custom_call" | custom-call | flops 3221225472 | bytes 10485760 | tf_op jit(solution)/shard_map/pallas_call | solution.py:222
  55.0 17.1 %shard_map.188 = (bf16[512,1024]{1,0:T(8,128)(2,1)S(1)}, bf16[16,1024,512]{2,1,0:T(8,128)(2,1)}, f32[8,8,512]{2,1,0:T(8,128)S(1)}) custom-call(bf16[512,1024]{1,0:T(8,128)(2,1)S(1)} %get-tuple-element.160.q_ref, bf16[512,2048]{1,0:T(8,128)(2,1)S(1)} %get-tuple-element.161.refs_0_.refs_2_, bf16[512,2048]{1,0:T(8,128)(2,1)S(1)} %collective-permute-done.6.refs_1_.refs_3_, ...), custom_call_target="tpu_custom_call" | custom-call | flops 8589934592 | bytes 16777216 | tf_op jit(solution)/shard_map/pallas_call | solution.py:300
  73.5 1.8 fusion.46.refs_8_
  80.0 42.1 %shard_map.189 = (bf16[2048,1024]{1,0:T(8,128)(2,1)}, bf16[2048,1024]{1,0:T(8,128)(2,1)}, bf16[512,4096]{1,0:T(8,128)(2,1)}, bf16[512,4096]{1,0:T(8,128)(2,1)}, ...) custom-call(bf16[512,1024]{1,0:T(8,128)(2,1)S(1)} %add_convert_fusio, ...), custom_call_target="tpu_custom_call" | custom-call | flops 25769803776 | bytes 33554432 | tf_op jit(solution)/shard_map/pallas_call | solution.py:508
  126.9 23.2 %shard_map.190 = (bf16[512,1024]{1,0:T(8,128)(2,1)}, bf16[2,512,1024]{2,1,0:T(8,128)(2,1)}, bf16[2,512,1024]{2,1,0:T(8,128)(2,1)}) custom-call(bf16[512,1024]{1,0:T(8,128)(2,1)} %copy-done.8, bf16[512,2048]{1,0:T(8,128)(2,1)} %copy-done.3, bf16[512,2048]{1,0:T(8,128)(2,1)} %copy-done.4, bf16[512,2048]{1,0:T(8,128)(2,1)} %copy-done.3, ...), custom_call_target="tpu_custom_call" | custom-call | flops 17179869184 | bytes 16777216 | tf_op jit(solution)/shard_map/pallas_call | solution.py:370
  150.2 5.9 %add_convert_fusion = (bf16[512,2048]{1,0:T(8,128)(2,1)}, bf16[512,2048]{1,0:T(8,128)(2,1)}) fusion(bf16[512,4096]{1,0:T(8,128)(2,1)} %collective-permute-done.11, bf16[512,4096]{1,0:T(8,128)(2,1)} %get-tuple-element.195), kind=kLoop, calls=%fused_computation | loop fusion | flops 8388608 | bytes 12582912 | tf_op jit(solution)/shard_map/convert_element_type | solution.py:62
  157.5 2.8 add_convert_fusion.5
  160.3 1.8 add_convert_fusion.4
  165.2 18.3 %shard_map.191 = (bf16[512,4096]{1,0:T(8,128)(2,1)}, bf16[512,4096]{1,0:T(8,128)(2,1)}, bf16[512,1024]{1,0:T(8,128)(2,1)S(1)}, bf16[512,1024]{1,0:T(8,128)(2,1)}, bf16[512,1024]{1,0:T(8,128)(2,1)}) custom-call(bf16[512,1024]{1,0:T(8,128)(2,1)} %get-tuple-element.204.refs_0_, bf16[2,512,1024]{2,1,0:T(8,128)(2,1)} %get-tuple-element.205.refs_1_, ...), custom_call_target="tpu_custom_call" | custom-call | flops 7516192768 | bytes 30408704 | tf_op jit(solution)/shard_map/pallas_call | solution.py:648
  183.5 4.5 %collective-permute-done.16 = bf16[1024,512]{1,0:T(8,128)(2,1)} collective-permute-done((bf16[1024,512]{1,0:T(8,128)(2,1)}, bf16[1024,512]{1,0:T(8,128)(2,1)}, u32[]{:S(2)}, u32[]{:S(2)}) %collective-permute-start.16) | collective-permute-done | bytes 1048608 | tf_op jit(solution)/shard_map/ppermute | solution.py:30
  189.1 2.4 fusion.31
  191.5 1.6 collective-permute-start.19
  197.9 2.6 add_convert_fusion.3
  200.5 1.6 add_convert_fusion.2
  202.1 11.3 %collective-permute-done.21 = bf16[128,1024]{1,0:T(8,128)(2,1)S(1)} collective-permute-done((bf16[128,1024]{1,0:T(8,128)(2,1)S(1)}, bf16[128,1024]{1,0:T(8,128)(2,1)S(1)}, u32[]{:S(2)}, u32[]{:S(2)}) %collective-permute-start.21) | collective-permute-done | bytes 262176 | tf_op jit(solution)/shard_map/ppermute | solution.py:30
  213.4 4.9 %collective-permute-done.23 = bf16[128,1024]{1,0:T(8,128)(2,1)S(1)} collective-permute-done((bf16[128,1024]{1,0:T(8,128)(2,1)S(1)}, bf16[128,1024]{1,0:T(8,128)(2,1)S(1)}, u32[]{:S(2)}, u32[]{:S(2)}) %collective-permute-start.23) | collective-permute-done | bytes 262176 | tf_op jit(solution)/shard_map/ppermute | solution.py:30
  220.7 2.7 fusion.30
  225.7 8.4 %shard_map.192 = (bf16[1536,1024]{1,0:T(8,128)(2,1)}, bf16[1536,1024]{1,0:T(8,128)(2,1)}) custom-call(bf16[512,1024]{1,0:T(8,128)(2,1)S(1)} %bitcast.250, bf16[512,1024]{1,0:T(8,128)(2,1)} %bitcast.311, bf16[512,256]{1,0:T(8,128)(2,1)S(1)} %pad_maximum_fusion.14.f_ref, bf16[512,1024]{1,0:T(8,128)(2,1)} %bitcast.274, ...), custom_call_target="tpu_custom_call" | custom-call | flops 3221225472 | bytes 16777216 | tf_op jit(solution)/shard_map/pallas_call | solution.py:710
  234.1 9.1 %collective-permute-done.24 = bf16[256,2048]{1,0:T(8,128)(2,1)} collective-permute-done((bf16[256,2048]{1,0:T(8,128)(2,1)}, bf16[256,2048]{1,0:T(8,128)(2,1)}, u32[]{:S(2)}, u32[]{:S(2)}) %collective-permute-start.24) | collective-permute-done | bytes 1048608 | tf_op jit(solution)/shard_map/ppermute | solution.py:30
  243.6 3.5 %fusion.23 = (bf16[128,2048]{1,0:T(8,128)(2,1)}, bf16[128,2048]{1,0:T(8,128)(2,1)}) fusion(bf16[1,2,128,2048]{3,2,1,0:T(8,128)(2,1)} %bitcast.75, s32[]{:T(128)S(6)} %select_n.213, bf16[1,2,2,128,4096]{4,3,2,1,0:T(8,128)(2,1)} %bitcast.43, s32[]{:T(128)S(6)} %select_n.217, bf16[1,2,2,128,4096]{4,3,2,1,0:T(8,128)(2,1)} %bitcast.255, ...), kind=kLoop, calls=%fused_computation.40 | loop fusion | flops 3145728 | bytes 4194320 | tf_op jit(solution)/shard_map/convert_element_type | solution.py:62
  250.2 1.7 constant_dynamic-slice_fusion.1
  251.8 2.3 add_convert_fusion.8
  254.1 2.3 add_convert_fusion.7
  256.4 5.4 %collective-permute-done.27 = bf16[128,2048]{1,0:T(8,128)(2,1)} collective-permute-done((bf16[128,2048]{1,0:T(8,128)(2,1)}, bf16[128,2048]{1,0:T(8,128)(2,1)}, u32[]{:S(2)}, u32[]{:S(2)}) %collective-permute-start.27) | collective-permute-done | bytes 524320 | tf_op jit(solution)/shard_map/ppermute | solution.py:30
  265.1 2.8 fusion.26
  269.8 13.7 %reduce-scatter.9.cloned.1.call-done = bf16[128,1024]{1,0:T(8,128)(2,1)} async-done(((bf16[512,1024]{1,0:T(8,128)(2,1)}), bf16[128,1024]{1,0:T(8,128)(2,1)}) %reduce-scatter.9.cloned.1.call-update) | async-done | bytes 262160 | tf_op jit(solution)/shard_map/reduce_scatter | solution.py:141
  283.5 4.6 %fusion.12 = f32[4,1,128,1024]{3,2,1,0:T(8,128)} fusion(bf16[2048,1024]{1,0:T(8,128)(2,1)} %param.18, bf16[1,128,1024]{2,1,0:T(8,128)(2,1)} %copy-done.15, bf16[1,128,1024]{2,1,0:T(8,128)(2,1)} %copy-done.17, bf16[1,128,1024]{2,1,0:T(8,128)(2,1)} %copy-done.19, bf16[1,128,1024]{2,1,0:T(8,128)(2,1)S(1)} %get-tuple-element.343), kind=kOutput, calls=%fused_computation.25 | convolution fusion | flops 1075314688 | bytes 5242880 | tf_op jit(solution)/shard_map/dot_general | solution.py:25
  288.1 1.7 fusion.37
  289.9 1.6 collective-permute-start.31
  292.9 2.6 fusion.15
  295.5 5.1 %collective-permute-done.31 = bf16[384,512]{1,0:T(8,128)(2,1)S(1)} collective-permute-done((bf16[384,512]{1,0:T(8,128)(2,1)S(1)}, bf16[384,512]{1,0:T(8,128)(2,1)S(1)}, u32[]{:S(2)}, u32[]{:S(2)}) %collective-permute-start.31) | collective-permute-done | bytes 393248 | tf_op jit(solution)/shard_map/ppermute | solution.py:30
  301.8 1.8 fusion.40
  310.0 2.7 collective-permute-done.34
  313.9 3.9 %collective-permute-done.33 = bf16[192,1024]{1,0:T(8,128)(2,1)S(1)} collective-permute-done((bf16[192,1024]{1,0:T(8,128)(2,1)S(1)}, bf16[192,1024]{1,0:T(8,128)(2,1)S(1)}, u32[]{:S(2)}, u32[]{:S(2)}) %collective-permute-start.33) | collective-permute-done | bytes 393248 | tf_op jit(solution)/shard_map/ppermute | solution.py:30
  317.7 1.7 slice_convert_fusion
  319.5 2.5 collective-permute-start.36
  322.1 1.5 collective-permute-start.37
  327.1 1.6 collective-permute-done.38
  328.7 2.1 collective-permute-done.36
  (228 shorter events, 64.9 us)
Async XLA Ops:
  7.2 211.2 %reduce-scatter.5.cloned.1.call-start = ((), (), s32[]{:S(2)}) async-start(), calls=%async_computation.4 | async-start | bytes 2621440 | tf_op jit(solution)/shard_map/reduce_scatter | solution.py:128
  9.3 11.9 %collective-permute-start = (f32[1,4,3,128]{3,1,2,0:T(4,128)S(1)}, f32[1,4,3,128]{3,1,2,0:T(4,128)S(1)}, u32[]{:S(2)}, u32[]{:S(2)}) collective-permute-start(f32[1,4,3,128]{3,1,2,0:T(4,128)S(1)} %bitcast.305), channel_id=1, source_target_pairs={{0,4},{4,0},{8,12},{12,8},{16,20},{20,16},{24,28},{28,24},{1,5},{5... | collective-permute-start | bytes 18440 | tf_op jit(solution)/shard_map/ppermute | solution.py:30
  21.2 6.1 %collective-permute-start.1 = (f32[2,4,3,128]{3,1,2,0:T(4,128)S(1)}, f32[2,4,3,128]{3,1,2,0:T(4,128)S(1)}, u32[]{:S(2)}, u32[]{:S(2)}) collective-permute-start(f32[2,4,3,128]{3,1,2,0:T(4,128)S(1)} %pad_maximum_fusion.18), channel_id=1, source_target_pairs={{0,8},{4,12},{8,0},{12,4},{16,24},{20,28},{24,16},{28,20},{1,9},{5... | collective-permute-start | bytes 36872 | tf_op jit(solution)/shard_map/ppermute | solution.py:30
  23.8 13.9 %collective-permute-start.3 = (bf16[128,1024]{1,0:T(8,128)(2,1)S(1)}, bf16[128,1024]{1,0:T(8,128)(2,1)S(1)}, u32[]{:S(2)}, u32[]{:S(2)}) collective-permute-start(bf16[128,1024]{1,0:T(8,128)(2,1)S(1)} %get-tuple-element.144), channel_id=1, source_target_pairs={{0,8},{4,12},{8,0},{12,4},{16,24},{20,28},{24,16},{28,20},{1,9},{5... | collective-permute-start | bytes 786440 | tf_op jit(solution)/shard_map/ppermute | solution.py:30
  23.9 13.8 %collective-permute-start.4 = (bf16[128,1024]{1,0:T(8,128)(2,1)S(1)}, bf16[128,1024]{1,0:T(8,128)(2,1)S(1)}, u32[]{:S(2)}, u32[]{:S(2)}) collective-permute-start(bf16[128,1024]{1,0:T(8,128)(2,1)S(1)} %get-tuple-element.145), channel_id=1, source_target_pairs={{0,16},{4,20},{8,24},{12,28},{16,0},{20,4},{24,8},{28,12},{1,17},{... | collective-permute-start | bytes 786440 | tf_op jit(solution)/shard_map/ppermute | solution.py:30
  25.9 12.9 %collective-permute-start.5 = (bf16[128,1024]{1,0:T(8,128)(2,1)S(1)}, bf16[128,1024]{1,0:T(8,128)(2,1)S(1)}, u32[]{:S(2)}, u32[]{:S(2)}) collective-permute-start(bf16[128,1024]{1,0:T(8,128)(2,1)S(1)} %get-tuple-element.146), channel_id=1, source_target_pairs={{0,24},{4,28},{8,16},{12,20},{16,8},{20,12},{24,0},{28,4},{1,25},{... | collective-permute-start | bytes 786440 | tf_op jit(solution)/shard_map/ppermute | solution.py:30
  27.3 10.4 %collective-permute-start.2 = (f32[4,4,3,128]{3,1,2,0:T(4,128)S(1)}, f32[4,4,3,128]{3,1,2,0:T(4,128)S(1)}, u32[]{:S(2)}, u32[]{:S(2)}) collective-permute-start(f32[4,4,3,128]{3,1,2,0:T(4,128)S(1)} %pad_maximum_fusion.17), channel_id=1, source_target_pairs={{0,16},{4,20},{8,24},{12,28},{16,0},{20,4},{24,8},{28,12},{1,17},{... | collective-permute-start | bytes 73736 | tf_op jit(solution)/shard_map/ppermute | solution.py:30
  50.2 21.9 %copy-start.3 = (bf16[512,2048]{1,0:T(8,128)(2,1)}, bf16[512,2048]{1,0:T(8,128)(2,1)S(1)}, u32[]{:S(2)}) copy-start(bf16[512,2048]{1,0:T(8,128)(2,1)S(1)} %get-tuple-element.161.refs_0_.refs_2_) | copy-start | bytes 6291460
  50.3 21.9 %copy-start.8 = (bf16[512,1024]{1,0:T(8,128)(2,1)}, bf16[512,1024]{1,0:T(8,128)(2,1)S(1)}, u32[]{:S(2)}) copy-start(bf16[512,1024]{1,0:T(8,128)(2,1)S(1)} %get-tuple-element.160.q_ref) | copy-start | bytes 3145732
  50.3 4.7 %collective-permute-start.6 = (bf16[512,2048]{1,0:T(8,128)(2,1)S(1)}, bf16[512,2048]{1,0:T(8,128)(2,1)S(1)}, u32[]{:S(2)}, u32[]{:S(2)}) collective-permute-start(bf16[512,2048]{1,0:T(8,128)(2,1)S(1)} %get-tuple-element.161.refs_0_.refs_2_), channel_id=1, source_target_pairs={{0,4},{4,0},{8,12},{12,8},{16,20},{20,16},{24,28},{28,24},{1,5},{5... | collective-permute-start | bytes 6291464 | tf_op jit(solution)/shard_map/ppermute | solution.py:30
  50.4 25.8 %collective-permute-start.7 = (bf16[128,2048]{1,0:T(8,128)(2,1)S(1)}, bf16[128,2048]{1,0:T(8,128)(2,1)S(1)}, u32[]{:S(2)}, u32[]{:S(2)}) collective-permute-start(bf16[128,2048]{1,0:T(8,128)(2,1)S(1)} %pad_maximum_fusion.7), channel_id=1, source_target_pairs={{0,8},{4,12},{8,0},{12,4},{16,24},{20,28},{24,16},{28,20},{1,9},{5... | collective-permute-start | bytes 1572872 | tf_op jit(solution)/shard_map/ppermute | solution.py:30
  51.8 25.3 %collective-permute-start.8 = (bf16[128,2048]{1,0:T(8,128)(2,1)S(1)}, bf16[128,2048]{1,0:T(8,128)(2,1)S(1)}, u32[]{:S(2)}, u32[]{:S(2)}) collective-permute-start(bf16[128,2048]{1,0:T(8,128)(2,1)S(1)} %pad_maximum_fusion.8), channel_id=1, source_target_pairs={{0,16},{4,20},{8,24},{12,28},{16,0},{20,4},{24,8},{28,12},{1,17},{... | collective-permute-start | bytes 1572872 | tf_op jit(solution)/shard_map/ppermute | solution.py:30
  53.3 23.8 %collective-permute-start.9 = (bf16[128,2048]{1,0:T(8,128)(2,1)S(1)}, bf16[128,2048]{1,0:T(8,128)(2,1)S(1)}, u32[]{:S(2)}, u32[]{:S(2)}) collective-permute-start(bf16[128,2048]{1,0:T(8,128)(2,1)S(1)} %pad_maximum_fusion.9), channel_id=1, source_target_pairs={{0,24},{4,28},{8,16},{12,20},{16,8},{20,12},{24,0},{28,4},{1,25},{... | collective-permute-start | bytes 1572872 | tf_op jit(solution)/shard_map/ppermute | solution.py:30
  54.9 17.2 %copy-start.4 = (bf16[512,2048]{1,0:T(8,128)(2,1)}, bf16[512,2048]{1,0:T(8,128)(2,1)S(1)}, u32[]{:S(2)}) copy-start(bf16[512,2048]{1,0:T(8,128)(2,1)S(1)} %collective-permute-done.6.refs_1_.refs_3_) | copy-start | bytes 6291460
  54.9 18.5 %copy-start.12 = (bf16[256,4096]{1,0:T(8,128)(2,1)S(1)}, bf16[256,4096]{1,0:T(8,128)(2,1)}, u32[]{:S(2)}) copy-start(bf16[256,4096]{1,0:T(8,128)(2,1)} %param.19) | copy-start | bytes 6291460
  122.0 28.0 %collective-permute-start.10 = (bf16[2048,1024]{1,0:T(8,128)(2,1)}, bf16[2048,1024]{1,0:T(8,128)(2,1)}, u32[]{:S(2)}, u32[]{:S(2)}) collective-permute-start(bf16[2048,1024]{1,0:T(8,128)(2,1)} %get-tuple-element.189), channel_id=1, source_target_pairs={{0,4},{4,0},{8,12},{12,8},{16,20},{20,16},{24,28},{28,24},{1,5},{5... | collective-permute-start | bytes 12582920 | tf_op jit(solution)/shard_map/ppermute | solution.py:30
  122.1 28.0 %collective-permute-start.11 = (bf16[512,4096]{1,0:T(8,128)(2,1)}, bf16[512,4096]{1,0:T(8,128)(2,1)}, u32[]{:S(2)}, u32[]{:S(2)}) collective-permute-start(bf16[512,4096]{1,0:T(8,128)(2,1)} %get-tuple-element.190), channel_id=1, source_target_pairs={{0,4},{4,0},{8,12},{12,8},{16,20},{20,16},{24,28},{28,24},{1,5},{5... | collective-permute-start | bytes 12582920 | tf_op jit(solution)/shard_map/ppermute | solution.py:30
  123.4 26.7 %collective-permute-start.12 = (bf16[128,1024]{1,0:T(8,128)(2,1)S(1)}, bf16[128,1024]{1,0:T(8,128)(2,1)}, u32[]{:S(2)}, u32[]{:S(2)}) collective-permute-start(bf16[128,1024]{1,0:T(8,128)(2,1)S(1)} %get-tuple-element.357), channel_id=1, source_target_pairs={{0,8},{4,12},{8,0},{12,4},{16,24},{20,28},{24,16},{28,20},{1,9},{5... | collective-permute-start | bytes 786440 | tf_op jit(solution)/shard_map/ppermute | solution.py:30
  124.8 25.3 %collective-permute-start.13 = (bf16[128,1024]{1,0:T(8,128)(2,1)S(1)}, bf16[128,1024]{1,0:T(8,128)(2,1)}, u32[]{:S(2)}, u32[]{:S(2)}) collective-permute-start(bf16[128,1024]{1,0:T(8,128)(2,1)S(1)} %get-tuple-element.356), channel_id=1, source_target_pairs={{0,16},{4,20},{8,24},{12,28},{16,0},{20,4},{24,8},{28,12},{1,17},{... | collective-permute-start | bytes 786440 | tf_op jit(solution)/shard_map/ppermute | solution.py:30
  126.3 23.8 %collective-permute-start.14 = (bf16[128,1024]{1,0:T(8,128)(2,1)S(1)}, bf16[128,1024]{1,0:T(8,128)(2,1)}, u32[]{:S(2)}, u32[]{:S(2)}) collective-permute-start(bf16[128,1024]{1,0:T(8,128)(2,1)S(1)} %get-tuple-element.355), channel_id=1, source_target_pairs={{0,24},{4,28},{8,16},{12,20},{16,8},{20,12},{24,0},{28,4},{1,25},{... | collective-permute-start | bytes 786440 | tf_op jit(solution)/shard_map/ppermute | solution.py:30
  150.1 6.0 %collective-permute-start.15 = (bf16[2,512,1024]{2,1,0:T(8,128)(2,1)}, bf16[2,512,1024]{2,1,0:T(8,128)(2,1)S(1)}, u32[]{:S(2)}, u32[]{:S(2)}) collective-permute-start(bf16[2,512,1024]{2,1,0:T(8,128)(2,1)} %get-tuple-element.199), channel_id=1, source_target_pairs={{0,4},{4,0},{8,12},{12,8},{16,20},{20,16},{24,28},{28,24},{1,5},{5... | collective-permute-start | bytes 6291464 | tf_op jit(solution)/shard_map/ppermute | solution.py:30
  162.1 25.9 %collective-permute-start.16 = (bf16[1024,512]{1,0:T(8,128)(2,1)}, bf16[1024,512]{1,0:T(8,128)(2,1)}, u32[]{:S(2)}, u32[]{:S(2)}) collective-permute-start(bf16[1024,512]{1,0:T(8,128)(2,1)} %bitcast.40), channel_id=1, source_target_pairs={{0,8},{4,12},{8,0},{12,4},{16,24},{20,28},{24,16},{28,20},{1,9},{5... | collective-permute-start | bytes 3145736 | tf_op jit(solution)/shard_map/ppermute | solution.py:30
  163.6 25.3 %collective-permute-start.17 = (bf16[1024,512]{1,0:T(8,128)(2,1)S(1)}, bf16[1024,512]{1,0:T(8,128)(2,1)}, u32[]{:S(2)}, u32[]{:S(2)}) collective-permute-start(bf16[1024,512]{1,0:T(8,128)(2,1)S(1)} %bitcast.273), channel_id=1, source_target_pairs={{0,16},{4,20},{8,24},{12,28},{16,0},{20,4},{24,8},{28,12},{1,17},{... | collective-permute-start | bytes 3145736 | tf_op jit(solution)/shard_map/ppermute | solution.py:30
  165.1 91.3 %reduce-scatter.7.cloned.1.call-start = ((), (), s32[]{:S(2)}) async-start(), calls=%async_computation.5 | async-start | bytes 2621440 | tf_op jit(solution)/shard_map/reduce_scatter | solution.py:128
  188.9 7.5 %collective-permute-start.18 = (bf16[512,4096]{1,0:T(8,128)(2,1)}, bf16[512,4096]{1,0:T(8,128)(2,1)}, u32[]{:S(2)}, u32[]{:S(2)}) collective-permute-start(bf16[512,4096]{1,0:T(8,128)(2,1)} %get-tuple-element.214), channel_id=1, source_target_pairs={{0,4},{4,0},{8,12},{12,8},{16,20},{20,16},{24,28},{28,24},{1,5},{5... | collective-permute-start | bytes 12582920 | tf_op jit(solution)/shard_map/ppermute | solution.py:30
  189.0 94.5 %reduce-scatter.9.cloned.1.call-start = ((), (), s32[]{:S(2)}) async-start(), calls=%async_computation.6 | async-start | bytes 1310720 | tf_op jit(solution)/shard_map/reduce_scatter | solution.py:141
  191.5 26.8 %collective-permute-start.19 = (bf16[512,512]{1,0:T(8,128)(2,1)S(1)}, bf16[512,512]{1,0:T(8,128)(2,1)S(1)}, u32[]{:S(2)}, u32[]{:S(2)}) collective-permute-start(bf16[512,512]{1,0:T(8,128)(2,1)S(1)} %get-tuple-element.218), channel_id=1, source_target_pairs={{0,16},{4,20},{8,24},{12,28},{16,0},{20,4},{24,8},{28,12},{1,17},{... | collective-permute-start | bytes 1572872 | tf_op jit(solution)/shard_map/ppermute | solution.py:30
  193.1 25.3 %collective-permute-start.20 = (bf16[512,512]{1,0:T(8,128)(2,1)S(1)}, bf16[512,512]{1,0:T(8,128)(2,1)S(1)}, u32[]{:S(2)}, u32[]{:S(2)}) collective-permute-start(bf16[512,512]{1,0:T(8,128)(2,1)S(1)} %get-tuple-element.219), channel_id=1, source_target_pairs={{0,8},{4,12},{8,0},{12,4},{16,24},{20,28},{24,16},{28,20},{1,9},{5... | collective-permute-start | bytes 1572872 | tf_op jit(solution)/shard_map/ppermute | solution.py:30
  193.7 19.7 %collective-permute-start.21 = (bf16[128,1024]{1,0:T(8,128)(2,1)S(1)}, bf16[128,1024]{1,0:T(8,128)(2,1)S(1)}, u32[]{:S(2)}, u32[]{:S(2)}) collective-permute-start(bf16[128,1024]{1,0:T(8,128)(2,1)S(1)} %get-tuple-element.353), channel_id=1, source_target_pairs={{0,8},{4,12},{8,0},{12,4},{16,24},{20,28},{24,16},{28,20},{1,9},{5... | collective-permute-start | bytes 786440 | tf_op jit(solution)/shard_map/ppermute | solution.py:30
  195.2 18.2 %collective-permute-start.22 = (bf16[128,1024]{1,0:T(8,128)(2,1)S(1)}, bf16[128,1024]{1,0:T(8,128)(2,1)S(1)}, u32[]{:S(2)}, u32[]{:S(2)}) collective-permute-start(bf16[128,1024]{1,0:T(8,128)(2,1)S(1)} %get-tuple-element.352), channel_id=1, source_target_pairs={{0,16},{4,20},{8,24},{12,28},{16,0},{20,4},{24,8},{28,12},{1,17},{... | collective-permute-start | bytes 786440 | tf_op jit(solution)/shard_map/ppermute | solution.py:30
  196.5 21.9 %collective-permute-start.23 = (bf16[128,1024]{1,0:T(8,128)(2,1)S(1)}, bf16[128,1024]{1,0:T(8,128)(2,1)S(1)}, u32[]{:S(2)}, u32[]{:S(2)}) collective-permute-start(bf16[128,1024]{1,0:T(8,128)(2,1)S(1)} %get-tuple-element.351), channel_id=1, source_target_pairs={{0,24},{4,28},{8,16},{12,20},{16,8},{20,12},{24,0},{28,4},{1,25},{... | collective-permute-start | bytes 786440 | tf_op jit(solution)/shard_map/ppermute | solution.py:30
  218.4 24.9 %collective-permute-start.24 = (bf16[256,2048]{1,0:T(8,128)(2,1)}, bf16[256,2048]{1,0:T(8,128)(2,1)}, u32[]{:S(2)}, u32[]{:S(2)}) collective-permute-start(bf16[256,2048]{1,0:T(8,128)(2,1)} %bitcast.44), channel_id=1, source_target_pairs={{0,8},{4,12},{8,0},{12,4},{16,24},{20,28},{24,16},{28,20},{1,9},{5... | collective-permute-start | bytes 3145736 | tf_op jit(solution)/shard_map/ppermute | solution.py:30
  219.0 24.3 %collective-permute-start.25 = (bf16[256,2048]{1,0:T(8,128)(2,1)S(1)}, bf16[256,2048]{1,0:T(8,128)(2,1)}, u32[]{:S(2)}, u32[]{:S(2)}) collective-permute-start(bf16[256,2048]{1,0:T(8,128)(2,1)S(1)} %bitcast.272), channel_id=1, source_target_pairs={{0,16},{4,20},{8,24},{12,28},{16,0},{20,4},{24,8},{28,12},{1,17},{... | collective-permute-start | bytes 3145736 | tf_op jit(solution)/shard_map/ppermute | solution.py:30
  243.3 8.5 %collective-permute-start.26 = (bf16[1536,1024]{1,0:T(8,128)(2,1)}, bf16[1536,1024]{1,0:T(8,128)(2,1)}, u32[]{:S(2)}, u32[]{:S(2)}) collective-permute-start(bf16[1536,1024]{1,0:T(8,128)(2,1)} %get-tuple-element.245), channel_id=1, source_target_pairs={{0,4},{4,0},{8,12},{12,8},{16,20},{20,16},{24,28},{28,24},{1,5},{5... | collective-permute-start | bytes 9437192 | tf_op jit(solution)/shard_map/ppermute | solution.py:30
  243.3 74.4 %reduce-scatter.11.cloned.1.call-start = ((), (), s32[]{:S(2)}) async-start(), calls=%async_computation.7 | async-start | bytes 1310720 | tf_op jit(solution)/shard_map/reduce_scatter | solution.py:141
  247.2 14.7 %collective-permute-start.27 = (bf16[128,2048]{1,0:T(8,128)(2,1)}, bf16[128,2048]{1,0:T(8,128)(2,1)}, u32[]{:S(2)}, u32[]{:S(2)}) collective-permute-start(bf16[128,2048]{1,0:T(8,128)(2,1)} %get-tuple-element.330), channel_id=1, source_target_pairs={{0,16},{4,20},{8,24},{12,28},{16,0},{20,4},{24,8},{28,12},{1,17},{... | collective-permute-start | bytes 1572872 | tf_op jit(solution)/shard_map/ppermute | solution.py:30
  248.6 14.4 %collective-permute-start.28 = (bf16[128,2048]{1,0:T(8,128)(2,1)}, bf16[128,2048]{1,0:T(8,128)(2,1)}, u32[]{:S(2)}, u32[]{:S(2)}) collective-permute-start(bf16[128,2048]{1,0:T(8,128)(2,1)} %get-tuple-element.329), channel_id=1, source_target_pairs={{0,8},{4,12},{8,0},{12,4},{16,24},{20,28},{24,16},{28,20},{1,9},{5... | collective-permute-start | bytes 1572872 | tf_op jit(solution)/shard_map/ppermute | solution.py:30
  263.0 20.5 %collective-permute-start.29 = (bf16[768,512]{1,0:T(8,128)(2,1)}, bf16[768,512]{1,0:T(8,128)(2,1)}, u32[]{:S(2)}, u32[]{:S(2)}) collective-permute-start(bf16[768,512]{1,0:T(8,128)(2,1)} %bitcast.282), channel_id=1, source_target_pairs={{0,8},{4,12},{8,0},{12,4},{16,24},{20,28},{24,16},{28,20},{1,9},{5... | collective-permute-start | bytes 2359304 | tf_op jit(solution)/shard_map/ppermute | solution.py:30
  264.5 19.0 %collective-permute-start.30 = (bf16[768,512]{1,0:T(8,128)(2,1)}, bf16[768,512]{1,0:T(8,128)(2,1)}, u32[]{:S(2)}, u32[]{:S(2)}) collective-permute-start(bf16[768,512]{1,0:T(8,128)(2,1)} %bitcast.281), channel_id=1, source_target_pairs={{0,16},{4,20},{8,24},{12,28},{16,0},{20,4},{24,8},{28,12},{1,17},{... | collective-permute-start | bytes 2359304 | tf_op jit(solution)/shard_map/ppermute | solution.py:30
  289.9 10.8 %collective-permute-start.31 = (bf16[384,512]{1,0:T(8,128)(2,1)S(1)}, bf16[384,512]{1,0:T(8,128)(2,1)S(1)}, u32[]{:S(2)}, u32[]{:S(2)}) collective-permute-start(bf16[384,512]{1,0:T(8,128)(2,1)S(1)} %get-tuple-element.340), channel_id=1, source_target_pairs={{0,16},{4,20},{8,24},{12,28},{16,0},{20,4},{24,8},{28,12},{1,17},{... | collective-permute-start | bytes 1179656 | tf_op jit(solution)/shard_map/ppermute | solution.py:30
  291.4 10.4 %collective-permute-start.32 = (bf16[384,512]{1,0:T(8,128)(2,1)S(1)}, bf16[384,512]{1,0:T(8,128)(2,1)S(1)}, u32[]{:S(2)}, u32[]{:S(2)}) collective-permute-start(bf16[384,512]{1,0:T(8,128)(2,1)S(1)} %get-tuple-element.339), channel_id=1, source_target_pairs={{0,8},{4,12},{8,0},{12,4},{16,24},{20,28},{24,16},{28,20},{1,9},{5... | collective-permute-start | bytes 1179656 | tf_op jit(solution)/shard_map/ppermute | solution.py:30
  303.8 13.9 %collective-permute-start.33 = (bf16[192,1024]{1,0:T(8,128)(2,1)S(1)}, bf16[192,1024]{1,0:T(8,128)(2,1)S(1)}, u32[]{:S(2)}, u32[]{:S(2)}) collective-permute-start(bf16[192,1024]{1,0:T(8,128)(2,1)S(1)} %pad_maximum_fusion.12), channel_id=1, source_target_pairs={{0,1},{1,0},{2,3},{3,2},{4,5},{5,4},{6,7},{7,6},{8,9},{9,8},{10,11... | collective-permute-start | bytes 1179656 | tf_op jit(solution)/shard_map/ppermute | solution.py:30
  305.8 6.9 %collective-permute-start.34 = (bf16[64,2048]{1,0:T(8,128)(2,1)S(1)}, bf16[64,2048]{1,0:T(8,128)(2,1)S(1)}, u32[]{:S(2)}, u32[]{:S(2)}) collective-permute-start(bf16[64,2048]{1,0:T(8,128)(2,1)S(1)} %bitcast.292), channel_id=1, source_target_pairs={{0,8},{4,12},{8,0},{12,4},{16,24},{20,28},{24,16},{28,20},{1,9},{5... | collective-permute-start | bytes 786440 | tf_op jit(solution)/shard_map/ppermute | solution.py:30
  307.4 6.5 %collective-permute-start.35 = (bf16[64,2048]{1,0:T(8,128)(2,1)S(1)}, bf16[64,2048]{1,0:T(8,128)(2,1)S(1)}, u32[]{:S(2)}, u32[]{:S(2)}) collective-permute-start(bf16[64,2048]{1,0:T(8,128)(2,1)S(1)} %bitcast.293), channel_id=1, source_target_pairs={{0,16},{4,20},{8,24},{12,28},{16,0},{20,4},{24,8},{28,12},{1,17},{... | collective-permute-start | bytes 786440 | tf_op jit(solution)/shard_map/ppermute | solution.py:30
  309.1 14.5 %copy-start.24 = (bf16[128,2048]{1,0:T(8,128)(2,1)S(1)}, bf16[128,2048]{1,0:T(8,128)(2,1)}, u32[]{:S(2)}) copy-start(bf16[128,2048]{1,0:T(8,128)(2,1)} %reduce-scatter.7.cloned.1.call-done) | copy-start | bytes 1572868
  319.5 11.3 %collective-permute-start.36 = (bf16[96,1024]{1,0:T(8,128)(2,1)S(1)}, bf16[96,1024]{1,0:T(8,128)(2,1)S(1)}, u32[]{:S(2)}, u32[]{:S(2)}) collective-permute-start(bf16[96,1024]{1,0:T(8,128)(2,1)S(1)} %pad_maximum_fusion.15), channel_id=1, source_target_pairs={{0,2},{1,3},{2,0},{3,1},{4,6},{5,7},{6,4},{7,5},{8,10},{9,11},{10,... | collective-permute-start | bytes 589832 | tf_op jit(solution)/shard_map/ppermute | solution.py:30
  322.1 5.0 %collective-permute-start.37 = (bf16[32,2048]{1,0:T(8,128)(2,1)S(1)}, bf16[32,2048]{1,0:T(8,128)(2,1)S(1)}, u32[]{:S(2)}, u32[]{:S(2)}) collective-permute-start(bf16[32,2048]{1,0:T(8,128)(2,1)S(1)} %fusion.62), channel_id=1, source_target_pairs={{0,16},{4,20},{8,24},{12,28},{16,0},{20,4},{24,8},{28,12},{1,17},{... | collective-permute-start | bytes 393224 | tf_op jit(solution)/shard_map/ppermute | solution.py:30
  323.6 5.0 %collective-permute-start.38 = (bf16[32,2048]{1,0:T(8,128)(2,1)S(1)}, bf16[32,2048]{1,0:T(8,128)(2,1)S(1)}, u32[]{:S(2)}, u32[]{:S(2)}) collective-permute-start(bf16[32,2048]{1,0:T(8,128)(2,1)S(1)} %fusion.61), channel_id=1, source_target_pairs={{0,8},{4,12},{8,0},{12,4},{16,24},{20,28},{24,16},{28,20},{1,9},{5... | collective-permute-start | bytes 393224 | tf_op jit(solution)/shard_map/ppermute | solution.py:30
  (28 other events, 153.7 us)
Sparse Core Ops, SparseCore 0:
  165.2 43.2 reduce-scatter.4
  211.5 43.1 reduce-scatter.6
  257.0 26.4 reduce-scatter.8
  285.7 30.0 reduce-scatter.10

commit v7 on v6

--- a/solution.py
+++ b/solution.py
@@ -715,7 +715,7 @@
         out_shape=[pltpu.HBM((width + 2 * few, width), BF)] * 2,
         scratch_shapes=[pltpu.VMEM((2 * width, frames), BF)] * 2
         + [pltpu.VMEM((few, frames), BF)] * 2,
-        compiler_params=params(52),
+        compiler_params=params(34),
         cost_estimate=cost(6 * frames * width * width, 6 * width * width + 20 * frames * width),
     )(inputs, skips, features, grad_in, *grad_mods)
 

time: 343 us -> 343 us (level)
  local copies, waits for them, and re-layouts: 6.86 us -> 10.7 us
    ppermute x39, waiting for transfers between devices: 66.8 us -> 62.9 us  [swap(): return lax.ppermute(values, axis_name, [(i, i ^ bits) for i in range(size)])]
  transfers between devices with their start and end apart: 43 -> 43, of which waited for: 21 -> 21; matrix products, arithmetic and copies ran while one was open for 19% -> 20% of each run, Pallas kernels for 20% -> 19%
where the time goes in v7:
time: 343 us; the launch traced here: 339 us
  Pallas kernels  115 us (34%)
  waiting for transfers between devices  77.3 us (23%)
  other arithmetic  61.1 us (18%)
  starting transfers between devices  42.7 us (12%)
  matrix products  17.8 us (5%)
  between operations  14.9 us (4%)
  local copies, waits for them, and re-layouts  10.7 us (3%)
    ppermute x39, waiting for transfers between devices, swap(): return lax.ppermute(values, axis_name, [(i, i ^ bits) for i in range(size)])  62.9 us
    ppermute x39, starting transfers between devices, swap(): return lax.ppermute(values, axis_name, [(i, i ^ bits) for i in range(size)])  42.4 us
    pallas_call x1, Pallas kernels, feed(): pl.pallas_call(functools.partial(feed_kernel, groups, seq_blocks(width)),...  42.1 us
    convert_element_type x19, other arithmetic, add_low(): functools.reduce(jnp.add, [term.astype(F32) for term in terms]).astype(BF)  35.6 us
    pallas_call x1, Pallas kernels, attend_back(): pl.pallas_call(functools.partial(attend_back_kernel, span), grid=(pairs,)...  23.2 us
    pallas_call x1, Pallas kernels, near(): pl.pallas_call(functools.partial(near_kernel, groups, len(dkv)), grid=(4...  18.2 us
    dot_general x9, matrix products, dot(): return lax.dot_general(left, right, dims, preferred_element_type=F32)  17.8 us
    pallas_call x1, Pallas kernels, attend(): pl.pallas_call(functools.partial(attend_kernel, span), grid=(pairs,), in_...  17.2 us
  transfers between devices with their start and end apart: 43, of which 21 were waited for; matrix products, arithmetic and copies ran while one was open for 20% of the time, Pallas kernels for 19%

profile of v7, /device:TPU:0, one launch (start us, length us, event | category | flops | bytes accessed | tf_op | source)
XLA Modules:
  0.0 339.4 jit_solution(17844795228257284793)
XLA Ops:
  10.5 3.3 fusion.7
  17.2 1.9 fusion.33
  19.1 1.6 fusion.75
  20.9 2.6 collective-permute-start.1
  23.5 2.0 collective-permute-start.4
  26.9 1.6 collective-permute-start.2
  28.5 1.6 dynamic-slice_bitcast_fusion
  30.3 7.0 %collective-permute-done.2 = f32[4,4,3,128]{3,1,2,0:T(4,128)S(1)} collective-permute-done((f32[4,4,3,128]{3,1,2,0:T(4,128)S(1)}, f32[4,4,3,128]{3,1,2,0:T(4,128)S(1)}, u32[]{:S(2)}, u32[]{:S(2)}) %collective-permute-start.2) | collective-permute-done | bytes 24608 | tf_op jit(solution)/shard_map/ppermute | solution.py:30
  39.1 1.9 fusion.66
  42.2 7.7 %shard_map.187 = (bf16[512,1024]{1,0:T(8,128)(2,1)S(1)}, bf16[512,2048]{1,0:T(8,128)(2,1)S(1)}) custom-call(bf16[512,1024]{1,0:T(8,128)(2,1)S(1)} %constant_dynamic-update-slice_fusion.x_ref.refs_4_, bf16[1024,3072]{1,0:T(8,128)(2,1)S(1)} %bitcast.249, f32[512,128]{1,0:T(8,128)S(1)} %slice.125.cos_ref, f32[512,128]{1,0:T(8,128)S(1)} %slice.126.sin_ref), custom_call_target="tpu_custom_call" | custom-call | flops 3221225472 | bytes 10485760 | tf_op jit(solution)/shard_map/pallas_call | solution.py:222
  54.6 17.2 %shard_map.188 = (bf16[512,1024]{1,0:T(8,128)(2,1)S(1)}, bf16[16,1024,512]{2,1,0:T(8,128)(2,1)}, f32[8,8,512]{2,1,0:T(8,128)S(1)}) custom-call(bf16[512,1024]{1,0:T(8,128)(2,1)S(1)} %get-tuple-element.160.q_ref, bf16[512,2048]{1,0:T(8,128)(2,1)S(1)} %get-tuple-element.161.refs_0_.refs_2_, bf16[512,2048]{1,0:T(8,128)(2,1)S(1)} %collective-permute-done.6.refs_1_.refs_3_, ...), custom_call_target="tpu_custom_call" | custom-call | flops 8589934592 | bytes 16777216 | tf_op jit(solution)/shard_map/pallas_call | solution.py:300
  73.2 1.8 fusion.46.refs_8_
  79.7 42.1 %shard_map.189 = (bf16[2048,1024]{1,0:T(8,128)(2,1)}, bf16[2048,1024]{1,0:T(8,128)(2,1)}, bf16[512,4096]{1,0:T(8,128)(2,1)}, bf16[512,4096]{1,0:T(8,128)(2,1)}, ...) custom-call(bf16[512,1024]{1,0:T(8,128)(2,1)S(1)} %add_convert_fusio, ...), custom_call_target="tpu_custom_call" | custom-call | flops 25769803776 | bytes 33554432 | tf_op jit(solution)/shard_map/pallas_call | solution.py:508
  126.6 23.2 %shard_map.190 = (bf16[512,1024]{1,0:T(8,128)(2,1)}, bf16[2,512,1024]{2,1,0:T(8,128)(2,1)}, bf16[2,512,1024]{2,1,0:T(8,128)(2,1)}) custom-call(bf16[512,1024]{1,0:T(8,128)(2,1)} %copy-done.9, bf16[512,2048]{1,0:T(8,128)(2,1)} %copy-done.3, bf16[512,2048]{1,0:T(8,128)(2,1)} %copy-done.4, bf16[512,2048]{1,0:T(8,128)(2,1)} %copy-done.3, ...), custom_call_target="tpu_custom_call" | custom-call | flops 17179869184 | bytes 16777216 | tf_op jit(solution)/shard_map/pallas_call | solution.py:370
  149.9 6.1 %add_convert_fusion = (bf16[512,2048]{1,0:T(8,128)(2,1)}, bf16[512,2048]{1,0:T(8,128)(2,1)}) fusion(bf16[512,4096]{1,0:T(8,128)(2,1)} %collective-permute-done.11, bf16[512,4096]{1,0:T(8,128)(2,1)} %get-tuple-element.195), kind=kLoop, calls=%fused_computation | loop fusion | flops 8388608 | bytes 12582912 | tf_op jit(solution)/shard_map/convert_element_type | solution.py:62
  156.0 2.9 add_convert_fusion.5
  158.9 1.8 add_convert_fusion.4
  163.8 18.2 %shard_map.191 = (bf16[512,4096]{1,0:T(8,128)(2,1)}, bf16[512,4096]{1,0:T(8,128)(2,1)}, bf16[512,1024]{1,0:T(8,128)(2,1)S(1)}, bf16[512,1024]{1,0:T(8,128)(2,1)}, bf16[512,1024]{1,0:T(8,128)(2,1)}) custom-call(bf16[512,1024]{1,0:T(8,128)(2,1)} %get-tuple-element.204.refs_0_, bf16[2,512,1024]{2,1,0:T(8,128)(2,1)} %get-tuple-element.205.refs_1_, ...), custom_call_target="tpu_custom_call" | custom-call | flops 7516192768 | bytes 30408704 | tf_op jit(solution)/shard_map/pallas_call | solution.py:648
  182.0 4.6 %collective-permute-done.16 = bf16[1024,512]{1,0:T(8,128)(2,1)} collective-permute-done((bf16[1024,512]{1,0:T(8,128)(2,1)}, bf16[1024,512]{1,0:T(8,128)(2,1)}, u32[]{:S(2)}, u32[]{:S(2)}) %collective-permute-start.16) | collective-permute-done | bytes 1048608 | tf_op jit(solution)/shard_map/ppermute | solution.py:30
  187.7 2.4 fusion.31
  190.1 1.6 collective-permute-start.19
  196.5 2.6 add_convert_fusion.3
  199.2 2.6 add_convert_fusion.2
  201.7 10.3 %collective-permute-done.21 = bf16[128,1024]{1,0:T(8,128)(2,1)S(1)} collective-permute-done((bf16[128,1024]{1,0:T(8,128)(2,1)S(1)}, bf16[128,1024]{1,0:T(8,128)(2,1)S(1)}, u32[]{:S(2)}, u32[]{:S(2)}) %collective-permute-start.21) | collective-permute-done | bytes 262176 | tf_op jit(solution)/shard_map/ppermute | solution.py:30
  212.1 4.9 %collective-permute-done.23 = bf16[128,1024]{1,0:T(8,128)(2,1)S(1)} collective-permute-done((bf16[128,1024]{1,0:T(8,128)(2,1)S(1)}, bf16[128,1024]{1,0:T(8,128)(2,1)S(1)}, u32[]{:S(2)}, u32[]{:S(2)}) %collective-permute-start.23) | collective-permute-done | bytes 262176 | tf_op jit(solution)/shard_map/ppermute | solution.py:30
  220.2 2.4 fusion.30
  228.1 6.6 %shard_map.192 = (bf16[1536,1024]{1,0:T(8,128)(2,1)}, bf16[1536,1024]{1,0:T(8,128)(2,1)}) custom-call(bf16[512,1024]{1,0:T(8,128)(2,1)S(1)} %bitcast.253, bf16[512,1024]{1,0:T(8,128)(2,1)S(1)} %bitcast.251, bf16[512,256]{1,0:T(8,128)(2,1)S(1)} %pad_maximum_fusion.14.f_ref, bf16[512,1024]{1,0:T(8,128)(2,1)S(1)} %bitcast.247, ...), custom_call_target="tpu_custom_call" | custom-call | flops 3221225472 | bytes 16777216 | tf_op jit(solution)/shard_map/pallas_call | solution.py:710
  234.7 7.1 %collective-permute-done.24 = bf16[256,2048]{1,0:T(8,128)(2,1)} collective-permute-done((bf16[256,2048]{1,0:T(8,128)(2,1)}, bf16[256,2048]{1,0:T(8,128)(2,1)}, u32[]{:S(2)}, u32[]{:S(2)}) %collective-permute-start.24) | collective-permute-done | bytes 1048608 | tf_op jit(solution)/shard_map/ppermute | solution.py:30
  242.4 3.5 %fusion.23 = (bf16[128,2048]{1,0:T(8,128)(2,1)}, bf16[128,2048]{1,0:T(8,128)(2,1)}) fusion(bf16[1,2,128,2048]{3,2,1,0:T(8,128)(2,1)} %bitcast.75, s32[]{:T(128)S(6)} %select_n.213, bf16[1,2,2,128,4096]{4,3,2,1,0:T(8,128)(2,1)} %bitcast.43, s32[]{:T(128)S(6)} %select_n.217, bf16[1,2,2,128,4096]{4,3,2,1,0:T(8,128)(2,1)} %bitcast.258, ...), kind=kLoop, calls=%fused_computation.40 | loop fusion | flops 3145728 | bytes 4194320 | tf_op jit(solution)/shard_map/convert_element_type | solution.py:62
  248.9 1.7 constant_dynamic-slice_fusion.1
  250.6 2.3 add_convert_fusion.8
  252.9 2.3 add_convert_fusion.7
  255.2 5.5 %collective-permute-done.27 = bf16[128,2048]{1,0:T(8,128)(2,1)} collective-permute-done((bf16[128,2048]{1,0:T(8,128)(2,1)}, bf16[128,2048]{1,0:T(8,128)(2,1)}, u32[]{:S(2)}, u32[]{:S(2)}) %collective-permute-start.27) | collective-permute-done | bytes 524320 | tf_op jit(solution)/shard_map/ppermute | solution.py:30
  261.7 1.5 collective-permute-start.29
  263.8 2.8 fusion.26
  268.4 14.3 %reduce-scatter.9.cloned.1.call-done = bf16[128,1024]{1,0:T(8,128)(2,1)} async-done(((bf16[512,1024]{1,0:T(8,128)(2,1)}), bf16[128,1024]{1,0:T(8,128)(2,1)}) %reduce-scatter.9.cloned.1.call-update) | async-done | bytes 262160 | tf_op jit(solution)/shard_map/reduce_scatter | solution.py:141
  282.8 4.6 %fusion.12 = f32[4,1,128,1024]{3,2,1,0:T(8,128)} fusion(bf16[2048,1024]{1,0:T(8,128)(2,1)} %param.18, bf16[1,128,1024]{2,1,0:T(8,128)(2,1)} %get-tuple-element.344, bf16[1,128,1024]{2,1,0:T(8,128)(2,1)} %get-tuple-element.345, bf16[1,128,1024]{2,1,0:T(8,128)(2,1)} %get-tuple-element.346, bf16[1,128,1024]{2,1,0:T(8,128)(2,1)S(1)} %copy-done.19), kind=kOutput, calls=%fused_computation.25 | convolution fusion | flops 1075314688 | bytes 5242880 | tf_op jit(solution)/shard_map/dot_general | solution.py:25
  287.4 1.7 fusion.37
  289.1 1.5 collective-permute-start.31
  292.1 2.6 fusion.15
  294.8 5.1 %collective-permute-done.31 = bf16[384,512]{1,0:T(8,128)(2,1)S(1)} collective-permute-done((bf16[384,512]{1,0:T(8,128)(2,1)S(1)}, bf16[384,512]{1,0:T(8,128)(2,1)S(1)}, u32[]{:S(2)}, u32[]{:S(2)}) %collective-permute-start.31) | collective-permute-done | bytes 393248 | tf_op jit(solution)/shard_map/ppermute | solution.py:30
  301.1 1.8 fusion.40
  309.2 2.7 collective-permute-done.34
  313.1 3.9 %collective-permute-done.33 = bf16[192,1024]{1,0:T(8,128)(2,1)S(1)} collective-permute-done((bf16[192,1024]{1,0:T(8,128)(2,1)S(1)}, bf16[192,1024]{1,0:T(8,128)(2,1)S(1)}, u32[]{:S(2)}, u32[]{:S(2)}) %collective-permute-start.33) | collective-permute-done | bytes 393248 | tf_op jit(solution)/shard_map/ppermute | solution.py:30
  317.0 1.7 slice_convert_fusion
  318.8 2.5 collective-permute-start.36
  326.3 1.6 collective-permute-done.38
  327.9 2.4 collective-permute-done.36
  (230 shorter events, 68.9 us)
Async XLA Ops:
  7.2 209.8 %reduce-scatter.5.cloned.1.call-start = ((), (), s32[]{:S(2)}) async-start(), calls=%async_computation.4 | async-start | bytes 2621440 | tf_op jit(solution)/shard_map/reduce_scatter | solution.py:128
  9.3 11.5 %collective-permute-start = (f32[1,4,3,128]{3,1,2,0:T(4,128)S(1)}, f32[1,4,3,128]{3,1,2,0:T(4,128)S(1)}, u32[]{:S(2)}, u32[]{:S(2)}) collective-permute-start(f32[1,4,3,128]{3,1,2,0:T(4,128)S(1)} %bitcast.306), channel_id=1, source_target_pairs={{0,4},{4,0},{8,12},{12,8},{16,20},{20,16},{24,28},{28,24},{1,5},{5... | collective-permute-start | bytes 18440 | tf_op jit(solution)/shard_map/ppermute | solution.py:30
  20.9 6.1 %collective-permute-start.1 = (f32[2,4,3,128]{3,1,2,0:T(4,128)S(1)}, f32[2,4,3,128]{3,1,2,0:T(4,128)S(1)}, u32[]{:S(2)}, u32[]{:S(2)}) collective-permute-start(f32[2,4,3,128]{3,1,2,0:T(4,128)S(1)} %pad_maximum_fusion.18), channel_id=1, source_target_pairs={{0,8},{4,12},{8,0},{12,4},{16,24},{20,28},{24,16},{28,20},{1,9},{5... | collective-permute-start | bytes 36872 | tf_op jit(solution)/shard_map/ppermute | solution.py:30
  23.4 13.9 %collective-permute-start.3 = (bf16[128,1024]{1,0:T(8,128)(2,1)S(1)}, bf16[128,1024]{1,0:T(8,128)(2,1)S(1)}, u32[]{:S(2)}, u32[]{:S(2)}) collective-permute-start(bf16[128,1024]{1,0:T(8,128)(2,1)S(1)} %get-tuple-element.144), channel_id=1, source_target_pairs={{0,8},{4,12},{8,0},{12,4},{16,24},{20,28},{24,16},{28,20},{1,9},{5... | collective-permute-start | bytes 786440 | tf_op jit(solution)/shard_map/ppermute | solution.py:30
  23.5 13.8 %collective-permute-start.4 = (bf16[128,1024]{1,0:T(8,128)(2,1)S(1)}, bf16[128,1024]{1,0:T(8,128)(2,1)S(1)}, u32[]{:S(2)}, u32[]{:S(2)}) collective-permute-start(bf16[128,1024]{1,0:T(8,128)(2,1)S(1)} %get-tuple-element.145), channel_id=1, source_target_pairs={{0,16},{4,20},{8,24},{12,28},{16,0},{20,4},{24,8},{28,12},{1,17},{... | collective-permute-start | bytes 786440 | tf_op jit(solution)/shard_map/ppermute | solution.py:30
  25.5 12.9 %collective-permute-start.5 = (bf16[128,1024]{1,0:T(8,128)(2,1)S(1)}, bf16[128,1024]{1,0:T(8,128)(2,1)S(1)}, u32[]{:S(2)}, u32[]{:S(2)}) collective-permute-start(bf16[128,1024]{1,0:T(8,128)(2,1)S(1)} %get-tuple-element.146), channel_id=1, source_target_pairs={{0,24},{4,28},{8,16},{12,20},{16,8},{20,12},{24,0},{28,4},{1,25},{... | collective-permute-start | bytes 786440 | tf_op jit(solution)/shard_map/ppermute | solution.py:30
  26.9 10.4 %collective-permute-start.2 = (f32[4,4,3,128]{3,1,2,0:T(4,128)S(1)}, f32[4,4,3,128]{3,1,2,0:T(4,128)S(1)}, u32[]{:S(2)}, u32[]{:S(2)}) collective-permute-start(f32[4,4,3,128]{3,1,2,0:T(4,128)S(1)} %pad_maximum_fusion.17), channel_id=1, source_target_pairs={{0,16},{4,20},{8,24},{12,28},{16,0},{20,4},{24,8},{28,12},{1,17},{... | collective-permute-start | bytes 73736 | tf_op jit(solution)/shard_map/ppermute | solution.py:30
  49.9 21.9 %copy-start.3 = (bf16[512,2048]{1,0:T(8,128)(2,1)}, bf16[512,2048]{1,0:T(8,128)(2,1)S(1)}, u32[]{:S(2)}) copy-start(bf16[512,2048]{1,0:T(8,128)(2,1)S(1)} %get-tuple-element.161.refs_0_.refs_2_) | copy-start | bytes 6291460
  49.9 21.9 %copy-start.9 = (bf16[512,1024]{1,0:T(8,128)(2,1)}, bf16[512,1024]{1,0:T(8,128)(2,1)S(1)}, u32[]{:S(2)}) copy-start(bf16[512,1024]{1,0:T(8,128)(2,1)S(1)} %get-tuple-element.160.q_ref) | copy-start | bytes 3145732
  49.9 4.7 %collective-permute-start.6 = (bf16[512,2048]{1,0:T(8,128)(2,1)S(1)}, bf16[512,2048]{1,0:T(8,128)(2,1)S(1)}, u32[]{:S(2)}, u32[]{:S(2)}) collective-permute-start(bf16[512,2048]{1,0:T(8,128)(2,1)S(1)} %get-tuple-element.161.refs_0_.refs_2_), channel_id=1, source_target_pairs={{0,4},{4,0},{8,12},{12,8},{16,20},{20,16},{24,28},{28,24},{1,5},{5... | collective-permute-start | bytes 6291464 | tf_op jit(solution)/shard_map/ppermute | solution.py:30
  50.0 25.9 %collective-permute-start.7 = (bf16[128,2048]{1,0:T(8,128)(2,1)S(1)}, bf16[128,2048]{1,0:T(8,128)(2,1)S(1)}, u32[]{:S(2)}, u32[]{:S(2)}) collective-permute-start(bf16[128,2048]{1,0:T(8,128)(2,1)S(1)} %pad_maximum_fusion.7), channel_id=1, source_target_pairs={{0,8},{4,12},{8,0},{12,4},{16,24},{20,28},{24,16},{28,20},{1,9},{5... | collective-permute-start | bytes 1572872 | tf_op jit(solution)/shard_map/ppermute | solution.py:30
  51.5 25.3 %collective-permute-start.8 = (bf16[128,2048]{1,0:T(8,128)(2,1)S(1)}, bf16[128,2048]{1,0:T(8,128)(2,1)S(1)}, u32[]{:S(2)}, u32[]{:S(2)}) collective-permute-start(bf16[128,2048]{1,0:T(8,128)(2,1)S(1)} %pad_maximum_fusion.8), channel_id=1, source_target_pairs={{0,16},{4,20},{8,24},{12,28},{16,0},{20,4},{24,8},{28,12},{1,17},{... | collective-permute-start | bytes 1572872 | tf_op jit(solution)/shard_map/ppermute | solution.py:30
  53.0 23.8 %collective-permute-start.9 = (bf16[128,2048]{1,0:T(8,128)(2,1)S(1)}, bf16[128,2048]{1,0:T(8,128)(2,1)S(1)}, u32[]{:S(2)}, u32[]{:S(2)}) collective-permute-start(bf16[128,2048]{1,0:T(8,128)(2,1)S(1)} %pad_maximum_fusion.9), channel_id=1, source_target_pairs={{0,24},{4,28},{8,16},{12,20},{16,8},{20,12},{24,0},{28,4},{1,25},{... | collective-permute-start | bytes 1572872 | tf_op jit(solution)/shard_map/ppermute | solution.py:30
  54.6 17.2 %copy-start.4 = (bf16[512,2048]{1,0:T(8,128)(2,1)}, bf16[512,2048]{1,0:T(8,128)(2,1)S(1)}, u32[]{:S(2)}) copy-start(bf16[512,2048]{1,0:T(8,128)(2,1)S(1)} %collective-permute-done.6.refs_1_.refs_3_) | copy-start | bytes 6291460
  54.6 18.6 %copy-start.17 = (bf16[256,4096]{1,0:T(8,128)(2,1)S(1)}, bf16[256,4096]{1,0:T(8,128)(2,1)}, u32[]{:S(2)}) copy-start(bf16[256,4096]{1,0:T(8,128)(2,1)} %param.19) | copy-start | bytes 6291460
  121.7 28.0 %collective-permute-start.10 = (bf16[2048,1024]{1,0:T(8,128)(2,1)}, bf16[2048,1024]{1,0:T(8,128)(2,1)}, u32[]{:S(2)}, u32[]{:S(2)}) collective-permute-start(bf16[2048,1024]{1,0:T(8,128)(2,1)} %get-tuple-element.189), channel_id=1, source_target_pairs={{0,4},{4,0},{8,12},{12,8},{16,20},{20,16},{24,28},{28,24},{1,5},{5... | collective-permute-start | bytes 12582920 | tf_op jit(solution)/shard_map/ppermute | solution.py:30
  121.8 28.0 %collective-permute-start.11 = (bf16[512,4096]{1,0:T(8,128)(2,1)}, bf16[512,4096]{1,0:T(8,128)(2,1)}, u32[]{:S(2)}, u32[]{:S(2)}) collective-permute-start(bf16[512,4096]{1,0:T(8,128)(2,1)} %get-tuple-element.190), channel_id=1, source_target_pairs={{0,4},{4,0},{8,12},{12,8},{16,20},{20,16},{24,28},{28,24},{1,5},{5... | collective-permute-start | bytes 12582920 | tf_op jit(solution)/shard_map/ppermute | solution.py:30
  123.1 26.7 %collective-permute-start.12 = (bf16[128,1024]{1,0:T(8,128)(2,1)S(1)}, bf16[128,1024]{1,0:T(8,128)(2,1)}, u32[]{:S(2)}, u32[]{:S(2)}) collective-permute-start(bf16[128,1024]{1,0:T(8,128)(2,1)S(1)} %get-tuple-element.357), channel_id=1, source_target_pairs={{0,8},{4,12},{8,0},{12,4},{16,24},{20,28},{24,16},{28,20},{1,9},{5... | collective-permute-start | bytes 786440 | tf_op jit(solution)/shard_map/ppermute | solution.py:30
  124.5 25.3 %collective-permute-start.13 = (bf16[128,1024]{1,0:T(8,128)(2,1)S(1)}, bf16[128,1024]{1,0:T(8,128)(2,1)}, u32[]{:S(2)}, u32[]{:S(2)}) collective-permute-start(bf16[128,1024]{1,0:T(8,128)(2,1)S(1)} %get-tuple-element.356), channel_id=1, source_target_pairs={{0,16},{4,20},{8,24},{12,28},{16,0},{20,4},{24,8},{28,12},{1,17},{... | collective-permute-start | bytes 786440 | tf_op jit(solution)/shard_map/ppermute | solution.py:30
  126.0 23.8 %collective-permute-start.14 = (bf16[128,1024]{1,0:T(8,128)(2,1)S(1)}, bf16[128,1024]{1,0:T(8,128)(2,1)}, u32[]{:S(2)}, u32[]{:S(2)}) collective-permute-start(bf16[128,1024]{1,0:T(8,128)(2,1)S(1)} %get-tuple-element.355), channel_id=1, source_target_pairs={{0,24},{4,28},{8,16},{12,20},{16,8},{20,12},{24,0},{28,4},{1,25},{... | collective-permute-start | bytes 786440 | tf_op jit(solution)/shard_map/ppermute | solution.py:30
  149.8 6.2 %collective-permute-start.15 = (bf16[2,512,1024]{2,1,0:T(8,128)(2,1)}, bf16[2,512,1024]{2,1,0:T(8,128)(2,1)}, u32[]{:S(2)}, u32[]{:S(2)}) collective-permute-start(bf16[2,512,1024]{2,1,0:T(8,128)(2,1)} %get-tuple-element.199), channel_id=1, source_target_pairs={{0,4},{4,0},{8,12},{12,8},{16,20},{20,16},{24,28},{28,24},{1,5},{5... | collective-permute-start | bytes 6291464 | tf_op jit(solution)/shard_map/ppermute | solution.py:30
  160.8 25.9 %collective-permute-start.16 = (bf16[1024,512]{1,0:T(8,128)(2,1)}, bf16[1024,512]{1,0:T(8,128)(2,1)}, u32[]{:S(2)}, u32[]{:S(2)}) collective-permute-start(bf16[1024,512]{1,0:T(8,128)(2,1)} %bitcast.40), channel_id=1, source_target_pairs={{0,8},{4,12},{8,0},{12,4},{16,24},{20,28},{24,16},{28,20},{1,9},{5... | collective-permute-start | bytes 3145736 | tf_op jit(solution)/shard_map/ppermute | solution.py:30
  162.2 25.3 %collective-permute-start.17 = (bf16[1024,512]{1,0:T(8,128)(2,1)S(1)}, bf16[1024,512]{1,0:T(8,128)(2,1)}, u32[]{:S(2)}, u32[]{:S(2)}) collective-permute-start(bf16[1024,512]{1,0:T(8,128)(2,1)S(1)} %bitcast.275), channel_id=1, source_target_pairs={{0,16},{4,20},{8,24},{12,28},{16,0},{20,4},{24,8},{28,12},{1,17},{... | collective-permute-start | bytes 3145736 | tf_op jit(solution)/shard_map/ppermute | solution.py:30
  163.7 91.4 %reduce-scatter.7.cloned.1.call-start = ((), (), s32[]{:S(2)}) async-start(), calls=%async_computation.5 | async-start | bytes 2621440 | tf_op jit(solution)/shard_map/reduce_scatter | solution.py:128
  187.6 7.5 %collective-permute-start.18 = (bf16[512,4096]{1,0:T(8,128)(2,1)}, bf16[512,4096]{1,0:T(8,128)(2,1)}, u32[]{:S(2)}, u32[]{:S(2)}) collective-permute-start(bf16[512,4096]{1,0:T(8,128)(2,1)} %get-tuple-element.214), channel_id=1, source_target_pairs={{0,4},{4,0},{8,12},{12,8},{16,20},{20,16},{24,28},{28,24},{1,5},{5... | collective-permute-start | bytes 12582920 | tf_op jit(solution)/shard_map/ppermute | solution.py:30
  187.6 95.1 %reduce-scatter.9.cloned.1.call-start = ((), (), s32[]{:S(2)}) async-start(), calls=%async_computation.6 | async-start | bytes 1310720 | tf_op jit(solution)/shard_map/reduce_scatter | solution.py:141
  190.1 26.8 %collective-permute-start.19 = (bf16[512,512]{1,0:T(8,128)(2,1)S(1)}, bf16[512,512]{1,0:T(8,128)(2,1)S(1)}, u32[]{:S(2)}, u32[]{:S(2)}) collective-permute-start(bf16[512,512]{1,0:T(8,128)(2,1)S(1)} %get-tuple-element.218), channel_id=1, source_target_pairs={{0,16},{4,20},{8,24},{12,28},{16,0},{20,4},{24,8},{28,12},{1,17},{... | collective-permute-start | bytes 1572872 | tf_op jit(solution)/shard_map/ppermute | solution.py:30
  191.7 25.3 %collective-permute-start.20 = (bf16[512,512]{1,0:T(8,128)(2,1)S(1)}, bf16[512,512]{1,0:T(8,128)(2,1)S(1)}, u32[]{:S(2)}, u32[]{:S(2)}) collective-permute-start(bf16[512,512]{1,0:T(8,128)(2,1)S(1)} %get-tuple-element.219), channel_id=1, source_target_pairs={{0,8},{4,12},{8,0},{12,4},{16,24},{20,28},{24,16},{28,20},{1,9},{5... | collective-permute-start | bytes 1572872 | tf_op jit(solution)/shard_map/ppermute | solution.py:30
  192.3 19.7 %collective-permute-start.21 = (bf16[128,1024]{1,0:T(8,128)(2,1)S(1)}, bf16[128,1024]{1,0:T(8,128)(2,1)S(1)}, u32[]{:S(2)}, u32[]{:S(2)}) collective-permute-start(bf16[128,1024]{1,0:T(8,128)(2,1)S(1)} %get-tuple-element.353), channel_id=1, source_target_pairs={{0,8},{4,12},{8,0},{12,4},{16,24},{20,28},{24,16},{28,20},{1,9},{5... | collective-permute-start | bytes 786440 | tf_op jit(solution)/shard_map/ppermute | solution.py:30
  193.9 18.2 %collective-permute-start.22 = (bf16[128,1024]{1,0:T(8,128)(2,1)S(1)}, bf16[128,1024]{1,0:T(8,128)(2,1)S(1)}, u32[]{:S(2)}, u32[]{:S(2)}) collective-permute-start(bf16[128,1024]{1,0:T(8,128)(2,1)S(1)} %get-tuple-element.352), channel_id=1, source_target_pairs={{0,16},{4,20},{8,24},{12,28},{16,0},{20,4},{24,8},{28,12},{1,17},{... | collective-permute-start | bytes 786440 | tf_op jit(solution)/shard_map/ppermute | solution.py:30
  195.1 21.9 %collective-permute-start.23 = (bf16[128,1024]{1,0:T(8,128)(2,1)S(1)}, bf16[128,1024]{1,0:T(8,128)(2,1)S(1)}, u32[]{:S(2)}, u32[]{:S(2)}) collective-permute-start(bf16[128,1024]{1,0:T(8,128)(2,1)S(1)} %get-tuple-element.351), channel_id=1, source_target_pairs={{0,24},{4,28},{8,16},{12,20},{16,8},{20,12},{24,0},{28,4},{1,25},{... | collective-permute-start | bytes 786440 | tf_op jit(solution)/shard_map/ppermute | solution.py:30
  217.0 24.9 %collective-permute-start.24 = (bf16[256,2048]{1,0:T(8,128)(2,1)}, bf16[256,2048]{1,0:T(8,128)(2,1)}, u32[]{:S(2)}, u32[]{:S(2)}) collective-permute-start(bf16[256,2048]{1,0:T(8,128)(2,1)} %bitcast.44), channel_id=1, source_target_pairs={{0,8},{4,12},{8,0},{12,4},{16,24},{20,28},{24,16},{28,20},{1,9},{5... | collective-permute-start | bytes 3145736 | tf_op jit(solution)/shard_map/ppermute | solution.py:30
  217.7 24.5 %collective-permute-start.25 = (bf16[256,2048]{1,0:T(8,128)(2,1)}, bf16[256,2048]{1,0:T(8,128)(2,1)}, u32[]{:S(2)}, u32[]{:S(2)}) collective-permute-start(bf16[256,2048]{1,0:T(8,128)(2,1)} %bitcast.45), channel_id=1, source_target_pairs={{0,16},{4,20},{8,24},{12,28},{16,0},{20,4},{24,8},{28,12},{1,17},{... | collective-permute-start | bytes 3145736 | tf_op jit(solution)/shard_map/ppermute | solution.py:30
  242.1 8.4 %collective-permute-start.26 = (bf16[1536,1024]{1,0:T(8,128)(2,1)}, bf16[1536,1024]{1,0:T(8,128)(2,1)}, u32[]{:S(2)}, u32[]{:S(2)}) collective-permute-start(bf16[1536,1024]{1,0:T(8,128)(2,1)} %get-tuple-element.245), channel_id=1, source_target_pairs={{0,4},{4,0},{8,12},{12,8},{16,20},{20,16},{24,28},{28,24},{1,5},{5... | collective-permute-start | bytes 9437192 | tf_op jit(solution)/shard_map/ppermute | solution.py:30
  242.2 74.8 %reduce-scatter.11.cloned.1.call-start = ((), (), s32[]{:S(2)}) async-start(), calls=%async_computation.7 | async-start | bytes 1310720 | tf_op jit(solution)/shard_map/reduce_scatter | solution.py:141
  245.9 14.7 %collective-permute-start.27 = (bf16[128,2048]{1,0:T(8,128)(2,1)}, bf16[128,2048]{1,0:T(8,128)(2,1)}, u32[]{:S(2)}, u32[]{:S(2)}) collective-permute-start(bf16[128,2048]{1,0:T(8,128)(2,1)} %get-tuple-element.330), channel_id=1, source_target_pairs={{0,16},{4,20},{8,24},{12,28},{16,0},{20,4},{24,8},{28,12},{1,17},{... | collective-permute-start | bytes 1572872 | tf_op jit(solution)/shard_map/ppermute | solution.py:30
  247.3 14.4 %collective-permute-start.28 = (bf16[128,2048]{1,0:T(8,128)(2,1)}, bf16[128,2048]{1,0:T(8,128)(2,1)}, u32[]{:S(2)}, u32[]{:S(2)}) collective-permute-start(bf16[128,2048]{1,0:T(8,128)(2,1)} %get-tuple-element.329), channel_id=1, source_target_pairs={{0,8},{4,12},{8,0},{12,4},{16,24},{20,28},{24,16},{28,20},{1,9},{5... | collective-permute-start | bytes 1572872 | tf_op jit(solution)/shard_map/ppermute | solution.py:30
  261.7 21.0 %collective-permute-start.29 = (bf16[768,512]{1,0:T(8,128)(2,1)}, bf16[768,512]{1,0:T(8,128)(2,1)}, u32[]{:S(2)}, u32[]{:S(2)}) collective-permute-start(bf16[768,512]{1,0:T(8,128)(2,1)} %bitcast.283), channel_id=1, source_target_pairs={{0,8},{4,12},{8,0},{12,4},{16,24},{20,28},{24,16},{28,20},{1,9},{5... | collective-permute-start | bytes 2359304 | tf_op jit(solution)/shard_map/ppermute | solution.py:30
  263.3 19.5 %collective-permute-start.30 = (bf16[768,512]{1,0:T(8,128)(2,1)}, bf16[768,512]{1,0:T(8,128)(2,1)}, u32[]{:S(2)}, u32[]{:S(2)}) collective-permute-start(bf16[768,512]{1,0:T(8,128)(2,1)} %bitcast.282), channel_id=1, source_target_pairs={{0,16},{4,20},{8,24},{12,28},{16,0},{20,4},{24,8},{28,12},{1,17},{... | collective-permute-start | bytes 2359304 | tf_op jit(solution)/shard_map/ppermute | solution.py:30
  266.7 16.1 %copy-start.19 = (bf16[1,128,1024]{2,1,0:T(8,128)(2,1)S(1)}, bf16[1,128,1024]{2,1,0:T(8,128)(2,1)}, u32[]{:S(2)}) copy-start(bf16[1,128,1024]{2,1,0:T(8,128)(2,1)} %get-tuple-element.343) | copy-start | bytes 786436
  289.1 10.8 %collective-permute-start.31 = (bf16[384,512]{1,0:T(8,128)(2,1)S(1)}, bf16[384,512]{1,0:T(8,128)(2,1)S(1)}, u32[]{:S(2)}, u32[]{:S(2)}) collective-permute-start(bf16[384,512]{1,0:T(8,128)(2,1)S(1)} %get-tuple-element.340), channel_id=1, source_target_pairs={{0,16},{4,20},{8,24},{12,28},{16,0},{20,4},{24,8},{28,12},{1,17},{... | collective-permute-start | bytes 1179656 | tf_op jit(solution)/shard_map/ppermute | solution.py:30
  290.7 10.4 %collective-permute-start.32 = (bf16[384,512]{1,0:T(8,128)(2,1)S(1)}, bf16[384,512]{1,0:T(8,128)(2,1)S(1)}, u32[]{:S(2)}, u32[]{:S(2)}) collective-permute-start(bf16[384,512]{1,0:T(8,128)(2,1)S(1)} %get-tuple-element.339), channel_id=1, source_target_pairs={{0,8},{4,12},{8,0},{12,4},{16,24},{20,28},{24,16},{28,20},{1,9},{5... | collective-permute-start | bytes 1179656 | tf_op jit(solution)/shard_map/ppermute | solution.py:30
  303.1 13.9 %collective-permute-start.33 = (bf16[192,1024]{1,0:T(8,128)(2,1)S(1)}, bf16[192,1024]{1,0:T(8,128)(2,1)S(1)}, u32[]{:S(2)}, u32[]{:S(2)}) collective-permute-start(bf16[192,1024]{1,0:T(8,128)(2,1)S(1)} %pad_maximum_fusion.12), channel_id=1, source_target_pairs={{0,1},{1,0},{2,3},{3,2},{4,5},{5,4},{6,7},{7,6},{8,9},{9,8},{10,11... | collective-permute-start | bytes 1179656 | tf_op jit(solution)/shard_map/ppermute | solution.py:30
  305.1 6.8 %collective-permute-start.34 = (bf16[64,2048]{1,0:T(8,128)(2,1)S(1)}, bf16[64,2048]{1,0:T(8,128)(2,1)S(1)}, u32[]{:S(2)}, u32[]{:S(2)}) collective-permute-start(bf16[64,2048]{1,0:T(8,128)(2,1)S(1)} %bitcast.293), channel_id=1, source_target_pairs={{0,8},{4,12},{8,0},{12,4},{16,24},{20,28},{24,16},{28,20},{1,9},{5... | collective-permute-start | bytes 786440 | tf_op jit(solution)/shard_map/ppermute | solution.py:30
  306.6 6.5 %collective-permute-start.35 = (bf16[64,2048]{1,0:T(8,128)(2,1)S(1)}, bf16[64,2048]{1,0:T(8,128)(2,1)S(1)}, u32[]{:S(2)}, u32[]{:S(2)}) collective-permute-start(bf16[64,2048]{1,0:T(8,128)(2,1)S(1)} %bitcast.294), channel_id=1, source_target_pairs={{0,16},{4,20},{8,24},{12,28},{16,0},{20,4},{24,8},{28,12},{1,17},{... | collective-permute-start | bytes 786440 | tf_op jit(solution)/shard_map/ppermute | solution.py:30
  318.8 11.5 %collective-permute-start.36 = (bf16[96,1024]{1,0:T(8,128)(2,1)S(1)}, bf16[96,1024]{1,0:T(8,128)(2,1)S(1)}, u32[]{:S(2)}, u32[]{:S(2)}) collective-permute-start(bf16[96,1024]{1,0:T(8,128)(2,1)S(1)} %pad_maximum_fusion.15), channel_id=1, source_target_pairs={{0,2},{1,3},{2,0},{3,1},{4,6},{5,7},{6,4},{7,5},{8,10},{9,11},{10,... | collective-permute-start | bytes 589832 | tf_op jit(solution)/shard_map/ppermute | solution.py:30
  321.3 5.0 %collective-permute-start.37 = (bf16[32,2048]{1,0:T(8,128)(2,1)S(1)}, bf16[32,2048]{1,0:T(8,128)(2,1)S(1)}, u32[]{:S(2)}, u32[]{:S(2)}) collective-permute-start(bf16[32,2048]{1,0:T(8,128)(2,1)S(1)} %fusion.62), channel_id=1, source_target_pairs={{0,16},{4,20},{8,24},{12,28},{16,0},{20,4},{24,8},{28,12},{1,17},{... | collective-permute-start | bytes 393224 | tf_op jit(solution)/shard_map/ppermute | solution.py:30
  322.9 5.0 %collective-permute-start.38 = (bf16[32,2048]{1,0:T(8,128)(2,1)S(1)}, bf16[32,2048]{1,0:T(8,128)(2,1)S(1)}, u32[]{:S(2)}, u32[]{:S(2)}) collective-permute-start(bf16[32,2048]{1,0:T(8,128)(2,1)S(1)} %fusion.61), channel_id=1, source_target_pairs={{0,8},{4,12},{8,0},{12,4},{16,24},{20,28},{24,16},{28,20},{1,9},{5... | collective-permute-start | bytes 393224 | tf_op jit(solution)/shard_map/ppermute | solution.py:30
  (29 other events, 156.1 us)
Sparse Core Ops, SparseCore 0:
  163.9 43.2 reduce-scatter.4
  210.1 43.1 reduce-scatter.6
  256.2 26.4 reduce-scatter.8
  285.0 29.7 reduce-scatter.10
